TPU v7x, 32 devices: a whole 2x2x4 slice. The times are simulated.
32 devices in a mesh: grp: 2 (over y), brick: 4 (over z), vec: 2 (over x), sub: 2 (over core).
Axes of the slice: x: 2, y: 2, z: 4, core: 2. Of those that a mesh axis runs over, the one named last changes fastest.
Arguments:
- vectors: float32 [128, 3, 2, 16384], P(('vec', 'sub'), None, None, ('grp', 'brick')), parts along dimension 3, may hold values from -6 to 6
- gauge_links: float32 [3, 3, 3, 2, 16384], P(None, None, None, None, ('grp', 'brick')), parts along dimension 4, may hold values from -1 to 1, as said below
- momenta: int32 [27, 3], replicated, may hold values from -3 to 3
Outputs:
- elementals: float32 [128, 54, 2, 128], P(('vec', 'sub'), 'grp', None, 'brick'), parts along dimension 1
There are 2 independent parts, one for each index of `grp`. A program takes and returns all parts, laid end to end along the dimension named above; an argument that names none is the same for every part. Nothing has to cross between parts.
Inputs may be any that keep to these rules, and one draw needn't show every extreme that they name: Each gauge_links[mu, :, :, :, s] is a unitary 3x3 complex matrix.
All inputs are finite; a program needn't handle non-finite values.
Results may differ from a plain program's by a relative error of at most 0.0049.
Values may be sent and summed in bfloat16 or wider, within the bound.
No kernel may reach another device: no remote copies, remote signals or barrier semaphores. Data moves between devices by JAX's collectives and lax.ppermute only.
A program may use at most 128 MiB of HBM per device.

v0:
```python
import math

import jax
import jax.numpy as jnp
from jax import lax
from jax.sharding import PartitionSpec as P

LY = 64
LZ = 8
ITERS = 2


KAPPA = 0.125


def from_behind(array, axis, by):
    peers = lax.axis_size(axis)
    return lax.ppermute(array, axis, [(i, (i + by) % peers) for i in range(peers)])


def padded_2(array, sides, width):
    for axis, dim in sides:
        peers, length = (lax.axis_size(axis), array.shape[dim])
        up = [(i, (i + 1) % peers) for i in range(peers)]
        down = [(j, i) for i, j in up]
        last = lax.slice_in_dim(array, length - width, length, axis=dim)
        initial = lax.slice_in_dim(array, 0, width, axis=dim)
        before = lax.ppermute(last, axis, up)
        after = lax.ppermute(initial, axis, down)
        array = jnp.concatenate([before, array, after], axis=dim)
    return array


def matrix_apply(matrix, source):
    matrix_real = matrix[:, :, 0][None]
    matrix_imag = matrix[:, :, 1][None]
    source_real = source[:, None, :, 0]
    source_imag = source[:, None, :, 1]
    real_part = jnp.sum(matrix_real * source_real - matrix_imag * source_imag, axis=2)
    imag_part = jnp.sum(matrix_real * source_imag + matrix_imag * source_real, axis=2)
    return jnp.stack([real_part, imag_part], axis=2)


def adjoint(matrix):
    return jnp.stack(
        [jnp.swapaxes(matrix[:, :, 0], 0, 1), -jnp.swapaxes(matrix[:, :, 1], 0, 1)], axis=2
    )


def step_depth(values, offset):
    depth_index = lax.iota(jnp.int32, values.shape[-1]) % LZ
    if offset > 0:
        return jnp.where(
            depth_index == LZ - 1, jnp.roll(values, LZ - 1, -1), jnp.roll(values, -1, -1)
        )
    return jnp.where(depth_index == 0, jnp.roll(values, 1 - LZ, -1), jnp.roll(values, 1, -1))


def step_column(values, offset):
    plane = LY * LZ
    column_index = lax.iota(jnp.int32, values.shape[-1]) // LZ % LY
    if offset > 0:
        return jnp.where(
            column_index == LY - 1, jnp.roll(values, plane - LZ, -1), jnp.roll(values, -LZ, -1)
        )
    return jnp.where(column_index == 0, jnp.roll(values, LZ - plane, -1), jnp.roll(values, LZ, -1))


def laplace_step(center, ahead, behind, here_links, back_links):
    forward = matrix_apply(here_links[0], ahead)
    backward = matrix_apply(adjoint(back_links), behind)
    total = forward + backward
    for direction, stepper in ((1, step_column), (2, step_depth)):
        forward = matrix_apply(here_links[direction], stepper(center, 1))
        backward = matrix_apply(adjoint(stepper(here_links[direction], -1)), stepper(center, -1))
        total = total + (forward + backward)
    return center + KAPPA * (total - 6.0 * center)


def shards(vectors, gauge_links, momenta):
    plane = LY * LZ
    local_sites = vectors.shape[3]
    raw_low = vectors.astype(jnp.bfloat16)
    field = vectors
    x_links = gauge_links[0]
    rim = from_behind(x_links[..., local_sites - plane :], "brick", 1)
    back_links = jnp.concatenate([rim, x_links[..., : local_sites - plane]], axis=3)
    for step in range(ITERS):
        padded = padded_2(field, (("brick", 3),), plane)
        field = laplace_step(
            padded[..., plane : plane + local_sites],
            padded[..., 2 * plane :],
            padded[..., :local_sites],
            gauge_links,
            back_links,
        )
    smeared_low = field.astype(jnp.bfloat16)
    raw_sites, smeared_sites = (
        lax.all_to_all(raw_low, ("vec", "sub"), split_axis=3, concat_axis=0, tiled=True),
        lax.all_to_all(smeared_low, ("vec", "sub"), split_axis=3, concat_axis=0, tiled=True),
    )
    groups = lax.axis_size(("vec", "sub"))
    total_vec = raw_sites.shape[0]
    width = raw_sites.shape[3]
    total_x = lax.axis_size("brick") * (local_sites // plane)
    first_site = lax.axis_index("brick") * local_sites + lax.axis_index(("vec", "sub")) * width
    site = first_site + lax.iota(jnp.int32, width)
    layer_index = (site // plane)[None]
    column_index = (site // LZ % LY)[None]
    depth_index = (site % LZ)[None]
    fraction = (
        jnp.mod(momenta[:, 0:1] * layer_index, total_x).astype(jnp.float32) / total_x
        + jnp.mod(momenta[:, 1:2] * column_index, LY).astype(jnp.float32) / LY
        + jnp.mod(momenta[:, 2:3] * depth_index, LZ).astype(jnp.float32) / LZ
    )
    angle = 2.0 * math.pi * fraction
    cosines = jnp.cos(angle)
    sines = jnp.sin(angle)
    right = smeared_sites.reshape((total_vec, 6 * width))
    scale = (3.0 * total_x * plane) ** (-0.5)

    def one_momentum(angles):
        cosine, sine = angles
        real_part = raw_sites[:, :, 0] * cosine - raw_sites[:, :, 1] * sine
        imag_part = raw_sites[:, :, 0] * sine + raw_sites[:, :, 1] * cosine
        phased = jnp.stack([real_part, imag_part], axis=2).astype(jnp.bfloat16)
        turned = jnp.stack([-phased[:, :, 1], phased[:, :, 0]], axis=2)
        left = jnp.concatenate(
            [
                phased.reshape((lax.axis_size(("vec", "sub")) * (total_vec // groups), 6 * width)),
                turned.reshape((lax.axis_size(("vec", "sub")) * (total_vec // groups), 6 * width)),
            ],
            axis=0,
        )
        product = lax.dot_general(
            left, right, (((1,), (1,)), ((), ())), preferred_element_type=jnp.float32
        )
        return product.reshape(
            (2, lax.axis_size(("vec", "sub")) * (total_vec // groups), total_vec)
        )

    blocks = lax.map(one_momentum, (cosines, sines))
    shares = lax.psum_scatter(
        jnp.transpose(blocks, (2, 0, 1, 3)) * scale, ("vec", "sub"), scatter_dimension=0, tiled=True
    )
    return lax.psum_scatter(shares, "brick", scatter_dimension=3, tiled=True)


def solution(mesh):
    in_specs = (
        P(("vec", "sub"), None, None, ("grp", "brick")),
        P(None, None, None, None, ("grp", "brick")),
        P(),
    )
    out_specs = P(("vec", "sub"), "grp", None, "brick")
    return jax.shard_map(shards, mesh=mesh, in_specs=in_specs, out_specs=out_specs, check_vma=False)
```

profile of v0, /device:TPU:0, one launch (start us, length us, event | category | flops | bytes accessed | tf_op | source)
XLA Modules:
  0.0 437.9 jit_solution(8413157391000246804)
XLA Ops:
  8.2 3.0 collective-permute-start.1
  17.3 5.7 %copy.252 = bf16[32,3,2,2048]{0,2,1,3:T(2,128)(2,1)} copy(bf16[32,3,2,2048]{3,0,2,1:T(8,128)(2,1)S(1)} %copy.339) | data formatting | bytes 1572864 | tf_op jit(solution)/shard_map/convert_element_type | solution.py:83
  23.0 5.4 %reshape.114 = bf16[4,2,49152]{2,1,0:T(2,128)(2,1)} reshape(bf16[2048,3,2,32]{3,2,1,0:T(2,128)(2,1)} %bitcast.170) | data formatting | bytes 1572864
  28.4 4.7 %all-to-all-start = ((bf16[4,2,49152]{2,1,0:T(2,128)(2,1)}), bf16[4,2,49152]{2,1,0:T(2,128)(2,1)}, u32[]{:S(2)}, u32[]{:S(2)}) async-start(bf16[4,2,49152]{2,1,0:T(2,128)(2,1)} %reshape.114), calls=%async_computation | async-start | bytes 1572864 | tf_op jit(solution)/shard_map/all_to_all | solution.py:99
  72.9 2.4 collective-permute-start.3
  82.0 3.2 collective-permute-done.4
  85.3 7.2 %collective-permute-done.3 = f32[32,3,2,512]{3,0,2,1:T(8,128)S(1)} collective-permute-done((f32[32,3,2,512]{3,0,2,1:T(8,128)S(1)}, f32[32,3,2,512]{3,0,2,1:T(8,128)S(1)}, u32[]{:S(2)}, u32[]{:S(2)}) %collective-permute-start.3) | collective-permute-done | bytes 393248 | tf_op jit(solution)/shard_map/ppermute | solution.py:29
  94.1 3.8 fusion.17
  97.9 7.5 %copy.282 = bf16[32,3,2,2048]{0,2,1,3:T(2,128)(2,1)S(1)} copy(bf16[32,3,2,2048]{3,0,2,1:T(8,128)(2,1)} %fusion.17) | data formatting | bytes 1572864 | tf_op jit(solution)/shard_map/convert_element_type | solution.py:97
  105.4 3.8 reshape.116
  109.2 3.6 all-to-all-start.1
  113.4 4.5 %reshape.115 = bf16[2048,3,2,32]{3,2,1,0:T(2,128)(2,1)} reshape(bf16[4,2,49152]{2,1,0:T(2,128)(2,1)} %all-to-all-done) | data formatting | bytes 1572864
  117.9 6.7 %copy.253 = bf16[4,32,3,2,512]{4,1,0,3,2:T(8,128)(2,1)S(1)} copy(bf16[4,32,3,2,512]{1,3,2,4,0:T(2,128)(2,1)} %bitcast.172) | data formatting | bytes 1572864 | tf_op jit(solution)/shard_map/all_to_all | solution.py:99
  124.7 2.9 reshape.117
  127.6 7.3 %copy.283 = bf16[4,32,3,2,512]{4,3,2,1,0:T(2,128)(2,1)S(1)} copy(bf16[4,32,3,2,512]{1,3,2,4,0:T(2,128)(2,1)} %bitcast.173) | data formatting | bytes 1572864 | tf_op jit(solution)/shard_map/all_to_all | solution.py:100
  136.3 98.4 %while.10 = (s32[]{:T(128)}, f32[27,2,128,128]{3,2,1,0:T(8,128)}, bf16[128,3,2,512]{3,0,2,1:T(8,128)(2,1)S(1)}, f32[27,512]{1,0:T(8,128)S(1)}, f32[27,512]{1,0:T...) while((s32[]{:T(128)}, f32[27,2,128,128]{3,2,1,0:T(8,128)}, bf16[128,3,2,512]{3,0,2,1:T(8,128)(2,1)S(1)}, ...), condition=%wide.region_25.26_spmd, body=%wide.region_24.25_spmd.sunk | while | flops 207421440 | bytes 12202077 | solution.py:142
  234.7 2.3 multiply_bitcast_fusion
  237.1 4.5 %copy.284 = f32[128,27,2,128]{3,2,1,0:T(2,128)} copy(f32[128,27,2,128]{3,0,2,1:T(8,128)S(1)} %multiply_bitcast_fusion) | data formatting | bytes 7077888 | tf_op jit(solution)/shard_map/mul | solution.py:144
  243.5 74.1 %all-reduce.3.cloned.1.call-done = f32[128,27,2,128]{3,2,1,0:T(2,128)} async-done(((f32[128,27,2,128]{3,2,1,0:T(2,128)}), f32[128,27,2,128]{3,2,1,0:T(2,128)}) %all-reduce.3.cloned.1.call-update) | async-done | bytes 3538960
  318.8 33.9 %copy.285 = f32[32,27,2,128]{2,1,0,3:T(8,128)} copy(f32[32,27,2,128]{3,2,1,0:T(2,128)S(1)} %constant_dynamic-slice_fusion.2) | data formatting | bytes 1769472
  352.7 31.7 %reshape.111 = f32[128,1728]{1,0:T(8,128)} reshape(f32[128,32,27,2]{3,2,1,0:T(8,128)} %bitcast.71) | data formatting | bytes 1769472
  384.4 25.4 %reduce-scatter.4.cloned.1.call-done = f32[32,1728]{1,0:T(8,128)} async-done(((f32[128,1728]{1,0:T(8,128)}), f32[32,1728]{1,0:T(8,128)}) %reduce-scatter.4.cloned.1.call-update) | async-done | bytes 221200
  409.8 8.8 %reshape.112 = f32[32,32,27,2]{3,2,1,0:T(8,128)} reshape(f32[32,1728]{1,0:T(8,128)} %reduce-scatter.4.cloned.1.call-done) | data formatting | bytes 442368
  418.6 11.9 %copy.286 = f32[32,27,2,32]{3,2,1,0:T(2,128)} copy(f32[32,27,2,32]{2,1,0,3:T(8,128)} %bitcast.166) | data formatting | bytes 442368
  (409 shorter events, 156.7 us)
Async XLA Ops:
  8.2 8.2 %copy-start = (f32[32,3,2,2048]{3,2,1,0:T(2,128)S(1)}, f32[32,3,2,2048]{3,2,1,0:T(2,128)}, u32[]{:S(2)}) copy-start(f32[32,3,2,2048]{3,2,1,0:T(2,128)} %param.5) | copy-start | bytes 4718596
  8.2 51.1 %collective-permute-start.1 = (f32[3,3,2,512]{3,2,1,0:T(2,128)}, f32[3,3,2,512]{3,2,1,0:T(2,128)S(1)}, u32[]{:S(2)}, u32[]{:S(2)}) collective-permute-start(f32[3,3,2,512]{3,2,1,0:T(2,128)} %slice.441), channel_id=1, source_target_pairs={{0,4},{4,8},{8,12},{12,0},{1,5},{5,9},{9,13},{13,1},{2,6},{6,10},{... | collective-permute-start | bytes 110600 | tf_op jit(solution)/shard_map/ppermute | solution.py:18
  13.5 49.2 %collective-permute-start = (f32[32,3,2,512]{3,0,2,1:T(8,128)}, f32[32,3,2,512]{3,0,2,1:T(8,128)}, u32[]{:S(2)}, u32[]{:S(2)}) collective-permute-start(f32[32,3,2,512]{3,0,2,1:T(8,128)} %copy.321), channel_id=1, source_target_pairs={{4,0},{8,4},{12,8},{0,12},{5,1},{9,5},{13,9},{1,13},{6,2},{10,6},{... | collective-permute-start | bytes 1179656 | tf_op jit(solution)/shard_map/ppermute | solution.py:29
  16.4 44.1 %collective-permute-start.2 = (f32[32,3,2,512]{3,0,2,1:T(8,128)}, f32[32,3,2,512]{3,0,2,1:T(8,128)}, u32[]{:S(2)}, u32[]{:S(2)}) collective-permute-start(f32[32,3,2,512]{3,0,2,1:T(8,128)} %copy.322), channel_id=1, source_target_pairs={{0,4},{4,8},{8,12},{12,0},{1,5},{5,9},{9,13},{13,1},{2,6},{6,10},{... | collective-permute-start | bytes 1179656 | tf_op jit(solution)/shard_map/ppermute | solution.py:28
  28.4 80.8 %all-to-all-start = ((bf16[4,2,49152]{2,1,0:T(2,128)(2,1)}), bf16[4,2,49152]{2,1,0:T(2,128)(2,1)}, u32[]{:S(2)}, u32[]{:S(2)}) async-start(bf16[4,2,49152]{2,1,0:T(2,128)(2,1)} %reshape.114), calls=%async_computation | async-start | bytes 1572864 | tf_op jit(solution)/shard_map/all_to_all | solution.py:99
  42.8 14.1 %copy-start.7 = (f32[3,3,1,2048]{3,1,2,0:T(4,128)}, f32[3,3,1,2048]{3,1,2,0:T(4,128)S(1)}, u32[]{:S(2)}) copy-start(f32[3,3,1,2048]{3,1,2,0:T(4,128)S(1)} %copy.343) | copy-start | bytes 221188
  42.9 14.0 %copy-start.9 = (f32[3,3,1,2048]{3,1,2,0:T(4,128)}, f32[3,3,1,2048]{3,1,2,0:T(4,128)S(1)}, u32[]{:S(2)}) copy-start(f32[3,3,1,2048]{3,1,2,0:T(4,128)S(1)} %copy.342) | copy-start | bytes 221188
  52.6 2.5 copy-start.17
  52.6 2.5 copy-start.19
  63.8 0.9 copy-start.12
  63.9 1.6 copy-start.5
  63.9 1.6 copy-start.6
  64.8 1.3 copy-start.1
  64.8 1.5 copy-start.2
  64.8 1.7 copy-start.3
  64.8 2.0 copy-start.4
  71.4 13.9 %collective-permute-start.4 = (f32[32,3,2,512]{3,0,2,1:T(8,128)S(1)}, f32[32,3,2,512]{3,0,2,1:T(8,128)S(1)}, u32[]{:S(2)}, u32[]{:S(2)}) collective-permute-start(f32[32,3,2,512]{3,0,2,1:T(8,128)S(1)} %get-tuple-element.114), channel_id=1, source_target_pairs={{0,4},{4,8},{8,12},{12,0},{1,5},{5,9},{9,13},{13,1},{2,6},{6,10},{... | collective-permute-start | bytes 1179656 | tf_op jit(solution)/shard_map/ppermute | solution.py:28
  72.9 19.6 %collective-permute-start.3 = (f32[32,3,2,512]{3,0,2,1:T(8,128)S(1)}, f32[32,3,2,512]{3,0,2,1:T(8,128)S(1)}, u32[]{:S(2)}, u32[]{:S(2)}) collective-permute-start(f32[32,3,2,512]{3,0,2,1:T(8,128)S(1)} %get-tuple-element.115), channel_id=1, source_target_pairs={{4,0},{8,4},{12,8},{0,12},{5,1},{9,5},{13,9},{1,13},{6,2},{10,6},{... | collective-permute-start | bytes 1179656 | tf_op jit(solution)/shard_map/ppermute | solution.py:29
  78.8 0.9 copy-start.10
  79.8 0.9 copy-start.16
  109.2 3.7 copy-start.21
  109.2 15.4 %all-to-all-start.1 = ((bf16[4,2,49152]{2,1,0:T(2,128)(2,1)}), bf16[4,2,49152]{2,1,0:T(2,128)(2,1)S(1)}, u32[]{:S(2)}, u32[]{:S(2)}) async-start(bf16[4,2,49152]{2,1,0:T(2,128)(2,1)} %reshape.116), calls=%async_computation.1 | async-start | bytes 1572864 | tf_op jit(solution)/shard_map/all_to_all | solution.py:100
  112.8 204.7 %all-reduce.3.cloned.1.call-start = ((), (), s32[]{:S(2)}) async-start(), calls=%async_computation.4 | async-start | bytes 7077888
  241.6 168.2 %reduce-scatter.4.cloned.1.call-start = ((), (), s32[]{:S(2)}) async-start(), calls=%async_computation.3 | async-start | bytes 1146880
  (8 other events, 6.7 us)
Sparse Core Ops, SparseCore 0:
  241.7 75.7 all-reduce.2
  384.5 25.2 reduce-scatter.3
where the time goes:
time: 443 us; the launch traced here: 438 us
  local copies, waits for them, and re-layouts  208 us (47%)
  waiting for transfers between devices  110 us (25%)
  matrix products  47 us (11%)
  other arithmetic  38.3 us (9%)
  starting transfers between devices  17.5 us (4%)
  between operations  15.4 us (3%)
    unnamed x81, local copies, waits for them, and re-layouts  119 us
    unnamed x4, waiting for transfers between devices  99.5 us
    dot_general x27, matrix products, one_momentum(): lax.dot_general(left, right, (((1,), (1,)), ((), ())), preferred_element_...  47 us
    dynamic_update_slice x27, local copies, waits for them, and re-layouts, shards(): blocks = lax.map(one_momentum, (cosines, sines))  17.9 us
    reduce_sum x12, other arithmetic, matrix_apply(): jnp.sum(matrix_real * source_real - matrix_imag * source_imag, axis=2)  11.3 us
    convert_element_type x27, local copies, waits for them, and re-layouts, one_momentum(): phased = jnp.stack([real_part, imag_part], axis=2).astype(jnp.bfloat16)  9.99 us
    another operation x27, local copies, waits for them, and re-layouts, one_momentum(): turned = jnp.stack([-phased[:, :, 1], phased[:, :, 0]], axis=2)  9.99 us
  transfers between devices with their start and end apart: 9, of which 4 were waited for; matrix products, arithmetic and copies ran while one was open for 19% of the time, Pallas kernels for 0%

commit v1 on v0

v1 whole, which is shorter than its diff:
```python
import functools
import math

import jax
import jax.numpy as jnp
from jax import lax
from jax.experimental import pallas as pl
from jax.experimental.pallas import tpu as pltpu
from jax.sharding import PartitionSpec as P

LY = 64
LZ = 8
ITERS = 2
KAPPA = 0.125
LANES = 128
ROWS = 16
VMEM_LIMIT = 56 * 1024 * 1024
VMEM = pl.BlockSpec(memory_space=pltpu.VMEM)
SMEM = pl.BlockSpec(memory_space=pltpu.SMEM)


def shifted(array, axis, by):
    peers = lax.axis_size(axis)
    return lax.ppermute(array, axis, [(i, (i + by) % peers) for i in range(peers)])


def link_row(direction, row, column, part):
    return ((direction * 3 + row) * 3 + column) * 2 + part


def add_hop(total, link, field, adjoint):
    for row in range(3):
        for column in range(3):
            if adjoint:
                real, imag = link(column, row, 0), link(column, row, 1)
            else:
                real, imag = link(row, column, 0), link(row, column, 1)
            source_real, source_imag = field[2 * column], field[2 * column + 1]
            if adjoint:
                add_real = real * source_real + imag * source_imag
                add_imag = real * source_imag - imag * source_real
            else:
                add_real = real * source_real - imag * source_imag
                add_imag = real * source_imag + imag * source_real
            for part, add in ((0, add_real), (1, add_imag)):
                old = total[2 * row + part]
                total[2 * row + part] = add if old is None else old + add


def group_size(ref):
    return min(ROWS, ref.shape[1])


def group_rows(group, ref):
    size = group_size(ref)
    return pl.ds(pl.multiple_of(group * size, size), size)


def lane_roll(value, by):
    return pltpu.roll(value, by % value.shape[-1], value.ndim - 1)


def depth_shift(value, offset):
    tiles = []
    depth = lax.broadcasted_iota(jnp.int32, (value.shape[0], LANES), 1) % LZ
    for start in range(0, value.shape[-1], LANES):
        tile = value[:, start : start + LANES]
        if offset > 0:
            tile = jnp.where(depth == LZ - 1, lane_roll(tile, LZ - 1), lane_roll(tile, -1))
        else:
            tile = jnp.where(depth == 0, lane_roll(tile, 1 - LZ), lane_roll(tile, 1))
        tiles.append(tile)
    return jnp.concatenate(tiles, axis=1)


def column_shift(value, offset):
    return lane_roll(value, -offset * LZ)


def smear_layer(layer, layers, group, field_ref, link_ref, back_ref, ahead_ref, behind_ref):
    plane = LY * LZ
    rows = group_rows(group, field_ref)
    here = pl.ds(layer * plane, plane)

    def load(ref, lanes):
        return [ref[k, rows, lanes].astype(jnp.float32) for k in range(6)]

    def links(ref, direction, lanes):
        return lambda r, c, part: ref[pl.ds(link_row(direction, r, c, part), 1), lanes]

    center = load(field_ref, here)
    if layer == layers - 1:
        ahead = load(ahead_ref, pl.ds(0, plane))
    else:
        ahead = load(field_ref, pl.ds((layer + 1) * plane, plane))
    total = [None] * 6
    add_hop(total, links(link_ref, 0, here), ahead, False)
    if layer == 0:
        behind = load(behind_ref, pl.ds(0, plane))
        total = [a + b for a, b in zip(total, behind)]
    else:
        before = pl.ds((layer - 1) * plane, plane)
        add_hop(total, links(link_ref, 0, before), load(field_ref, before), True)
    for direction, shift in ((1, column_shift), (2, depth_shift)):
        add_hop(total, links(link_ref, direction, here), [shift(v, 1) for v in center], False)
        add_hop(total, links(back_ref, direction - 1, here), [shift(v, -1) for v in center], True)
    return [c + KAPPA * (t - 6.0 * c) for c, t in zip(center, total)]


def smear_kernel(last, field_ref, link_ref, back_ref, ahead_ref, behind_ref, out_ref, *edges):
    plane = LY * LZ
    layers = field_ref.shape[2] // plane
    for layer in range(layers):
        here = pl.ds(layer * plane, plane)

        @pl.loop(0, field_ref.shape[1] // group_size(field_ref))
        def _(group):
            rows = group_rows(group, field_ref)
            new = smear_layer(layer, layers, group, field_ref, link_ref, back_ref, ahead_ref, behind_ref)
            for k in range(6):
                out_ref[k, rows, here] = new[k]

    if not last:
        first_ref, turned_ref = edges
        write_edges(out_ref, link_ref, first_ref, turned_ref)


def write_edges(field_ref, link_ref, first_ref, turned_ref):
    plane = LY * LZ
    end = pl.ds(field_ref.shape[2] - plane, plane)
    first_ref[...] = field_ref[:, :, pl.ds(0, plane)].astype(jnp.bfloat16)

    @pl.loop(0, field_ref.shape[1] // group_size(field_ref))
    def _(group):
        rows = group_rows(group, field_ref)
        turned = [None] * 6
        source = [field_ref[k, rows, end] for k in range(6)]
        add_hop(turned, lambda r, c, part: link_ref[pl.ds(link_row(0, r, c, part), 1), end], source, True)
        for k in range(6):
            turned_ref[k, rows, :] = turned[k].astype(jnp.bfloat16)


def edge_kernel(field_ref, link_ref, first_ref, turned_ref, back_ref):
    write_edges(field_ref, link_ref, first_ref, turned_ref)
    plane = LY * LZ
    for layer in range(link_ref.shape[1] // plane):
        here = pl.ds(layer * plane, plane)
        for base, shift in ((0, column_shift), (18, depth_shift)):
            back_ref[base : base + 18, here] = shift(link_ref[18 + base : 36 + base, here], -1)


def params():
    return pltpu.CompilerParams(vmem_limit_bytes=VMEM_LIMIT)


def edges_of(field, links):
    plane = LY * LZ
    edge = jax.ShapeDtypeStruct((6, field.shape[1], plane), jnp.bfloat16)
    return pl.pallas_call(
        edge_kernel,
        out_shape=(edge, edge, jax.ShapeDtypeStruct((36, field.shape[2]), jnp.float32)),
        in_specs=[VMEM] * 2,
        out_specs=(VMEM,) * 3,
        compiler_params=params(),
        name="edges",
    )(field, links)


def smear(field, links, back, ahead, behind, last):
    plane = LY * LZ
    edge = jax.ShapeDtypeStruct((6, field.shape[1], plane), jnp.bfloat16)
    shapes = (jax.ShapeDtypeStruct(field.shape, jnp.float32),) + (() if last else (edge, edge))
    return pl.pallas_call(
        functools.partial(smear_kernel, last),
        out_shape=shapes,
        in_specs=[VMEM] * 5,
        out_specs=(VMEM,) * len(shapes),
        compiler_params=params(),
        cost_estimate=pl.CostEstimate(flops=field.size * 80, bytes_accessed=field.size * 8, transcendentals=0),
        name="smear",
    )(field, links, back, ahead, behind)


def product_kernel(groups, scale, slot_ref, field_ref, table_ref, *refs):
    raw_refs, out_refs, (left_ref, right_ref, total_ref) = refs[:groups], refs[groups : 2 * groups], refs[2 * groups :]
    count = table_ref.shape[0] // 2
    vectors = field_ref.shape[1]
    total_ref[...] = jnp.zeros_like(total_ref)

    @pl.loop(0, field_ref.shape[2] // LANES)
    def _(tile):
        lanes = pl.ds(pl.multiple_of(tile * LANES, LANES), LANES)
        field = [field_ref[k, :, lanes] for k in range(6)]
        for p in range(count):
            cosine = table_ref[pl.ds(2 * p, 1), lanes]
            sine = table_ref[pl.ds(2 * p + 1, 1), lanes]
            for color in range(3):
                real, imag = field[2 * color], field[2 * color + 1]
                rows = pl.ds(p * vectors, vectors)
                left_ref[rows, pl.ds(2 * color * LANES, LANES)] = (cosine * real + sine * imag).astype(jnp.bfloat16)
                left_ref[rows, pl.ds((2 * color + 1) * LANES, LANES)] = (cosine * imag - sine * real).astype(jnp.bfloat16)
        for g, raw_ref in enumerate(raw_refs):
            width = raw_ref.shape[1]
            for color in range(3):
                real, imag = raw_ref[2 * color, :, lanes], raw_ref[2 * color + 1, :, lanes]
                first = pl.ds(2 * g * width, width)
                second = pl.ds((2 * g + 1) * width, width)
                one = pl.ds(2 * color * LANES, LANES)
                two = pl.ds((2 * color + 1) * LANES, LANES)
                right_ref[first, one] = real
                right_ref[first, two] = imag
                right_ref[second, one] = -imag
                right_ref[second, two] = real
        total_ref[...] += lax.dot_general(
            left_ref[...], right_ref[...], (((1,), (1,)), ((), ())), preferred_element_type=jnp.float32
        )

    turned = jnp.transpose(total_ref[...] * scale)
    width = turned.shape[0] // groups
    for g in range(groups):
        block = turned[g * width : (g + 1) * width].astype(out_refs[0].dtype)
        for slot in range(groups):

            @pl.when(slot_ref[g] == slot)
            def _():
                out_refs[slot][...] = block


def product(slots, field, table, raws, scale, dtype):
    groups = len(raws)
    vectors = field.shape[1]
    count = table.shape[0] // 2
    width = 2 * vectors
    out = jax.ShapeDtypeStruct((width, count * vectors), dtype)
    depth = 6 * LANES
    return pl.pallas_call(
        functools.partial(product_kernel, groups, scale),
        out_shape=(out,) * groups,
        in_specs=[SMEM] + [VMEM] * (2 + groups),
        out_specs=(VMEM,) * groups,
        scratch_shapes=[
            pltpu.VMEM((count * vectors, depth), jnp.bfloat16),
            pltpu.VMEM((groups * width, depth), jnp.bfloat16),
            pltpu.VMEM((count * vectors, groups * width), jnp.float32),
        ],
        compiler_params=params(),
        name="product",
    )(slots, field, table, *raws)


def phase_table(momenta, total_x, first_site, sites):
    plane = LY * LZ
    site = first_site + lax.iota(jnp.int32, sites)
    fraction = (
        jnp.mod(momenta[:, 0:1] * (site // plane)[None], total_x).astype(jnp.float32) / total_x
        + jnp.mod(momenta[:, 1:2] * (site // LZ % LY)[None], LY).astype(jnp.float32) / LY
        + jnp.mod(momenta[:, 2:3] * (site % LZ)[None], LZ).astype(jnp.float32) / LZ
    )
    angle = 2.0 * math.pi * fraction
    return jnp.stack([jnp.cos(angle), jnp.sin(angle)], axis=1).reshape((2 * momenta.shape[0], sites))


def shards(vectors, gauge_links, momenta):
    plane = LY * LZ
    bricks, vecs, subs = (lax.axis_size(axis) for axis in ("brick", "vec", "sub"))
    groups = vecs * subs
    assert groups == bricks
    width, sites = vectors.shape[0], vectors.shape[3]
    total_x = bricks * (sites // plane)
    brick, vec, sub = (lax.axis_index(axis) for axis in ("brick", "vec", "sub"))
    links = gauge_links.reshape((54, sites))
    field = jnp.transpose(vectors.reshape((width, 6, sites)), (1, 0, 2))
    raw = field.astype(jnp.bfloat16)
    first, turned, back = edges_of(field, links)

    offsets = [(a, 0) for a in range(vecs)]
    raws = [raw] + [shifted(raw, "vec", a) for a in range(1, vecs)]
    for b in range(1, subs):
        for a in range(vecs):
            raws.append(shifted(raws[a], "sub", b))
            offsets.append((a, b))
    table = phase_table(momenta, total_x, brick * sites, sites)

    for step in range(ITERS):
        ahead = shifted(first, "brick", -1)
        behind = shifted(turned, "brick", 1)
        field, *edges = smear(field, links, back, ahead, behind, step == ITERS - 1)
        if edges:
            first, turned = edges

    owners = jnp.stack([(vec - a) % vecs * subs + (sub - b) % subs for a, b in offsets])
    slots = ((owners - brick) % groups).astype(jnp.int32)
    scale = (3.0 * total_x * plane) ** (-0.5)
    blocks = product(slots, field, table, raws, scale, jnp.bfloat16)
    shares = []
    for slot, block in enumerate(blocks):
        pairs = [
            (b * groups + g, g * groups + (b + slot) % groups) for b in range(bricks) for g in range(groups)
        ]
        shares.append(lax.ppermute(block, ("brick", "vec", "sub"), pairs))
    total = functools.reduce(jnp.add, [share.astype(jnp.float32) for share in shares])
    count = momenta.shape[0]
    return jnp.transpose(total.reshape((2, width, count, width)), (1, 2, 0, 3))


def solution(mesh):
    in_specs = (
        P(("vec", "sub"), None, None, ("grp", "brick")),
        P(None, None, None, None, ("grp", "brick")),
        P(),
    )
    out_specs = P(("vec", "sub"), "grp", None, "brick")
    return jax.shard_map(shards, mesh=mesh, in_specs=in_specs, out_specs=out_specs, check_vma=False)
```

time: 443 us -> 108 us (0.24); the launches traced: 438 us -> 108 us
  local copies, waits for them, and re-layouts: 208 us -> 14.5 us
  waiting for transfers between devices: 110 us -> 33.2 us
  matrix products: 47 us -> 0 us
  Pallas kernels: 0 us -> 32.6 us
  other arithmetic: 38.3 us -> 9.75 us
  between operations: 15.4 us -> 0.2 us
    unnamed x81 -> x17, local copies, waits for them, and re-layouts: 119 us -> 3.76 us
    unnamed x4 -> x0, waiting for transfers between devices: 99.5 us -> none
    dot_general x27 -> x0, matrix products: 47 us -> none  [one_momentum(): lax.dot_general(left, right, (((1,), (1,)), ((), ())), preferred_element_...]
    pallas_call x0 -> x4, Pallas kernels: none -> 32.6 us  [the longest x2 16.1 us: smear(): pl.pallas_call(functools.partial(smear_kernel, last), out_shape=shapes, i...]
    convert_element_type x29 -> x0, local copies, waits for them, and re-layouts: 23.2 us -> none  [the longest x27 9.99 us: one_momentum(): phased = jnp.stack([real_part, imag_part], axis=2).astype(jnp.bfloat16)]
    ppermute x5 -> x11, waiting for transfers between devices: 10.5 us -> 33.2 us  [the longest x7 17.1 us: shifted(): lax.ppermute(array, axis, [(i, (i + by) % peers) for i in range(peers)])]
    dynamic_update_slice x27 -> x0, local copies, waits for them, and re-layouts: 17.9 us -> none  [shards(): blocks = lax.map(one_momentum, (cosines, sines))]
    all_to_all x2 -> x0, local copies, waits for them, and re-layouts: 14.1 us -> none  [the longest x1 7.32 us: shards(): lax.all_to_all(smeared_low, ('vec', 'sub'), split_axis=3, concat_axis=0,...]
  transfers between devices with their start and end apart: 9 -> 11, of which waited for: 4 -> 5; matrix products, arithmetic and copies ran while one was open for 19% -> 17% of each run, Pallas kernels for 0% -> 17%
where the time goes in v1:
time: 108 us
  waiting for transfers between devices  33.2 us (31%)
  Pallas kernels  32.6 us (30%)
  starting transfers between devices  17.6 us (16%)
  local copies, waits for them, and re-layouts  14.5 us (13%)
  other arithmetic  9.75 us (9%)
    ppermute x7, waiting for transfers between devices, shifted(): lax.ppermute(array, axis, [(i, (i + by) % peers) for i in range(peers)])  17.1 us
    ppermute x4, waiting for transfers between devices, shards(): shares.append(lax.ppermute(block, ('brick', 'vec', 'sub'), pairs))  16.1 us
    pallas_call x2, Pallas kernels, smear(): pl.pallas_call(functools.partial(smear_kernel, last), out_shape=shapes, i...  16.1 us
    pallas_call x1, Pallas kernels, product(): pl.pallas_call(functools.partial(product_kernel, groups, scale), out_shap...  13.9 us
    ppermute x7, starting transfers between devices, shifted(): lax.ppermute(array, axis, [(i, (i + by) % peers) for i in range(peers)])  10.5 us
    cos x1, other arithmetic, phase_table(): jnp.cos(angle)  8.51 us
    ppermute x4, starting transfers between devices, shards(): shares.append(lax.ppermute(block, ('brick', 'vec', 'sub'), pairs))  7.16 us
    sin x1, local copies, waits for them, and re-layouts, phase_table(): jnp.sin(angle)  5.59 us
  transfers between devices with their start and end apart: 11, of which 5 were waited for; matrix products, arithmetic and copies ran while one was open for 17% of the time, Pallas kernels for 17%

profile of v1, /device:TPU:0, one launch (start us, length us, event | category | flops | bytes accessed | tf_op | source)
XLA Modules:
  0.0 107.9 jit_solution(7346075081973145767)
XLA Ops:
  0.0 2.3 %copy.6 = f32[32,3,2,2048]{3,0,2,1:T(8,128)S(1)} copy(f32[32,3,2,2048]{3,2,1,0:T(2,128)} %param.3) | data formatting | bytes 3145728 | tf_op args[0]
  2.4 3.0 %collective-permute-start.4 = (bf16[6,32,2048]{2,1,0:T(8,128)(2,1)S(1)}, bf16[6,32,2048]{2,1,0:T(8,128)(2,1)S(1)}, u32[]{:S(2)}, u32[]{:S(2)}) collective-permute-start(bf16[6,32,2048]{2,1,0:T(8,128)(2,1)S(1)} %bitcast_convert_fusion.refs_0_), channel_id=1, source_target_pairs={{0,2},{2,0},{1,3},{3,1},{4,6},{6,4},{5,7},{7,5},{8,10},{10,8},{9,1... | collective-permute-start | bytes 2359304 | tf_op jit(solution)/shard_map/ppermute | solution.py:24
  5.5 2.1 %reshape.461.link_ref = f32[54,2048]{1,0:T(8,128)} reshape(f32[3,3,3,2,2048]{4,3,2,1,0:T(2,128)} %param.4) | data formatting | bytes 884736 | tf_op jit(solution)/shard_map/reshape | solution.py:271
  7.5 2.6 %edges.1 = (bf16[6,32,512]{2,1,0:T(8,128)(2,1)}, bf16[6,32,512]{2,1,0:T(8,128)(2,1)}, f32[36,2048]{1,0:T(8,128)}) custom-call(f32[6,32,2048]{2,1,0:T(8,128)} %bitcast.15, f32[54,2048]{1,0:T(8,128)} %reshape.461.link_ref), custom_call_target="tpu_custom_call" | custom-call | tf_op jit(solution)/shard_map/edges/pallas_call | solution.py:159
  10.2 3.6 %collective-permute-start = (bf16[6,32,512]{2,1,0:T(8,128)(2,1)}, bf16[6,32,512]{2,1,0:T(8,128)(2,1)S(1)}, u32[]{:S(2)}, u32[]{:S(2)}) collective-permute-start(bf16[6,32,512]{2,1,0:T(8,128)(2,1)} %get-tuple-element.16), channel_id=1, source_target_pairs={{0,12},{4,0},{8,4},{12,8},{1,13},{5,1},{9,5},{13,9},{2,14},{6,2},{... | collective-permute-start | bytes 589832 | tf_op jit(solution)/shard_map/ppermute | solution.py:24
  13.8 9.2 %collective-permute-done.4.refs_1_ = bf16[6,32,2048]{2,1,0:T(8,128)(2,1)S(1)} collective-permute-done((bf16[6,32,2048]{2,1,0:T(8,128)(2,1)S(1)}, bf16[6,32,2048]{2,1,0:T(8,128)(2,1)S(1)}, u32[]{:S(2)}, u32[]{:S(2)}) %collective-permute-start.4) | collective-permute-done | bytes 786464 | tf_op jit(solution)/shard_map/ppermute | solution.py:24
  23.0 8.5 %fusion.20 = (f32[27,1,2048]{2,1,0:T(1,128)S(1)}, f32[27,1,2048]{2,1,0:T(1,128)S(1)}) fusion(s32[2048]{0:T(1024)S(1)} %get-tuple-element.30, s32[27]{0:T(128)S(1)} %get-tuple-element.28, s32[2048]{0:T(1024)S(1)} %get-tuple-element.31, s32[27]{0:T(128)S(1)} %get-tuple-element.29, s32[2048]{0:T(1024)S(1)} %add_select_fusion.3, s32[27]{0:T(128)S(1)} %get-tuple-element.27), kind=kLoop, calls=%fused_computation.52 | loop fusion | flops 2488320 | bytes 467268 | tf_op jit(solution)/shard_map/cos | solution.py:260
  31.5 5.6 %sin.10 = f32[27,1,2048]{2,1,0:T(1,128)S(1)} sine(f32[27,1,2048]{2,1,0:T(1,128)S(1)} %get-tuple-element.26) | non-fusion elementwise | bytes 442368 | tf_op jit(solution)/shard_map/sin | solution.py:260
  37.9 8.2 %smear.2 = (f32[6,32,2048]{2,1,0:T(8,128)}, bf16[6,32,512]{2,1,0:T(8,128)(2,1)}, bf16[6,32,512]{2,1,0:T(8,128)(2,1)}) custom-call(f32[6,32,2048]{2,1,0:T(8,128)} %bitcast.16, f32[54,2048]{1,0:T(8,128)} %reshape.461.link_ref, f32[36,2048]{1,0:T(8,128)} %get-tuple-element.15.back_ref, bf16[6,32,512]{2,1,0:T(8,128)(2,1)} %copy-done.5, bf16[6,32,512]{2,1,0:T(8,128)(2,1)} %copy-done.6), custom_call_target="tpu_custom_call" | custom-call | flops 31457280 | bytes 3145728 | tf_op jit(solution)/shard_map/smear/pallas_call | solution.py:173
  46.1 3.9 %collective-permute-start.2 = (bf16[6,32,512]{2,1,0:T(8,128)(2,1)}, bf16[6,32,512]{2,1,0:T(8,128)(2,1)S(1)}, u32[]{:S(2)}, u32[]{:S(2)}) collective-permute-start(bf16[6,32,512]{2,1,0:T(8,128)(2,1)} %get-tuple-element.19), channel_id=1, source_target_pairs={{0,12},{4,0},{8,4},{12,8},{1,13},{5,1},{9,5},{13,9},{2,14},{6,2},{... | collective-permute-start | bytes 589832 | tf_op jit(solution)/shard_map/ppermute | solution.py:24
  50.4 1.1 %reshape.462.table_ref = f32[54,2048]{1,0:T(8,128)} reshape(f32[27,2,2048]{2,1,0:T(2,128)S(1)} %pad_maximum_fusion) | data formatting | bytes 884736 | tf_op jit(solution)/shard_map/reshape | solution.py:260
  51.5 0.7 and_select_fusion.3.slot_ref
  52.1 3.4 %collective-permute-done.2.ahead_ref = bf16[6,32,512]{2,1,0:T(8,128)(2,1)S(1)} collective-permute-done((bf16[6,32,512]{2,1,0:T(8,128)(2,1)}, bf16[6,32,512]{2,1,0:T(8,128)(2,1)S(1)}, u32[]{:S(2)}, u32[]{:S(2)}) %collective-permute-start.2) | collective-permute-done | bytes 196640 | tf_op jit(solution)/shard_map/ppermute | solution.py:24
  55.5 4.6 %collective-permute-done.3.behind_ref = bf16[6,32,512]{2,1,0:T(8,128)(2,1)S(1)} collective-permute-done((bf16[6,32,512]{2,1,0:T(8,128)(2,1)}, bf16[6,32,512]{2,1,0:T(8,128)(2,1)S(1)}, u32[]{:S(2)}, u32[]{:S(2)}) %collective-permute-start.3) | collective-permute-done | bytes 196640 | tf_op jit(solution)/shard_map/ppermute | solution.py:24
  60.1 0.7 copy-done.4
  60.8 7.9 %smear.3.field_ref = f32[6,32,2048]{2,1,0:T(8,128)} custom-call(f32[6,32,2048]{2,1,0:T(8,128)} %get-tuple-element.18.field_ref, f32[54,2048]{1,0:T(8,128)} %reshape.461.link_ref, f32[36,2048]{1,0:T(8,128)} %get-tuple-element.15.back_ref, bf16[6,32,512]{2,1,0:T(8,128)(2,1)} %copy-done.3, bf16[6,32,512]{2,1,0:T(8,128)(2,1)} %copy-done.4), custom_call_target="tpu_custom_call" | custom-call | flops 31457280 | bytes 3145728 | tf_op jit(solution)/shard_map/smear/pallas_call | solution.py:173
  68.7 13.9 %product.1 = (bf16[64,864]{1,0:T(8,128)(2,1)}, bf16[64,864]{1,0:T(8,128)(2,1)}, bf16[64,864]{1,0:T(8,128)(2,1)}, bf16[64,864]{1,0:T(8,128)(2,1)}) custom-call(s32[4]{0:T(128)} %and_select_fusion.3.slot_ref, f32[6,32,2048]{2,1,0:T(8,128)} %smear.3.field_ref, f32[54,2048]{1,0:T(8,128)} %reshape.462.table_ref, bf16[6,32,2048]{2,1,0:T(8,128)(2,1)} %copy-done.1, ...), custom_call_target="tpu_custom_call" | custom-call | tf_op jit(solution)/shard_map/product/pallas_call | solution.py:236
  82.6 0.8 collective-permute-start.10
  83.4 1.5 %collective-permute-start.7 = (bf16[64,864]{1,0:T(8,128)(2,1)}, bf16[64,864]{1,0:T(8,128)(2,1)S(1)}, u32[]{:S(2)}, u32[]{:S(2)}) collective-permute-start(bf16[64,864]{1,0:T(8,128)(2,1)} %get-tuple-element.21), channel_id=1, source_target_pairs={{0,0},{1,4},{2,8},{3,12},{4,1},{5,5},{6,9},{7,13},{8,2},{9,6},{10,... | collective-permute-start | bytes 331784 | tf_op jit(solution)/shard_map/ppermute | solution.py:300
  84.9 1.7 %collective-permute-start.8 = (bf16[64,864]{1,0:T(8,128)(2,1)}, bf16[64,864]{1,0:T(8,128)(2,1)S(1)}, u32[]{:S(2)}, u32[]{:S(2)}) collective-permute-start(bf16[64,864]{1,0:T(8,128)(2,1)} %get-tuple-element.22), channel_id=1, source_target_pairs={{0,1},{1,5},{2,9},{3,13},{4,2},{5,6},{6,10},{7,14},{8,3},{9,7},{10... | collective-permute-start | bytes 331784 | tf_op jit(solution)/shard_map/ppermute | solution.py:300
  86.7 3.1 %collective-permute-start.9 = (bf16[64,864]{1,0:T(8,128)(2,1)}, bf16[64,864]{1,0:T(8,128)(2,1)S(1)}, u32[]{:S(2)}, u32[]{:S(2)}) collective-permute-start(bf16[64,864]{1,0:T(8,128)(2,1)} %get-tuple-element.23), channel_id=1, source_target_pairs={{0,2},{1,6},{2,10},{3,14},{4,3},{5,7},{6,11},{7,15},{8,0},{9,4},{1... | collective-permute-start | bytes 331784 | tf_op jit(solution)/shard_map/ppermute | solution.py:300
  89.7 6.7 %collective-permute-done.8 = bf16[64,864]{1,0:T(8,128)(2,1)S(1)} collective-permute-done((bf16[64,864]{1,0:T(8,128)(2,1)}, bf16[64,864]{1,0:T(8,128)(2,1)S(1)}, u32[]{:S(2)}, u32[]{:S(2)}) %collective-permute-start.8) | collective-permute-done | bytes 110624 | tf_op jit(solution)/shard_map/ppermute | solution.py:300
  96.5 9.4 %collective-permute-done.9 = bf16[64,864]{1,0:T(8,128)(2,1)S(1)} collective-permute-done((bf16[64,864]{1,0:T(8,128)(2,1)}, bf16[64,864]{1,0:T(8,128)(2,1)S(1)}, u32[]{:S(2)}, u32[]{:S(2)}) %collective-permute-start.9) | collective-permute-done | bytes 110624 | tf_op jit(solution)/shard_map/ppermute | solution.py:300
  106.3 1.6 %copy.7 = f32[32,27,2,32]{3,2,1,0:T(2,128)} copy(f32[32,27,2,32]{3,1,0,2:T(8,128)S(1)} %bitcast.17) | data formatting | bytes 442368 | tf_op jit(solution)/shard_map/transpose | solution.py:303
  (32 shorter events, 1.8 us)
Async XLA Ops:
  2.3 5.2 %copy-start = (f32[32,3,2,2048]{3,0,2,1:T(8,128)}, f32[32,3,2,2048]{3,0,2,1:T(8,128)S(1)}, u32[]{:S(2)}) copy-start(f32[32,3,2,2048]{3,0,2,1:T(8,128)S(1)} %copy.6) | copy-start | bytes 4718596
  2.4 29.1 %copy-start.1 = (bf16[6,32,2048]{2,1,0:T(8,128)(2,1)}, bf16[6,32,2048]{2,1,0:T(8,128)(2,1)S(1)}, u32[]{:S(2)}) copy-start(bf16[6,32,2048]{2,1,0:T(8,128)(2,1)S(1)} %bitcast_convert_fusion.refs_0_) | copy-start | bytes 2359300
  2.4 11.4 %copy-start.7 = (s32[27,3]{0,1:T(4,128)S(1)}, s32[27,3]{0,1:T(4,128)}, u32[]{:S(2)}) copy-start(s32[27,3]{0,1:T(4,128)} %param.5) | copy-start | bytes 976
  2.4 20.5 %collective-permute-start.4 = (bf16[6,32,2048]{2,1,0:T(8,128)(2,1)S(1)}, bf16[6,32,2048]{2,1,0:T(8,128)(2,1)S(1)}, u32[]{:S(2)}, u32[]{:S(2)}) collective-permute-start(bf16[6,32,2048]{2,1,0:T(8,128)(2,1)S(1)} %bitcast_convert_fusion.refs_0_), channel_id=1, source_target_pairs={{0,2},{2,0},{1,3},{3,1},{4,6},{6,4},{5,7},{7,5},{8,10},{10,8},{9,1... | collective-permute-start | bytes 2359304 | tf_op jit(solution)/shard_map/ppermute | solution.py:24
  5.4 63.3 %collective-permute-start.5 = (bf16[6,32,2048]{2,1,0:T(8,128)(2,1)S(1)}, bf16[6,32,2048]{2,1,0:T(8,128)(2,1)}, u32[]{:S(2)}, u32[]{:S(2)}) collective-permute-start(bf16[6,32,2048]{2,1,0:T(8,128)(2,1)S(1)} %bitcast_convert_fusion.refs_0_), channel_id=1, source_target_pairs={{0,1},{1,0},{2,3},{3,2},{4,5},{5,4},{6,7},{7,6},{8,9},{9,8},{10,11... | collective-permute-start | bytes 2359304 | tf_op jit(solution)/shard_map/ppermute | solution.py:24
  10.2 27.0 %collective-permute-start = (bf16[6,32,512]{2,1,0:T(8,128)(2,1)}, bf16[6,32,512]{2,1,0:T(8,128)(2,1)S(1)}, u32[]{:S(2)}, u32[]{:S(2)}) collective-permute-start(bf16[6,32,512]{2,1,0:T(8,128)(2,1)} %get-tuple-element.16), channel_id=1, source_target_pairs={{0,12},{4,0},{8,4},{12,8},{1,13},{5,1},{9,5},{13,9},{2,14},{6,2},{... | collective-permute-start | bytes 589832 | tf_op jit(solution)/shard_map/ppermute | solution.py:24
  13.8 23.4 %collective-permute-start.1 = (bf16[6,32,512]{2,1,0:T(8,128)(2,1)}, bf16[6,32,512]{2,1,0:T(8,128)(2,1)S(1)}, u32[]{:S(2)}, u32[]{:S(2)}) collective-permute-start(bf16[6,32,512]{2,1,0:T(8,128)(2,1)} %get-tuple-element.17), channel_id=1, source_target_pairs={{0,4},{4,8},{8,12},{12,0},{1,5},{5,9},{9,13},{13,1},{2,6},{6,10},{... | collective-permute-start | bytes 589832 | tf_op jit(solution)/shard_map/ppermute | solution.py:24
  23.0 23.1 %copy-start.2 = (bf16[6,32,2048]{2,1,0:T(8,128)(2,1)}, bf16[6,32,2048]{2,1,0:T(8,128)(2,1)S(1)}, u32[]{:S(2)}) copy-start(bf16[6,32,2048]{2,1,0:T(8,128)(2,1)S(1)} %collective-permute-done.4.refs_1_) | copy-start | bytes 2359300
  23.0 45.7 %collective-permute-start.6 = (bf16[6,32,2048]{2,1,0:T(8,128)(2,1)S(1)}, bf16[6,32,2048]{2,1,0:T(8,128)(2,1)}, u32[]{:S(2)}, u32[]{:S(2)}) collective-permute-start(bf16[6,32,2048]{2,1,0:T(8,128)(2,1)S(1)} %collective-permute-done.4.refs_1_), channel_id=1, source_target_pairs={{0,1},{1,0},{2,3},{3,2},{4,5},{5,4},{6,7},{7,6},{8,9},{9,8},{10,11... | collective-permute-start | bytes 2359304 | tf_op jit(solution)/shard_map/ppermute | solution.py:24
  37.1 0.7 copy-start.5
  37.2 0.7 copy-start.6
  46.1 9.4 %collective-permute-start.2 = (bf16[6,32,512]{2,1,0:T(8,128)(2,1)}, bf16[6,32,512]{2,1,0:T(8,128)(2,1)S(1)}, u32[]{:S(2)}, u32[]{:S(2)}) collective-permute-start(bf16[6,32,512]{2,1,0:T(8,128)(2,1)} %get-tuple-element.19), channel_id=1, source_target_pairs={{0,12},{4,0},{8,4},{12,8},{1,13},{5,1},{9,5},{13,9},{2,14},{6,2},{... | collective-permute-start | bytes 589832 | tf_op jit(solution)/shard_map/ppermute | solution.py:24
  49.9 10.2 %collective-permute-start.3 = (bf16[6,32,512]{2,1,0:T(8,128)(2,1)}, bf16[6,32,512]{2,1,0:T(8,128)(2,1)S(1)}, u32[]{:S(2)}, u32[]{:S(2)}) collective-permute-start(bf16[6,32,512]{2,1,0:T(8,128)(2,1)} %get-tuple-element.20), channel_id=1, source_target_pairs={{0,4},{4,8},{8,12},{12,0},{1,5},{5,9},{9,13},{13,1},{2,6},{6,10},{... | collective-permute-start | bytes 589832 | tf_op jit(solution)/shard_map/ppermute | solution.py:24
  55.5 4.6 %copy-start.3 = (bf16[6,32,512]{2,1,0:T(8,128)(2,1)}, bf16[6,32,512]{2,1,0:T(8,128)(2,1)S(1)}, u32[]{:S(2)}) copy-start(bf16[6,32,512]{2,1,0:T(8,128)(2,1)S(1)} %collective-permute-done.2.ahead_ref) | copy-start | bytes 589828
  60.1 0.7 copy-start.4
  82.6 7.2 %collective-permute-start.10 = (bf16[64,864]{1,0:T(8,128)(2,1)}, bf16[64,864]{1,0:T(8,128)(2,1)S(1)}, u32[]{:S(2)}, u32[]{:S(2)}) collective-permute-start(bf16[64,864]{1,0:T(8,128)(2,1)} %get-tuple-element.24), channel_id=1, source_target_pairs={{0,3},{1,7},{2,11},{3,15},{4,0},{5,4},{6,8},{7,12},{8,1},{9,5},{10... | collective-permute-start | bytes 331784 | tf_op jit(solution)/shard_map/ppermute | solution.py:300
  83.4 6.4 %collective-permute-start.7 = (bf16[64,864]{1,0:T(8,128)(2,1)}, bf16[64,864]{1,0:T(8,128)(2,1)S(1)}, u32[]{:S(2)}, u32[]{:S(2)}) collective-permute-start(bf16[64,864]{1,0:T(8,128)(2,1)} %get-tuple-element.21), channel_id=1, source_target_pairs={{0,0},{1,4},{2,8},{3,12},{4,1},{5,5},{6,9},{7,13},{8,2},{9,6},{10,... | collective-permute-start | bytes 331784 | tf_op jit(solution)/shard_map/ppermute | solution.py:300
  84.9 11.5 %collective-permute-start.8 = (bf16[64,864]{1,0:T(8,128)(2,1)}, bf16[64,864]{1,0:T(8,128)(2,1)S(1)}, u32[]{:S(2)}, u32[]{:S(2)}) collective-permute-start(bf16[64,864]{1,0:T(8,128)(2,1)} %get-tuple-element.22), channel_id=1, source_target_pairs={{0,1},{1,5},{2,9},{3,13},{4,2},{5,6},{6,10},{7,14},{8,3},{9,7},{10... | collective-permute-start | bytes 331784 | tf_op jit(solution)/shard_map/ppermute | solution.py:300
  86.7 19.2 %collective-permute-start.9 = (bf16[64,864]{1,0:T(8,128)(2,1)}, bf16[64,864]{1,0:T(8,128)(2,1)S(1)}, u32[]{:S(2)}, u32[]{:S(2)}) collective-permute-start(bf16[64,864]{1,0:T(8,128)(2,1)} %get-tuple-element.23), channel_id=1, source_target_pairs={{0,2},{1,6},{2,10},{3,14},{4,3},{5,7},{6,11},{7,15},{8,0},{9,4},{1... | collective-permute-start | bytes 331784 | tf_op jit(solution)/shard_map/ppermute | solution.py:300

commit v2 on v1

v2 whole, which is shorter than its diff:
```python
import functools
import math

import jax
import jax.numpy as jnp
from jax import lax
from jax.experimental import pallas as pl
from jax.experimental.pallas import tpu as pltpu
from jax.sharding import PartitionSpec as P

LY = 64
LZ = 8
ITERS = 2
KAPPA = 0.125
LANES = 128
PLANE = LY * LZ
TILES = PLANE // LANES
ROWS = 16
LOW = jnp.bfloat16
WIDE = jnp.float32
VMEM_LIMIT = 48 * 1024 * 1024
VMEM = pl.BlockSpec(memory_space=pltpu.VMEM)
SMEM = pl.BlockSpec(memory_space=pltpu.SMEM)


def shifted(array, axis, by):
    peers = lax.axis_size(axis)
    return lax.ppermute(array, axis, [(i, (i + by) % peers) for i in range(peers)])


def add_hop(total, link, field, adjoint):
    for row in range(3):
        for column in range(3):
            if adjoint:
                real, imag = link(column, row, 0), link(column, row, 1)
            else:
                real, imag = link(row, column, 0), link(row, column, 1)
            source_real, source_imag = field[2 * column], field[2 * column + 1]
            if adjoint:
                add_real = real * source_real + imag * source_imag
                add_imag = real * source_imag - imag * source_real
            else:
                add_real = real * source_real - imag * source_imag
                add_imag = real * source_imag + imag * source_real
            for part, add in ((0, add_real), (1, add_imag)):
                old = total[2 * row + part]
                total[2 * row + part] = add if old is None else old + add


def lane_roll(value, by):
    return pltpu.roll(value, by % LANES, 1)


def lanes_at(layer, tile):
    return pl.ds(pl.multiple_of(layer * PLANE + tile * LANES, LANES), LANES)


def row_groups(ref):
    size = min(ROWS, ref.shape[1])
    return [pl.ds(start, size) for start in range(0, ref.shape[1], size)]


def load(ref, rows, lanes):
    return [ref[k, rows, lanes].astype(WIDE) for k in range(6)]


def store(ref, rows, lanes, values):
    for k in range(6):
        ref[k, rows, lanes] = values[k].astype(ref.dtype)


def link_at(link_ref, direction, layer, tile):
    tiles = link_ref.shape[0] // 54

    def get(row, column, part):
        matrix = (direction * 3 + row) * 3 + column
        return link_ref[pl.ds((matrix * tiles + layer * TILES + tile) * 2 + part, 1), :]

    return get


def plane_hops(total, link_ref, back_ref, layer, tile, rows, fetch):
    here = fetch(tile)
    after, before = fetch((tile + 1) % TILES), fetch((tile + TILES - 1) % TILES)
    lane = lax.broadcasted_iota(jnp.int32, (rows.size, LANES), 1)
    ahead = [jnp.where(lane >= LANES - LZ, lane_roll(b, -LZ), lane_roll(a, -LZ)) for a, b in zip(here, after)]
    add_hop(total, link_at(link_ref, 1, layer, tile), ahead, False)
    behind = [jnp.where(lane < LZ, lane_roll(b, LZ), lane_roll(a, LZ)) for a, b in zip(here, before)]
    lanes = lanes_at(layer, tile)
    add_hop(total, lambda r, c, part: back_ref[part, pl.ds(3 * r + c, 1), lanes], behind, True)
    depth = lane % LZ
    ahead = [jnp.where(depth == LZ - 1, lane_roll(a, LZ - 1), lane_roll(a, -1)) for a in here]
    add_hop(total, link_at(link_ref, 2, layer, tile), ahead, False)
    turned = [None] * 6
    add_hop(turned, link_at(link_ref, 2, layer, tile), here, True)
    for k in range(6):
        total[k] += jnp.where(depth == 0, lane_roll(turned[k], 1 - LZ), lane_roll(turned[k], 1))
    return here


def combined(here, total):
    return [(1.0 - 6.0 * KAPPA) * a + KAPPA * b for a, b in zip(here, total)]


def open_kernel(vector_ref, link_ref, field_ref, inner_ref, rim_ref, first_ref, turned_ref):
    vectors, sites = field_ref.shape[1:]
    tiles = sites // LANES
    layers = sites // PLANE
    stride = 6 * tiles
    for k in range(6):
        for tile in range(tiles):
            row = ((k // 2) * tiles + tile) * 2 + k % 2
            value = vector_ref[pl.ds(row, vectors, stride=stride), :]
            field_ref[k, :, pl.ds(tile * LANES, LANES)] = value
            low = value.astype(LOW)
            layer, column = divmod(tile, TILES)
            if layer == 0:
                first_ref[k, :, pl.ds(column * LANES, LANES)] = low
                rim_ref[k, :, pl.ds(column * LANES, LANES)] = low
            elif layer == layers - 1:
                rim_ref[k, :, pl.ds(PLANE + column * LANES, LANES)] = low
            else:
                inner_ref[k, :, pl.ds(tile * LANES - PLANE, LANES)] = low

    @pl.loop(0, TILES)
    def _(tile):
        for rows in row_groups(field_ref):
            turned = [None] * 6
            source = load(field_ref, rows, lanes_at(layers - 1, tile))
            add_hop(turned, link_at(link_ref, 0, layers - 1, tile), source, True)
            store(turned_ref, rows, lanes_at(0, tile), turned)


def rim_kernel(field_ref, link_ref, low_ref, high_ref, first_ref, turned_ref, back_ref):
    sites = field_ref.shape[2]
    tiles, layers = sites // LANES, sites // PLANE
    lane = lax.broadcasted_iota(jnp.int32, (9, LANES), 1)
    for layer in range(layers):
        for part in range(2):
            row = lambda tile: (9 * tiles + layer * TILES + tile) * 2 + part
            value = [link_ref[pl.ds(row(tile), 9, stride=2 * tiles), :] for tile in range(TILES)]
            value = [lane_roll(v, LZ) for v in value]
            for tile in range(TILES):
                back_ref[part, pl.ds(0, 9), lanes_at(layer, tile)] = jnp.where(lane < LZ, value[tile - 1], value[tile])

    for layer, out_ref in ((0, low_ref), (layers - 1, high_ref)):

        @pl.loop(0, TILES)
        def _(tile):
            for rows in row_groups(field_ref):
                total = [None] * 6
                if layer == 0:
                    source = load(field_ref, rows, lanes_at(1, tile))
                    add_hop(total, link_at(link_ref, 0, 0, tile), source, False)
                else:
                    source = load(field_ref, rows, lanes_at(layer - 1, tile))
                    add_hop(total, link_at(link_ref, 0, layer - 1, tile), source, True)
                fetch = lambda t: load(field_ref, rows, lanes_at(layer, t))
                here = plane_hops(total, link_ref, back_ref, layer, tile, rows, fetch)
                new = combined(here, total)
                store(out_ref, rows, lanes_at(0, tile), new)
                if layer == 0:
                    store(first_ref, rows, lanes_at(0, tile), new)
                else:
                    turned = [None] * 6
                    add_hop(turned, link_at(link_ref, 0, layer, tile), new, True)
                    store(turned_ref, rows, lanes_at(0, tile), turned)


def unit_phase(turns):
    half = math.pi * (turns - jnp.round(turns))
    square = half * half
    cosine, sine = 1.0, 1.0
    for order in range(12, 0, -2):
        sine = 1.0 - square * sine * (1.0 / (order * (order + 1)))
        cosine = 1.0 - square * cosine * (1.0 / (order * (order - 1)))
    sine = half * sine
    return 1.0 - 2.0 * sine * sine, 2.0 * sine * cosine


def inner_kernel(total_x, place_ref, field_ref, link_ref, back_ref, momenta_ref, out_ref, table_ref):
    layers = field_ref.shape[2] // PLANE
    count = momenta_ref.shape[0]
    momenta = momenta_ref[...].astype(WIDE)
    lane = lax.broadcasted_iota(jnp.int32, (count, LANES), 1)

    @pl.loop(0, TILES)
    def _(tile):
        column = (tile * (LANES // LZ) + lane // LZ).astype(WIDE)
        depth = (lane % LZ).astype(WIDE)
        turns = [momenta[:, 1:2] * column / LY, momenta[:, 2:3] * depth / LZ]
        part = sum(t - jnp.round(t) for t in turns)
        for layer in range(layers):
            along = momenta[:, 0:1] * (place_ref[0] + layer).astype(WIDE) / total_x
            cosine, sine = unit_phase(along - jnp.round(along) + part)
            table_ref[0, :, lanes_at(layer, tile)] = cosine
            table_ref[1, :, lanes_at(layer, tile)] = sine

    for layer in range(1, layers - 1):

        @pl.loop(0, TILES)
        def _(tile):
            for rows in row_groups(field_ref):
                total = [None] * 6
                add_hop(total, link_at(link_ref, 0, layer, tile), load(field_ref, rows, lanes_at(layer + 1, tile)), False)
                before = load(field_ref, rows, lanes_at(layer - 1, tile))
                add_hop(total, link_at(link_ref, 0, layer - 1, tile), before, True)
                fetch = lambda t: load(field_ref, rows, lanes_at(layer, t))
                here = plane_hops(total, link_ref, back_ref, layer, tile, rows, fetch)
                store(out_ref, rows, lanes_at(layer - 1, tile), combined(here, total))


def second_kernel(field_ref, link_ref, back_ref, low_ref, high_ref, inner_ref, ahead_ref, behind_ref, out_ref, rim_ref, one_ref):
    layers = field_ref.shape[2] // PLANE

    @pl.loop(0, TILES)
    def _(tile):
        for rows in row_groups(field_ref):
            lanes = lanes_at(0, tile)
            low = [a + KAPPA * b for a, b in zip(load(low_ref, rows, lanes), load(behind_ref, rows, lanes))]
            store(one_ref, rows, lanes, low)
            hop = [None] * 6
            add_hop(hop, link_at(link_ref, 0, layers - 1, tile), load(ahead_ref, rows, lanes), False)
            high = [a + KAPPA * b for a, b in zip(load(high_ref, rows, lanes), hop)]
            store(one_ref, rows, lanes_at(1, tile), high)

    def fetch_from(layer, rows):
        if layer == 0:
            return lambda t: load(one_ref, rows, lanes_at(0, t))
        if layer == layers - 1:
            return lambda t: load(one_ref, rows, lanes_at(1, t))
        return lambda t: load(inner_ref, rows, lanes_at(layer - 1, t))

    for layer in range(layers):

        @pl.loop(0, TILES)
        def _(tile):
            for rows in row_groups(field_ref):
                total = [None] * 6
                if layer < layers - 1:
                    add_hop(total, link_at(link_ref, 0, layer, tile), fetch_from(layer + 1, rows)(tile), False)
                if layer > 0:
                    add_hop(total, link_at(link_ref, 0, layer - 1, tile), fetch_from(layer - 1, rows)(tile), True)
                here = plane_hops(total, link_ref, back_ref, layer, tile, rows, fetch_from(layer, rows))
                if layer in (0, layers - 1):
                    own = load(field_ref, rows, lanes_at(layer, tile))
                    total = [a + KAPPA * b for a, b in zip(total, own)]
                    store(rim_ref, rows, lanes_at(min(layer, 1), tile), combined(here, total))
                else:
                    store(out_ref, rows, lanes_at(layer - 1, tile), combined(here, total))


def add_products(field_ref, raw_refs, table_ref, total_ref, left_ref, right_ref, table_tile):
    count = table_ref.shape[1]
    vectors = field_ref.shape[1]

    @pl.loop(0, field_ref.shape[2] // LANES)
    def _(tile):
        lanes = pl.ds(pl.multiple_of(tile * LANES, LANES), LANES)
        phases = pl.ds(pl.multiple_of(table_tile(tile) * LANES, LANES), LANES)
        field = [field_ref[k, :, lanes] for k in range(6)]
        for p in range(count):
            cosine = table_ref[0, pl.ds(p, 1), phases]
            sine = table_ref[1, pl.ds(p, 1), phases]
            rows = pl.ds(p * vectors, vectors)
            for color in range(3):
                real, imag = field[2 * color], field[2 * color + 1]
                left_ref[rows, pl.ds(2 * color * LANES, LANES)] = (cosine * real + sine * imag).astype(LOW)
                left_ref[rows, pl.ds((2 * color + 1) * LANES, LANES)] = (cosine * imag - sine * real).astype(LOW)
        for g, raw_ref in enumerate(raw_refs):
            width = raw_ref.shape[1]
            for color in range(3):
                real, imag = raw_ref[2 * color, :, lanes], raw_ref[2 * color + 1, :, lanes]
                first = pl.ds(2 * g * width, width)
                second = pl.ds((2 * g + 1) * width, width)
                one = pl.ds(2 * color * LANES, LANES)
                two = pl.ds((2 * color + 1) * LANES, LANES)
                right_ref[first, one] = real
                right_ref[first, two] = imag
                right_ref[second, one] = -imag
                right_ref[second, two] = real
        total_ref[...] += lax.dot_general(
            left_ref[...], right_ref[...], (((1,), (1,)), ((), ())), preferred_element_type=WIDE
        )


def inner_product_kernel(groups, field_ref, table_ref, *refs):
    raw_refs, (total_ref, left_ref, right_ref) = refs[:groups], refs[groups:]
    total_ref[...] = jnp.zeros_like(total_ref)
    add_products(field_ref, raw_refs, table_ref, total_ref, left_ref, right_ref, lambda tile: tile + TILES)


def last_product_kernel(groups, scale, slot_ref, rim_ref, ahead_ref, behind_ref, link_ref, start_ref, table_ref, *refs):
    raw_refs, out_refs, (field_ref, total_ref, left_ref, right_ref) = (
        refs[:groups],
        refs[groups : 2 * groups],
        refs[2 * groups :],
    )
    tiles = table_ref.shape[2] // LANES

    @pl.loop(0, TILES)
    def _(tile):
        for rows in row_groups(field_ref):
            lanes = lanes_at(0, tile)
            low = [a + KAPPA * b for a, b in zip(load(rim_ref, rows, lanes), load(behind_ref, rows, lanes))]
            store(field_ref, rows, lanes, low)
            hop = [None] * 6
            add_hop(hop, link_at(link_ref, 0, tiles // TILES - 1, tile), load(ahead_ref, rows, lanes), False)
            high = lanes_at(1, tile)
            store(field_ref, rows, high, [a + KAPPA * b for a, b in zip(load(rim_ref, rows, high), hop)])

    total_ref[...] = start_ref[...]
    skip = tiles - 2 * TILES
    table_tile = lambda tile: tile + jnp.where(tile >= TILES, skip, 0)
    add_products(field_ref, raw_refs, table_ref, total_ref, left_ref, right_ref, table_tile)
    turned = jnp.transpose(total_ref[...] * scale)
    width = turned.shape[0] // groups
    for g in range(groups):
        block = turned[g * width : (g + 1) * width].astype(out_refs[0].dtype)
        for slot in range(groups):

            @pl.when(slot_ref[g] == slot)
            def _():
                out_refs[slot][...] = block


def call(kernel, name, shapes, operands, flops=0, scratch=(), smem=False):
    return pl.pallas_call(
        kernel,
        out_shape=tuple(jax.ShapeDtypeStruct(shape, dtype) for shape, dtype in shapes),
        in_specs=[SMEM if smem and i == 0 else VMEM for i in range(len(operands))],
        out_specs=(VMEM,) * len(shapes),
        scratch_shapes=list(scratch),
        compiler_params=pltpu.CompilerParams(vmem_limit_bytes=VMEM_LIMIT),
        cost_estimate=pl.CostEstimate(flops=flops, bytes_accessed=1 << 20, transcendentals=0),
        name=name,
    )(*operands)


def shards(vectors, gauge_links, momenta):
    bricks, vecs, subs = (lax.axis_size(axis) for axis in ("brick", "vec", "sub"))
    groups = vecs * subs
    width, sites = vectors.shape[0], vectors.shape[3]
    layers, tiles = sites // PLANE, sites // LANES
    assert groups == bricks and layers > 2 and ITERS == 2
    total_x = bricks * layers
    count = momenta.shape[0]
    brick, vec, sub = (lax.axis_index(axis) for axis in ("brick", "vec", "sub"))
    tiled_vectors = jnp.swapaxes(vectors.reshape((width, 3, 2, tiles, LANES)), 2, 3).reshape((-1, LANES))
    links = jnp.swapaxes(gauge_links.reshape((27, 2, tiles, LANES)), 1, 2).reshape((-1, LANES))
    full, edge, rim, inner = (
        (6, width, sites),
        (6, width, PLANE),
        (6, width, 2 * PLANE),
        (6, width, sites - 2 * PLANE),
    )
    field, raw_inner, raw_rim, first, turned = call(
        open_kernel,
        "open",
        ((full, WIDE), (inner, LOW), (rim, LOW), (edge, LOW), (edge, LOW)),
        (tiled_vectors, links),
    )
    ahead = shifted(first, "brick", -1)
    behind = shifted(turned, "brick", 1)

    def gathered(raw):
        raws = [raw] + [shifted(raw, "vec", a) for a in range(1, vecs)]
        return raws + [shifted(raws[a], "sub", b) for b in range(1, subs) for a in range(vecs)]

    offsets = [(a, b) for b in range(subs) for a in range(vecs)]
    raws_inner, raws_rim = gathered(raw_inner), gathered(raw_rim)
    low, high, first, turned, back = call(
        rim_kernel,
        "rim",
        ((edge, WIDE), (edge, WIDE), (edge, LOW), (edge, LOW), ((2, 16, sites), WIDE)),
        (field, links),
        flops=1 << 24,
    )
    ahead_one = shifted(first, "brick", -1)
    behind_one = shifted(turned, "brick", 1)
    place = (brick * layers).astype(jnp.int32).reshape((1,))
    one, table = call(
        functools.partial(inner_kernel, total_x),
        "inner",
        ((inner, WIDE), ((2, count, sites), WIDE)),
        (place, field, links, back, momenta),
        flops=1 << 24,
        smem=True,
    )
    smeared, rest = call(
        second_kernel,
        "second",
        ((inner, WIDE), (rim, WIDE)),
        (field, links, back, low, high, one, ahead, behind),
        flops=1 << 25,
        scratch=(pltpu.VMEM(rim, WIDE),),
    )
    product = (count * width, groups * 2 * width)
    depth = 6 * LANES
    scratch = (pltpu.VMEM((product[0], depth), LOW), pltpu.VMEM((product[1], depth), LOW))
    (start,) = call(
        functools.partial(inner_product_kernel, groups),
        "inner_product",
        ((product, WIDE),),
        (smeared, table, *raws_inner),
        flops=1 << 32,
        scratch=scratch,
    )
    owners = jnp.stack([(vec - a) % vecs * subs + (sub - b) % subs for a, b in offsets])
    slots = ((owners - brick) % groups).astype(jnp.int32)
    scale = (3.0 * total_x * PLANE) ** (-0.5)
    blocks = call(
        functools.partial(last_product_kernel, groups, scale),
        "last_product",
        (((2 * width, count * width), LOW),) * groups,
        (slots, rest, ahead_one, behind_one, links, start, table, *raws_rim),
        flops=1 << 32,
        scratch=(pltpu.VMEM(rim, WIDE), pltpu.VMEM(product, WIDE)) + scratch,
        smem=True,
    )
    shares = []
    for slot, block in enumerate(blocks):
        pairs = [(b * groups + g, g * groups + (b + slot) % groups) for b in range(bricks) for g in range(groups)]
        shares.append(lax.ppermute(block, ("brick", "vec", "sub"), pairs))
    total = functools.reduce(jnp.add, [share.astype(WIDE) for share in shares])
    return jnp.transpose(total.reshape((2, width, count, width)), (1, 2, 0, 3))


def solution(mesh):
    in_specs = (
        P(("vec", "sub"), None, None, ("grp", "brick")),
        P(None, None, None, None, ("grp", "brick")),
        P(),
    )
    out_specs = P(("vec", "sub"), "grp", None, "brick")
    return jax.shard_map(shards, mesh=mesh, in_specs=in_specs, out_specs=out_specs, check_vma=False)
```

time: 108 us -> 76.9 us (0.71)
  the two profiles are of different devices: /device:TPU:0 before, /device:TPU:6 now
where the time goes in v2:
time: 76.9 us; the launch traced here: 76.7 us
  waiting for transfers between devices  29.7 us (39%)
  Pallas kernels  26 us (34%)
  starting transfers between devices  16.3 us (21%)
  local copies, waits for them, and re-layouts  4.54 us (6%)
    pallas_call x6, Pallas kernels, call(): pl.pallas_call(kernel, out_shape=tuple((jax.ShapeDtypeStruct(shape, dtype...  26 us
    ppermute x4, waiting for transfers between devices, shards(): shares.append(lax.ppermute(block, ('brick', 'vec', 'sub'), pairs))  14.9 us
    ppermute x10, waiting for transfers between devices, shifted(): lax.ppermute(array, axis, [(i, (i + by) % peers) for i in range(peers)])  14.7 us
    ppermute x4, starting transfers between devices, shards(): shares.append(lax.ppermute(block, ('brick', 'vec', 'sub'), pairs))  8.27 us
    ppermute x10, starting transfers between devices, shifted(): lax.ppermute(array, axis, [(i, (i + by) % peers) for i in range(peers)])  8.01 us
    unnamed x9, local copies, waits for them, and re-layouts  2.54 us
    transpose x1, local copies, waits for them, and re-layouts, shards(): return jnp.transpose(total.reshape((2, width, count, width)), (1, 2, 0, 3))  1.61 us
  transfers between devices with their start and end apart: 14, of which 6 were waited for; matrix products, arithmetic and copies ran while one was open for 0% of the time, Pallas kernels for 23%

profile of v2, /device:TPU:6, one launch (start us, length us, event | category | flops | bytes accessed | tf_op | source)
XLA Modules:
  0.0 76.7 jit_solution(5434295364560753151)
XLA Ops:
  0.0 1.0 %copy-done = f32[3,3,3,2,2048]{4,3,2,1,0:T(2,128)S(1)} copy-done((f32[3,3,3,2,2048]{4,3,2,1,0:T(2,128)S(1)}, f32[3,3,3,2,2048]{4,3,2,1,0:T(2,128)}, u32[]{:S(2)}) %copy-start) | copy-done | bytes 442392
  1.0 1.4 %copy-done.2 = f32[32,3,2,2048]{3,2,1,0:T(2,128)S(1)} copy-done((f32[32,3,2,2048]{3,2,1,0:T(2,128)S(1)}, f32[32,3,2,2048]{3,2,1,0:T(2,128)}, u32[]{:S(2)}) %copy-start.2) | copy-done | bytes 1572888
  2.4 2.0 %open.1 = (f32[6,32,2048]{2,1,0:T(8,128)S(1)}, bf16[6,32,1024]{2,1,0:T(8,128)(2,1)}, bf16[6,32,1024]{2,1,0:T(8,128)(2,1)S(1)}, bf16[6,32,512]{2,1,0:T(8,128)(2,1)}, bf16[6,32,512]{2,1,0:T(8,128)(2,1)S(1)}) custom-call(f32[3072,128]{1,0:T(8,128)S(1)} %bitcast.21, f32[864,128]{1,0:T(8,128)S(1)} %bitcast.16), custom_call_target="tpu_custom_call" | custom-call | bytes 1048576 | tf_op jit(solution)/shard_map/open/pallas_call | solution.py:328
  4.4 0.5 collective-permute-start.4
  5.0 1.5 %collective-permute-start.7 = (bf16[6,32,1024]{2,1,0:T(8,128)(2,1)S(1)}, bf16[6,32,1024]{2,1,0:T(8,128)(2,1)S(1)}, u32[]{:S(2)}, u32[]{:S(2)}) collective-permute-start(bf16[6,32,1024]{2,1,0:T(8,128)(2,1)S(1)} %get-tuple-element.36.refs_0_), channel_id=1, source_target_pairs={{0,2},{2,0},{1,3},{3,1},{4,6},{6,4},{5,7},{7,5},{8,10},{10,8},{9,1... | collective-permute-start | bytes 1179656 | tf_op jit(solution)/shard_map/ppermute | solution.py:28
  6.5 10.3 %collective-permute-done.4.refs_1_ = bf16[6,32,1024]{2,1,0:T(8,128)(2,1)} collective-permute-done((bf16[6,32,1024]{2,1,0:T(8,128)(2,1)}, bf16[6,32,1024]{2,1,0:T(8,128)(2,1)}, u32[]{:S(2)}, u32[]{:S(2)}) %collective-permute-start.4) | collective-permute-done | bytes 393248 | tf_op jit(solution)/shard_map/ppermute | solution.py:28
  16.7 3.6 %collective-permute-start = (bf16[6,32,512]{2,1,0:T(8,128)(2,1)}, bf16[6,32,512]{2,1,0:T(8,128)(2,1)S(1)}, u32[]{:S(2)}, u32[]{:S(2)}) collective-permute-start(bf16[6,32,512]{2,1,0:T(8,128)(2,1)} %get-tuple-element.28), channel_id=1, source_target_pairs={{0,12},{4,0},{8,4},{12,8},{1,13},{5,1},{9,5},{13,9},{2,14},{6,2},{... | collective-permute-start | bytes 589832 | tf_op jit(solution)/shard_map/ppermute | solution.py:28
  20.5 2.6 %rim.1 = (f32[6,32,512]{2,1,0:T(8,128)S(1)}, f32[6,32,512]{2,1,0:T(8,128)S(1)}, bf16[6,32,512]{2,1,0:T(8,128)(2,1)S(1)}, bf16[6,32,512]{2,1,0:T(8,128)(2,1)S(1)}, f32[2,16,2048]{2,1,0:T(8,128)S(1)}) custom-call(f32[6,32,2048]{2,1,0:T(8,128)S(1)} %get-tuple-element.23.field_ref, f32[864,128]{1,0:T(8,128)S(1)} %bitcast.17), custom_call_target="tpu_custom_call" | custom-call | flops 16777216 | bytes 1048576 | tf_op jit(solution)/shard_map/rim/pallas_call | solution.py:328
  23.1 3.3 %inner.1 = (f32[6,32,1024]{2,1,0:T(8,128)S(1)}, f32[2,27,2048]{2,1,0:T(8,128)S(1)}) custom-call(s32[1]{0:T(128)} %bitcast.12.place_ref, f32[6,32,2048]{2,1,0:T(8,128)S(1)} %get-tuple-element.23.field_ref, f32[864,128]{1,0:T(8,128)S(1)} %bitcast.18, f32[2,16,2048]{2,1,0:T(8,128)S(1)} %get-tuple-element.24.back_ref, s32[27,3]{1,0:T(8,128)S(1)} %copy.10.momenta_ref), custom_call_target="tpu_custom_call" | custom-call | flops 16777216 | bytes 1048576 | tf_op jit(solution)/shard_map/inner/pallas_call | solution.py:328
  26.8 3.7 %collective-permute-done.1.behind_ref = bf16[6,32,512]{2,1,0:T(8,128)(2,1)S(1)} collective-permute-done((bf16[6,32,512]{2,1,0:T(8,128)(2,1)S(1)}, bf16[6,32,512]{2,1,0:T(8,128)(2,1)S(1)}, u32[]{:S(2)}, u32[]{:S(2)}) %collective-permute-start.1) | collective-permute-done | bytes 196640 | tf_op jit(solution)/shard_map/ppermute | solution.py:28
  30.5 1.5 %collective-permute-start.2 = (bf16[6,32,512]{2,1,0:T(8,128)(2,1)S(1)}, bf16[6,32,512]{2,1,0:T(8,128)(2,1)S(1)}, u32[]{:S(2)}, u32[]{:S(2)}) collective-permute-start(bf16[6,32,512]{2,1,0:T(8,128)(2,1)S(1)} %get-tuple-element.31), channel_id=1, source_target_pairs={{0,12},{4,0},{8,4},{12,8},{1,13},{5,1},{9,5},{13,9},{2,14},{6,2},{... | collective-permute-start | bytes 589832 | tf_op jit(solution)/shard_map/ppermute | solution.py:28
  32.0 5.2 %second.1 = (f32[6,32,1024]{2,1,0:T(8,128)S(1)}, f32[6,32,1024]{2,1,0:T(8,128)S(1)}) custom-call(f32[6,32,2048]{2,1,0:T(8,128)S(1)} %get-tuple-element.23.field_ref, f32[864,128]{1,0:T(8,128)S(1)} %bitcast.19, f32[2,16,2048]{2,1,0:T(8,128)S(1)} %get-tuple-element.24.back_ref, f32[6,32,512]{2,1,0:T(8,128)S(1)} %get-tuple-element.25.low_ref, ...), custom_call_target="tpu_custom_call" | custom-call | flops 33554432 | bytes 1048576 | tf_op jit(solution)/shard_map/second/pallas_call | solution.py:328
  37.3 0.5 collective-permute-start.3
  37.9 6.5 %inner_product.1.start_ref = f32[864,256]{1,0:T(8,128)S(1)} custom-call(f32[6,32,1024]{2,1,0:T(8,128)S(1)} %get-tuple-element.33.field_ref, f32[2,27,2048]{2,1,0:T(8,128)S(1)} %get-tuple-element.34.table_ref, bf16[6,32,1024]{2,1,0:T(8,128)(2,1)} %get-tuple-element.35.refs_0_, bf16[6,32,1024]{2,1,0:T(8,128)(2,1)} %collective-permute-done.4.refs_1_, ...), custom_call_target="tpu_custom_call" | custom-call | flops 4294967296 | bytes 1048576 | tf_op jit(solution)/shard_map/inner_product/pallas_call | solution.py:328
  44.4 0.7 collective-permute-done.3.behind_ref
  45.1 6.3 %last_product.1 = (bf16[64,864]{1,0:T(8,128)(2,1)S(1)}, bf16[64,864]{1,0:T(8,128)(2,1)S(1)}, bf16[64,864]{1,0:T(8,128)(2,1)S(1)}, bf16[64,864]{1,0:T(8,128)(2,1)S(1)}) custom-call(s32[4]{0:T(128)S(1)} %and_select_fusion.slot_ref, f32[6,32,1024]{2,1,0:T(8,128)S(1)} %get-tuple-element.30.rim_ref, bf16[6,32,512]{2,1,0:T(8,128)(2,1)S(1)} %collective-permute-done.2.ahead_ref, ...), custom_call_target="tpu_custom_call" | custom-call | flops 4294967296 | bytes 1048576 | tf_op jit(solution)/shard_map/last_product/pallas_call | solution.py:328
  51.4 0.6 collective-permute-start.13
  52.1 0.5 collective-permute-start.12
  52.6 2.1 %collective-permute-start.11 = (bf16[64,864]{1,0:T(8,128)(2,1)S(1)}, bf16[64,864]{1,0:T(8,128)(2,1)S(1)}, u32[]{:S(2)}, u32[]{:S(2)}) collective-permute-start(bf16[64,864]{1,0:T(8,128)(2,1)S(1)} %get-tuple-element.38), channel_id=1, source_target_pairs={{0,1},{1,5},{2,9},{3,13},{4,2},{5,6},{6,10},{7,14},{8,3},{9,7},{10... | collective-permute-start | bytes 331784 | tf_op jit(solution)/shard_map/ppermute | solution.py:424
  54.7 5.0 %collective-permute-start.10 = (bf16[64,864]{1,0:T(8,128)(2,1)S(1)}, bf16[64,864]{1,0:T(8,128)(2,1)S(1)}, u32[]{:S(2)}, u32[]{:S(2)}) collective-permute-start(bf16[64,864]{1,0:T(8,128)(2,1)S(1)} %get-tuple-element.37), channel_id=1, source_target_pairs={{0,0},{1,4},{2,8},{3,12},{4,1},{5,5},{6,9},{7,13},{8,2},{9,6},{10,... | collective-permute-start | bytes 331784 | tf_op jit(solution)/shard_map/ppermute | solution.py:424
  59.7 0.6 collective-permute-done.13
  60.3 3.0 %collective-permute-done.11 = bf16[64,864]{1,0:T(8,128)(2,1)S(1)} collective-permute-done((bf16[64,864]{1,0:T(8,128)(2,1)S(1)}, bf16[64,864]{1,0:T(8,128)(2,1)S(1)}, u32[]{:S(2)}, u32[]{:S(2)}) %collective-permute-start.11) | collective-permute-done | bytes 110624 | tf_op jit(solution)/shard_map/ppermute | solution.py:424
  63.4 11.3 %collective-permute-done.10 = bf16[64,864]{1,0:T(8,128)(2,1)S(1)} collective-permute-done((bf16[64,864]{1,0:T(8,128)(2,1)S(1)}, bf16[64,864]{1,0:T(8,128)(2,1)S(1)}, u32[]{:S(2)}, u32[]{:S(2)}) %collective-permute-start.10) | collective-permute-done | bytes 110624 | tf_op jit(solution)/shard_map/ppermute | solution.py:424
  75.1 1.6 %copy.11 = f32[32,27,2,32]{3,2,1,0:T(2,128)} copy(f32[32,27,2,32]{3,1,0,2:T(8,128)S(1)} %bitcast.22) | data formatting | bytes 442368 | tf_op jit(solution)/shard_map/transpose | solution.py:426
  (23 shorter events, 1.0 us)
Async XLA Ops:
  0.0 20.4 %copy-start.3 = (s32[27,3]{0,1:T(4,128)S(1)}, s32[27,3]{0,1:T(4,128)}, u32[]{:S(2)}) copy-start(s32[27,3]{0,1:T(4,128)} %param.5) | copy-start | bytes 976
  0.0 1.0 %copy-start = (f32[3,3,3,2,2048]{4,3,2,1,0:T(2,128)S(1)}, f32[3,3,3,2,2048]{4,3,2,1,0:T(2,128)}, u32[]{:S(2)}) copy-start(f32[3,3,3,2,2048]{4,3,2,1,0:T(2,128)} %param.4) | copy-start | bytes 1327108
  1.0 1.4 %copy-start.2 = (f32[32,3,2,2048]{3,2,1,0:T(2,128)S(1)}, f32[32,3,2,2048]{3,2,1,0:T(2,128)}, u32[]{:S(2)}) copy-start(f32[32,3,2,2048]{3,2,1,0:T(2,128)} %param.3) | copy-start | bytes 4718596
  2.4 18.0 %copy-start.1 = (f32[3,3,3,2,2048]{4,3,2,1,0:T(2,128)S(1)}, f32[3,3,3,2,2048]{4,3,2,1,0:T(2,128)}, u32[]{:S(2)}) copy-start(f32[3,3,3,2,2048]{4,3,2,1,0:T(2,128)} %param.4) | copy-start | bytes 1327108
  4.4 12.3 %collective-permute-start.4 = (bf16[6,32,1024]{2,1,0:T(8,128)(2,1)}, bf16[6,32,1024]{2,1,0:T(8,128)(2,1)}, u32[]{:S(2)}, u32[]{:S(2)}) collective-permute-start(bf16[6,32,1024]{2,1,0:T(8,128)(2,1)} %get-tuple-element.35.refs_0_), channel_id=1, source_target_pairs={{0,2},{2,0},{1,3},{3,1},{4,6},{6,4},{5,7},{7,5},{8,10},{10,8},{9,1... | collective-permute-start | bytes 1179656 | tf_op jit(solution)/shard_map/ppermute | solution.py:28
  5.0 32.3 %collective-permute-start.5 = (bf16[6,32,1024]{2,1,0:T(8,128)(2,1)}, bf16[6,32,1024]{2,1,0:T(8,128)(2,1)}, u32[]{:S(2)}, u32[]{:S(2)}) collective-permute-start(bf16[6,32,1024]{2,1,0:T(8,128)(2,1)} %get-tuple-element.35.refs_0_), channel_id=1, source_target_pairs={{0,1},{1,0},{2,3},{3,2},{4,5},{5,4},{6,7},{7,6},{8,9},{9,8},{10,11... | collective-permute-start | bytes 1179656 | tf_op jit(solution)/shard_map/ppermute | solution.py:28
  5.0 32.9 %collective-permute-start.7 = (bf16[6,32,1024]{2,1,0:T(8,128)(2,1)S(1)}, bf16[6,32,1024]{2,1,0:T(8,128)(2,1)S(1)}, u32[]{:S(2)}, u32[]{:S(2)}) collective-permute-start(bf16[6,32,1024]{2,1,0:T(8,128)(2,1)S(1)} %get-tuple-element.36.refs_0_), channel_id=1, source_target_pairs={{0,2},{2,0},{1,3},{3,1},{4,6},{6,4},{5,7},{7,5},{8,10},{10,8},{9,1... | collective-permute-start | bytes 1179656 | tf_op jit(solution)/shard_map/ppermute | solution.py:28
  16.7 21.1 %collective-permute-start.6 = (bf16[6,32,1024]{2,1,0:T(8,128)(2,1)}, bf16[6,32,1024]{2,1,0:T(8,128)(2,1)}, u32[]{:S(2)}, u32[]{:S(2)}) collective-permute-start(bf16[6,32,1024]{2,1,0:T(8,128)(2,1)} %collective-permute-done.4.refs_1_), channel_id=1, source_target_pairs={{0,1},{1,0},{2,3},{3,2},{4,5},{5,4},{6,7},{7,6},{8,9},{9,8},{10,11... | collective-permute-start | bytes 1179656 | tf_op jit(solution)/shard_map/ppermute | solution.py:28
  16.7 9.7 %collective-permute-start = (bf16[6,32,512]{2,1,0:T(8,128)(2,1)}, bf16[6,32,512]{2,1,0:T(8,128)(2,1)S(1)}, u32[]{:S(2)}, u32[]{:S(2)}) collective-permute-start(bf16[6,32,512]{2,1,0:T(8,128)(2,1)} %get-tuple-element.28), channel_id=1, source_target_pairs={{0,12},{4,0},{8,4},{12,8},{1,13},{5,1},{9,5},{13,9},{2,14},{6,2},{... | collective-permute-start | bytes 589832 | tf_op jit(solution)/shard_map/ppermute | solution.py:28
  20.3 10.2 %collective-permute-start.1 = (bf16[6,32,512]{2,1,0:T(8,128)(2,1)S(1)}, bf16[6,32,512]{2,1,0:T(8,128)(2,1)S(1)}, u32[]{:S(2)}, u32[]{:S(2)}) collective-permute-start(bf16[6,32,512]{2,1,0:T(8,128)(2,1)S(1)} %get-tuple-element.29), channel_id=1, source_target_pairs={{0,4},{4,8},{8,12},{12,0},{1,5},{5,9},{9,13},{13,1},{2,6},{6,10},{... | collective-permute-start | bytes 589832 | tf_op jit(solution)/shard_map/ppermute | solution.py:28
  26.5 18.6 %collective-permute-start.8 = (bf16[6,32,1024]{2,1,0:T(8,128)(2,1)S(1)}, bf16[6,32,1024]{2,1,0:T(8,128)(2,1)S(1)}, u32[]{:S(2)}, u32[]{:S(2)}) collective-permute-start(bf16[6,32,1024]{2,1,0:T(8,128)(2,1)S(1)} %get-tuple-element.36.refs_0_), channel_id=1, source_target_pairs={{0,1},{1,0},{2,3},{3,2},{4,5},{5,4},{6,7},{7,6},{8,9},{9,8},{10,11... | collective-permute-start | bytes 1179656 | tf_op jit(solution)/shard_map/ppermute | solution.py:28
  30.5 13.9 %collective-permute-start.2 = (bf16[6,32,512]{2,1,0:T(8,128)(2,1)S(1)}, bf16[6,32,512]{2,1,0:T(8,128)(2,1)S(1)}, u32[]{:S(2)}, u32[]{:S(2)}) collective-permute-start(bf16[6,32,512]{2,1,0:T(8,128)(2,1)S(1)} %get-tuple-element.31), channel_id=1, source_target_pairs={{0,12},{4,0},{8,4},{12,8},{1,13},{5,1},{9,5},{13,9},{2,14},{6,2},{... | collective-permute-start | bytes 589832 | tf_op jit(solution)/shard_map/ppermute | solution.py:28
  37.3 7.8 %collective-permute-start.3 = (bf16[6,32,512]{2,1,0:T(8,128)(2,1)S(1)}, bf16[6,32,512]{2,1,0:T(8,128)(2,1)S(1)}, u32[]{:S(2)}, u32[]{:S(2)}) collective-permute-start(bf16[6,32,512]{2,1,0:T(8,128)(2,1)S(1)} %get-tuple-element.32), channel_id=1, source_target_pairs={{0,4},{4,8},{8,12},{12,0},{1,5},{5,9},{9,13},{13,1},{2,6},{6,10},{... | collective-permute-start | bytes 589832 | tf_op jit(solution)/shard_map/ppermute | solution.py:28
  37.8 7.2 %collective-permute-start.9 = (bf16[6,32,1024]{2,1,0:T(8,128)(2,1)S(1)}, bf16[6,32,1024]{2,1,0:T(8,128)(2,1)S(1)}, u32[]{:S(2)}, u32[]{:S(2)}) collective-permute-start(bf16[6,32,1024]{2,1,0:T(8,128)(2,1)S(1)} %collective-permute-done.7.refs_1_), channel_id=1, source_target_pairs={{0,1},{1,0},{2,3},{3,2},{4,5},{5,4},{6,7},{7,6},{8,9},{9,8},{10,11... | collective-permute-start | bytes 1179656 | tf_op jit(solution)/shard_map/ppermute | solution.py:28
  51.4 8.9 %collective-permute-start.13 = (bf16[64,864]{1,0:T(8,128)(2,1)S(1)}, bf16[64,864]{1,0:T(8,128)(2,1)S(1)}, u32[]{:S(2)}, u32[]{:S(2)}) collective-permute-start(bf16[64,864]{1,0:T(8,128)(2,1)S(1)} %get-tuple-element.40), channel_id=1, source_target_pairs={{0,3},{1,7},{2,11},{3,15},{4,0},{5,4},{6,8},{7,12},{8,1},{9,5},{10... | collective-permute-start | bytes 331784 | tf_op jit(solution)/shard_map/ppermute | solution.py:424
  52.1 8.2 %collective-permute-start.12 = (bf16[64,864]{1,0:T(8,128)(2,1)S(1)}, bf16[64,864]{1,0:T(8,128)(2,1)S(1)}, u32[]{:S(2)}, u32[]{:S(2)}) collective-permute-start(bf16[64,864]{1,0:T(8,128)(2,1)S(1)} %get-tuple-element.39), channel_id=1, source_target_pairs={{0,2},{1,6},{2,10},{3,14},{4,3},{5,7},{6,11},{7,15},{8,0},{9,4},{1... | collective-permute-start | bytes 331784 | tf_op jit(solution)/shard_map/ppermute | solution.py:424
  52.6 10.8 %collective-permute-start.11 = (bf16[64,864]{1,0:T(8,128)(2,1)S(1)}, bf16[64,864]{1,0:T(8,128)(2,1)S(1)}, u32[]{:S(2)}, u32[]{:S(2)}) collective-permute-start(bf16[64,864]{1,0:T(8,128)(2,1)S(1)} %get-tuple-element.38), channel_id=1, source_target_pairs={{0,1},{1,5},{2,9},{3,13},{4,2},{5,6},{6,10},{7,14},{8,3},{9,7},{10... | collective-permute-start | bytes 331784 | tf_op jit(solution)/shard_map/ppermute | solution.py:424
  54.7 20.0 %collective-permute-start.10 = (bf16[64,864]{1,0:T(8,128)(2,1)S(1)}, bf16[64,864]{1,0:T(8,128)(2,1)S(1)}, u32[]{:S(2)}, u32[]{:S(2)}) collective-permute-start(bf16[64,864]{1,0:T(8,128)(2,1)S(1)} %get-tuple-element.37), channel_id=1, source_target_pairs={{0,0},{1,4},{2,8},{3,12},{4,1},{5,5},{6,9},{7,13},{8,2},{9,6},{10,... | collective-permute-start | bytes 331784 | tf_op jit(solution)/shard_map/ppermute | solution.py:424

commit v3 on v2

v3 whole, which is shorter than its diff:
```python
import functools
import math

import jax
import jax.numpy as jnp
from jax import lax
from jax.experimental import pallas as pl
from jax.experimental.pallas import tpu as pltpu
from jax.sharding import PartitionSpec as P

LY = 64
LZ = 8
ITERS = 2
KAPPA = 0.125
LANES = 128
PLANE = LY * LZ
TILES = PLANE // LANES
ROWS = 16
BYTES = 1 << 20
LOW = jnp.bfloat16
WIDE = jnp.float32
STEP = 2
CHUNKS = 2
VMEM_LIMIT = 40 * 1024 * 1024
VMEM = pl.BlockSpec(memory_space=pltpu.VMEM)
SMEM = pl.BlockSpec(memory_space=pltpu.SMEM)


def shifted(array, axis, by):
    peers = lax.axis_size(axis)
    return lax.ppermute(array, axis, [(i, (i + by) % peers) for i in range(peers)])


def add_hop(total, link, field, adjoint):
    for row in range(3):
        for column in range(3):
            if adjoint:
                real, imag = link(column, row, 0), link(column, row, 1)
            else:
                real, imag = link(row, column, 0), link(row, column, 1)
            source_real, source_imag = field[2 * column], field[2 * column + 1]
            if adjoint:
                add_real = real * source_real + imag * source_imag
                add_imag = real * source_imag - imag * source_real
            else:
                add_real = real * source_real - imag * source_imag
                add_imag = real * source_imag + imag * source_real
            for part, add in ((0, add_real), (1, add_imag)):
                old = total[2 * row + part]
                total[2 * row + part] = add if old is None else old + add


def lane_roll(value, by):
    return pltpu.roll(value, by % LANES, 1)


def lanes_at(layer, tile):
    return pl.ds(pl.multiple_of(layer * PLANE + tile * LANES, LANES), LANES)


def row_groups(ref):
    size = min(ROWS, ref.shape[1])
    return [pl.ds(start, size) for start in range(0, ref.shape[1], size)]


def load(ref, rows, lanes):
    return [ref[k, rows, lanes].astype(WIDE) for k in range(6)]


def store(ref, rows, lanes, values):
    for k in range(6):
        ref[k, rows, lanes] = values[k].astype(ref.dtype)


def link_at(link_ref, direction, layer, tile):
    tiles = link_ref.shape[0] // 54

    def get(row, column, part):
        matrix = (direction * 3 + row) * 3 + column
        return link_ref[pl.ds((matrix * tiles + layer * TILES + tile) * 2 + part, 1), :]

    return get


def plane_hops(total, link_ref, back_ref, layer, tile, rows, fetch):
    here = fetch(tile)
    after, before = fetch((tile + 1) % TILES), fetch((tile + TILES - 1) % TILES)
    lane = lax.broadcasted_iota(jnp.int32, (rows.size, LANES), 1)
    ahead = [jnp.where(lane >= LANES - LZ, lane_roll(b, -LZ), lane_roll(a, -LZ)) for a, b in zip(here, after)]
    add_hop(total, link_at(link_ref, 1, layer, tile), ahead, False)
    behind = [jnp.where(lane < LZ, lane_roll(b, LZ), lane_roll(a, LZ)) for a, b in zip(here, before)]
    lanes = lanes_at(layer, tile)
    add_hop(total, lambda r, c, part: back_ref[part, pl.ds(3 * r + c, 1), lanes], behind, True)
    depth = lane % LZ
    ahead = [jnp.where(depth == LZ - 1, lane_roll(a, LZ - 1), lane_roll(a, -1)) for a in here]
    add_hop(total, link_at(link_ref, 2, layer, tile), ahead, False)
    turned = [None] * 6
    add_hop(turned, link_at(link_ref, 2, layer, tile), here, True)
    for k in range(6):
        total[k] += jnp.where(depth == 0, lane_roll(turned[k], 1 - LZ), lane_roll(turned[k], 1))
    return here


def combined(here, total):
    return [(1.0 - 6.0 * KAPPA) * a + KAPPA * b for a, b in zip(here, total)]


def first_step(layer, tile, rows, field_ref, link_ref, back_ref):
    layers = field_ref.shape[2] // PLANE
    total = [None] * 6
    if layer < layers - 1:
        source = load(field_ref, rows, lanes_at(layer + 1, tile))
        add_hop(total, link_at(link_ref, 0, layer, tile), source, False)
    if layer > 0:
        source = load(field_ref, rows, lanes_at(layer - 1, tile))
        add_hop(total, link_at(link_ref, 0, layer - 1, tile), source, True)
    fetch = lambda t: load(field_ref, rows, lanes_at(layer, t))
    return combined(plane_hops(total, link_ref, back_ref, layer, tile, rows, fetch), total)


def open_kernel(vector_ref, link_ref, field_ref, raw_ref, down_ref, up_ref, rim_ref, back_ref):
    vectors, sites = field_ref.shape[1:]
    tiles, layers = sites // LANES, sites // PLANE
    stride = 6 * tiles
    for k in range(6):
        for tile in range(tiles):
            row = ((k // 2) * tiles + tile) * 2 + k % 2
            value = vector_ref[pl.ds(row, vectors, stride=stride), :]
            field_ref[k, :, pl.ds(tile * LANES, LANES)] = value
            low = value.astype(LOW)
            raw_ref[k, :, pl.ds(tile * LANES, LANES)] = low
            if tile < TILES:
                down_ref[k, :, pl.ds(tile * LANES, LANES)] = low
    lane = lax.broadcasted_iota(jnp.int32, (9, LANES), 1)
    for layer in range(layers):
        for part in range(2):
            row = lambda tile: (9 * tiles + layer * TILES + tile) * 2 + part
            value = [link_ref[pl.ds(row(tile), 9, stride=2 * tiles), :] for tile in range(TILES)]
            value = [lane_roll(v, LZ) for v in value]
            for tile in range(TILES):
                back_ref[part, pl.ds(0, 9), lanes_at(layer, tile)] = jnp.where(lane < LZ, value[tile - 1], value[tile])

    for place, layer in enumerate((0, layers - 1)):

        @pl.loop(0, TILES)
        def _(tile):
            lanes = lanes_at(0, tile)
            for rows in row_groups(field_ref):
                new = first_step(layer, tile, rows, field_ref, link_ref, back_ref)
                store(rim_ref, rows, lanes_at(place, tile), new)
                if place == 0:
                    store(down_ref.at[pl.ds(6, 6)], rows, lanes, new)
                else:
                    here = load(field_ref, rows, lanes_at(layer, tile))
                    for part, source in enumerate((here, new)):
                        turned = [None] * 6
                        add_hop(turned, link_at(link_ref, 0, layer, tile), source, True)
                        store(up_ref.at[pl.ds(6 * part, 6)], rows, lanes, turned)


def unit_phase(turns):
    half = math.pi * (turns - jnp.round(turns))
    square = half * half
    cosine, sine = 1.0, 1.0
    for order in range(12, 0, -2):
        sine = 1.0 - square * sine * (1.0 / (order * (order + 1)))
        cosine = 1.0 - square * cosine * (1.0 / (order * (order - 1)))
    sine = half * sine
    return 1.0 - 2.0 * sine * sine, 2.0 * sine * cosine


def local_kernel(
    total_x, place_ref, field_ref, link_ref, back_ref, rim_ref, momenta_ref, out_ref, table_ref, one_ref
):
    layers = field_ref.shape[2] // PLANE
    count = momenta_ref.shape[0]
    momenta = momenta_ref[...].astype(WIDE)
    lane = lax.broadcasted_iota(jnp.int32, (count, LANES), 1)

    @pl.loop(0, TILES)
    def _(tile):
        column = (tile * (LANES // LZ) + lane // LZ).astype(WIDE)
        depth = (lane % LZ).astype(WIDE)
        turns = [momenta[:, 1:2] * column / LY, momenta[:, 2:3] * depth / LZ]
        part = sum(t - jnp.round(t) for t in turns)
        for layer in range(layers):
            along = momenta[:, 0:1] * (place_ref[0] + layer).astype(WIDE) / total_x
            cosine, sine = unit_phase(along - jnp.round(along) + part)
            table_ref[0, :, lanes_at(layer, tile)] = cosine
            table_ref[1, :, lanes_at(layer, tile)] = sine


    one_ref[:, :, pl.ds(0, PLANE)] = rim_ref[:, :, pl.ds(0, PLANE)]
    one_ref[:, :, pl.ds((layers - 1) * PLANE, PLANE)] = rim_ref[:, :, pl.ds(PLANE, PLANE)]
    for layer in range(1, layers - 1):

        @pl.loop(0, TILES)
        def _(tile):
            for rows in row_groups(field_ref):
                new = first_step(layer, tile, rows, field_ref, link_ref, back_ref)
                store(one_ref, rows, lanes_at(layer, tile), new)

    for layer in range(layers):

        @pl.loop(0, TILES)
        def _(tile):
            for rows in row_groups(field_ref):
                new = first_step(layer, tile, rows, one_ref, link_ref, back_ref)
                if layer in (0, layers - 1):
                    own = load(field_ref, rows, lanes_at(layer, tile))
                    new = [a + KAPPA * KAPPA * b for a, b in zip(new, own)]
                store(out_ref, rows, lanes_at(layer, tile), new)


def close_kernel(part_ref, ahead_ref, behind_ref, link_ref, back_ref, out_ref, change_ref):
    layers = part_ref.shape[2] // PLANE
    fresh, older = pl.ds(6, 6), pl.ds(0, 6)

    @pl.loop(0, TILES)
    def _(tile):
        lanes = lanes_at(0, tile)
        for rows in row_groups(part_ref):
            low = load(behind_ref.at[older], rows, lanes)
            store(change_ref, rows, lanes, [KAPPA * a for a in low])
            high = [None] * 6
            add_hop(high, link_at(link_ref, 0, layers - 1, tile), load(ahead_ref.at[older], rows, lanes), False)
            store(change_ref, rows, lanes_at(1, tile), [KAPPA * a for a in high])

    for layer in range(layers):

        @pl.loop(0, TILES)
        def _(tile):
            lanes = lanes_at(0, tile)
            for rows in row_groups(part_ref):
                new = load(part_ref, rows, lanes_at(layer, tile))
                change = lambda place, t: load(change_ref, rows, lanes_at(place, t))
                hops = [None] * 6
                if layer == 1:
                    add_hop(hops, link_at(link_ref, 0, 0, tile), change(0, tile), True)
                if layer == layers - 2:
                    add_hop(hops, link_at(link_ref, 0, layer, tile), change(1, tile), False)
                if layer == 0:
                    came = load(behind_ref.at[fresh], rows, lanes)
                    hops = came if hops[0] is None else [a + b for a, b in zip(hops, came)]
                if layer == layers - 1:
                    add_hop(hops, link_at(link_ref, 0, layer, tile), load(ahead_ref.at[fresh], rows, lanes), False)
                for place, edge in ((0, 0), (1, layers - 1)):
                    if layer == edge:
                        here = plane_hops(hops, link_ref, back_ref, layer, tile, rows, lambda t: change(place, t))
                        new = [a + (1.0 - 6.0 * KAPPA) * b for a, b in zip(new, here)]
                if hops[0] is not None:
                    new = [a + KAPPA * b for a, b in zip(new, hops)]
                store(out_ref, rows, lanes_at(layer, tile), new)


def product_kernel(groups, begin, count, scale, slot_ref, field_ref, table_ref, *refs):
    raw_refs, out_refs, (total_ref, left_ref, right_ref) = refs[:groups], refs[groups : 2 * groups], refs[2 * groups :]
    vectors = field_ref.shape[1]
    depth = 6 * LANES
    step = left_ref.shape[1] // depth
    total_ref[...] = jnp.zeros_like(total_ref)

    @pl.loop(0, field_ref.shape[2] // LANES // step)
    def _(block):
        for part in range(step):
            lanes = pl.ds(pl.multiple_of((block * step + part) * LANES, LANES), LANES)
            field = [field_ref[k, :, lanes] for k in range(6)]
            one = [pl.ds(part * depth + 2 * color * LANES, LANES) for color in range(3)]
            two = [pl.ds(part * depth + (2 * color + 1) * LANES, LANES) for color in range(3)]
            for p in range(count):
                cosine = table_ref[0, pl.ds(begin + p, 1), lanes]
                sine = table_ref[1, pl.ds(begin + p, 1), lanes]
                rows = pl.ds(p * vectors, vectors)
                for color in range(3):
                    real, imag = field[2 * color], field[2 * color + 1]
                    right_ref[rows, one[color]] = (cosine * real + sine * imag).astype(LOW)
                    right_ref[rows, two[color]] = (cosine * imag - sine * real).astype(LOW)
            for g, raw_ref in enumerate(raw_refs):
                width = raw_ref.shape[1]
                first = pl.ds(2 * g * width, width)
                second = pl.ds((2 * g + 1) * width, width)
                for color in range(3):
                    real, imag = raw_ref[2 * color, :, lanes], raw_ref[2 * color + 1, :, lanes]
                    left_ref[first, one[color]] = real
                    left_ref[first, two[color]] = imag
                    left_ref[second, one[color]] = -imag
                    left_ref[second, two[color]] = real
        total_ref[...] += lax.dot_general(
            left_ref[...], right_ref[...], (((1,), (1,)), ((), ())), preferred_element_type=WIDE
        )

    width = total_ref.shape[0] // groups
    for g in range(groups):
        block = (total_ref[pl.ds(g * width, width), :] * scale).astype(out_refs[0].dtype)
        for slot in range(groups):

            @pl.when(slot_ref[g] == slot)
            def _():
                out_refs[slot][...] = block


def call(kernel, name, shapes, operands, flops=0, scratch=(), smem=False):
    return pl.pallas_call(
        kernel,
        out_shape=tuple(jax.ShapeDtypeStruct(shape, dtype) for shape, dtype in shapes),
        in_specs=[SMEM if smem and i == 0 else VMEM for i in range(len(operands))],
        out_specs=(VMEM,) * len(shapes),
        scratch_shapes=list(scratch),
        compiler_params=pltpu.CompilerParams(vmem_limit_bytes=VMEM_LIMIT),
        cost_estimate=pl.CostEstimate(flops=flops, bytes_accessed=BYTES, transcendentals=0),
        name=name,
    )(*operands)


def shards(vectors, gauge_links, momenta):
    bricks, vecs, subs = (lax.axis_size(axis) for axis in ("brick", "vec", "sub"))
    groups = vecs * subs
    width, sites = vectors.shape[0], vectors.shape[3]
    layers, tiles = sites // PLANE, sites // LANES
    assert groups == bricks and layers > 1 and ITERS == 2
    total_x = bricks * layers
    count = momenta.shape[0]
    brick, vec, sub = (lax.axis_index(axis) for axis in ("brick", "vec", "sub"))
    tiled_vectors = jnp.swapaxes(vectors.reshape((width, 3, 2, tiles, LANES)), 2, 3).reshape((-1, LANES))
    links = jnp.swapaxes(gauge_links.reshape((27, 2, tiles, LANES)), 1, 2).reshape((-1, LANES))
    full, faces = (6, width, sites), (12, width, PLANE)
    field, raw, down, up, rim, back = call(
        open_kernel,
        "open",
        ((full, WIDE), (full, LOW), (faces, LOW), (faces, LOW), ((6, width, 2 * PLANE), WIDE), ((2, 16, sites), WIDE)),
        (tiled_vectors, links),
        flops=1 << 24,
    )
    ahead, behind = shifted(down, "brick", -1), shifted(up, "brick", 1)
    across = [shifted(raw, "vec", a) for a in range(1, vecs)]
    beside = [shifted(raw, "sub", b) for b in range(1, subs)]
    place = (brick * layers).astype(jnp.int32).reshape((1,))
    part, table = call(
        functools.partial(local_kernel, total_x),
        "local",
        ((full, WIDE), ((2, count, sites), WIDE)),
        (place, field, links, back, rim, momenta),
        flops=1 << 25,
        scratch=(pltpu.VMEM(full, WIDE),),
        smem=True,
    )
    *across, ahead, behind, part = lax.optimization_barrier((*across, ahead, behind, part))
    raws = [raw, *across, *beside]
    raws += [shifted(array, "sub", b) for b in range(1, subs) for array in across]
    offsets = [(a, 0) for a in range(vecs)] + [(0, b) for b in range(1, subs)]
    offsets += [(a, b) for b in range(1, subs) for a in range(1, vecs)]
    (smeared,) = call(
        close_kernel,
        "close",
        ((full, WIDE),),
        (part, ahead, behind, links, back),
        flops=1 << 24,
        scratch=(pltpu.VMEM((6, width, 2 * PLANE), WIDE),),
    )
    owners = jnp.stack([(vec - a) % vecs * subs + (sub - b) % subs for a, b in offsets])
    slots = ((owners - brick) % groups).astype(jnp.int32)
    scale = (3.0 * total_x * PLANE) ** (-0.5)
    depth = STEP * 6 * LANES
    totals = []
    bounds = [count * n // CHUNKS for n in range(CHUNKS + 1)]
    for begin, end in zip(bounds[:-1], bounds[1:]):
        columns = (end - begin) * width
        blocks = call(
            functools.partial(product_kernel, groups, begin, end - begin, scale),
            "product",
            (((2 * width, columns), LOW),) * groups,
            (slots, smeared, table, *raws),
            flops=1 << 31,
            scratch=(
                pltpu.VMEM((groups * 2 * width, columns), WIDE),
                pltpu.VMEM((groups * 2 * width, depth), LOW),
                pltpu.VMEM((columns, depth), LOW),
            ),
            smem=True,
        )
        shares = []
        for slot, block in enumerate(blocks):
            pairs = [(b * groups + g, g * groups + (b + slot) % groups) for b in range(bricks) for g in range(groups)]
            shares.append(lax.ppermute(block, ("brick", "vec", "sub"), pairs))
        total = functools.reduce(jnp.add, [share.astype(WIDE) for share in shares])
        totals.append(total.reshape((2, width, end - begin, width)))
    return jnp.transpose(jnp.concatenate(totals, axis=2), (1, 2, 0, 3))


def solution(mesh):
    in_specs = (
        P(("vec", "sub"), None, None, ("grp", "brick")),
        P(None, None, None, None, ("grp", "brick")),
        P(),
    )
    out_specs = P(("vec", "sub"), "grp", None, "brick")
    return jax.shard_map(shards, mesh=mesh, in_specs=in_specs, out_specs=out_specs, check_vma=False)
```

time: 76.9 us -> 75.6 us (0.983)
  the two profiles are of different devices: /device:TPU:6 before, /device:TPU:1 now
where the time goes in v3:
time: 75.6 us; the launch traced here: 75.3 us
  Pallas kernels  32.5 us (43%)
  starting transfers between devices  21 us (28%)
  waiting for transfers between devices  13.5 us (18%)
  local copies, waits for them, and re-layouts  7.81 us (10%)
    pallas_call x5, Pallas kernels, call(): pl.pallas_call(kernel, out_shape=tuple((jax.ShapeDtypeStruct(shape, dtype...  32.5 us
    ppermute x8, starting transfers between devices, shards(): shares.append(lax.ppermute(block, ('brick', 'vec', 'sub'), pairs))  12.5 us
    ppermute x5, starting transfers between devices, shifted(): lax.ppermute(array, axis, [(i, (i + by) % peers) for i in range(peers)])  8.47 us
    ppermute x8, waiting for transfers between devices, shards(): shares.append(lax.ppermute(block, ('brick', 'vec', 'sub'), pairs))  7.99 us
    unnamed x17, local copies, waits for them, and re-layouts  5.9 us
    ppermute x5, waiting for transfers between devices, shifted(): lax.ppermute(array, axis, [(i, (i + by) % peers) for i in range(peers)])  5.55 us
    transpose x1, local copies, waits for them, and re-layouts, shards(): return jnp.transpose(jnp.concatenate(totals, axis=2), (1, 2, 0, 3))  1.61 us
  transfers between devices with their start and end apart: 13, of which 3 were waited for; matrix products, arithmetic and copies ran while one was open for 0% of the time, Pallas kernels for 27%

profile of v3, /device:TPU:1, one launch (start us, length us, event | category | flops | bytes accessed | tf_op | source)
XLA Modules:
  0.0 75.3 jit_solution(1747971568628927341)
XLA Ops:
  0.0 1.0 %copy-done = f32[3,3,3,2,2048]{4,3,2,1,0:T(2,128)S(1)} copy-done((f32[3,3,3,2,2048]{4,3,2,1,0:T(2,128)S(1)}, f32[3,3,3,2,2048]{4,3,2,1,0:T(2,128)}, u32[]{:S(2)}) %copy-start) | copy-done | bytes 442392
  1.0 1.4 %copy-done.2 = f32[32,3,2,2048]{3,2,1,0:T(2,128)S(1)} copy-done((f32[32,3,2,2048]{3,2,1,0:T(2,128)S(1)}, f32[32,3,2,2048]{3,2,1,0:T(2,128)}, u32[]{:S(2)}) %copy-start.2) | copy-done | bytes 1572888
  2.4 4.8 %open.1 = (f32[6,32,2048]{2,1,0:T(8,128)S(1)}, bf16[6,32,2048]{2,1,0:T(8,128)(2,1)}, bf16[12,32,512]{2,1,0:T(8,128)(2,1)}, bf16[12,32,512]{2,1,0:T(8,128)(2,1)},...) custom-call(f32[3072,128]{1,0:T(8,128)S(1)} %bitcast.20, f32[864,128]{1,0:T(8,128)S(1)} %bitcast.17), custom_call_target="tpu_custom_call" | custom-call | flops 16777216 | bytes 1048576 | tf_op jit(solution)/shard_map/open/pallas_call | solution.py:303
  7.2 2.0 %collective-permute-start = (bf16[6,32,2048]{2,1,0:T(8,128)(2,1)}, bf16[6,32,2048]{2,1,0:T(8,128)(2,1)}, u32[]{:S(2)}, u32[]{:S(2)}) collective-permute-start(bf16[6,32,2048]{2,1,0:T(8,128)(2,1)} %get-tuple-element.25.refs_0_), channel_id=1, source_target_pairs={{0,2},{2,0},{1,3},{3,1},{4,6},{6,4},{5,7},{7,5},{8,10},{10,8},{9,1... | collective-permute-start | bytes 2359304 | tf_op jit(solution)/shard_map/ppermute | solution.py:31
  9.3 3.3 %collective-permute-start.1 = (bf16[12,32,512]{2,1,0:T(8,128)(2,1)}, bf16[12,32,512]{2,1,0:T(8,128)(2,1)S(1)}, u32[]{:S(2)}, u32[]{:S(2)}) collective-permute-start(bf16[12,32,512]{2,1,0:T(8,128)(2,1)} %get-tuple-element.26), channel_id=1, source_target_pairs={{0,12},{4,0},{8,4},{12,8},{1,13},{5,1},{9,5},{13,9},{2,14},{6,2},{... | collective-permute-start | bytes 1179656 | tf_op jit(solution)/shard_map/ppermute | solution.py:31
  12.6 1.2 %collective-permute-start.3 = (bf16[6,32,2048]{2,1,0:T(8,128)(2,1)}, bf16[6,32,2048]{2,1,0:T(8,128)(2,1)}, u32[]{:S(2)}, u32[]{:S(2)}) collective-permute-start(bf16[6,32,2048]{2,1,0:T(8,128)(2,1)} %get-tuple-element.25.refs_0_), channel_id=1, source_target_pairs={{0,1},{1,0},{2,3},{3,2},{4,5},{5,4},{6,7},{7,6},{8,9},{9,8},{10,11... | collective-permute-start | bytes 2359304 | tf_op jit(solution)/shard_map/ppermute | solution.py:31
  13.9 8.3 %local.1 = (f32[6,32,2048]{2,1,0:T(8,128)S(1)}, f32[2,27,2048]{2,1,0:T(8,128)S(1)}) custom-call(s32[1]{0:T(128)} %bitcast.10.place_ref, f32[6,32,2048]{2,1,0:T(8,128)S(1)} %get-tuple-element.28.field_ref, f32[864,128]{1,0:T(8,128)S(1)} %bitcast.18, f32[2,16,2048]{2,1,0:T(8,128)S(1)} %get-tuple-element.29.back_ref, ...), custom_call_target="tpu_custom_call" | custom-call | flops 33554432 | bytes 1048576 | tf_op jit(solution)/shard_map/local/pallas_call | solution.py:303
  22.2 1.1 %copy-done.3 = f32[6,32,2048]{2,1,0:T(8,128)} copy-done((f32[6,32,2048]{2,1,0:T(8,128)}, f32[6,32,2048]{2,1,0:T(8,128)S(1)}, u32[]{:S(2)}) %copy-start.3) | copy-done | bytes 1572888
  23.3 0.8 %copy-done.5 = f32[2,27,2048]{2,1,0:T(8,128)} copy-done((f32[2,27,2048]{2,1,0:T(8,128)}, f32[2,27,2048]{2,1,0:T(8,128)S(1)}, u32[]{:S(2)}) %copy-start.5) | copy-done | bytes 442392
  24.1 5.5 %collective-permute-done.2.behind_ref = bf16[12,32,512]{2,1,0:T(8,128)(2,1)} collective-permute-done((bf16[12,32,512]{2,1,0:T(8,128)(2,1)}, bf16[12,32,512]{2,1,0:T(8,128)(2,1)}, u32[]{:S(2)}, u32[]{:S(2)}) %collective-permute-start.2) | collective-permute-done | bytes 393248 | tf_op jit(solution)/shard_map/ppermute | solution.py:31
  29.7 1.9 %collective-permute-start.4 = (bf16[6,32,2048]{2,1,0:T(8,128)(2,1)}, bf16[6,32,2048]{2,1,0:T(8,128)(2,1)S(1)}, u32[]{:S(2)}, u32[]{:S(2)}) collective-permute-start(bf16[6,32,2048]{2,1,0:T(8,128)(2,1)} %collective-permute-done.refs_1_), channel_id=1, source_target_pairs={{0,1},{1,0},{2,3},{3,2},{4,5},{5,4},{6,7},{7,6},{8,9},{9,8},{10,11... | collective-permute-start | bytes 2359304 | tf_op jit(solution)/shard_map/ppermute | solution.py:31
  31.6 1.4 %copy-done.4 = f32[6,32,2048]{2,1,0:T(8,128)S(1)} copy-done((f32[6,32,2048]{2,1,0:T(8,128)S(1)}, f32[6,32,2048]{2,1,0:T(8,128)}, u32[]{:S(2)}) %copy-start.4) | copy-done | bytes 1572888
  33.1 4.0 %close.1.field_ref = f32[6,32,2048]{2,1,0:T(8,128)S(1)} custom-call(f32[6,32,2048]{2,1,0:T(8,128)S(1)} %copy-done.4, bf16[12,32,512]{2,1,0:T(8,128)(2,1)S(1)} %collective-permute-done.1.ahead_ref, bf16[12,32,512]{2,1,0:T(8,128)(2,1)} %collective-permute-done.2.behind_ref, f32[864,128]{1,0:T(8,128)S(1)} %bitcast.19, f32[2,16,2048]{2,1,0:T(8,128)S(1)} %get-tuple-element.29.back_ref), custom_call_target="tpu_custom_call" | custom-call | flops 16777216 | bytes 1048576 | tf_op jit(solution)/shard_map/close/pallas_call | solution.py:303
  37.1 7.6 %product.2 = (bf16[64,416]{1,0:T(8,128)(2,1)S(1)}, bf16[64,416]{1,0:T(8,128)(2,1)S(1)}, bf16[64,416]{1,0:T(8,128)(2,1)S(1)}, bf16[64,416]{1,0:T(8,128)(2,1)S(1)}) custom-call(s32[4]{0:T(128)S(1)} %and_select_fusion.slot_ref, f32[6,32,2048]{2,1,0:T(8,128)S(1)} %close.1.field_ref, f32[2,27,2048]{2,1,0:T(8,128)S(1)} %copy-done.6, ...), custom_call_target="tpu_custom_call" | custom-call | flops 2147483648 | bytes 1048576 | tf_op jit(solution)/shard_map/product/pallas_call | solution.py:303
  44.7 3.1 %collective-permute-start.5 = (bf16[64,416]{1,0:T(8,128)(2,1)S(1)}, bf16[64,416]{1,0:T(8,128)(2,1)S(1)}, u32[]{:S(2)}, u32[]{:S(2)}) collective-permute-start(bf16[64,416]{1,0:T(8,128)(2,1)S(1)} %get-tuple-element.37), channel_id=1, source_target_pairs={{0,0},{1,4},{2,8},{3,12},{4,1},{5,5},{6,9},{7,13},{8,2},{9,6},{10,... | collective-permute-start | bytes 159752 | tf_op jit(solution)/shard_map/ppermute | solution.py:384
  48.7 3.0 %collective-permute-start.8 = (bf16[64,416]{1,0:T(8,128)(2,1)S(1)}, bf16[64,416]{1,0:T(8,128)(2,1)S(1)}, u32[]{:S(2)}, u32[]{:S(2)}) collective-permute-start(bf16[64,416]{1,0:T(8,128)(2,1)S(1)} %get-tuple-element.40), channel_id=1, source_target_pairs={{0,3},{1,7},{2,11},{3,15},{4,0},{5,4},{6,8},{7,12},{8,1},{9,5},{10... | collective-permute-start | bytes 159752 | tf_op jit(solution)/shard_map/ppermute | solution.py:384
  51.7 7.9 %product.3 = (bf16[64,448]{1,0:T(8,128)(2,1)S(1)}, bf16[64,448]{1,0:T(8,128)(2,1)S(1)}, bf16[64,448]{1,0:T(8,128)(2,1)S(1)}, bf16[64,448]{1,0:T(8,128)(2,1)S(1)}) custom-call(s32[4]{0:T(128)S(1)} %and_select_fusion.slot_ref, f32[6,32,2048]{2,1,0:T(8,128)S(1)} %close.1.field_ref, f32[2,27,2048]{2,1,0:T(8,128)S(1)} %copy-done.6, ...), custom_call_target="tpu_custom_call" | custom-call | flops 2147483648 | bytes 1048576 | tf_op jit(solution)/shard_map/product/pallas_call | solution.py:303
  59.6 1.2 %collective-permute-start.10 = (bf16[64,448]{1,0:T(8,128)(2,1)S(1)}, bf16[64,448]{1,0:T(8,128)(2,1)S(1)}, u32[]{:S(2)}, u32[]{:S(2)}) collective-permute-start(bf16[64,448]{1,0:T(8,128)(2,1)S(1)} %get-tuple-element.42), channel_id=1, source_target_pairs={{0,1},{1,5},{2,9},{3,13},{4,2},{5,6},{6,10},{7,14},{8,3},{9,7},{10... | collective-permute-start | bytes 172040 | tf_op jit(solution)/shard_map/ppermute | solution.py:384
  60.8 0.8 %collective-permute-start.11 = (bf16[64,448]{1,0:T(8,128)(2,1)S(1)}, bf16[64,448]{1,0:T(8,128)(2,1)S(1)}, u32[]{:S(2)}, u32[]{:S(2)}) collective-permute-start(bf16[64,448]{1,0:T(8,128)(2,1)S(1)} %get-tuple-element.43), channel_id=1, source_target_pairs={{0,2},{1,6},{2,10},{3,14},{4,3},{5,7},{6,11},{7,15},{8,0},{9,4},{1... | collective-permute-start | bytes 172040 | tf_op jit(solution)/shard_map/ppermute | solution.py:384
  61.6 1.6 %collective-permute-start.12 = (bf16[64,448]{1,0:T(8,128)(2,1)S(1)}, bf16[64,448]{1,0:T(8,128)(2,1)S(1)}, u32[]{:S(2)}, u32[]{:S(2)}) collective-permute-start(bf16[64,448]{1,0:T(8,128)(2,1)S(1)} %get-tuple-element.44), channel_id=1, source_target_pairs={{0,3},{1,7},{2,11},{3,15},{4,0},{5,4},{6,8},{7,12},{8,1},{9,5},{10... | collective-permute-start | bytes 172040 | tf_op jit(solution)/shard_map/ppermute | solution.py:384
  63.2 1.9 %collective-permute-start.9 = (bf16[64,448]{1,0:T(8,128)(2,1)S(1)}, bf16[64,448]{1,0:T(8,128)(2,1)S(1)}, u32[]{:S(2)}, u32[]{:S(2)}) collective-permute-start(bf16[64,448]{1,0:T(8,128)(2,1)S(1)} %get-tuple-element.41), channel_id=1, source_target_pairs={{0,0},{1,4},{2,8},{3,12},{4,1},{5,5},{6,9},{7,13},{8,2},{9,6},{10,... | collective-permute-start | bytes 172040 | tf_op jit(solution)/shard_map/ppermute | solution.py:384
  65.4 2.0 %collective-permute-done.11 = bf16[64,448]{1,0:T(8,128)(2,1)S(1)} collective-permute-done((bf16[64,448]{1,0:T(8,128)(2,1)S(1)}, bf16[64,448]{1,0:T(8,128)(2,1)S(1)}, u32[]{:S(2)}, u32[]{:S(2)}) %collective-permute-start.11) | collective-permute-done | bytes 57376 | tf_op jit(solution)/shard_map/ppermute | solution.py:384
  67.3 6.0 %collective-permute-done.12 = bf16[64,448]{1,0:T(8,128)(2,1)S(1)} collective-permute-done((bf16[64,448]{1,0:T(8,128)(2,1)S(1)}, bf16[64,448]{1,0:T(8,128)(2,1)S(1)}, u32[]{:S(2)}, u32[]{:S(2)}) %collective-permute-start.12) | collective-permute-done | bytes 57376 | tf_op jit(solution)/shard_map/ppermute | solution.py:384
  73.7 1.6 %copy.12 = f32[32,27,2,32]{3,2,1,0:T(2,128)} copy(f32[32,27,2,32]{3,1,0,2:T(8,128)S(1)} %maximum_bitcast_fusion) | data formatting | bytes 442368 | tf_op jit(solution)/shard_map/transpose | solution.py:387
  (31 shorter events, 1.6 us)
Async XLA Ops:
  0.0 13.8 %copy-start.7 = (s32[27,3]{0,1:T(4,128)S(1)}, s32[27,3]{0,1:T(4,128)}, u32[]{:S(2)}) copy-start(s32[27,3]{0,1:T(4,128)} %param.5) | copy-start | bytes 976
  0.0 1.0 %copy-start = (f32[3,3,3,2,2048]{4,3,2,1,0:T(2,128)S(1)}, f32[3,3,3,2,2048]{4,3,2,1,0:T(2,128)}, u32[]{:S(2)}) copy-start(f32[3,3,3,2,2048]{4,3,2,1,0:T(2,128)} %param.4) | copy-start | bytes 1327108
  1.0 1.4 %copy-start.2 = (f32[32,3,2,2048]{3,2,1,0:T(2,128)S(1)}, f32[32,3,2,2048]{3,2,1,0:T(2,128)}, u32[]{:S(2)}) copy-start(f32[32,3,2,2048]{3,2,1,0:T(2,128)} %param.3) | copy-start | bytes 4718596
  2.4 11.5 %copy-start.1 = (f32[3,3,3,2,2048]{4,3,2,1,0:T(2,128)S(1)}, f32[3,3,3,2,2048]{4,3,2,1,0:T(2,128)}, u32[]{:S(2)}) copy-start(f32[3,3,3,2,2048]{4,3,2,1,0:T(2,128)} %param.4) | copy-start | bytes 1327108
  7.2 22.5 %collective-permute-start = (bf16[6,32,2048]{2,1,0:T(8,128)(2,1)}, bf16[6,32,2048]{2,1,0:T(8,128)(2,1)}, u32[]{:S(2)}, u32[]{:S(2)}) collective-permute-start(bf16[6,32,2048]{2,1,0:T(8,128)(2,1)} %get-tuple-element.25.refs_0_), channel_id=1, source_target_pairs={{0,2},{2,0},{1,3},{3,1},{4,6},{6,4},{5,7},{7,5},{8,10},{10,8},{9,1... | collective-permute-start | bytes 2359304 | tf_op jit(solution)/shard_map/ppermute | solution.py:31
  9.3 14.9 %collective-permute-start.1 = (bf16[12,32,512]{2,1,0:T(8,128)(2,1)}, bf16[12,32,512]{2,1,0:T(8,128)(2,1)S(1)}, u32[]{:S(2)}, u32[]{:S(2)}) collective-permute-start(bf16[12,32,512]{2,1,0:T(8,128)(2,1)} %get-tuple-element.26), channel_id=1, source_target_pairs={{0,12},{4,0},{8,4},{12,8},{1,13},{5,1},{9,5},{13,9},{2,14},{6,2},{... | collective-permute-start | bytes 1179656 | tf_op jit(solution)/shard_map/ppermute | solution.py:31
  12.6 17.1 %collective-permute-start.2 = (bf16[12,32,512]{2,1,0:T(8,128)(2,1)}, bf16[12,32,512]{2,1,0:T(8,128)(2,1)}, u32[]{:S(2)}, u32[]{:S(2)}) collective-permute-start(bf16[12,32,512]{2,1,0:T(8,128)(2,1)} %get-tuple-element.27), channel_id=1, source_target_pairs={{0,4},{4,8},{8,12},{12,0},{1,5},{5,9},{9,13},{13,1},{2,6},{6,10},{... | collective-permute-start | bytes 1179656 | tf_op jit(solution)/shard_map/ppermute | solution.py:31
  12.6 24.5 %collective-permute-start.3 = (bf16[6,32,2048]{2,1,0:T(8,128)(2,1)}, bf16[6,32,2048]{2,1,0:T(8,128)(2,1)}, u32[]{:S(2)}, u32[]{:S(2)}) collective-permute-start(bf16[6,32,2048]{2,1,0:T(8,128)(2,1)} %get-tuple-element.25.refs_0_), channel_id=1, source_target_pairs={{0,1},{1,0},{2,3},{3,2},{4,5},{5,4},{6,7},{7,6},{8,9},{9,8},{10,11... | collective-permute-start | bytes 2359304 | tf_op jit(solution)/shard_map/ppermute | solution.py:31
  22.2 1.2 %copy-start.3 = (f32[6,32,2048]{2,1,0:T(8,128)}, f32[6,32,2048]{2,1,0:T(8,128)S(1)}, u32[]{:S(2)}) copy-start(f32[6,32,2048]{2,1,0:T(8,128)S(1)} %get-tuple-element.32.part_ref) | copy-start | bytes 4718596
  23.3 0.8 %copy-start.5 = (f32[2,27,2048]{2,1,0:T(8,128)}, f32[2,27,2048]{2,1,0:T(8,128)S(1)}, u32[]{:S(2)}) copy-start(f32[2,27,2048]{2,1,0:T(8,128)S(1)} %get-tuple-element.35.table_ref) | copy-start | bytes 1327108
  29.7 7.4 %collective-permute-start.4 = (bf16[6,32,2048]{2,1,0:T(8,128)(2,1)}, bf16[6,32,2048]{2,1,0:T(8,128)(2,1)S(1)}, u32[]{:S(2)}, u32[]{:S(2)}) collective-permute-start(bf16[6,32,2048]{2,1,0:T(8,128)(2,1)} %collective-permute-done.refs_1_), channel_id=1, source_target_pairs={{0,1},{1,0},{2,3},{3,2},{4,5},{5,4},{6,7},{7,6},{8,9},{9,8},{10,11... | collective-permute-start | bytes 2359304 | tf_op jit(solution)/shard_map/ppermute | solution.py:31
  31.6 1.4 %copy-start.4 = (f32[6,32,2048]{2,1,0:T(8,128)S(1)}, f32[6,32,2048]{2,1,0:T(8,128)}, u32[]{:S(2)}) copy-start(f32[6,32,2048]{2,1,0:T(8,128)} %copy-done.3) | copy-start | bytes 4718596
  33.1 4.0 %copy-start.6 = (f32[2,27,2048]{2,1,0:T(8,128)S(1)}, f32[2,27,2048]{2,1,0:T(8,128)}, u32[]{:S(2)}) copy-start(f32[2,27,2048]{2,1,0:T(8,128)} %copy-done.5) | copy-start | bytes 1327108
  44.7 16.1 %collective-permute-start.5 = (bf16[64,416]{1,0:T(8,128)(2,1)S(1)}, bf16[64,416]{1,0:T(8,128)(2,1)S(1)}, u32[]{:S(2)}, u32[]{:S(2)}) collective-permute-start(bf16[64,416]{1,0:T(8,128)(2,1)S(1)} %get-tuple-element.37), channel_id=1, source_target_pairs={{0,0},{1,4},{2,8},{3,12},{4,1},{5,5},{6,9},{7,13},{8,2},{9,6},{10,... | collective-permute-start | bytes 159752 | tf_op jit(solution)/shard_map/ppermute | solution.py:384
  47.8 13.7 %collective-permute-start.6 = (bf16[64,416]{1,0:T(8,128)(2,1)S(1)}, bf16[64,416]{1,0:T(8,128)(2,1)S(1)}, u32[]{:S(2)}, u32[]{:S(2)}) collective-permute-start(bf16[64,416]{1,0:T(8,128)(2,1)S(1)} %get-tuple-element.38), channel_id=1, source_target_pairs={{0,1},{1,5},{2,9},{3,13},{4,2},{5,6},{6,10},{7,14},{8,3},{9,7},{10... | collective-permute-start | bytes 159752 | tf_op jit(solution)/shard_map/ppermute | solution.py:384
  47.9 15.3 %collective-permute-start.7 = (bf16[64,416]{1,0:T(8,128)(2,1)S(1)}, bf16[64,416]{1,0:T(8,128)(2,1)S(1)}, u32[]{:S(2)}, u32[]{:S(2)}) collective-permute-start(bf16[64,416]{1,0:T(8,128)(2,1)S(1)} %get-tuple-element.39), channel_id=1, source_target_pairs={{0,2},{1,6},{2,10},{3,14},{4,3},{5,7},{6,11},{7,15},{8,0},{9,4},{1... | collective-permute-start | bytes 159752 | tf_op jit(solution)/shard_map/ppermute | solution.py:384
  48.7 16.5 %collective-permute-start.8 = (bf16[64,416]{1,0:T(8,128)(2,1)S(1)}, bf16[64,416]{1,0:T(8,128)(2,1)S(1)}, u32[]{:S(2)}, u32[]{:S(2)}) collective-permute-start(bf16[64,416]{1,0:T(8,128)(2,1)S(1)} %get-tuple-element.40), channel_id=1, source_target_pairs={{0,3},{1,7},{2,11},{3,15},{4,0},{5,4},{6,8},{7,12},{8,1},{9,5},{10... | collective-permute-start | bytes 159752 | tf_op jit(solution)/shard_map/ppermute | solution.py:384
  59.6 5.8 %collective-permute-start.10 = (bf16[64,448]{1,0:T(8,128)(2,1)S(1)}, bf16[64,448]{1,0:T(8,128)(2,1)S(1)}, u32[]{:S(2)}, u32[]{:S(2)}) collective-permute-start(bf16[64,448]{1,0:T(8,128)(2,1)S(1)} %get-tuple-element.42), channel_id=1, source_target_pairs={{0,1},{1,5},{2,9},{3,13},{4,2},{5,6},{6,10},{7,14},{8,3},{9,7},{10... | collective-permute-start | bytes 172040 | tf_op jit(solution)/shard_map/ppermute | solution.py:384
  60.8 6.5 %collective-permute-start.11 = (bf16[64,448]{1,0:T(8,128)(2,1)S(1)}, bf16[64,448]{1,0:T(8,128)(2,1)S(1)}, u32[]{:S(2)}, u32[]{:S(2)}) collective-permute-start(bf16[64,448]{1,0:T(8,128)(2,1)S(1)} %get-tuple-element.43), channel_id=1, source_target_pairs={{0,2},{1,6},{2,10},{3,14},{4,3},{5,7},{6,11},{7,15},{8,0},{9,4},{1... | collective-permute-start | bytes 172040 | tf_op jit(solution)/shard_map/ppermute | solution.py:384
  61.6 11.8 %collective-permute-start.12 = (bf16[64,448]{1,0:T(8,128)(2,1)S(1)}, bf16[64,448]{1,0:T(8,128)(2,1)S(1)}, u32[]{:S(2)}, u32[]{:S(2)}) collective-permute-start(bf16[64,448]{1,0:T(8,128)(2,1)S(1)} %get-tuple-element.44), channel_id=1, source_target_pairs={{0,3},{1,7},{2,11},{3,15},{4,0},{5,4},{6,8},{7,12},{8,1},{9,5},{10... | collective-permute-start | bytes 172040 | tf_op jit(solution)/shard_map/ppermute | solution.py:384
  63.2 10.1 %collective-permute-start.9 = (bf16[64,448]{1,0:T(8,128)(2,1)S(1)}, bf16[64,448]{1,0:T(8,128)(2,1)S(1)}, u32[]{:S(2)}, u32[]{:S(2)}) collective-permute-start(bf16[64,448]{1,0:T(8,128)(2,1)S(1)} %get-tuple-element.41), channel_id=1, source_target_pairs={{0,0},{1,4},{2,8},{3,12},{4,1},{5,5},{6,9},{7,13},{8,2},{9,6},{10,... | collective-permute-start | bytes 172040 | tf_op jit(solution)/shard_map/ppermute | solution.py:384

commit v4 on v3

--- a/solution.py
+++ b/solution.py
@@ -20,7 +20,7 @@
 LOW = jnp.bfloat16
 WIDE = jnp.float32
 STEP = 2
-CHUNKS = 2
+CHUNKS = 1
 VMEM_LIMIT = 40 * 1024 * 1024
 VMEM = pl.BlockSpec(memory_space=pltpu.VMEM)
 SMEM = pl.BlockSpec(memory_space=pltpu.SMEM)

time: 75.6 us -> 76.9 us (1.017)
  waiting for transfers between devices: 13.5 us -> 23.5 us
  starting transfers between devices: 21 us -> 15.4 us
  Pallas kernels: 32.5 us -> 29.7 us
    ppermute x8 -> x4, waiting for transfers between devices: 7.99 us -> 17.9 us  [shards(): shares.append(lax.ppermute(block, ('brick', 'vec', 'sub'), pairs))]
    ppermute x8 -> x4, starting transfers between devices: 12.5 us -> 6.94 us  [shards(): shares.append(lax.ppermute(block, ('brick', 'vec', 'sub'), pairs))]
    pallas_call x5 -> x4, Pallas kernels: 32.5 us -> 29.7 us  [call(): pl.pallas_call(kernel, out_shape=tuple((jax.ShapeDtypeStruct(shape, dtype...]
  transfers between devices with their start and end apart: 13 -> 9, of which waited for: 3 -> 3; matrix products, arithmetic and copies ran while one was open for 0% -> 0% of each run, Pallas kernels for 27% -> 16%
where the time goes in v4:
time: 76.9 us; the launch traced here: 76.7 us
  Pallas kernels  29.7 us (39%)
  waiting for transfers between devices  23.5 us (31%)
  starting transfers between devices  15.4 us (20%)
  local copies, waits for them, and re-layouts  7.91 us (10%)
    pallas_call x4, Pallas kernels, call(): pl.pallas_call(kernel, out_shape=tuple((jax.ShapeDtypeStruct(shape, dtype...  29.7 us
    ppermute x4, waiting for transfers between devices, shards(): shares.append(lax.ppermute(block, ('brick', 'vec', 'sub'), pairs))  17.9 us
    ppermute x5, starting transfers between devices, shifted(): lax.ppermute(array, axis, [(i, (i + by) % peers) for i in range(peers)])  8.47 us
    ppermute x4, starting transfers between devices, shards(): shares.append(lax.ppermute(block, ('brick', 'vec', 'sub'), pairs))  6.94 us
    unnamed x17, local copies, waits for them, and re-layouts  5.92 us
    ppermute x5, waiting for transfers between devices, shifted(): lax.ppermute(array, axis, [(i, (i + by) % peers) for i in range(peers)])  5.54 us
    transpose x1, local copies, waits for them, and re-layouts, shards(): return jnp.transpose(jnp.concatenate(totals, axis=2), (1, 2, 0, 3))  1.61 us
  transfers between devices with their start and end apart: 9, of which 3 were waited for; matrix products, arithmetic and copies ran while one was open for 0% of the time, Pallas kernels for 16%

profile of v4, /device:TPU:1, one launch (start us, length us, event | category | flops | bytes accessed | tf_op | source)
XLA Modules:
  0.0 76.7 jit_solution(16805290952094341350)
XLA Ops:
  0.0 1.0 %copy-done = f32[3,3,3,2,2048]{4,3,2,1,0:T(2,128)S(1)} copy-done((f32[3,3,3,2,2048]{4,3,2,1,0:T(2,128)S(1)}, f32[3,3,3,2,2048]{4,3,2,1,0:T(2,128)}, u32[]{:S(2)}) %copy-start) | copy-done | bytes 442392
  1.0 1.4 %copy-done.2 = f32[32,3,2,2048]{3,2,1,0:T(2,128)S(1)} copy-done((f32[32,3,2,2048]{3,2,1,0:T(2,128)S(1)}, f32[32,3,2,2048]{3,2,1,0:T(2,128)}, u32[]{:S(2)}) %copy-start.2) | copy-done | bytes 1572888
  2.4 4.8 %open.1 = (f32[6,32,2048]{2,1,0:T(8,128)S(1)}, bf16[6,32,2048]{2,1,0:T(8,128)(2,1)}, bf16[12,32,512]{2,1,0:T(8,128)(2,1)}, bf16[12,32,512]{2,1,0:T(8,128)(2,1)},...) custom-call(f32[3072,128]{1,0:T(8,128)S(1)} %bitcast.19, f32[864,128]{1,0:T(8,128)S(1)} %bitcast.16), custom_call_target="tpu_custom_call" | custom-call | flops 16777216 | bytes 1048576 | tf_op jit(solution)/shard_map/open/pallas_call | solution.py:303
  7.2 2.0 %collective-permute-start = (bf16[6,32,2048]{2,1,0:T(8,128)(2,1)}, bf16[6,32,2048]{2,1,0:T(8,128)(2,1)}, u32[]{:S(2)}, u32[]{:S(2)}) collective-permute-start(bf16[6,32,2048]{2,1,0:T(8,128)(2,1)} %get-tuple-element.21.refs_0_), channel_id=1, source_target_pairs={{0,2},{2,0},{1,3},{3,1},{4,6},{6,4},{5,7},{7,5},{8,10},{10,8},{9,1... | collective-permute-start | bytes 2359304 | tf_op jit(solution)/shard_map/ppermute | solution.py:31
  9.2 3.3 %collective-permute-start.1 = (bf16[12,32,512]{2,1,0:T(8,128)(2,1)}, bf16[12,32,512]{2,1,0:T(8,128)(2,1)S(1)}, u32[]{:S(2)}, u32[]{:S(2)}) collective-permute-start(bf16[12,32,512]{2,1,0:T(8,128)(2,1)} %get-tuple-element.22), channel_id=1, source_target_pairs={{0,12},{4,0},{8,4},{12,8},{1,13},{5,1},{9,5},{13,9},{2,14},{6,2},{... | collective-permute-start | bytes 1179656 | tf_op jit(solution)/shard_map/ppermute | solution.py:31
  12.6 1.2 %collective-permute-start.3 = (bf16[6,32,2048]{2,1,0:T(8,128)(2,1)}, bf16[6,32,2048]{2,1,0:T(8,128)(2,1)}, u32[]{:S(2)}, u32[]{:S(2)}) collective-permute-start(bf16[6,32,2048]{2,1,0:T(8,128)(2,1)} %get-tuple-element.21.refs_0_), channel_id=1, source_target_pairs={{0,1},{1,0},{2,3},{3,2},{4,5},{5,4},{6,7},{7,6},{8,9},{9,8},{10,11... | collective-permute-start | bytes 2359304 | tf_op jit(solution)/shard_map/ppermute | solution.py:31
  13.8 0.1 copy.10.momenta_ref
  13.9 8.3 %local.1 = (f32[6,32,2048]{2,1,0:T(8,128)S(1)}, f32[2,27,2048]{2,1,0:T(8,128)S(1)}) custom-call(s32[1]{0:T(128)} %bitcast.10.place_ref, f32[6,32,2048]{2,1,0:T(8,128)S(1)} %get-tuple-element.24.field_ref, f32[864,128]{1,0:T(8,128)S(1)} %bitcast.17, f32[2,16,2048]{2,1,0:T(8,128)S(1)} %get-tuple-element.25.back_ref, ...), custom_call_target="tpu_custom_call" | custom-call | flops 33554432 | bytes 1048576 | tf_op jit(solution)/shard_map/local/pallas_call | solution.py:303
  22.2 1.2 %copy-done.3 = f32[6,32,2048]{2,1,0:T(8,128)} copy-done((f32[6,32,2048]{2,1,0:T(8,128)}, f32[6,32,2048]{2,1,0:T(8,128)S(1)}, u32[]{:S(2)}) %copy-start.3) | copy-done | bytes 1572888
  23.4 0.8 %copy-done.5 = f32[2,27,2048]{2,1,0:T(8,128)} copy-done((f32[2,27,2048]{2,1,0:T(8,128)}, f32[2,27,2048]{2,1,0:T(8,128)S(1)}, u32[]{:S(2)}) %copy-start.5) | copy-done | bytes 442392
  24.1 5.5 %collective-permute-done.2.behind_ref = bf16[12,32,512]{2,1,0:T(8,128)(2,1)} collective-permute-done((bf16[12,32,512]{2,1,0:T(8,128)(2,1)}, bf16[12,32,512]{2,1,0:T(8,128)(2,1)}, u32[]{:S(2)}, u32[]{:S(2)}) %collective-permute-start.2) | collective-permute-done | bytes 393248 | tf_op jit(solution)/shard_map/ppermute | solution.py:31
  29.7 1.9 %collective-permute-start.4 = (bf16[6,32,2048]{2,1,0:T(8,128)(2,1)}, bf16[6,32,2048]{2,1,0:T(8,128)(2,1)S(1)}, u32[]{:S(2)}, u32[]{:S(2)}) collective-permute-start(bf16[6,32,2048]{2,1,0:T(8,128)(2,1)} %collective-permute-done.refs_1_), channel_id=1, source_target_pairs={{0,1},{1,0},{2,3},{3,2},{4,5},{5,4},{6,7},{7,6},{8,9},{9,8},{10,11... | collective-permute-start | bytes 2359304 | tf_op jit(solution)/shard_map/ppermute | solution.py:31
  31.5 0.1 and_select_fusion.slot_ref
  31.6 1.4 %copy-done.4 = f32[6,32,2048]{2,1,0:T(8,128)S(1)} copy-done((f32[6,32,2048]{2,1,0:T(8,128)S(1)}, f32[6,32,2048]{2,1,0:T(8,128)}, u32[]{:S(2)}) %copy-start.4) | copy-done | bytes 1572888
  33.0 4.0 %close.1.field_ref = f32[6,32,2048]{2,1,0:T(8,128)S(1)} custom-call(f32[6,32,2048]{2,1,0:T(8,128)S(1)} %copy-done.4, bf16[12,32,512]{2,1,0:T(8,128)(2,1)S(1)} %collective-permute-done.1.ahead_ref, bf16[12,32,512]{2,1,0:T(8,128)(2,1)} %collective-permute-done.2.behind_ref, f32[864,128]{1,0:T(8,128)S(1)} %bitcast.18, f32[2,16,2048]{2,1,0:T(8,128)S(1)} %get-tuple-element.25.back_ref), custom_call_target="tpu_custom_call" | custom-call | flops 16777216 | bytes 1048576 | tf_op jit(solution)/shard_map/close/pallas_call | solution.py:303
  37.1 12.6 %product.1 = (bf16[64,864]{1,0:T(8,128)(2,1)S(1)}, bf16[64,864]{1,0:T(8,128)(2,1)S(1)}, bf16[64,864]{1,0:T(8,128)(2,1)S(1)}, bf16[64,864]{1,0:T(8,128)(2,1)S(1)}) custom-call(s32[4]{0:T(128)S(1)} %and_select_fusion.slot_ref, f32[6,32,2048]{2,1,0:T(8,128)S(1)} %close.1.field_ref, f32[2,27,2048]{2,1,0:T(8,128)S(1)} %copy-done.6, ...), custom_call_target="tpu_custom_call" | custom-call | flops 2147483648 | bytes 1048576 | tf_op jit(solution)/shard_map/product/pallas_call | solution.py:303
  49.7 3.1 %collective-permute-start.5 = (bf16[64,864]{1,0:T(8,128)(2,1)S(1)}, bf16[64,864]{1,0:T(8,128)(2,1)S(1)}, u32[]{:S(2)}, u32[]{:S(2)}) collective-permute-start(bf16[64,864]{1,0:T(8,128)(2,1)S(1)} %get-tuple-element.33), channel_id=1, source_target_pairs={{0,0},{1,4},{2,8},{3,12},{4,1},{5,5},{6,9},{7,13},{8,2},{9,6},{10,... | collective-permute-start | bytes 331784 | tf_op jit(solution)/shard_map/ppermute | solution.py:384
  52.9 0.1 collective-permute-start.6
  53.0 0.7 collective-permute-start.7
  53.7 3.0 %collective-permute-start.8 = (bf16[64,864]{1,0:T(8,128)(2,1)S(1)}, bf16[64,864]{1,0:T(8,128)(2,1)S(1)}, u32[]{:S(2)}, u32[]{:S(2)}) collective-permute-start(bf16[64,864]{1,0:T(8,128)(2,1)S(1)} %get-tuple-element.36), channel_id=1, source_target_pairs={{0,3},{1,7},{2,11},{3,15},{4,0},{5,4},{6,8},{7,12},{8,1},{9,5},{10... | collective-permute-start | bytes 331784 | tf_op jit(solution)/shard_map/ppermute | solution.py:384
  56.7 7.1 %collective-permute-done.7 = bf16[64,864]{1,0:T(8,128)(2,1)S(1)} collective-permute-done((bf16[64,864]{1,0:T(8,128)(2,1)S(1)}, bf16[64,864]{1,0:T(8,128)(2,1)S(1)}, u32[]{:S(2)}, u32[]{:S(2)}) %collective-permute-start.7) | collective-permute-done | bytes 110624 | tf_op jit(solution)/shard_map/ppermute | solution.py:384
  63.8 10.8 %collective-permute-done.8 = bf16[64,864]{1,0:T(8,128)(2,1)S(1)} collective-permute-done((bf16[64,864]{1,0:T(8,128)(2,1)S(1)}, bf16[64,864]{1,0:T(8,128)(2,1)S(1)}, u32[]{:S(2)}, u32[]{:S(2)}) %collective-permute-start.8) | collective-permute-done | bytes 110624 | tf_op jit(solution)/shard_map/ppermute | solution.py:384
  74.7 0.4 reshape.23
  75.1 1.6 %copy.11 = f32[32,27,2,32]{3,2,1,0:T(2,128)} copy(f32[32,27,2,32]{3,1,0,2:T(8,128)S(1)} %bitcast.20) | data formatting | bytes 442368 | tf_op jit(solution)/shard_map/transpose | solution.py:387
  (19 shorter events, 0.1 us)
Async XLA Ops:
  0.0 13.8 %copy-start.7 = (s32[27,3]{0,1:T(4,128)S(1)}, s32[27,3]{0,1:T(4,128)}, u32[]{:S(2)}) copy-start(s32[27,3]{0,1:T(4,128)} %param.5) | copy-start | bytes 976
  0.0 1.0 %copy-start = (f32[3,3,3,2,2048]{4,3,2,1,0:T(2,128)S(1)}, f32[3,3,3,2,2048]{4,3,2,1,0:T(2,128)}, u32[]{:S(2)}) copy-start(f32[3,3,3,2,2048]{4,3,2,1,0:T(2,128)} %param.4) | copy-start | bytes 1327108
  1.0 1.4 %copy-start.2 = (f32[32,3,2,2048]{3,2,1,0:T(2,128)S(1)}, f32[32,3,2,2048]{3,2,1,0:T(2,128)}, u32[]{:S(2)}) copy-start(f32[32,3,2,2048]{3,2,1,0:T(2,128)} %param.3) | copy-start | bytes 4718596
  2.4 11.5 %copy-start.1 = (f32[3,3,3,2,2048]{4,3,2,1,0:T(2,128)S(1)}, f32[3,3,3,2,2048]{4,3,2,1,0:T(2,128)}, u32[]{:S(2)}) copy-start(f32[3,3,3,2,2048]{4,3,2,1,0:T(2,128)} %param.4) | copy-start | bytes 1327108
  7.2 22.5 %collective-permute-start = (bf16[6,32,2048]{2,1,0:T(8,128)(2,1)}, bf16[6,32,2048]{2,1,0:T(8,128)(2,1)}, u32[]{:S(2)}, u32[]{:S(2)}) collective-permute-start(bf16[6,32,2048]{2,1,0:T(8,128)(2,1)} %get-tuple-element.21.refs_0_), channel_id=1, source_target_pairs={{0,2},{2,0},{1,3},{3,1},{4,6},{6,4},{5,7},{7,5},{8,10},{10,8},{9,1... | collective-permute-start | bytes 2359304 | tf_op jit(solution)/shard_map/ppermute | solution.py:31
  9.2 14.9 %collective-permute-start.1 = (bf16[12,32,512]{2,1,0:T(8,128)(2,1)}, bf16[12,32,512]{2,1,0:T(8,128)(2,1)S(1)}, u32[]{:S(2)}, u32[]{:S(2)}) collective-permute-start(bf16[12,32,512]{2,1,0:T(8,128)(2,1)} %get-tuple-element.22), channel_id=1, source_target_pairs={{0,12},{4,0},{8,4},{12,8},{1,13},{5,1},{9,5},{13,9},{2,14},{6,2},{... | collective-permute-start | bytes 1179656 | tf_op jit(solution)/shard_map/ppermute | solution.py:31
  12.6 17.1 %collective-permute-start.2 = (bf16[12,32,512]{2,1,0:T(8,128)(2,1)}, bf16[12,32,512]{2,1,0:T(8,128)(2,1)}, u32[]{:S(2)}, u32[]{:S(2)}) collective-permute-start(bf16[12,32,512]{2,1,0:T(8,128)(2,1)} %get-tuple-element.23), channel_id=1, source_target_pairs={{0,4},{4,8},{8,12},{12,0},{1,5},{5,9},{9,13},{13,1},{2,6},{6,10},{... | collective-permute-start | bytes 1179656 | tf_op jit(solution)/shard_map/ppermute | solution.py:31
  12.6 24.5 %collective-permute-start.3 = (bf16[6,32,2048]{2,1,0:T(8,128)(2,1)}, bf16[6,32,2048]{2,1,0:T(8,128)(2,1)}, u32[]{:S(2)}, u32[]{:S(2)}) collective-permute-start(bf16[6,32,2048]{2,1,0:T(8,128)(2,1)} %get-tuple-element.21.refs_0_), channel_id=1, source_target_pairs={{0,1},{1,0},{2,3},{3,2},{4,5},{5,4},{6,7},{7,6},{8,9},{9,8},{10,11... | collective-permute-start | bytes 2359304 | tf_op jit(solution)/shard_map/ppermute | solution.py:31
  22.2 1.2 %copy-start.3 = (f32[6,32,2048]{2,1,0:T(8,128)}, f32[6,32,2048]{2,1,0:T(8,128)S(1)}, u32[]{:S(2)}) copy-start(f32[6,32,2048]{2,1,0:T(8,128)S(1)} %get-tuple-element.28.part_ref) | copy-start | bytes 4718596
  23.3 0.8 %copy-start.5 = (f32[2,27,2048]{2,1,0:T(8,128)}, f32[2,27,2048]{2,1,0:T(8,128)S(1)}, u32[]{:S(2)}) copy-start(f32[2,27,2048]{2,1,0:T(8,128)S(1)} %get-tuple-element.31.table_ref) | copy-start | bytes 1327108
  29.7 7.4 %collective-permute-start.4 = (bf16[6,32,2048]{2,1,0:T(8,128)(2,1)}, bf16[6,32,2048]{2,1,0:T(8,128)(2,1)S(1)}, u32[]{:S(2)}, u32[]{:S(2)}) collective-permute-start(bf16[6,32,2048]{2,1,0:T(8,128)(2,1)} %collective-permute-done.refs_1_), channel_id=1, source_target_pairs={{0,1},{1,0},{2,3},{3,2},{4,5},{5,4},{6,7},{7,6},{8,9},{9,8},{10,11... | collective-permute-start | bytes 2359304 | tf_op jit(solution)/shard_map/ppermute | solution.py:31
  31.6 1.4 %copy-start.4 = (f32[6,32,2048]{2,1,0:T(8,128)S(1)}, f32[6,32,2048]{2,1,0:T(8,128)}, u32[]{:S(2)}) copy-start(f32[6,32,2048]{2,1,0:T(8,128)} %copy-done.3) | copy-start | bytes 4718596
  33.0 4.0 %copy-start.6 = (f32[2,27,2048]{2,1,0:T(8,128)S(1)}, f32[2,27,2048]{2,1,0:T(8,128)}, u32[]{:S(2)}) copy-start(f32[2,27,2048]{2,1,0:T(8,128)} %copy-done.5) | copy-start | bytes 1327108
  49.7 7.0 %collective-permute-start.5 = (bf16[64,864]{1,0:T(8,128)(2,1)S(1)}, bf16[64,864]{1,0:T(8,128)(2,1)S(1)}, u32[]{:S(2)}, u32[]{:S(2)}) collective-permute-start(bf16[64,864]{1,0:T(8,128)(2,1)S(1)} %get-tuple-element.33), channel_id=1, source_target_pairs={{0,0},{1,4},{2,8},{3,12},{4,1},{5,5},{6,9},{7,13},{8,2},{9,6},{10,... | collective-permute-start | bytes 331784 | tf_op jit(solution)/shard_map/ppermute | solution.py:384
  52.9 3.8 %collective-permute-start.6 = (bf16[64,864]{1,0:T(8,128)(2,1)S(1)}, bf16[64,864]{1,0:T(8,128)(2,1)S(1)}, u32[]{:S(2)}, u32[]{:S(2)}) collective-permute-start(bf16[64,864]{1,0:T(8,128)(2,1)S(1)} %get-tuple-element.34), channel_id=1, source_target_pairs={{0,1},{1,5},{2,9},{3,13},{4,2},{5,6},{6,10},{7,14},{8,3},{9,7},{10... | collective-permute-start | bytes 331784 | tf_op jit(solution)/shard_map/ppermute | solution.py:384
  53.0 10.8 %collective-permute-start.7 = (bf16[64,864]{1,0:T(8,128)(2,1)S(1)}, bf16[64,864]{1,0:T(8,128)(2,1)S(1)}, u32[]{:S(2)}, u32[]{:S(2)}) collective-permute-start(bf16[64,864]{1,0:T(8,128)(2,1)S(1)} %get-tuple-element.35), channel_id=1, source_target_pairs={{0,2},{1,6},{2,10},{3,14},{4,3},{5,7},{6,11},{7,15},{8,0},{9,4},{1... | collective-permute-start | bytes 331784 | tf_op jit(solution)/shard_map/ppermute | solution.py:384
  53.7 20.9 %collective-permute-start.8 = (bf16[64,864]{1,0:T(8,128)(2,1)S(1)}, bf16[64,864]{1,0:T(8,128)(2,1)S(1)}, u32[]{:S(2)}, u32[]{:S(2)}) collective-permute-start(bf16[64,864]{1,0:T(8,128)(2,1)S(1)} %get-tuple-element.36), channel_id=1, source_target_pairs={{0,3},{1,7},{2,11},{3,15},{4,0},{5,4},{6,8},{7,12},{8,1},{9,5},{10... | collective-permute-start | bytes 331784 | tf_op jit(solution)/shard_map/ppermute | solution.py:384

commit v5 on v4

--- a/solution.py
+++ b/solution.py
@@ -20,7 +20,6 @@
 LOW = jnp.bfloat16
 WIDE = jnp.float32
 STEP = 2
-CHUNKS = 1
 VMEM_LIMIT = 40 * 1024 * 1024
 VMEM = pl.BlockSpec(memory_space=pltpu.VMEM)
 SMEM = pl.BlockSpec(memory_space=pltpu.SMEM)
@@ -253,8 +252,9 @@
                 store(out_ref, rows, lanes_at(layer, tile), new)
 
 
-def product_kernel(groups, begin, count, scale, slot_ref, field_ref, table_ref, *refs):
-    raw_refs, out_refs, (total_ref, left_ref, right_ref) = refs[:groups], refs[groups : 2 * groups], refs[2 * groups :]
+def product_kernel(columns, begin, count, scale, slot_ref, field_ref, table_ref, *refs):
+    groups = len(columns)
+    raw_refs, out_refs, (total_ref, left_ref, right_ref) = refs[:groups], refs[groups:-3], refs[-3:]
     vectors = field_ref.shape[1]
     depth = 6 * LANES
     step = left_ref.shape[1] // depth
@@ -291,12 +291,8 @@
 
     width = total_ref.shape[0] // groups
     for g in range(groups):
-        block = (total_ref[pl.ds(g * width, width), :] * scale).astype(out_refs[0].dtype)
-        for slot in range(groups):
-
-            @pl.when(slot_ref[g] == slot)
-            def _():
-                out_refs[slot][...] = block
+        block = total_ref[pl.ds(g * width, width), :] * scale
+        out_refs[columns[g]][slot_ref[g]] = block.astype(LOW)
 
 
 def call(kernel, name, shapes, operands, flops=0, scratch=(), smem=False):
@@ -357,34 +353,40 @@
         flops=1 << 24,
         scratch=(pltpu.VMEM((6, width, 2 * PLANE), WIDE),),
     )
-    owners = jnp.stack([(vec - a) % vecs * subs + (sub - b) % subs for a, b in offsets])
-    slots = ((owners - brick) % groups).astype(jnp.int32)
+    brick_vec, brick_sub = brick // subs, brick % subs
+    slots = jnp.stack([(sub - b - brick_sub) % subs for a, b in offsets]).astype(jnp.int32)
     scale = (3.0 * total_x * PLANE) ** (-0.5)
     depth = STEP * 6 * LANES
-    totals = []
-    bounds = [count * n // CHUNKS for n in range(CHUNKS + 1)]
-    for begin, end in zip(bounds[:-1], bounds[1:]):
-        columns = (end - begin) * width
-        blocks = call(
-            functools.partial(product_kernel, groups, begin, end - begin, scale),
-            "product",
-            (((2 * width, columns), LOW),) * groups,
-            (slots, smeared, table, *raws),
-            flops=1 << 31,
-            scratch=(
-                pltpu.VMEM((groups * 2 * width, columns), WIDE),
-                pltpu.VMEM((groups * 2 * width, depth), LOW),
-                pltpu.VMEM((columns, depth), LOW),
-            ),
-            smem=True,
-        )
-        shares = []
-        for slot, block in enumerate(blocks):
-            pairs = [(b * groups + g, g * groups + (b + slot) % groups) for b in range(bricks) for g in range(groups)]
-            shares.append(lax.ppermute(block, ("brick", "vec", "sub"), pairs))
-        total = functools.reduce(jnp.add, [share.astype(WIDE) for share in shares])
-        totals.append(total.reshape((2, width, end - begin, width)))
-    return jnp.transpose(jnp.concatenate(totals, axis=2), (1, 2, 0, 3))
+    columns = count * width
+    blocks = call(
+        functools.partial(product_kernel, [-a % vecs for a, b in offsets], 0, count, scale),
+        "product",
+        (((subs, 2 * width, columns), LOW),) * vecs,
+        (slots, smeared, table, *raws),
+        flops=1 << 32,
+        scratch=(
+            pltpu.VMEM((groups * 2 * width, columns), WIDE),
+            pltpu.VMEM((groups * 2 * width, depth), LOW),
+            pltpu.VMEM((columns, depth), LOW),
+        ),
+        smem=True,
+    )
+    held = [shifted(block, "vec", a) if a else block for a, block in enumerate(blocks)]
+    shares = []
+    for q in range(vecs):
+        place = (vec - brick_vec - q) % vecs
+        block = held[0]
+        for a in range(1, vecs):
+            block = jnp.where(place == a, held[a], block)
+        for r in range(subs):
+            pairs = [
+                (b * subs + s, ((b // subs + q) % vecs * subs + s) * subs + (b % subs + r) % subs)
+                for b in range(bricks)
+                for s in range(subs)
+            ]
+            shares.append(lax.ppermute(block[r], ("brick", "sub"), pairs))
+    total = functools.reduce(jnp.add, [share.astype(WIDE) for share in shares])
+    return jnp.transpose(total.reshape((2, width, count, width)), (1, 2, 0, 3))
 
 
 def solution(mesh):

time: 76.9 us -> 75.4 us (0.980)
  the two profiles are of different devices: /device:TPU:1 before, /device:TPU:0 now
where the time goes in v5:
time: 75.4 us; the launch traced here: 74.6 us
  Pallas kernels  29.6 us (39%)
  waiting for transfers between devices  24.7 us (33%)
  starting transfers between devices  12 us (16%)
  local copies, waits for them, and re-layouts  7.92 us (11%)
    pallas_call x4, Pallas kernels, call(): pl.pallas_call(kernel, out_shape=tuple((jax.ShapeDtypeStruct(shape, dtype...  29.6 us
    ppermute x6, waiting for transfers between devices, shifted(): lax.ppermute(array, axis, [(i, (i + by) % peers) for i in range(peers)])  14.9 us
    ppermute x4, waiting for transfers between devices, shards(): shares.append(lax.ppermute(block[r], ('brick', 'sub'), pairs))  9.85 us
    ppermute x6, starting transfers between devices, shifted(): lax.ppermute(array, axis, [(i, (i + by) % peers) for i in range(peers)])  7.15 us
    unnamed x17, local copies, waits for them, and re-layouts  5.89 us
    ppermute x4, starting transfers between devices, shards(): shares.append(lax.ppermute(block[r], ('brick', 'sub'), pairs))  4.87 us
    transpose x1, local copies, waits for them, and re-layouts, shards(): return jnp.transpose(total.reshape((2, width, count, width)), (1, 2, 0, 3))  1.61 us
  transfers between devices with their start and end apart: 10, of which 4 were waited for; matrix products, arithmetic and copies ran while one was open for 0% of the time, Pallas kernels for 16%

profile of v5, /device:TPU:0, one launch (start us, length us, event | category | flops | bytes accessed | tf_op | source)
XLA Modules:
  0.0 74.6 jit_solution(9414794777740260856)
XLA Ops:
  0.0 1.0 %copy-done = f32[3,3,3,2,2048]{4,3,2,1,0:T(2,128)S(1)} copy-done((f32[3,3,3,2,2048]{4,3,2,1,0:T(2,128)S(1)}, f32[3,3,3,2,2048]{4,3,2,1,0:T(2,128)}, u32[]{:S(2)}) %copy-start) | copy-done | bytes 442392
  1.0 1.4 %copy-done.2 = f32[32,3,2,2048]{3,2,1,0:T(2,128)S(1)} copy-done((f32[32,3,2,2048]{3,2,1,0:T(2,128)S(1)}, f32[32,3,2,2048]{3,2,1,0:T(2,128)}, u32[]{:S(2)}) %copy-start.2) | copy-done | bytes 1572888
  2.4 4.8 %open.1 = (f32[6,32,2048]{2,1,0:T(8,128)S(1)}, bf16[6,32,2048]{2,1,0:T(8,128)(2,1)}, bf16[12,32,512]{2,1,0:T(8,128)(2,1)}, bf16[12,32,512]{2,1,0:T(8,128)(2,1)},...) custom-call(f32[3072,128]{1,0:T(8,128)S(1)} %bitcast.25, f32[864,128]{1,0:T(8,128)S(1)} %bitcast.22), custom_call_target="tpu_custom_call" | custom-call | flops 16777216 | bytes 1048576 | tf_op jit(solution)/shard_map/open/pallas_call | solution.py:299
  7.2 2.9 %collective-permute-start = (bf16[6,32,2048]{2,1,0:T(8,128)(2,1)}, bf16[6,32,2048]{2,1,0:T(8,128)(2,1)}, u32[]{:S(2)}, u32[]{:S(2)}) collective-permute-start(bf16[6,32,2048]{2,1,0:T(8,128)(2,1)} %get-tuple-element.19.refs_0_), channel_id=1, source_target_pairs={{0,2},{2,0},{1,3},{3,1},{4,6},{6,4},{5,7},{7,5},{8,10},{10,8},{9,1... | collective-permute-start | bytes 2359304 | tf_op jit(solution)/shard_map/ppermute | solution.py:30
  10.2 3.6 %collective-permute-start.1 = (bf16[12,32,512]{2,1,0:T(8,128)(2,1)}, bf16[12,32,512]{2,1,0:T(8,128)(2,1)S(1)}, u32[]{:S(2)}, u32[]{:S(2)}) collective-permute-start(bf16[12,32,512]{2,1,0:T(8,128)(2,1)} %get-tuple-element.20), channel_id=1, source_target_pairs={{0,12},{4,0},{8,4},{12,8},{1,13},{5,1},{9,5},{13,9},{2,14},{6,2},{... | collective-permute-start | bytes 1179656 | tf_op jit(solution)/shard_map/ppermute | solution.py:30
  13.8 0.1 copy.10.momenta_ref
  13.9 8.3 %local.1 = (f32[6,32,2048]{2,1,0:T(8,128)S(1)}, f32[2,27,2048]{2,1,0:T(8,128)S(1)}) custom-call(s32[1]{0:T(128)} %bitcast.8.place_ref, f32[6,32,2048]{2,1,0:T(8,128)S(1)} %get-tuple-element.22.field_ref, f32[864,128]{1,0:T(8,128)S(1)} %bitcast.23, f32[2,16,2048]{2,1,0:T(8,128)S(1)} %get-tuple-element.23.back_ref, ...), custom_call_target="tpu_custom_call" | custom-call | flops 33554432 | bytes 1048576 | tf_op jit(solution)/shard_map/local/pallas_call | solution.py:299
  22.1 1.2 %copy-done.3 = f32[6,32,2048]{2,1,0:T(8,128)} copy-done((f32[6,32,2048]{2,1,0:T(8,128)}, f32[6,32,2048]{2,1,0:T(8,128)S(1)}, u32[]{:S(2)}) %copy-start.3) | copy-done | bytes 1572888
  23.3 0.8 %copy-done.5 = f32[2,27,2048]{2,1,0:T(8,128)} copy-done((f32[2,27,2048]{2,1,0:T(8,128)}, f32[2,27,2048]{2,1,0:T(8,128)S(1)}, u32[]{:S(2)}) %copy-start.5) | copy-done | bytes 442392
  24.1 7.4 %collective-permute-done.2.behind_ref = bf16[12,32,512]{2,1,0:T(8,128)(2,1)} collective-permute-done((bf16[12,32,512]{2,1,0:T(8,128)(2,1)}, bf16[12,32,512]{2,1,0:T(8,128)(2,1)}, u32[]{:S(2)}, u32[]{:S(2)}) %collective-permute-start.2) | collective-permute-done | bytes 393248 | tf_op jit(solution)/shard_map/ppermute | solution.py:30
  31.5 0.1 pad_add_fusion.slot_ref
  31.6 1.4 %copy-done.4 = f32[6,32,2048]{2,1,0:T(8,128)S(1)} copy-done((f32[6,32,2048]{2,1,0:T(8,128)S(1)}, f32[6,32,2048]{2,1,0:T(8,128)}, u32[]{:S(2)}) %copy-start.4) | copy-done | bytes 1572888
  33.0 4.0 %close.1.field_ref = f32[6,32,2048]{2,1,0:T(8,128)S(1)} custom-call(f32[6,32,2048]{2,1,0:T(8,128)S(1)} %copy-done.4, bf16[12,32,512]{2,1,0:T(8,128)(2,1)S(1)} %collective-permute-done.1.ahead_ref, bf16[12,32,512]{2,1,0:T(8,128)(2,1)} %collective-permute-done.2.behind_ref, f32[864,128]{1,0:T(8,128)S(1)} %bitcast.24, f32[2,16,2048]{2,1,0:T(8,128)S(1)} %get-tuple-element.23.back_ref), custom_call_target="tpu_custom_call" | custom-call | flops 16777216 | bytes 1048576 | tf_op jit(solution)/shard_map/close/pallas_call | solution.py:299
  37.0 12.5 %product.1 = (bf16[2,64,864]{2,1,0:T(8,128)(2,1)S(1)}, bf16[2,64,864]{2,1,0:T(8,128)(2,1)S(1)}) custom-call(s32[4]{0:T(128)S(1)} %pad_add_fusion.slot_ref, f32[6,32,2048]{2,1,0:T(8,128)S(1)} %close.1.field_ref, f32[2,27,2048]{2,1,0:T(8,128)S(1)} %copy-done.6, bf16[6,32,2048]{2,1,0:T(8,128)(2,1)} %get-tuple-element.19.refs_0_, ...), custom_call_target="tpu_custom_call" | custom-call | flops 4294967296 | bytes 1048576 | tf_op jit(solution)/shard_map/product/pallas_call | solution.py:299
  49.6 0.6 collective-permute-start.5
  50.2 7.5 %collective-permute-done.5 = bf16[2,64,864]{2,1,0:T(8,128)(2,1)S(1)} collective-permute-done((bf16[2,64,864]{2,1,0:T(8,128)(2,1)S(1)}, bf16[2,64,864]{2,1,0:T(8,128)(2,1)S(1)}, u32[]{:S(2)}, u32[]{:S(2)}) %collective-permute-start.5) | collective-permute-done | bytes 221216 | tf_op jit(solution)/shard_map/ppermute | solution.py:30
  57.7 0.7 collective-permute-start.6
  58.4 3.0 %collective-permute-start.7 = (bf16[64,864]{1,0:T(8,128)(2,1)S(1)}, bf16[64,864]{1,0:T(8,128)(2,1)S(1)}, u32[]{:S(2)}, u32[]{:S(2)}) collective-permute-start(bf16[64,864]{1,0:T(8,128)(2,1)S(1)} %get-tuple-element.36), channel_id=1, source_target_pairs={{0,1},{1,5},{4,0},{5,4},{8,9},{9,13},{12,8},{13,12},{2,3},{3,7},{6... | collective-permute-start | bytes 331784 | tf_op jit(solution)/shard_map/ppermute | solution.py:387
  61.5 0.8 %collective-permute-start.8 = (bf16[64,864]{1,0:T(8,128)(2,1)S(1)}, bf16[64,864]{1,0:T(8,128)(2,1)S(1)}, u32[]{:S(2)}, u32[]{:S(2)}) collective-permute-start(bf16[64,864]{1,0:T(8,128)(2,1)S(1)} %get-tuple-element.37), channel_id=1, source_target_pairs={{0,8},{1,12},{4,9},{5,13},{8,0},{9,4},{12,1},{13,5},{2,10},{3,14},... | collective-permute-start | bytes 331784 | tf_op jit(solution)/shard_map/ppermute | solution.py:387
  62.2 0.4 collective-permute-start.9
  62.6 2.6 %collective-permute-done.7 = bf16[64,864]{1,0:T(8,128)(2,1)S(1)} collective-permute-done((bf16[64,864]{1,0:T(8,128)(2,1)S(1)}, bf16[64,864]{1,0:T(8,128)(2,1)S(1)}, u32[]{:S(2)}, u32[]{:S(2)}) %collective-permute-start.7) | collective-permute-done | bytes 110624 | tf_op jit(solution)/shard_map/ppermute | solution.py:387
  65.3 7.2 %collective-permute-done.8 = bf16[64,864]{1,0:T(8,128)(2,1)S(1)} collective-permute-done((bf16[64,864]{1,0:T(8,128)(2,1)S(1)}, bf16[64,864]{1,0:T(8,128)(2,1)S(1)}, u32[]{:S(2)}, u32[]{:S(2)}) %collective-permute-start.8) | collective-permute-done | bytes 110624 | tf_op jit(solution)/shard_map/ppermute | solution.py:387
  72.6 0.4 reshape.23
  72.9 1.6 %copy.11 = f32[32,27,2,32]{3,2,1,0:T(2,128)} copy(f32[32,27,2,32]{3,1,0,2:T(8,128)S(1)} %bitcast.26) | data formatting | bytes 442368 | tf_op jit(solution)/shard_map/transpose | solution.py:389
  (24 shorter events, 0.2 us)
Async XLA Ops:
  0.0 13.8 %copy-start.7 = (s32[27,3]{0,1:T(4,128)S(1)}, s32[27,3]{0,1:T(4,128)}, u32[]{:S(2)}) copy-start(s32[27,3]{0,1:T(4,128)} %param.5) | copy-start | bytes 976
  0.0 1.0 %copy-start = (f32[3,3,3,2,2048]{4,3,2,1,0:T(2,128)S(1)}, f32[3,3,3,2,2048]{4,3,2,1,0:T(2,128)}, u32[]{:S(2)}) copy-start(f32[3,3,3,2,2048]{4,3,2,1,0:T(2,128)} %param.4) | copy-start | bytes 1327108
  1.0 1.4 %copy-start.2 = (f32[32,3,2,2048]{3,2,1,0:T(2,128)S(1)}, f32[32,3,2,2048]{3,2,1,0:T(2,128)}, u32[]{:S(2)}) copy-start(f32[32,3,2,2048]{3,2,1,0:T(2,128)} %param.3) | copy-start | bytes 4718596
  2.4 11.4 %copy-start.1 = (f32[3,3,3,2,2048]{4,3,2,1,0:T(2,128)S(1)}, f32[3,3,3,2,2048]{4,3,2,1,0:T(2,128)}, u32[]{:S(2)}) copy-start(f32[3,3,3,2,2048]{4,3,2,1,0:T(2,128)} %param.4) | copy-start | bytes 1327108
  7.2 24.3 %collective-permute-start = (bf16[6,32,2048]{2,1,0:T(8,128)(2,1)}, bf16[6,32,2048]{2,1,0:T(8,128)(2,1)}, u32[]{:S(2)}, u32[]{:S(2)}) collective-permute-start(bf16[6,32,2048]{2,1,0:T(8,128)(2,1)} %get-tuple-element.19.refs_0_), channel_id=1, source_target_pairs={{0,2},{2,0},{1,3},{3,1},{4,6},{6,4},{5,7},{7,5},{8,10},{10,8},{9,1... | collective-permute-start | bytes 2359304 | tf_op jit(solution)/shard_map/ppermute | solution.py:30
  10.2 13.9 %collective-permute-start.1 = (bf16[12,32,512]{2,1,0:T(8,128)(2,1)}, bf16[12,32,512]{2,1,0:T(8,128)(2,1)S(1)}, u32[]{:S(2)}, u32[]{:S(2)}) collective-permute-start(bf16[12,32,512]{2,1,0:T(8,128)(2,1)} %get-tuple-element.20), channel_id=1, source_target_pairs={{0,12},{4,0},{8,4},{12,8},{1,13},{5,1},{9,5},{13,9},{2,14},{6,2},{... | collective-permute-start | bytes 1179656 | tf_op jit(solution)/shard_map/ppermute | solution.py:30
  13.8 17.7 %collective-permute-start.2 = (bf16[12,32,512]{2,1,0:T(8,128)(2,1)}, bf16[12,32,512]{2,1,0:T(8,128)(2,1)}, u32[]{:S(2)}, u32[]{:S(2)}) collective-permute-start(bf16[12,32,512]{2,1,0:T(8,128)(2,1)} %get-tuple-element.21), channel_id=1, source_target_pairs={{0,4},{4,8},{8,12},{12,0},{1,5},{5,9},{9,13},{13,1},{2,6},{6,10},{... | collective-permute-start | bytes 1179656 | tf_op jit(solution)/shard_map/ppermute | solution.py:30
  13.8 23.3 %collective-permute-start.3 = (bf16[6,32,2048]{2,1,0:T(8,128)(2,1)}, bf16[6,32,2048]{2,1,0:T(8,128)(2,1)}, u32[]{:S(2)}, u32[]{:S(2)}) collective-permute-start(bf16[6,32,2048]{2,1,0:T(8,128)(2,1)} %get-tuple-element.19.refs_0_), channel_id=1, source_target_pairs={{0,1},{1,0},{2,3},{3,2},{4,5},{5,4},{6,7},{7,6},{8,9},{9,8},{10,11... | collective-permute-start | bytes 2359304 | tf_op jit(solution)/shard_map/ppermute | solution.py:30
  22.1 1.2 %copy-start.3 = (f32[6,32,2048]{2,1,0:T(8,128)}, f32[6,32,2048]{2,1,0:T(8,128)S(1)}, u32[]{:S(2)}) copy-start(f32[6,32,2048]{2,1,0:T(8,128)S(1)} %get-tuple-element.26.part_ref) | copy-start | bytes 4718596
  23.3 0.8 %copy-start.5 = (f32[2,27,2048]{2,1,0:T(8,128)}, f32[2,27,2048]{2,1,0:T(8,128)S(1)}, u32[]{:S(2)}) copy-start(f32[2,27,2048]{2,1,0:T(8,128)S(1)} %get-tuple-element.29.table_ref) | copy-start | bytes 1327108
  31.5 5.5 %collective-permute-start.4 = (bf16[6,32,2048]{2,1,0:T(8,128)(2,1)}, bf16[6,32,2048]{2,1,0:T(8,128)(2,1)S(1)}, u32[]{:S(2)}, u32[]{:S(2)}) collective-permute-start(bf16[6,32,2048]{2,1,0:T(8,128)(2,1)} %collective-permute-done.refs_1_), channel_id=1, source_target_pairs={{0,1},{1,0},{2,3},{3,2},{4,5},{5,4},{6,7},{7,6},{8,9},{9,8},{10,11... | collective-permute-start | bytes 2359304 | tf_op jit(solution)/shard_map/ppermute | solution.py:30
  31.6 1.4 %copy-start.4 = (f32[6,32,2048]{2,1,0:T(8,128)S(1)}, f32[6,32,2048]{2,1,0:T(8,128)}, u32[]{:S(2)}) copy-start(f32[6,32,2048]{2,1,0:T(8,128)} %copy-done.3) | copy-start | bytes 4718596
  33.0 4.0 %copy-start.6 = (f32[2,27,2048]{2,1,0:T(8,128)S(1)}, f32[2,27,2048]{2,1,0:T(8,128)}, u32[]{:S(2)}) copy-start(f32[2,27,2048]{2,1,0:T(8,128)} %copy-done.5) | copy-start | bytes 1327108
  49.6 8.1 %collective-permute-start.5 = (bf16[2,64,864]{2,1,0:T(8,128)(2,1)S(1)}, bf16[2,64,864]{2,1,0:T(8,128)(2,1)S(1)}, u32[]{:S(2)}, u32[]{:S(2)}) collective-permute-start(bf16[2,64,864]{2,1,0:T(8,128)(2,1)S(1)} %get-tuple-element.31), channel_id=1, source_target_pairs={{0,2},{2,0},{1,3},{3,1},{4,6},{6,4},{5,7},{7,5},{8,10},{10,8},{9,1... | collective-permute-start | bytes 663560 | tf_op jit(solution)/shard_map/ppermute | solution.py:30
  57.7 4.9 %collective-permute-start.6 = (bf16[64,864]{1,0:T(8,128)(2,1)S(1)}, bf16[64,864]{1,0:T(8,128)(2,1)S(1)}, u32[]{:S(2)}, u32[]{:S(2)}) collective-permute-start(bf16[64,864]{1,0:T(8,128)(2,1)S(1)} %get-tuple-element.35), channel_id=1, source_target_pairs={{0,0},{1,4},{4,1},{5,5},{8,8},{9,12},{12,9},{13,13},{2,2},{3,6},{6... | collective-permute-start | bytes 331784 | tf_op jit(solution)/shard_map/ppermute | solution.py:387
  58.4 6.8 %collective-permute-start.7 = (bf16[64,864]{1,0:T(8,128)(2,1)S(1)}, bf16[64,864]{1,0:T(8,128)(2,1)S(1)}, u32[]{:S(2)}, u32[]{:S(2)}) collective-permute-start(bf16[64,864]{1,0:T(8,128)(2,1)S(1)} %get-tuple-element.36), channel_id=1, source_target_pairs={{0,1},{1,5},{4,0},{5,4},{8,9},{9,13},{12,8},{13,12},{2,3},{3,7},{6... | collective-permute-start | bytes 331784 | tf_op jit(solution)/shard_map/ppermute | solution.py:387
  61.5 11.0 %collective-permute-start.8 = (bf16[64,864]{1,0:T(8,128)(2,1)S(1)}, bf16[64,864]{1,0:T(8,128)(2,1)S(1)}, u32[]{:S(2)}, u32[]{:S(2)}) collective-permute-start(bf16[64,864]{1,0:T(8,128)(2,1)S(1)} %get-tuple-element.37), channel_id=1, source_target_pairs={{0,8},{1,12},{4,9},{5,13},{8,0},{9,4},{12,1},{13,5},{2,10},{3,14},... | collective-permute-start | bytes 331784 | tf_op jit(solution)/shard_map/ppermute | solution.py:387
  62.2 10.3 %collective-permute-start.9 = (bf16[64,864]{1,0:T(8,128)(2,1)S(1)}, bf16[64,864]{1,0:T(8,128)(2,1)S(1)}, u32[]{:S(2)}, u32[]{:S(2)}) collective-permute-start(bf16[64,864]{1,0:T(8,128)(2,1)S(1)} %get-tuple-element.38), channel_id=1, source_target_pairs={{0,9},{1,13},{4,8},{5,12},{8,1},{9,5},{12,0},{13,4},{2,11},{3,15},... | collective-permute-start | bytes 331784 | tf_op jit(solution)/shard_map/ppermute | solution.py:387

commit v6 on v5

--- a/solution.py
+++ b/solution.py
@@ -117,7 +117,7 @@
     return combined(plane_hops(total, link_ref, back_ref, layer, tile, rows, fetch), total)
 
 
-def open_kernel(vector_ref, link_ref, field_ref, raw_ref, down_ref, up_ref, rim_ref, back_ref):
+def open_kernel(vector_ref, link_ref, field_ref, raw_ref, down_ref, up_ref):
     vectors, sites = field_ref.shape[1:]
     tiles, layers = sites // LANES, sites // PLANE
     stride = 6 * tiles
@@ -130,6 +130,19 @@
             raw_ref[k, :, pl.ds(tile * LANES, LANES)] = low
             if tile < TILES:
                 down_ref[k, :, pl.ds(tile * LANES, LANES)] = low
+
+    @pl.loop(0, TILES)
+    def _(tile):
+        for rows in row_groups(field_ref):
+            turned = [None] * 6
+            source = load(field_ref, rows, lanes_at(layers - 1, tile))
+            add_hop(turned, link_at(link_ref, 0, layers - 1, tile), source, True)
+            store(up_ref, rows, lanes_at(0, tile), turned)
+
+
+def rim_kernel(field_ref, link_ref, down_ref, up_ref, rim_ref, back_ref):
+    sites = field_ref.shape[2]
+    tiles, layers = sites // LANES, sites // PLANE
     lane = lax.broadcasted_iota(jnp.int32, (9, LANES), 1)
     for layer in range(layers):
         for part in range(2):
@@ -148,13 +161,11 @@
                 new = first_step(layer, tile, rows, field_ref, link_ref, back_ref)
                 store(rim_ref, rows, lanes_at(place, tile), new)
                 if place == 0:
-                    store(down_ref.at[pl.ds(6, 6)], rows, lanes, new)
+                    store(down_ref, rows, lanes, new)
                 else:
-                    here = load(field_ref, rows, lanes_at(layer, tile))
-                    for part, source in enumerate((here, new)):
-                        turned = [None] * 6
-                        add_hop(turned, link_at(link_ref, 0, layer, tile), source, True)
-                        store(up_ref.at[pl.ds(6 * part, 6)], rows, lanes, turned)
+                    turned = [None] * 6
+                    add_hop(turned, link_at(link_ref, 0, layer, tile), new, True)
+                    store(up_ref, rows, lanes, turned)
 
 
 def unit_phase(turns):
@@ -211,25 +222,23 @@
                 store(out_ref, rows, lanes_at(layer, tile), new)
 
 
-def close_kernel(part_ref, ahead_ref, behind_ref, link_ref, back_ref, out_ref, change_ref):
+def close_kernel(part_ref, ahead_ref, behind_ref, link_ref, back_ref, out_ref, token_ref, change_ref):
     layers = part_ref.shape[2] // PLANE
-    fresh, older = pl.ds(6, 6), pl.ds(0, 6)
+    token_ref[...] = jnp.zeros_like(token_ref)
 
     @pl.loop(0, TILES)
     def _(tile):
         lanes = lanes_at(0, tile)
         for rows in row_groups(part_ref):
-            low = load(behind_ref.at[older], rows, lanes)
-            store(change_ref, rows, lanes, [KAPPA * a for a in low])
+            store(change_ref, rows, lanes, [KAPPA * a for a in load(behind_ref, rows, lanes)])
             high = [None] * 6
-            add_hop(high, link_at(link_ref, 0, layers - 1, tile), load(ahead_ref.at[older], rows, lanes), False)
+            add_hop(high, link_at(link_ref, 0, layers - 1, tile), load(ahead_ref, rows, lanes), False)
             store(change_ref, rows, lanes_at(1, tile), [KAPPA * a for a in high])
 
     for layer in range(layers):
 
         @pl.loop(0, TILES)
         def _(tile):
-            lanes = lanes_at(0, tile)
             for rows in row_groups(part_ref):
                 new = load(part_ref, rows, lanes_at(layer, tile))
                 change = lambda place, t: load(change_ref, rows, lanes_at(place, t))
@@ -238,13 +247,10 @@
                     add_hop(hops, link_at(link_ref, 0, 0, tile), change(0, tile), True)
                 if layer == layers - 2:
                     add_hop(hops, link_at(link_ref, 0, layer, tile), change(1, tile), False)
-                if layer == 0:
-                    came = load(behind_ref.at[fresh], rows, lanes)
-                    hops = came if hops[0] is None else [a + b for a, b in zip(hops, came)]
-                if layer == layers - 1:
-                    add_hop(hops, link_at(link_ref, 0, layer, tile), load(ahead_ref.at[fresh], rows, lanes), False)
                 for place, edge in ((0, 0), (1, layers - 1)):
                     if layer == edge:
+                        if hops[0] is None:
+                            hops = [jnp.zeros_like(a) for a in new]
                         here = plane_hops(hops, link_ref, back_ref, layer, tile, rows, lambda t: change(place, t))
                         new = [a + (1.0 - 6.0 * KAPPA) * b for a, b in zip(new, here)]
                 if hops[0] is not None:
@@ -252,24 +258,39 @@
                 store(out_ref, rows, lanes_at(layer, tile), new)
 
 
-def product_kernel(columns, begin, count, scale, slot_ref, field_ref, table_ref, *refs):
+def face_kernel(most_ref, ahead_ref, behind_ref, link_ref, token_ref, out_ref):
+    layers = most_ref.shape[2] // PLANE
+
+    @pl.loop(0, TILES)
+    def _(tile):
+        lanes, high = lanes_at(0, tile), lanes_at(1, tile)
+        for rows in row_groups(most_ref):
+            new = zip(load(most_ref, rows, lanes), load(behind_ref, rows, lanes))
+            store(out_ref, rows, lanes, [a + KAPPA * b for a, b in new])
+            hop = [None] * 6
+            add_hop(hop, link_at(link_ref, 0, layers - 1, tile), load(ahead_ref, rows, lanes), False)
+            new = zip(load(most_ref, rows, lanes_at(layers - 1, tile)), hop)
+            store(out_ref, rows, high, [a + KAPPA * b for a, b in new])
+
+
+def product_kernel(columns, count, scale, slot_ref, most_ref, face_ref, table_ref, *refs):
     groups = len(columns)
     raw_refs, out_refs, (total_ref, left_ref, right_ref) = refs[:groups], refs[groups:-3], refs[-3:]
-    vectors = field_ref.shape[1]
+    vectors = most_ref.shape[1]
+    layers = most_ref.shape[2] // PLANE
     depth = 6 * LANES
     step = left_ref.shape[1] // depth
     total_ref[...] = jnp.zeros_like(total_ref)
 
-    @pl.loop(0, field_ref.shape[2] // LANES // step)
-    def _(block):
+    def add(field_ref, place):
         for part in range(step):
-            lanes = pl.ds(pl.multiple_of((block * step + part) * LANES, LANES), LANES)
-            field = [field_ref[k, :, lanes] for k in range(6)]
+            own, lanes = place(part)
+            field = [field_ref[k, :, own] for k in range(6)]
             one = [pl.ds(part * depth + 2 * color * LANES, LANES) for color in range(3)]
             two = [pl.ds(part * depth + (2 * color + 1) * LANES, LANES) for color in range(3)]
             for p in range(count):
-                cosine = table_ref[0, pl.ds(begin + p, 1), lanes]
-                sine = table_ref[1, pl.ds(begin + p, 1), lanes]
+                cosine = table_ref[0, pl.ds(p, 1), lanes]
+                sine = table_ref[1, pl.ds(p, 1), lanes]
                 rows = pl.ds(p * vectors, vectors)
                 for color in range(3):
                     real, imag = field[2 * color], field[2 * color + 1]
@@ -289,6 +310,18 @@
             left_ref[...], right_ref[...], (((1,), (1,)), ((), ())), preferred_element_type=WIDE
         )
 
+    blocks = TILES // step
+
+    @pl.loop(0, (layers - 2) * blocks)
+    def _(block):
+        add(most_ref, lambda part: (lanes_at(1, block * step + part),) * 2)
+
+    @pl.loop(0, 2 * blocks)
+    def _(block):
+        layer = block // blocks * (layers - 1)
+        tile = block % blocks * step
+        add(face_ref, lambda part: (lanes_at(0, block * step + part), lanes_at(layer, tile + part)))
+
     width = total_ref.shape[0] // groups
     for g in range(groups):
         block = total_ref[pl.ds(g * width, width), :] * scale
@@ -319,17 +352,24 @@
     brick, vec, sub = (lax.axis_index(axis) for axis in ("brick", "vec", "sub"))
     tiled_vectors = jnp.swapaxes(vectors.reshape((width, 3, 2, tiles, LANES)), 2, 3).reshape((-1, LANES))
     links = jnp.swapaxes(gauge_links.reshape((27, 2, tiles, LANES)), 1, 2).reshape((-1, LANES))
-    full, faces = (6, width, sites), (12, width, PLANE)
-    field, raw, down, up, rim, back = call(
+    full, face = (6, width, sites), (6, width, PLANE)
+    field, raw, down, up = call(
         open_kernel,
         "open",
-        ((full, WIDE), (full, LOW), (faces, LOW), (faces, LOW), ((6, width, 2 * PLANE), WIDE), ((2, 16, sites), WIDE)),
+        ((full, WIDE), (full, LOW), (face, LOW), (face, LOW)),
         (tiled_vectors, links),
-        flops=1 << 24,
+        flops=1 << 22,
     )
     ahead, behind = shifted(down, "brick", -1), shifted(up, "brick", 1)
     across = [shifted(raw, "vec", a) for a in range(1, vecs)]
-    beside = [shifted(raw, "sub", b) for b in range(1, subs)]
+    down_two, up_two, rim, back = call(
+        rim_kernel,
+        "rim",
+        ((face, LOW), (face, LOW), ((6, width, 2 * PLANE), WIDE), ((2, 16, sites), WIDE)),
+        (field, links),
+        flops=1 << 24,
+    )
+    ahead_two, behind_two = shifted(down_two, "brick", -1), shifted(up_two, "brick", 1)
     place = (brick * layers).astype(jnp.int32).reshape((1,))
     part, table = call(
         functools.partial(local_kernel, total_x),
@@ -340,18 +380,24 @@
         scratch=(pltpu.VMEM(full, WIDE),),
         smem=True,
     )
-    *across, ahead, behind, part = lax.optimization_barrier((*across, ahead, behind, part))
-    raws = [raw, *across, *beside]
-    raws += [shifted(array, "sub", b) for b in range(1, subs) for array in across]
-    offsets = [(a, 0) for a in range(vecs)] + [(0, b) for b in range(1, subs)]
-    offsets += [(a, b) for b in range(1, subs) for a in range(1, vecs)]
-    (smeared,) = call(
+    most, token = call(
         close_kernel,
         "close",
-        ((full, WIDE),),
+        ((full, WIDE), ((8, LANES), WIDE)),
         (part, ahead, behind, links, back),
         flops=1 << 24,
         scratch=(pltpu.VMEM((6, width, 2 * PLANE), WIDE),),
+    )
+    late, token = lax.optimization_barrier((raw, token))
+    *across, ahead_two, behind_two, token = lax.optimization_barrier((*across, ahead_two, behind_two, token))
+    raws = [raw, *across] + [shifted(array, "sub", b) for b in range(1, subs) for array in (late, *across)]
+    offsets = [(a, b) for b in range(subs) for a in range(vecs)]
+    (faces,) = call(
+        face_kernel,
+        "face",
+        (((6, width, 2 * PLANE), WIDE),),
+        (most, ahead_two, behind_two, links, token),
+        flops=1 << 22,
     )
     brick_vec, brick_sub = brick // subs, brick % subs
     slots = jnp.stack([(sub - b - brick_sub) % subs for a, b in offsets]).astype(jnp.int32)
@@ -359,10 +405,10 @@
     depth = STEP * 6 * LANES
     columns = count * width
     blocks = call(
-        functools.partial(product_kernel, [-a % vecs for a, b in offsets], 0, count, scale),
+        functools.partial(product_kernel, [-a % vecs for a, b in offsets], count, scale),
         "product",
         (((subs, 2 * width, columns), LOW),) * vecs,
-        (slots, smeared, table, *raws),
+        (slots, most, faces, table, *raws),
         flops=1 << 32,
         scratch=(
             pltpu.VMEM((groups * 2 * width, columns), WIDE),

time: 75.4 us -> 71.5 us (0.948)
  waiting for transfers between devices: 24.7 us -> 17.8 us
  starting transfers between devices: 12 us -> 17.6 us
  local copies, waits for them, and re-layouts: 7.92 us -> 4.57 us
  Pallas kernels: 29.6 us -> 31 us
    ppermute x6 -> x8, waiting for transfers between devices: 14.9 us -> 9.92 us  [shifted(): lax.ppermute(array, axis, [(i, (i + by) % peers) for i in range(peers)])]
    ppermute x6 -> x8, starting transfers between devices: 7.15 us -> 11.6 us  [shifted(): lax.ppermute(array, axis, [(i, (i + by) % peers) for i in range(peers)])]
    unnamed x17 -> x13, local copies, waits for them, and re-layouts: 5.89 us -> 2.53 us
    ppermute x4, waiting for transfers between devices: 9.85 us -> 7.88 us  [shards(): shares.append(lax.ppermute(block[r], ('brick', 'sub'), pairs))]
    pallas_call x4 -> x6, Pallas kernels: 29.6 us -> 31 us  [call(): pl.pallas_call(kernel, out_shape=tuple((jax.ShapeDtypeStruct(shape, dtype...]
    ppermute x4, starting transfers between devices: 4.87 us -> 5.99 us  [shards(): shares.append(lax.ppermute(block[r], ('brick', 'sub'), pairs))]
  transfers between devices with their start and end apart: 10 -> 12, of which waited for: 4 -> 5; matrix products, arithmetic and copies ran while one was open for 0% -> 0% of each run, Pallas kernels for 16% -> 23%
where the time goes in v6:
time: 71.5 us; the launch traced here: 71.3 us
  Pallas kernels  31 us (43%)
  waiting for transfers between devices  17.8 us (25%)
  starting transfers between devices  17.6 us (25%)
  local copies, waits for them, and re-layouts  4.57 us (6%)
    pallas_call x6, Pallas kernels, call(): pl.pallas_call(kernel, out_shape=tuple((jax.ShapeDtypeStruct(shape, dtype...  31 us
    ppermute x8, starting transfers between devices, shifted(): lax.ppermute(array, axis, [(i, (i + by) % peers) for i in range(peers)])  11.6 us
    ppermute x8, waiting for transfers between devices, shifted(): lax.ppermute(array, axis, [(i, (i + by) % peers) for i in range(peers)])  9.92 us
    ppermute x4, waiting for transfers between devices, shards(): shares.append(lax.ppermute(block[r], ('brick', 'sub'), pairs))  7.88 us
    ppermute x4, starting transfers between devices, shards(): shares.append(lax.ppermute(block[r], ('brick', 'sub'), pairs))  5.99 us
    unnamed x13, local copies, waits for them, and re-layouts  2.53 us
    transpose x1, local copies, waits for them, and re-layouts, shards(): return jnp.transpose(total.reshape((2, width, count, width)), (1, 2, 0, 3))  1.61 us
  transfers between devices with their start and end apart: 12, of which 5 were waited for; matrix products, arithmetic and copies ran while one was open for 0% of the time, Pallas kernels for 23%

profile of v6, /device:TPU:0, one launch (start us, length us, event | category | flops | bytes accessed | tf_op | source)
XLA Modules:
  0.0 71.3 jit_solution(2400916673581467158)
XLA Ops:
  0.0 1.0 %copy-done = f32[3,3,3,2,2048]{4,3,2,1,0:T(2,128)S(1)} copy-done((f32[3,3,3,2,2048]{4,3,2,1,0:T(2,128)S(1)}, f32[3,3,3,2,2048]{4,3,2,1,0:T(2,128)}, u32[]{:S(2)}) %copy-start) | copy-done | bytes 442392
  1.0 1.4 %copy-done.2 = f32[32,3,2,2048]{3,2,1,0:T(2,128)S(1)} copy-done((f32[32,3,2,2048]{3,2,1,0:T(2,128)S(1)}, f32[32,3,2,2048]{3,2,1,0:T(2,128)}, u32[]{:S(2)}) %copy-start.2) | copy-done | bytes 1572888
  2.4 2.2 %open.1 = (f32[6,32,2048]{2,1,0:T(8,128)S(1)}, bf16[6,32,2048]{2,1,0:T(8,128)(2,1)}, bf16[6,32,512]{2,1,0:T(8,128)(2,1)}, bf16[6,32,512]{2,1,0:T(8,128)(2,1)}) custom-call(f32[3072,128]{1,0:T(8,128)S(1)} %bitcast.27, f32[864,128]{1,0:T(8,128)S(1)} %bitcast.22), custom_call_target="tpu_custom_call" | custom-call | flops 4194304 | bytes 1048576 | tf_op jit(solution)/shard_map/open/pallas_call | solution.py:332
  4.6 2.9 %collective-permute-start.2 = (bf16[6,32,2048]{2,1,0:T(8,128)(2,1)}, bf16[6,32,2048]{2,1,0:T(8,128)(2,1)}, u32[]{:S(2)}, u32[]{:S(2)}) collective-permute-start(bf16[6,32,2048]{2,1,0:T(8,128)(2,1)} %get-tuple-element.42.refs_0_), channel_id=1, source_target_pairs={{0,2},{2,0},{1,3},{3,1},{4,6},{6,4},{5,7},{7,5},{8,10},{10,8},{9,1... | collective-permute-start | bytes 2359304 | tf_op jit(solution)/shard_map/ppermute | solution.py:30
  7.5 3.6 %collective-permute-start = (bf16[6,32,512]{2,1,0:T(8,128)(2,1)}, bf16[6,32,512]{2,1,0:T(8,128)(2,1)}, u32[]{:S(2)}, u32[]{:S(2)}) collective-permute-start(bf16[6,32,512]{2,1,0:T(8,128)(2,1)} %get-tuple-element.29), channel_id=1, source_target_pairs={{0,12},{4,0},{8,4},{12,8},{1,13},{5,1},{9,5},{13,9},{2,14},{6,2},{... | collective-permute-start | bytes 589832 | tf_op jit(solution)/shard_map/ppermute | solution.py:30
  11.2 3.4 %rim.1 = (bf16[6,32,512]{2,1,0:T(8,128)(2,1)}, bf16[6,32,512]{2,1,0:T(8,128)(2,1)}, f32[6,32,1024]{2,1,0:T(8,128)S(1)}, f32[2,16,2048]{2,1,0:T(8,128)S(1)}) custom-call(f32[6,32,2048]{2,1,0:T(8,128)S(1)} %get-tuple-element.25.field_ref, f32[864,128]{1,0:T(8,128)S(1)} %bitcast.23), custom_call_target="tpu_custom_call" | custom-call | flops 16777216 | bytes 1048576 | tf_op jit(solution)/shard_map/rim/pallas_call | solution.py:332
  14.6 3.8 %collective-permute-start.3 = (bf16[6,32,512]{2,1,0:T(8,128)(2,1)}, bf16[6,32,512]{2,1,0:T(8,128)(2,1)S(1)}, u32[]{:S(2)}, u32[]{:S(2)}) collective-permute-start(bf16[6,32,512]{2,1,0:T(8,128)(2,1)} %get-tuple-element.33), channel_id=1, source_target_pairs={{0,12},{4,0},{8,4},{12,8},{1,13},{5,1},{9,5},{13,9},{2,14},{6,2},{... | collective-permute-start | bytes 589832 | tf_op jit(solution)/shard_map/ppermute | solution.py:30
  18.4 0.1 copy.10.momenta_ref
  18.5 8.3 %local.1 = (f32[6,32,2048]{2,1,0:T(8,128)S(1)}, f32[2,27,2048]{2,1,0:T(8,128)S(1)}) custom-call(s32[1]{0:T(128)} %bitcast.2.place_ref, f32[6,32,2048]{2,1,0:T(8,128)S(1)} %get-tuple-element.25.field_ref, f32[864,128]{1,0:T(8,128)S(1)} %bitcast.24, f32[2,16,2048]{2,1,0:T(8,128)S(1)} %get-tuple-element.26.back_ref, ...), custom_call_target="tpu_custom_call" | custom-call | flops 33554432 | bytes 1048576 | tf_op jit(solution)/shard_map/local/pallas_call | solution.py:332
  26.8 4.1 %close.1 = (f32[6,32,2048]{2,1,0:T(8,128)S(1)}, f32[8,128]{1,0:T(8,128)S(1)}) custom-call(f32[6,32,2048]{2,1,0:T(8,128)S(1)} %get-tuple-element.28.part_ref, bf16[6,32,512]{2,1,0:T(8,128)(2,1)} %collective-permute-done.ahead_ref, bf16[6,32,512]{2,1,0:T(8,128)(2,1)} %collective-permute-done.1.behind_ref, f32[864,128]{1,0:T(8,128)S(1)} %bitcast.25, ...), custom_call_target="tpu_custom_call" | custom-call | flops 16777216 | bytes 1048576 | tf_op jit(solution)/shard_map/close/pallas_call | solution.py:332
  31.0 0.5 collective-permute-start.6
  31.7 0.3 face.1.face_ref
  31.9 1.7 %collective-permute-done.5.refs_2_ = bf16[6,32,2048]{2,1,0:T(8,128)(2,1)} collective-permute-done((bf16[6,32,2048]{2,1,0:T(8,128)(2,1)}, bf16[6,32,2048]{2,1,0:T(8,128)(2,1)}, u32[]{:S(2)}, u32[]{:S(2)}) %collective-permute-start.5) | collective-permute-done | bytes 786464 | tf_op jit(solution)/shard_map/ppermute | solution.py:30
  33.6 1.1 %collective-permute-done.6.refs_3_ = bf16[6,32,2048]{2,1,0:T(8,128)(2,1)} collective-permute-done((bf16[6,32,2048]{2,1,0:T(8,128)(2,1)}, bf16[6,32,2048]{2,1,0:T(8,128)(2,1)}, u32[]{:S(2)}, u32[]{:S(2)}) %collective-permute-start.6) | collective-permute-done | bytes 786464 | tf_op jit(solution)/shard_map/ppermute | solution.py:30
  34.7 12.8 %product.1 = (bf16[2,64,864]{2,1,0:T(8,128)(2,1)S(1)}, bf16[2,64,864]{2,1,0:T(8,128)(2,1)S(1)}) custom-call(s32[4]{0:T(128)S(1)} %pad_add_fusion.slot_ref, f32[6,32,2048]{2,1,0:T(8,128)S(1)} %get-tuple-element.31.most_ref, f32[6,32,1024]{2,1,0:T(8,128)S(1)} %face.1.face_ref, f32[2,27,2048]{2,1,0:T(8,128)S(1)} %copy-done.4, ...), custom_call_target="tpu_custom_call" | custom-call | flops 4294967296 | bytes 1048576 | tf_op jit(solution)/shard_map/product/pallas_call | solution.py:332
  47.5 0.6 collective-permute-start.7
  48.1 7.1 %collective-permute-done.7 = bf16[2,64,864]{2,1,0:T(8,128)(2,1)S(1)} collective-permute-done((bf16[2,64,864]{2,1,0:T(8,128)(2,1)S(1)}, bf16[2,64,864]{2,1,0:T(8,128)(2,1)S(1)}, u32[]{:S(2)}, u32[]{:S(2)}) %collective-permute-start.7) | collective-permute-done | bytes 221216 | tf_op jit(solution)/shard_map/ppermute | solution.py:30
  55.3 0.6 collective-permute-start.10
  56.0 0.7 collective-permute-start.8
  56.6 4.7 %collective-permute-start.9 = (bf16[64,864]{1,0:T(8,128)(2,1)S(1)}, bf16[64,864]{1,0:T(8,128)(2,1)S(1)}, u32[]{:S(2)}, u32[]{:S(2)}) collective-permute-start(bf16[64,864]{1,0:T(8,128)(2,1)S(1)} %get-tuple-element.48), channel_id=1, source_target_pairs={{0,1},{1,5},{4,0},{5,4},{8,9},{9,13},{12,8},{13,12},{2,3},{3,7},{6... | collective-permute-start | bytes 331784 | tf_op jit(solution)/shard_map/ppermute | solution.py:433
  61.3 5.3 %collective-permute-done.10 = bf16[64,864]{1,0:T(8,128)(2,1)S(1)} collective-permute-done((bf16[64,864]{1,0:T(8,128)(2,1)S(1)}, bf16[64,864]{1,0:T(8,128)(2,1)S(1)}, u32[]{:S(2)}, u32[]{:S(2)}) %collective-permute-start.10) | collective-permute-done | bytes 110624 | tf_op jit(solution)/shard_map/ppermute | solution.py:433
  66.6 2.6 %collective-permute-done.9 = bf16[64,864]{1,0:T(8,128)(2,1)S(1)} collective-permute-done((bf16[64,864]{1,0:T(8,128)(2,1)S(1)}, bf16[64,864]{1,0:T(8,128)(2,1)S(1)}, u32[]{:S(2)}, u32[]{:S(2)}) %collective-permute-start.9) | collective-permute-done | bytes 110624 | tf_op jit(solution)/shard_map/ppermute | solution.py:433
  69.3 0.4 reshape.23
  69.7 1.6 %copy.11 = f32[32,27,2,32]{3,2,1,0:T(2,128)} copy(f32[32,27,2,32]{3,1,0,2:T(8,128)S(1)} %bitcast.28) | data formatting | bytes 442368 | tf_op jit(solution)/shard_map/transpose | solution.py:435
  (26 shorter events, 0.3 us)
Async XLA Ops:
  0.0 1.0 %copy-start = (f32[3,3,3,2,2048]{4,3,2,1,0:T(2,128)S(1)}, f32[3,3,3,2,2048]{4,3,2,1,0:T(2,128)}, u32[]{:S(2)}) copy-start(f32[3,3,3,2,2048]{4,3,2,1,0:T(2,128)} %param.4) | copy-start | bytes 1327108
  1.0 1.4 %copy-start.2 = (f32[32,3,2,2048]{3,2,1,0:T(2,128)S(1)}, f32[32,3,2,2048]{3,2,1,0:T(2,128)}, u32[]{:S(2)}) copy-start(f32[32,3,2,2048]{3,2,1,0:T(2,128)} %param.3) | copy-start | bytes 4718596
  2.4 8.7 %copy-start.1 = (f32[3,3,3,2,2048]{4,3,2,1,0:T(2,128)S(1)}, f32[3,3,3,2,2048]{4,3,2,1,0:T(2,128)}, u32[]{:S(2)}) copy-start(f32[3,3,3,2,2048]{4,3,2,1,0:T(2,128)} %param.4) | copy-start | bytes 1327108
  2.4 16.0 %copy-start.5 = (s32[27,3]{0,1:T(4,128)S(1)}, s32[27,3]{0,1:T(4,128)}, u32[]{:S(2)}) copy-start(s32[27,3]{0,1:T(4,128)} %param.5) | copy-start | bytes 976
  4.6 26.4 %collective-permute-start.2 = (bf16[6,32,2048]{2,1,0:T(8,128)(2,1)}, bf16[6,32,2048]{2,1,0:T(8,128)(2,1)}, u32[]{:S(2)}, u32[]{:S(2)}) collective-permute-start(bf16[6,32,2048]{2,1,0:T(8,128)(2,1)} %get-tuple-element.42.refs_0_), channel_id=1, source_target_pairs={{0,2},{2,0},{1,3},{3,1},{4,6},{6,4},{5,7},{7,5},{8,10},{10,8},{9,1... | collective-permute-start | bytes 2359304 | tf_op jit(solution)/shard_map/ppermute | solution.py:30
  7.5 19.2 %collective-permute-start = (bf16[6,32,512]{2,1,0:T(8,128)(2,1)}, bf16[6,32,512]{2,1,0:T(8,128)(2,1)}, u32[]{:S(2)}, u32[]{:S(2)}) collective-permute-start(bf16[6,32,512]{2,1,0:T(8,128)(2,1)} %get-tuple-element.29), channel_id=1, source_target_pairs={{0,12},{4,0},{8,4},{12,8},{1,13},{5,1},{9,5},{13,9},{2,14},{6,2},{... | collective-permute-start | bytes 589832 | tf_op jit(solution)/shard_map/ppermute | solution.py:30
  11.2 15.6 %collective-permute-start.1 = (bf16[6,32,512]{2,1,0:T(8,128)(2,1)}, bf16[6,32,512]{2,1,0:T(8,128)(2,1)}, u32[]{:S(2)}, u32[]{:S(2)}) collective-permute-start(bf16[6,32,512]{2,1,0:T(8,128)(2,1)} %get-tuple-element.30), channel_id=1, source_target_pairs={{0,4},{4,8},{8,12},{12,0},{1,5},{5,9},{9,13},{13,1},{2,6},{6,10},{... | collective-permute-start | bytes 589832 | tf_op jit(solution)/shard_map/ppermute | solution.py:30
  14.6 16.4 %collective-permute-start.3 = (bf16[6,32,512]{2,1,0:T(8,128)(2,1)}, bf16[6,32,512]{2,1,0:T(8,128)(2,1)S(1)}, u32[]{:S(2)}, u32[]{:S(2)}) collective-permute-start(bf16[6,32,512]{2,1,0:T(8,128)(2,1)} %get-tuple-element.33), channel_id=1, source_target_pairs={{0,12},{4,0},{8,4},{12,8},{1,13},{5,1},{9,5},{13,9},{2,14},{6,2},{... | collective-permute-start | bytes 589832 | tf_op jit(solution)/shard_map/ppermute | solution.py:30
  18.4 12.6 %collective-permute-start.4 = (bf16[6,32,512]{2,1,0:T(8,128)(2,1)}, bf16[6,32,512]{2,1,0:T(8,128)(2,1)S(1)}, u32[]{:S(2)}, u32[]{:S(2)}) collective-permute-start(bf16[6,32,512]{2,1,0:T(8,128)(2,1)} %get-tuple-element.34), channel_id=1, source_target_pairs={{0,4},{4,8},{8,12},{12,0},{1,5},{5,9},{9,13},{13,1},{2,6},{6,10},{... | collective-permute-start | bytes 589832 | tf_op jit(solution)/shard_map/ppermute | solution.py:30
  26.8 4.3 %copy-start.3 = (f32[2,27,2048]{2,1,0:T(8,128)}, f32[2,27,2048]{2,1,0:T(8,128)S(1)}, u32[]{:S(2)}) copy-start(f32[2,27,2048]{2,1,0:T(8,128)S(1)} %get-tuple-element.40.table_ref) | copy-start | bytes 1327108
  30.9 2.7 %collective-permute-start.5 = (bf16[6,32,2048]{2,1,0:T(8,128)(2,1)}, bf16[6,32,2048]{2,1,0:T(8,128)(2,1)}, u32[]{:S(2)}, u32[]{:S(2)}) collective-permute-start(bf16[6,32,2048]{2,1,0:T(8,128)(2,1)} %get-tuple-element.42.refs_0_), channel_id=1, source_target_pairs={{0,1},{1,0},{2,3},{3,2},{4,5},{5,4},{6,7},{7,6},{8,9},{9,8},{10,11... | collective-permute-start | bytes 2359304 | tf_op jit(solution)/shard_map/ppermute | solution.py:30
  31.0 3.7 %collective-permute-start.6 = (bf16[6,32,2048]{2,1,0:T(8,128)(2,1)}, bf16[6,32,2048]{2,1,0:T(8,128)(2,1)}, u32[]{:S(2)}, u32[]{:S(2)}) collective-permute-start(bf16[6,32,2048]{2,1,0:T(8,128)(2,1)} %collective-permute-done.2.refs_1_), channel_id=1, source_target_pairs={{0,1},{1,0},{2,3},{3,2},{4,5},{5,4},{6,7},{7,6},{8,9},{9,8},{10,11... | collective-permute-start | bytes 2359304 | tf_op jit(solution)/shard_map/ppermute | solution.py:30
  31.7 3.1 %copy-start.4 = (f32[2,27,2048]{2,1,0:T(8,128)S(1)}, f32[2,27,2048]{2,1,0:T(8,128)}, u32[]{:S(2)}) copy-start(f32[2,27,2048]{2,1,0:T(8,128)} %copy-done.3) | copy-start | bytes 1327108
  47.5 7.7 %collective-permute-start.7 = (bf16[2,64,864]{2,1,0:T(8,128)(2,1)S(1)}, bf16[2,64,864]{2,1,0:T(8,128)(2,1)S(1)}, u32[]{:S(2)}, u32[]{:S(2)}) collective-permute-start(bf16[2,64,864]{2,1,0:T(8,128)(2,1)S(1)} %get-tuple-element.43), channel_id=1, source_target_pairs={{0,2},{2,0},{1,3},{3,1},{4,6},{6,4},{5,7},{7,5},{8,10},{10,8},{9,1... | collective-permute-start | bytes 663560 | tf_op jit(solution)/shard_map/ppermute | solution.py:30
  55.3 11.3 %collective-permute-start.10 = (bf16[64,864]{1,0:T(8,128)(2,1)S(1)}, bf16[64,864]{1,0:T(8,128)(2,1)S(1)}, u32[]{:S(2)}, u32[]{:S(2)}) collective-permute-start(bf16[64,864]{1,0:T(8,128)(2,1)S(1)} %get-tuple-element.49), channel_id=1, source_target_pairs={{0,8},{1,12},{4,9},{5,13},{8,0},{9,4},{12,1},{13,5},{2,10},{3,14},... | collective-permute-start | bytes 331784 | tf_op jit(solution)/shard_map/ppermute | solution.py:433
  55.9 10.7 %collective-permute-start.11 = (bf16[64,864]{1,0:T(8,128)(2,1)S(1)}, bf16[64,864]{1,0:T(8,128)(2,1)S(1)}, u32[]{:S(2)}, u32[]{:S(2)}) collective-permute-start(bf16[64,864]{1,0:T(8,128)(2,1)S(1)} %get-tuple-element.50), channel_id=1, source_target_pairs={{0,9},{1,13},{4,8},{5,12},{8,1},{9,5},{12,0},{13,4},{2,11},{3,15},... | collective-permute-start | bytes 331784 | tf_op jit(solution)/shard_map/ppermute | solution.py:433
  56.0 10.7 %collective-permute-start.8 = (bf16[64,864]{1,0:T(8,128)(2,1)S(1)}, bf16[64,864]{1,0:T(8,128)(2,1)S(1)}, u32[]{:S(2)}, u32[]{:S(2)}) collective-permute-start(bf16[64,864]{1,0:T(8,128)(2,1)S(1)} %get-tuple-element.47), channel_id=1, source_target_pairs={{0,0},{1,4},{4,1},{5,5},{8,8},{9,12},{12,9},{13,13},{2,2},{3,6},{6... | collective-permute-start | bytes 331784 | tf_op jit(solution)/shard_map/ppermute | solution.py:433
  56.6 12.6 %collective-permute-start.9 = (bf16[64,864]{1,0:T(8,128)(2,1)S(1)}, bf16[64,864]{1,0:T(8,128)(2,1)S(1)}, u32[]{:S(2)}, u32[]{:S(2)}) collective-permute-start(bf16[64,864]{1,0:T(8,128)(2,1)S(1)} %get-tuple-element.48), channel_id=1, source_target_pairs={{0,1},{1,5},{4,0},{5,4},{8,9},{9,13},{12,8},{13,12},{2,3},{3,7},{6... | collective-permute-start | bytes 331784 | tf_op jit(solution)/shard_map/ppermute | solution.py:433

commit v7 on v6

--- a/solution.py
+++ b/solution.py
@@ -22,6 +22,7 @@
 STEP = 2
 VMEM_LIMIT = 40 * 1024 * 1024
 VMEM = pl.BlockSpec(memory_space=pltpu.VMEM)
+AWAY = pl.BlockSpec(memory_space=pl.ANY)
 SMEM = pl.BlockSpec(memory_space=pltpu.SMEM)
 
 
@@ -117,7 +118,7 @@
     return combined(plane_hops(total, link_ref, back_ref, layer, tile, rows, fetch), total)
 
 
-def open_kernel(vector_ref, link_ref, field_ref, raw_ref, down_ref, up_ref):
+def open_kernel(vector_ref, edge_ref, field_ref, raw_ref, down_ref, up_ref):
     vectors, sites = field_ref.shape[1:]
     tiles, layers = sites // LANES, sites // PLANE
     stride = 6 * tiles
@@ -136,7 +137,8 @@
         for rows in row_groups(field_ref):
             turned = [None] * 6
             source = load(field_ref, rows, lanes_at(layers - 1, tile))
-            add_hop(turned, link_at(link_ref, 0, layers - 1, tile), source, True)
+            link = lambda row, column, part: edge_ref[pl.ds(((3 * row + column) * TILES + tile) * 2 + part, 1), :]
+            add_hop(turned, link, source, True)
             store(up_ref, rows, lanes_at(0, tile), turned)
 
 
@@ -180,8 +182,9 @@
 
 
 def local_kernel(
-    total_x, place_ref, field_ref, link_ref, back_ref, rim_ref, momenta_ref, out_ref, table_ref, one_ref
+    total_x, place_ref, field_ref, link_ref, back_ref, rim_ref, momenta_ref, *refs
 ):
+    out_ref, table_ref, one_ref = refs[-3:]
     layers = field_ref.shape[2] // PLANE
     count = momenta_ref.shape[0]
     momenta = momenta_ref[...].astype(WIDE)
@@ -275,12 +278,30 @@
 
 def product_kernel(columns, count, scale, slot_ref, most_ref, face_ref, table_ref, *refs):
     groups = len(columns)
-    raw_refs, out_refs, (total_ref, left_ref, right_ref) = refs[:groups], refs[groups:-3], refs[-3:]
+    away_refs, out_refs, (total_ref, left_ref, right_ref, held_ref, copied) = refs[:groups], refs[groups:-5], refs[-5:]
+    raw_refs = [held_ref.at[g] for g in range(groups)]
     vectors = most_ref.shape[1]
     layers = most_ref.shape[2] // PLANE
     depth = 6 * LANES
     step = left_ref.shape[1] // depth
+
+    def copies(layer):
+        here = pl.ds(pl.multiple_of(layer * PLANE, PLANE), PLANE)
+        return [
+            pltpu.make_async_copy(away_refs[g].at[:, :, here], held_ref.at[g, :, :, here], copied.at[g, layer])
+            for g in range(groups)
+        ]
+
+    for layer in (*range(1, layers - 1), 0, layers - 1):
+        for copy in copies(layer):
+            copy.start()
     total_ref[...] = jnp.zeros_like(total_ref)
+
+    def ready(layer, block):
+        @pl.when(block % blocks == 0)
+        def _():
+            for copy in copies(layer):
+                copy.wait()
 
     def add(field_ref, place):
         for part in range(step):
@@ -314,12 +335,14 @@
 
     @pl.loop(0, (layers - 2) * blocks)
     def _(block):
+        ready(1 + block // blocks, block)
         add(most_ref, lambda part: (lanes_at(1, block * step + part),) * 2)
 
     @pl.loop(0, 2 * blocks)
     def _(block):
         layer = block // blocks * (layers - 1)
         tile = block % blocks * step
+        ready(layer, block)
         add(face_ref, lambda part: (lanes_at(0, block * step + part), lanes_at(layer, tile + part)))
 
     width = total_ref.shape[0] // groups
@@ -328,11 +351,11 @@
         out_refs[columns[g]][slot_ref[g]] = block.astype(LOW)
 
 
-def call(kernel, name, shapes, operands, flops=0, scratch=(), smem=False):
+def call(kernel, name, shapes, operands, flops=0, scratch=(), smem=False, away=0):
     return pl.pallas_call(
         kernel,
         out_shape=tuple(jax.ShapeDtypeStruct(shape, dtype) for shape, dtype in shapes),
-        in_specs=[SMEM if smem and i == 0 else VMEM for i in range(len(operands))],
+        in_specs=([SMEM] if smem else []) + [VMEM] * (len(operands) - smem - away) + [AWAY] * away,
         out_specs=(VMEM,) * len(shapes),
         scratch_shapes=list(scratch),
         compiler_params=pltpu.CompilerParams(vmem_limit_bytes=VMEM_LIMIT),
@@ -351,17 +374,20 @@
     count = momenta.shape[0]
     brick, vec, sub = (lax.axis_index(axis) for axis in ("brick", "vec", "sub"))
     tiled_vectors = jnp.swapaxes(vectors.reshape((width, 3, 2, tiles, LANES)), 2, 3).reshape((-1, LANES))
-    links = jnp.swapaxes(gauge_links.reshape((27, 2, tiles, LANES)), 1, 2).reshape((-1, LANES))
+    links = jnp.swapaxes(gauge_links.reshape((27, 2, tiles, LANES)), 1, 2)
+    edge = links[:9, tiles - TILES :].reshape((-1, LANES))
+    links = links.reshape((-1, LANES))
     full, face = (6, width, sites), (6, width, PLANE)
     field, raw, down, up = call(
         open_kernel,
         "open",
         ((full, WIDE), (full, LOW), (face, LOW), (face, LOW)),
-        (tiled_vectors, links),
+        (tiled_vectors, edge),
         flops=1 << 22,
     )
     ahead, behind = shifted(down, "brick", -1), shifted(up, "brick", 1)
     across = [shifted(raw, "vec", a) for a in range(1, vecs)]
+    beside = [shifted(raw, "sub", b) for b in range(1, subs)]
     down_two, up_two, rim, back = call(
         rim_kernel,
         "rim",
@@ -375,7 +401,8 @@
         functools.partial(local_kernel, total_x),
         "local",
         ((full, WIDE), ((2, count, sites), WIDE)),
-        (place, field, links, back, rim, momenta),
+        (place, field, links, back, rim, momenta, *beside),
+        away=subs - 1,
         flops=1 << 25,
         scratch=(pltpu.VMEM(full, WIDE),),
         smem=True,
@@ -388,10 +415,10 @@
         flops=1 << 24,
         scratch=(pltpu.VMEM((6, width, 2 * PLANE), WIDE),),
     )
-    late, token = lax.optimization_barrier((raw, token))
     *across, ahead_two, behind_two, token = lax.optimization_barrier((*across, ahead_two, behind_two, token))
-    raws = [raw, *across] + [shifted(array, "sub", b) for b in range(1, subs) for array in (late, *across)]
-    offsets = [(a, b) for b in range(subs) for a in range(vecs)]
+    raws = [raw, *across, *beside] + [shifted(array, "sub", b) for b in range(1, subs) for array in across]
+    offsets = [(a, 0) for a in range(vecs)] + [(0, b) for b in range(1, subs)]
+    offsets += [(a, b) for b in range(1, subs) for a in range(1, vecs)]
     (faces,) = call(
         face_kernel,
         "face",
@@ -409,11 +436,14 @@
         "product",
         (((subs, 2 * width, columns), LOW),) * vecs,
         (slots, most, faces, table, *raws),
+        away=groups,
         flops=1 << 32,
         scratch=(
             pltpu.VMEM((groups * 2 * width, columns), WIDE),
             pltpu.VMEM((groups * 2 * width, depth), LOW),
             pltpu.VMEM((columns, depth), LOW),
+            pltpu.VMEM((groups, *full), LOW),
+            pltpu.SemaphoreType.DMA((groups, layers)),
         ),
         smem=True,
     )

time: 71.5 us -> 72.3 us (1.011)
  local copies, waits for them, and re-layouts: 4.57 us -> 6.48 us
    unnamed x13 -> x15, local copies, waits for them, and re-layouts: 2.53 us -> 3.6 us
    slice x0 -> x1, local copies, waits for them, and re-layouts: none -> 0.84 us  [shards(): edge = links[:9, tiles - TILES:].reshape((-1, LANES))]
  transfers between devices with their start and end apart: 12 -> 12, of which waited for: 5 -> 4; matrix products, arithmetic and copies ran while one was open for 0% -> 0% of each run, Pallas kernels for 23% -> 22%
where the time goes in v7:
time: 72.3 us; the launch traced here: 72 us
  Pallas kernels  30.9 us (43%)
  waiting for transfers between devices  17.2 us (24%)
  starting transfers between devices  17 us (24%)
  local copies, waits for them, and re-layouts  6.48 us (9%)
    pallas_call x6, Pallas kernels, call(): pl.pallas_call(kernel, out_shape=tuple((jax.ShapeDtypeStruct(shape, dtype...  30.9 us
    ppermute x8, starting transfers between devices, shifted(): lax.ppermute(array, axis, [(i, (i + by) % peers) for i in range(peers)])  11 us
    ppermute x8, waiting for transfers between devices, shifted(): lax.ppermute(array, axis, [(i, (i + by) % peers) for i in range(peers)])  9.33 us
    ppermute x4, waiting for transfers between devices, shards(): shares.append(lax.ppermute(block[r], ('brick', 'sub'), pairs))  7.88 us
    ppermute x4, starting transfers between devices, shards(): shares.append(lax.ppermute(block[r], ('brick', 'sub'), pairs))  5.98 us
    unnamed x15, local copies, waits for them, and re-layouts  3.6 us
    transpose x1, local copies, waits for them, and re-layouts, shards(): return jnp.transpose(total.reshape((2, width, count, width)), (1, 2, 0, 3))  1.61 us
  transfers between devices with their start and end apart: 12, of which 4 were waited for; matrix products, arithmetic and copies ran while one was open for 0% of the time, Pallas kernels for 22%

profile of v7, /device:TPU:0, one launch (start us, length us, event | category | flops | bytes accessed | tf_op | source)
XLA Modules:
  0.0 72.0 jit_solution(1192607429483023393)
XLA Ops:
  0.0 0.8 %slice.20 = f32[9,4,2,128]{3,2,1,0:T(2,128)S(1)} slice(f32[27,16,2,128]{3,2,1,0:T(2,128)} %bitcast.23), slice={[0:9], [12:16], [0:2], [0:128]} | slice | bytes 73728 | tf_op jit(solution)/shard_map/slice | solution.py:378
  0.8 1.4 %copy-done.1 = f32[32,3,2,2048]{3,2,1,0:T(2,128)S(1)} copy-done((f32[32,3,2,2048]{3,2,1,0:T(2,128)S(1)}, f32[32,3,2,2048]{3,2,1,0:T(2,128)}, u32[]{:S(2)}) %copy-start.1) | copy-done | bytes 1572888
  2.3 2.2 %open.1 = (f32[6,32,2048]{2,1,0:T(8,128)S(1)}, bf16[6,32,2048]{2,1,0:T(8,128)(2,1)}, bf16[6,32,512]{2,1,0:T(8,128)(2,1)}, bf16[6,32,512]{2,1,0:T(8,128)(2,1)}) custom-call(f32[3072,128]{1,0:T(8,128)S(1)} %bitcast.28, f32[72,128]{1,0:T(8,128)S(1)} %bitcast.29), custom_call_target="tpu_custom_call" | custom-call | flops 4194304 | bytes 1048576 | tf_op jit(solution)/shard_map/open/pallas_call | solution.py:355
  4.4 0.5 collective-permute-start
  4.9 2.5 %collective-permute-start.3 = (bf16[6,32,2048]{2,1,0:T(8,128)(2,1)}, bf16[6,32,2048]{2,1,0:T(8,128)(2,1)}, u32[]{:S(2)}, u32[]{:S(2)}) collective-permute-start(bf16[6,32,2048]{2,1,0:T(8,128)(2,1)} %get-tuple-element.26.refs_0_), channel_id=1, source_target_pairs={{0,2},{2,0},{1,3},{3,1},{4,6},{6,4},{5,7},{7,5},{8,10},{10,8},{9,1... | collective-permute-start | bytes 2359304 | tf_op jit(solution)/shard_map/ppermute | solution.py:31
  7.4 3.6 %collective-permute-start.1 = (bf16[6,32,512]{2,1,0:T(8,128)(2,1)}, bf16[6,32,512]{2,1,0:T(8,128)(2,1)}, u32[]{:S(2)}, u32[]{:S(2)}) collective-permute-start(bf16[6,32,512]{2,1,0:T(8,128)(2,1)} %get-tuple-element.28), channel_id=1, source_target_pairs={{0,12},{4,0},{8,4},{12,8},{1,13},{5,1},{9,5},{13,9},{2,14},{6,2},{... | collective-permute-start | bytes 589832 | tf_op jit(solution)/shard_map/ppermute | solution.py:31
  11.0 3.4 %rim.1 = (bf16[6,32,512]{2,1,0:T(8,128)(2,1)}, bf16[6,32,512]{2,1,0:T(8,128)(2,1)}, f32[6,32,1024]{2,1,0:T(8,128)S(1)}, f32[2,16,2048]{2,1,0:T(8,128)S(1)}) custom-call(f32[6,32,2048]{2,1,0:T(8,128)S(1)} %get-tuple-element.23.field_ref, f32[864,128]{1,0:T(8,128)S(1)} %bitcast.24), custom_call_target="tpu_custom_call" | custom-call | flops 16777216 | bytes 1048576 | tf_op jit(solution)/shard_map/rim/pallas_call | solution.py:355
  14.4 0.9 %copy-done.2 = f32[6,32,1024]{2,1,0:T(8,128)} copy-done((f32[6,32,1024]{2,1,0:T(8,128)}, f32[6,32,1024]{2,1,0:T(8,128)S(1)}, u32[]{:S(2)}) %copy-start.2) | copy-done | bytes 786456
  15.3 3.8 %collective-permute-start.4 = (bf16[6,32,512]{2,1,0:T(8,128)(2,1)}, bf16[6,32,512]{2,1,0:T(8,128)(2,1)S(1)}, u32[]{:S(2)}, u32[]{:S(2)}) collective-permute-start(bf16[6,32,512]{2,1,0:T(8,128)(2,1)} %get-tuple-element.31), channel_id=1, source_target_pairs={{0,12},{4,0},{8,4},{12,8},{1,13},{5,1},{9,5},{13,9},{2,14},{6,2},{... | collective-permute-start | bytes 589832 | tf_op jit(solution)/shard_map/ppermute | solution.py:31
  19.3 1.1 %copy-done.3 = f32[6,32,1024]{2,1,0:T(8,128)S(1)} copy-done((f32[6,32,1024]{2,1,0:T(8,128)S(1)}, f32[6,32,1024]{2,1,0:T(8,128)}, u32[]{:S(2)}) %copy-start.3) | copy-done | bytes 786456
  20.4 8.3 %local.1 = (f32[6,32,2048]{2,1,0:T(8,128)S(1)}, f32[2,27,2048]{2,1,0:T(8,128)S(1)}) custom-call(s32[1]{0:T(128)} %bitcast.2.place_ref, f32[6,32,2048]{2,1,0:T(8,128)S(1)} %get-tuple-element.23.field_ref, f32[864,128]{1,0:T(8,128)S(1)} %bitcast.25, f32[2,16,2048]{2,1,0:T(8,128)S(1)} %get-tuple-element.24.back_ref, f32[6,32,1024]{2,1,0:T(8,128)S(1)} %copy-done.3, ...), custom_call_target="tpu_custom_call" | custom-call | flops 33554432 | bytes 1048576 | tf_op jit(solution)/shard_map/local/pallas_call | solution.py:355
  28.7 4.1 %close.1 = (f32[6,32,2048]{2,1,0:T(8,128)S(1)}, f32[8,128]{1,0:T(8,128)S(1)}) custom-call(f32[6,32,2048]{2,1,0:T(8,128)S(1)} %get-tuple-element.27.part_ref, bf16[6,32,512]{2,1,0:T(8,128)(2,1)} %collective-permute-done.1.ahead_ref, bf16[6,32,512]{2,1,0:T(8,128)(2,1)} %collective-permute-done.2.behind_ref, f32[864,128]{1,0:T(8,128)S(1)} %bitcast.26, ...), custom_call_target="tpu_custom_call" | custom-call | flops 16777216 | bytes 1048576 | tf_op jit(solution)/shard_map/close/pallas_call | solution.py:355
  33.1 0.3 face.1.face_ref
  33.3 2.2 %collective-permute-done.6.refs_3_ = bf16[6,32,2048]{2,1,0:T(8,128)(2,1)} collective-permute-done((bf16[6,32,2048]{2,1,0:T(8,128)(2,1)}, bf16[6,32,2048]{2,1,0:T(8,128)(2,1)}, u32[]{:S(2)}, u32[]{:S(2)}) %collective-permute-start.6) | collective-permute-done | bytes 786464 | tf_op jit(solution)/shard_map/ppermute | solution.py:31
  35.5 12.7 %product.1 = (bf16[2,64,864]{2,1,0:T(8,128)(2,1)S(1)}, bf16[2,64,864]{2,1,0:T(8,128)(2,1)S(1)}) custom-call(s32[4]{0:T(128)S(1)} %pad_add_fusion.slot_ref, f32[6,32,2048]{2,1,0:T(8,128)S(1)} %get-tuple-element.30.most_ref, f32[6,32,1024]{2,1,0:T(8,128)S(1)} %face.1.face_ref, f32[2,27,2048]{2,1,0:T(8,128)S(1)} %copy-done.5, ...), custom_call_target="tpu_custom_call" | custom-call | flops 4294967296 | bytes 1048576 | tf_op jit(solution)/shard_map/product/pallas_call | solution.py:355
  48.3 0.6 collective-permute-start.7
  48.9 7.1 %collective-permute-done.7 = bf16[2,64,864]{2,1,0:T(8,128)(2,1)S(1)} collective-permute-done((bf16[2,64,864]{2,1,0:T(8,128)(2,1)S(1)}, bf16[2,64,864]{2,1,0:T(8,128)(2,1)S(1)}, u32[]{:S(2)}, u32[]{:S(2)}) %collective-permute-start.7) | collective-permute-done | bytes 221216 | tf_op jit(solution)/shard_map/ppermute | solution.py:31
  56.1 0.6 collective-permute-start.10
  56.7 0.7 collective-permute-start.8
  57.4 4.7 %collective-permute-start.9 = (bf16[64,864]{1,0:T(8,128)(2,1)S(1)}, bf16[64,864]{1,0:T(8,128)(2,1)S(1)}, u32[]{:S(2)}, u32[]{:S(2)}) collective-permute-start(bf16[64,864]{1,0:T(8,128)(2,1)S(1)} %get-tuple-element.44), channel_id=1, source_target_pairs={{0,1},{1,5},{4,0},{5,4},{8,9},{9,13},{12,8},{13,12},{2,3},{3,7},{6... | collective-permute-start | bytes 331784 | tf_op jit(solution)/shard_map/ppermute | solution.py:463
  62.1 5.3 %collective-permute-done.10 = bf16[64,864]{1,0:T(8,128)(2,1)S(1)} collective-permute-done((bf16[64,864]{1,0:T(8,128)(2,1)S(1)}, bf16[64,864]{1,0:T(8,128)(2,1)S(1)}, u32[]{:S(2)}, u32[]{:S(2)}) %collective-permute-start.10) | collective-permute-done | bytes 110624 | tf_op jit(solution)/shard_map/ppermute | solution.py:463
  67.4 2.6 %collective-permute-done.9 = bf16[64,864]{1,0:T(8,128)(2,1)S(1)} collective-permute-done((bf16[64,864]{1,0:T(8,128)(2,1)S(1)}, bf16[64,864]{1,0:T(8,128)(2,1)S(1)}, u32[]{:S(2)}, u32[]{:S(2)}) %collective-permute-start.9) | collective-permute-done | bytes 110624 | tf_op jit(solution)/shard_map/ppermute | solution.py:463
  70.0 0.4 reshape.27
  70.4 1.6 %copy.11 = f32[32,27,2,32]{3,2,1,0:T(2,128)} copy(f32[32,27,2,32]{3,1,0,2:T(8,128)S(1)} %bitcast.30) | data formatting | bytes 442368 | tf_op jit(solution)/shard_map/transpose | solution.py:465
  (29 shorter events, 0.4 us)
Async XLA Ops:
  0.0 11.0 %copy-start = (f32[3,3,3,2,2048]{4,3,2,1,0:T(2,128)S(1)}, f32[3,3,3,2,2048]{4,3,2,1,0:T(2,128)}, u32[]{:S(2)}) copy-start(f32[3,3,3,2,2048]{4,3,2,1,0:T(2,128)} %param.4) | copy-start | bytes 1327108
  0.8 1.4 %copy-start.1 = (f32[32,3,2,2048]{3,2,1,0:T(2,128)S(1)}, f32[32,3,2,2048]{3,2,1,0:T(2,128)}, u32[]{:S(2)}) copy-start(f32[32,3,2,2048]{3,2,1,0:T(2,128)} %param.3) | copy-start | bytes 4718596
  2.3 16.9 %copy-start.6 = (s32[27,3]{0,1:T(4,128)S(1)}, s32[27,3]{0,1:T(4,128)}, u32[]{:S(2)}) copy-start(s32[27,3]{0,1:T(4,128)} %param.5) | copy-start | bytes 976
  4.4 14.7 %collective-permute-start = (bf16[6,32,2048]{2,1,0:T(8,128)(2,1)}, bf16[6,32,2048]{2,1,0:T(8,128)(2,1)S(1)}, u32[]{:S(2)}, u32[]{:S(2)}) collective-permute-start(bf16[6,32,2048]{2,1,0:T(8,128)(2,1)} %get-tuple-element.26.refs_0_), channel_id=1, source_target_pairs={{0,1},{1,0},{2,3},{3,2},{4,5},{5,4},{6,7},{7,6},{8,9},{9,8},{10,11... | collective-permute-start | bytes 2359304 | tf_op jit(solution)/shard_map/ppermute | solution.py:31
  4.9 27.9 %collective-permute-start.3 = (bf16[6,32,2048]{2,1,0:T(8,128)(2,1)}, bf16[6,32,2048]{2,1,0:T(8,128)(2,1)}, u32[]{:S(2)}, u32[]{:S(2)}) collective-permute-start(bf16[6,32,2048]{2,1,0:T(8,128)(2,1)} %get-tuple-element.26.refs_0_), channel_id=1, source_target_pairs={{0,2},{2,0},{1,3},{3,1},{4,6},{6,4},{5,7},{7,5},{8,10},{10,8},{9,1... | collective-permute-start | bytes 2359304 | tf_op jit(solution)/shard_map/ppermute | solution.py:31
  7.4 21.3 %collective-permute-start.1 = (bf16[6,32,512]{2,1,0:T(8,128)(2,1)}, bf16[6,32,512]{2,1,0:T(8,128)(2,1)}, u32[]{:S(2)}, u32[]{:S(2)}) collective-permute-start(bf16[6,32,512]{2,1,0:T(8,128)(2,1)} %get-tuple-element.28), channel_id=1, source_target_pairs={{0,12},{4,0},{8,4},{12,8},{1,13},{5,1},{9,5},{13,9},{2,14},{6,2},{... | collective-permute-start | bytes 589832 | tf_op jit(solution)/shard_map/ppermute | solution.py:31
  11.0 17.7 %collective-permute-start.2 = (bf16[6,32,512]{2,1,0:T(8,128)(2,1)}, bf16[6,32,512]{2,1,0:T(8,128)(2,1)}, u32[]{:S(2)}, u32[]{:S(2)}) collective-permute-start(bf16[6,32,512]{2,1,0:T(8,128)(2,1)} %get-tuple-element.29), channel_id=1, source_target_pairs={{0,4},{4,8},{8,12},{12,0},{1,5},{5,9},{9,13},{13,1},{2,6},{6,10},{... | collective-permute-start | bytes 589832 | tf_op jit(solution)/shard_map/ppermute | solution.py:31
  14.4 0.9 %copy-start.2 = (f32[6,32,1024]{2,1,0:T(8,128)}, f32[6,32,1024]{2,1,0:T(8,128)S(1)}, u32[]{:S(2)}) copy-start(f32[6,32,1024]{2,1,0:T(8,128)S(1)} %get-tuple-element.25.rim_ref) | copy-start | bytes 2359300
  15.3 17.5 %collective-permute-start.4 = (bf16[6,32,512]{2,1,0:T(8,128)(2,1)}, bf16[6,32,512]{2,1,0:T(8,128)(2,1)S(1)}, u32[]{:S(2)}, u32[]{:S(2)}) collective-permute-start(bf16[6,32,512]{2,1,0:T(8,128)(2,1)} %get-tuple-element.31), channel_id=1, source_target_pairs={{0,12},{4,0},{8,4},{12,8},{1,13},{5,1},{9,5},{13,9},{2,14},{6,2},{... | collective-permute-start | bytes 589832 | tf_op jit(solution)/shard_map/ppermute | solution.py:31
  19.1 13.7 %collective-permute-start.5 = (bf16[6,32,512]{2,1,0:T(8,128)(2,1)}, bf16[6,32,512]{2,1,0:T(8,128)(2,1)S(1)}, u32[]{:S(2)}, u32[]{:S(2)}) collective-permute-start(bf16[6,32,512]{2,1,0:T(8,128)(2,1)} %get-tuple-element.32), channel_id=1, source_target_pairs={{0,4},{4,8},{8,12},{12,0},{1,5},{5,9},{9,13},{13,1},{2,6},{6,10},{... | collective-permute-start | bytes 589832 | tf_op jit(solution)/shard_map/ppermute | solution.py:31
  19.3 1.1 %copy-start.3 = (f32[6,32,1024]{2,1,0:T(8,128)S(1)}, f32[6,32,1024]{2,1,0:T(8,128)}, u32[]{:S(2)}) copy-start(f32[6,32,1024]{2,1,0:T(8,128)} %copy-done.2) | copy-start | bytes 2359300
  28.6 4.2 %copy-start.4 = (f32[2,27,2048]{2,1,0:T(8,128)}, f32[2,27,2048]{2,1,0:T(8,128)S(1)}, u32[]{:S(2)}) copy-start(f32[2,27,2048]{2,1,0:T(8,128)S(1)} %get-tuple-element.37.table_ref) | copy-start | bytes 1327108
  32.8 2.7 %collective-permute-start.6 = (bf16[6,32,2048]{2,1,0:T(8,128)(2,1)}, bf16[6,32,2048]{2,1,0:T(8,128)(2,1)}, u32[]{:S(2)}, u32[]{:S(2)}) collective-permute-start(bf16[6,32,2048]{2,1,0:T(8,128)(2,1)} %collective-permute-done.3.refs_1_), channel_id=1, source_target_pairs={{0,1},{1,0},{2,3},{3,2},{4,5},{5,4},{6,7},{7,6},{8,9},{9,8},{10,11... | collective-permute-start | bytes 2359304 | tf_op jit(solution)/shard_map/ppermute | solution.py:31
  33.1 2.5 %copy-start.5 = (f32[2,27,2048]{2,1,0:T(8,128)S(1)}, f32[2,27,2048]{2,1,0:T(8,128)}, u32[]{:S(2)}) copy-start(f32[2,27,2048]{2,1,0:T(8,128)} %copy-done.4) | copy-start | bytes 1327108
  48.3 7.7 %collective-permute-start.7 = (bf16[2,64,864]{2,1,0:T(8,128)(2,1)S(1)}, bf16[2,64,864]{2,1,0:T(8,128)(2,1)S(1)}, u32[]{:S(2)}, u32[]{:S(2)}) collective-permute-start(bf16[2,64,864]{2,1,0:T(8,128)(2,1)S(1)} %get-tuple-element.39), channel_id=1, source_target_pairs={{0,2},{2,0},{1,3},{3,1},{4,6},{6,4},{5,7},{7,5},{8,10},{10,8},{9,1... | collective-permute-start | bytes 663560 | tf_op jit(solution)/shard_map/ppermute | solution.py:31
  56.1 11.3 %collective-permute-start.10 = (bf16[64,864]{1,0:T(8,128)(2,1)S(1)}, bf16[64,864]{1,0:T(8,128)(2,1)S(1)}, u32[]{:S(2)}, u32[]{:S(2)}) collective-permute-start(bf16[64,864]{1,0:T(8,128)(2,1)S(1)} %get-tuple-element.45), channel_id=1, source_target_pairs={{0,8},{1,12},{4,9},{5,13},{8,0},{9,4},{12,1},{13,5},{2,10},{3,14},... | collective-permute-start | bytes 331784 | tf_op jit(solution)/shard_map/ppermute | solution.py:463
  56.7 10.7 %collective-permute-start.11 = (bf16[64,864]{1,0:T(8,128)(2,1)S(1)}, bf16[64,864]{1,0:T(8,128)(2,1)S(1)}, u32[]{:S(2)}, u32[]{:S(2)}) collective-permute-start(bf16[64,864]{1,0:T(8,128)(2,1)S(1)} %get-tuple-element.46), channel_id=1, source_target_pairs={{0,9},{1,13},{4,8},{5,12},{8,1},{9,5},{12,0},{13,4},{2,11},{3,15},... | collective-permute-start | bytes 331784 | tf_op jit(solution)/shard_map/ppermute | solution.py:463
  56.7 10.7 %collective-permute-start.8 = (bf16[64,864]{1,0:T(8,128)(2,1)S(1)}, bf16[64,864]{1,0:T(8,128)(2,1)S(1)}, u32[]{:S(2)}, u32[]{:S(2)}) collective-permute-start(bf16[64,864]{1,0:T(8,128)(2,1)S(1)} %get-tuple-element.43), channel_id=1, source_target_pairs={{0,0},{1,4},{4,1},{5,5},{8,8},{9,12},{12,9},{13,13},{2,2},{3,6},{6... | collective-permute-start | bytes 331784 | tf_op jit(solution)/shard_map/ppermute | solution.py:463
  57.4 12.6 %collective-permute-start.9 = (bf16[64,864]{1,0:T(8,128)(2,1)S(1)}, bf16[64,864]{1,0:T(8,128)(2,1)S(1)}, u32[]{:S(2)}, u32[]{:S(2)}) collective-permute-start(bf16[64,864]{1,0:T(8,128)(2,1)S(1)} %get-tuple-element.44), channel_id=1, source_target_pairs={{0,1},{1,5},{4,0},{5,4},{8,9},{9,13},{12,8},{13,12},{2,3},{3,7},{6... | collective-permute-start | bytes 331784 | tf_op jit(solution)/shard_map/ppermute | solution.py:463

commit v8 on v7

--- a/solution.py
+++ b/solution.py
@@ -276,7 +276,7 @@
             store(out_ref, rows, high, [a + KAPPA * b for a, b in new])
 
 
-def product_kernel(columns, count, scale, slot_ref, most_ref, face_ref, table_ref, *refs):
+def product_kernel(columns, begin, count, scale, slot_ref, most_ref, face_ref, table_ref, *refs):
     groups = len(columns)
     away_refs, out_refs, (total_ref, left_ref, right_ref, held_ref, copied) = refs[:groups], refs[groups:-5], refs[-5:]
     raw_refs = [held_ref.at[g] for g in range(groups)]
@@ -310,8 +310,8 @@
             one = [pl.ds(part * depth + 2 * color * LANES, LANES) for color in range(3)]
             two = [pl.ds(part * depth + (2 * color + 1) * LANES, LANES) for color in range(3)]
             for p in range(count):
-                cosine = table_ref[0, pl.ds(p, 1), lanes]
-                sine = table_ref[1, pl.ds(p, 1), lanes]
+                cosine = table_ref[0, pl.ds(begin + p, 1), lanes]
+                sine = table_ref[1, pl.ds(begin + p, 1), lanes]
                 rows = pl.ds(p * vectors, vectors)
                 for color in range(3):
                     real, imag = field[2 * color], field[2 * color + 1]
@@ -387,7 +387,6 @@
     )
     ahead, behind = shifted(down, "brick", -1), shifted(up, "brick", 1)
     across = [shifted(raw, "vec", a) for a in range(1, vecs)]
-    beside = [shifted(raw, "sub", b) for b in range(1, subs)]
     down_two, up_two, rim, back = call(
         rim_kernel,
         "rim",
@@ -401,8 +400,7 @@
         functools.partial(local_kernel, total_x),
         "local",
         ((full, WIDE), ((2, count, sites), WIDE)),
-        (place, field, links, back, rim, momenta, *beside),
-        away=subs - 1,
+        (place, field, links, back, rim, momenta),
         flops=1 << 25,
         scratch=(pltpu.VMEM(full, WIDE),),
         smem=True,
@@ -415,10 +413,10 @@
         flops=1 << 24,
         scratch=(pltpu.VMEM((6, width, 2 * PLANE), WIDE),),
     )
+    late, token = lax.optimization_barrier((raw, token))
     *across, ahead_two, behind_two, token = lax.optimization_barrier((*across, ahead_two, behind_two, token))
-    raws = [raw, *across, *beside] + [shifted(array, "sub", b) for b in range(1, subs) for array in across]
-    offsets = [(a, 0) for a in range(vecs)] + [(0, b) for b in range(1, subs)]
-    offsets += [(a, b) for b in range(1, subs) for a in range(1, vecs)]
+    raws = [raw, *across] + [shifted(array, "sub", b) for b in range(1, subs) for array in (late, *across)]
+    offsets = [(a, b) for b in range(subs) for a in range(vecs)]
     (faces,) = call(
         face_kernel,
         "face",
@@ -430,39 +428,50 @@
     slots = jnp.stack([(sub - b - brick_sub) % subs for a, b in offsets]).astype(jnp.int32)
     scale = (3.0 * total_x * PLANE) ** (-0.5)
     depth = STEP * 6 * LANES
-    columns = count * width
-    blocks = call(
-        functools.partial(product_kernel, [-a % vecs for a, b in offsets], count, scale),
-        "product",
-        (((subs, 2 * width, columns), LOW),) * vecs,
-        (slots, most, faces, table, *raws),
-        away=groups,
-        flops=1 << 32,
-        scratch=(
-            pltpu.VMEM((groups * 2 * width, columns), WIDE),
-            pltpu.VMEM((groups * 2 * width, depth), LOW),
-            pltpu.VMEM((columns, depth), LOW),
-            pltpu.VMEM((groups, *full), LOW),
-            pltpu.SemaphoreType.DMA((groups, layers)),
-        ),
-        smem=True,
-    )
-    held = [shifted(block, "vec", a) if a else block for a, block in enumerate(blocks)]
-    shares = []
-    for q in range(vecs):
-        place = (vec - brick_vec - q) % vecs
-        block = held[0]
-        for a in range(1, vecs):
-            block = jnp.where(place == a, held[a], block)
-        for r in range(subs):
-            pairs = [
-                (b * subs + s, ((b // subs + q) % vecs * subs + s) * subs + (b % subs + r) % subs)
-                for b in range(bricks)
-                for s in range(subs)
-            ]
-            shares.append(lax.ppermute(block[r], ("brick", "sub"), pairs))
-    total = functools.reduce(jnp.add, [share.astype(WIDE) for share in shares])
-    return jnp.transpose(total.reshape((2, width, count, width)), (1, 2, 0, 3))
+    unit = max(1, 2 * LANES // width)
+    middle = unit * round(0.6 * count / unit) if unit < count else count // 2
+    chunks = []
+    for begin, end in ((0, middle), (middle, count)):
+        columns = (end - begin) * width
+        blocks = call(
+            functools.partial(product_kernel, [-a % vecs for a, b in offsets], begin, end - begin, scale),
+            "product",
+            (((subs, 2 * width, columns), LOW),) * vecs,
+            (slots, most, faces, table, *raws),
+            away=groups,
+            flops=1 << 31,
+            scratch=(
+                pltpu.VMEM((groups * 2 * width, columns), WIDE),
+                pltpu.VMEM((groups * 2 * width, depth), LOW),
+                pltpu.VMEM((columns, depth), LOW),
+                pltpu.VMEM((groups, *full), LOW),
+                pltpu.SemaphoreType.DMA((groups, layers)),
+            ),
+            smem=True,
+        )
+        chunks.append([blocks[0], *(shifted(block, "vec", a) for a, block in enumerate(blocks) if a)])
+    (*held, chunks[1][0]) = lax.optimization_barrier((*chunks[0], chunks[1][0]))
+    chunks[0] = held
+    totals = []
+    for held, size in zip(chunks, (middle, count - middle)):
+        shares = []
+        for q in range(vecs):
+            place = (vec - brick_vec - q) % vecs
+            block = held[0]
+            for a in range(1, vecs):
+                block = jnp.where(place == a, held[a], block)
+            for r in range(subs):
+                pairs = [
+                    (b * subs + s, ((b // subs + q) % vecs * subs + s) * subs + (b % subs + r) % subs)
+                    for b in range(bricks)
+                    for s in range(subs)
+                ]
+                shares.append(lax.ppermute(block[r], ("brick", "sub"), pairs))
+        if held is chunks[0]:
+            *shares, chunks[1][0] = lax.optimization_barrier((*shares, chunks[1][0]))
+        total = functools.reduce(jnp.add, [share.astype(WIDE) for share in shares])
+        totals.append(total.reshape((2, width, size, width)))
+    return jnp.transpose(jnp.concatenate(totals, axis=2), (1, 2, 0, 3))
 
 
 def solution(mesh):

time: 72.3 us -> 75.7 us (1.047)
  starting transfers between devices: 17 us -> 23.1 us
  waiting for transfers between devices: 17.2 us -> 12.3 us
  Pallas kernels: 30.9 us -> 34.8 us
  local copies, waits for them, and re-layouts: 6.48 us -> 3.4 us
  other arithmetic: 0.18 us -> 1.56 us
    ppermute x8 -> x9, waiting for transfers between devices: 9.33 us -> 2.81 us  [shifted(): lax.ppermute(array, axis, [(i, (i + by) % peers) for i in range(peers)])]
    ppermute x4 -> x8, starting transfers between devices: 5.98 us -> 9.98 us  [shards(): shares.append(lax.ppermute(block[r], ('brick', 'sub'), pairs))]
    pallas_call x6 -> x7, Pallas kernels: 30.9 us -> 34.8 us  [call(): pl.pallas_call(kernel, out_shape=tuple((jax.ShapeDtypeStruct(shape, dtype...]
    ppermute x8 -> x9, starting transfers between devices: 11 us -> 13.1 us  [shifted(): lax.ppermute(array, axis, [(i, (i + by) % peers) for i in range(peers)])]
    unnamed x15 -> x11, local copies, waits for them, and re-layouts: 3.6 us -> 1.52 us
    ppermute x4 -> x8, waiting for transfers between devices: 7.88 us -> 9.53 us  [shards(): shares.append(lax.ppermute(block[r], ('brick', 'sub'), pairs))]
    transpose x1 -> x0, local copies, waits for them, and re-layouts: 1.61 us -> none  [shards(): return jnp.transpose(total.reshape((2, width, count, width)), (1, 2, 0, 3))]
    transpose x0 -> x1, other arithmetic: none -> 1.37 us  [shards(): return jnp.transpose(jnp.concatenate(totals, axis=2), (1, 2, 0, 3))]
  transfers between devices with their start and end apart: 12 -> 17, of which waited for: 4 -> 7; matrix products, arithmetic and copies ran while one was open for 0% -> 1% of each run, Pallas kernels for 22% -> 31%
where the time goes in v8:
time: 75.7 us; the launch traced here: 75.5 us
  Pallas kernels  34.8 us (46%)
  starting transfers between devices  23.1 us (31%)
  waiting for transfers between devices  12.3 us (16%)
  local copies, waits for them, and re-layouts  3.4 us (4%)
  other arithmetic  1.56 us (2%)
    pallas_call x7, Pallas kernels, call(): pl.pallas_call(kernel, out_shape=tuple((jax.ShapeDtypeStruct(shape, dtype...  34.8 us
    ppermute x9, starting transfers between devices, shifted(): lax.ppermute(array, axis, [(i, (i + by) % peers) for i in range(peers)])  13.1 us
    ppermute x8, starting transfers between devices, shards(): shares.append(lax.ppermute(block[r], ('brick', 'sub'), pairs))  9.98 us
    ppermute x8, waiting for transfers between devices, shards(): shares.append(lax.ppermute(block[r], ('brick', 'sub'), pairs))  9.53 us
    ppermute x9, waiting for transfers between devices, shifted(): lax.ppermute(array, axis, [(i, (i + by) % peers) for i in range(peers)])  2.81 us
    unnamed x11, local copies, waits for them, and re-layouts  1.52 us
  transfers between devices with their start and end apart: 17, of which 7 were waited for; matrix products, arithmetic and copies ran while one was open for 1% of the time, Pallas kernels for 31%

profile of v8, /device:TPU:0, one launch (start us, length us, event | category | flops | bytes accessed | tf_op | source)
XLA Modules:
  0.0 75.5 jit_solution(7392665122148487549)
XLA Ops:
  0.0 0.8 %slice.36 = f32[9,4,2,128]{3,2,1,0:T(2,128)S(1)} slice(f32[27,16,2,128]{3,2,1,0:T(2,128)} %bitcast.32), slice={[0:9], [12:16], [0:2], [0:128]} | slice | bytes 73728 | tf_op jit(solution)/shard_map/slice | solution.py:378
  0.8 1.4 %copy-done.1 = f32[32,3,2,2048]{3,2,1,0:T(2,128)S(1)} copy-done((f32[32,3,2,2048]{3,2,1,0:T(2,128)S(1)}, f32[32,3,2,2048]{3,2,1,0:T(2,128)}, u32[]{:S(2)}) %copy-start.1) | copy-done | bytes 1572888
  2.3 2.2 %open.1 = (f32[6,32,2048]{2,1,0:T(8,128)S(1)}, bf16[6,32,2048]{2,1,0:T(8,128)(2,1)}, bf16[6,32,512]{2,1,0:T(8,128)(2,1)}, bf16[6,32,512]{2,1,0:T(8,128)(2,1)}) custom-call(f32[3072,128]{1,0:T(8,128)S(1)} %bitcast.37, f32[72,128]{1,0:T(8,128)S(1)} %bitcast.38), custom_call_target="tpu_custom_call" | custom-call | flops 4194304 | bytes 1048576 | tf_op jit(solution)/shard_map/open/pallas_call | solution.py:355
  4.4 2.9 %collective-permute-start.2 = (bf16[6,32,2048]{2,1,0:T(8,128)(2,1)}, bf16[6,32,2048]{2,1,0:T(8,128)(2,1)}, u32[]{:S(2)}, u32[]{:S(2)}) collective-permute-start(bf16[6,32,2048]{2,1,0:T(8,128)(2,1)} %get-tuple-element.52.refs_0_), channel_id=1, source_target_pairs={{0,2},{2,0},{1,3},{3,1},{4,6},{6,4},{5,7},{7,5},{8,10},{10,8},{9,1... | collective-permute-start | bytes 2359304 | tf_op jit(solution)/shard_map/ppermute | solution.py:31
  7.4 3.6 %collective-permute-start = (bf16[6,32,512]{2,1,0:T(8,128)(2,1)}, bf16[6,32,512]{2,1,0:T(8,128)(2,1)}, u32[]{:S(2)}, u32[]{:S(2)}) collective-permute-start(bf16[6,32,512]{2,1,0:T(8,128)(2,1)} %get-tuple-element.39), channel_id=1, source_target_pairs={{0,12},{4,0},{8,4},{12,8},{1,13},{5,1},{9,5},{13,9},{2,14},{6,2},{... | collective-permute-start | bytes 589832 | tf_op jit(solution)/shard_map/ppermute | solution.py:31
  11.0 3.4 %rim.1 = (bf16[6,32,512]{2,1,0:T(8,128)(2,1)}, bf16[6,32,512]{2,1,0:T(8,128)(2,1)}, f32[6,32,1024]{2,1,0:T(8,128)S(1)}, f32[2,16,2048]{2,1,0:T(8,128)S(1)}) custom-call(f32[6,32,2048]{2,1,0:T(8,128)S(1)} %get-tuple-element.35.field_ref, f32[864,128]{1,0:T(8,128)S(1)} %bitcast.33), custom_call_target="tpu_custom_call" | custom-call | flops 16777216 | bytes 1048576 | tf_op jit(solution)/shard_map/rim/pallas_call | solution.py:355
  14.4 3.8 %collective-permute-start.3 = (bf16[6,32,512]{2,1,0:T(8,128)(2,1)}, bf16[6,32,512]{2,1,0:T(8,128)(2,1)S(1)}, u32[]{:S(2)}, u32[]{:S(2)}) collective-permute-start(bf16[6,32,512]{2,1,0:T(8,128)(2,1)} %get-tuple-element.43), channel_id=1, source_target_pairs={{0,12},{4,0},{8,4},{12,8},{1,13},{5,1},{9,5},{13,9},{2,14},{6,2},{... | collective-permute-start | bytes 589832 | tf_op jit(solution)/shard_map/ppermute | solution.py:31
  18.3 8.3 %local.1 = (f32[6,32,2048]{2,1,0:T(8,128)S(1)}, f32[2,27,2048]{2,1,0:T(8,128)S(1)}) custom-call(s32[1]{0:T(128)} %bitcast.2.place_ref, f32[6,32,2048]{2,1,0:T(8,128)S(1)} %get-tuple-element.35.field_ref, f32[864,128]{1,0:T(8,128)S(1)} %bitcast.34, f32[2,16,2048]{2,1,0:T(8,128)S(1)} %get-tuple-element.36.back_ref, ...), custom_call_target="tpu_custom_call" | custom-call | flops 33554432 | bytes 1048576 | tf_op jit(solution)/shard_map/local/pallas_call | solution.py:355
  26.6 4.1 %close.1 = (f32[6,32,2048]{2,1,0:T(8,128)S(1)}, f32[8,128]{1,0:T(8,128)S(1)}) custom-call(f32[6,32,2048]{2,1,0:T(8,128)S(1)} %get-tuple-element.38.part_ref, bf16[6,32,512]{2,1,0:T(8,128)(2,1)} %collective-permute-done.ahead_ref, bf16[6,32,512]{2,1,0:T(8,128)(2,1)} %collective-permute-done.1.behind_ref, f32[864,128]{1,0:T(8,128)S(1)} %bitcast.35, ...), custom_call_target="tpu_custom_call" | custom-call | flops 16777216 | bytes 1048576 | tf_op jit(solution)/shard_map/close/pallas_call | solution.py:355
  31.7 1.7 %collective-permute-done.5.refs_2_ = bf16[6,32,2048]{2,1,0:T(8,128)(2,1)} collective-permute-done((bf16[6,32,2048]{2,1,0:T(8,128)(2,1)}, bf16[6,32,2048]{2,1,0:T(8,128)(2,1)}, u32[]{:S(2)}, u32[]{:S(2)}) %collective-permute-start.5) | collective-permute-done | bytes 786464 | tf_op jit(solution)/shard_map/ppermute | solution.py:31
  33.4 1.1 %collective-permute-done.6.refs_3_ = bf16[6,32,2048]{2,1,0:T(8,128)(2,1)} collective-permute-done((bf16[6,32,2048]{2,1,0:T(8,128)(2,1)}, bf16[6,32,2048]{2,1,0:T(8,128)(2,1)}, u32[]{:S(2)}, u32[]{:S(2)}) %collective-permute-start.6) | collective-permute-done | bytes 786464 | tf_op jit(solution)/shard_map/ppermute | solution.py:31
  34.5 9.1 %product.2 = (bf16[2,64,512]{2,1,0:T(8,128)(2,1)S(1)}, bf16[2,64,512]{2,1,0:T(8,128)(2,1)S(1)}) custom-call(s32[4]{0:T(128)S(1)} %pad_add_fusion.slot_ref, f32[6,32,2048]{2,1,0:T(8,128)S(1)} %get-tuple-element.41.most_ref, f32[6,32,1024]{2,1,0:T(8,128)S(1)} %face.1.face_ref, f32[2,27,2048]{2,1,0:T(8,128)S(1)} %copy-done.3, ...), custom_call_target="tpu_custom_call" | custom-call | flops 2147483648 | bytes 1048576 | tf_op jit(solution)/shard_map/product/pallas_call | solution.py:355
  44.2 7.5 %product.3 = (bf16[2,64,352]{2,1,0:T(8,128)(2,1)S(1)}, bf16[2,64,352]{2,1,0:T(8,128)(2,1)S(1)}) custom-call(s32[4]{0:T(128)S(1)} %pad_add_fusion.slot_ref, f32[6,32,2048]{2,1,0:T(8,128)S(1)} %get-tuple-element.41.most_ref, f32[6,32,1024]{2,1,0:T(8,128)S(1)} %face.1.face_ref, f32[2,27,2048]{2,1,0:T(8,128)S(1)} %copy-done.3, ...), custom_call_target="tpu_custom_call" | custom-call | flops 2147483648 | bytes 1048576 | tf_op jit(solution)/shard_map/product/pallas_call | solution.py:355
  51.8 1.6 %collective-permute-start.12 = (bf16[2,64,352]{2,1,0:T(8,128)(2,1)S(1)}, bf16[2,64,352]{2,1,0:T(8,128)(2,1)S(1)}, u32[]{:S(2)}, u32[]{:S(2)}) collective-permute-start(bf16[2,64,352]{2,1,0:T(8,128)(2,1)S(1)} %get-tuple-element.63), channel_id=1, source_target_pairs={{0,2},{2,0},{1,3},{3,1},{4,6},{6,4},{5,7},{7,5},{8,10},{10,8},{9,1... | collective-permute-start | bytes 270344 | tf_op jit(solution)/shard_map/ppermute | solution.py:31
  54.0 0.7 collective-permute-start.8
  54.7 4.7 %collective-permute-start.9 = (bf16[64,512]{1,0:T(8,128)(2,1)S(1)}, bf16[64,512]{1,0:T(8,128)(2,1)S(1)}, u32[]{:S(2)}, u32[]{:S(2)}) collective-permute-start(bf16[64,512]{1,0:T(8,128)(2,1)S(1)} %get-tuple-element.71), channel_id=1, source_target_pairs={{0,1},{1,5},{4,0},{5,4},{8,9},{9,13},{12,8},{13,12},{2,3},{3,7},{6... | collective-permute-start | bytes 196616 | tf_op jit(solution)/shard_map/ppermute | solution.py:469
  59.4 2.4 %collective-permute-done.10 = bf16[64,512]{1,0:T(8,128)(2,1)S(1)} collective-permute-done((bf16[64,512]{1,0:T(8,128)(2,1)S(1)}, bf16[64,512]{1,0:T(8,128)(2,1)S(1)}, u32[]{:S(2)}, u32[]{:S(2)}) %collective-permute-start.10) | collective-permute-done | bytes 65568 | tf_op jit(solution)/shard_map/ppermute | solution.py:469
  61.8 2.2 %collective-permute-done.9 = bf16[64,512]{1,0:T(8,128)(2,1)S(1)} collective-permute-done((bf16[64,512]{1,0:T(8,128)(2,1)S(1)}, bf16[64,512]{1,0:T(8,128)(2,1)S(1)}, u32[]{:S(2)}, u32[]{:S(2)}) %collective-permute-start.9) | collective-permute-done | bytes 65568 | tf_op jit(solution)/shard_map/ppermute | solution.py:469
  64.1 0.7 collective-permute-start.13
  64.7 1.0 %collective-permute-start.14 = (bf16[64,352]{1,0:T(8,128)(2,1)S(1)}, bf16[64,352]{1,0:T(8,128)(2,1)S(1)}, u32[]{:S(2)}, u32[]{:S(2)}) collective-permute-start(bf16[64,352]{1,0:T(8,128)(2,1)S(1)} %get-tuple-element.74), channel_id=1, source_target_pairs={{0,1},{1,5},{4,0},{5,4},{8,9},{9,13},{12,8},{13,12},{2,3},{3,7},{6... | collective-permute-start | bytes 135176 | tf_op jit(solution)/shard_map/ppermute | solution.py:469
  65.7 2.0 %collective-permute-start.15 = (bf16[64,352]{1,0:T(8,128)(2,1)S(1)}, bf16[64,352]{1,0:T(8,128)(2,1)S(1)}, u32[]{:S(2)}, u32[]{:S(2)}) collective-permute-start(bf16[64,352]{1,0:T(8,128)(2,1)S(1)} %get-tuple-element.75), channel_id=1, source_target_pairs={{0,8},{1,12},{4,9},{5,13},{8,0},{9,4},{12,1},{13,5},{2,10},{3,14},... | collective-permute-start | bytes 135176 | tf_op jit(solution)/shard_map/ppermute | solution.py:469
  69.3 3.2 %collective-permute-done.15 = bf16[64,352]{1,0:T(8,128)(2,1)S(1)} collective-permute-done((bf16[64,352]{1,0:T(8,128)(2,1)S(1)}, bf16[64,352]{1,0:T(8,128)(2,1)S(1)}, u32[]{:S(2)}, u32[]{:S(2)}) %collective-permute-start.15) | collective-permute-done | bytes 45088 | tf_op jit(solution)/shard_map/ppermute | solution.py:469
  72.5 1.1 %collective-permute-done.16 = bf16[64,352]{1,0:T(8,128)(2,1)S(1)} collective-permute-done((bf16[64,352]{1,0:T(8,128)(2,1)S(1)}, bf16[64,352]{1,0:T(8,128)(2,1)S(1)}, u32[]{:S(2)}, u32[]{:S(2)}) %collective-permute-start.16) | collective-permute-done | bytes 45088 | tf_op jit(solution)/shard_map/ppermute | solution.py:469
  74.1 1.4 %maximum_bitcast_fusion = f32[32,27,2,32]{3,2,1,0:T(2,128)} fusion(f32[2,32,11,32]{3,0,2,1:T(2,128)S(1)} %copy.14, f32[2,32,16,32]{3,0,2,1:T(2,128)S(1)} %copy.13), kind=kLoop, calls=%fused_computation | loop fusion | flops 55296 | bytes 442368 | tf_op jit(solution)/shard_map/transpose | solution.py:474
  (43 shorter events, 4.4 us)
Async XLA Ops:
  0.0 11.0 %copy-start = (f32[3,3,3,2,2048]{4,3,2,1,0:T(2,128)S(1)}, f32[3,3,3,2,2048]{4,3,2,1,0:T(2,128)}, u32[]{:S(2)}) copy-start(f32[3,3,3,2,2048]{4,3,2,1,0:T(2,128)} %param.4) | copy-start | bytes 1327108
  0.8 1.4 %copy-start.1 = (f32[32,3,2,2048]{3,2,1,0:T(2,128)S(1)}, f32[32,3,2,2048]{3,2,1,0:T(2,128)}, u32[]{:S(2)}) copy-start(f32[32,3,2,2048]{3,2,1,0:T(2,128)} %param.3) | copy-start | bytes 4718596
  2.3 15.9 %copy-start.4 = (s32[27,3]{0,1:T(4,128)S(1)}, s32[27,3]{0,1:T(4,128)}, u32[]{:S(2)}) copy-start(s32[27,3]{0,1:T(4,128)} %param.5) | copy-start | bytes 976
  4.4 26.4 %collective-permute-start.2 = (bf16[6,32,2048]{2,1,0:T(8,128)(2,1)}, bf16[6,32,2048]{2,1,0:T(8,128)(2,1)}, u32[]{:S(2)}, u32[]{:S(2)}) collective-permute-start(bf16[6,32,2048]{2,1,0:T(8,128)(2,1)} %get-tuple-element.52.refs_0_), channel_id=1, source_target_pairs={{0,2},{2,0},{1,3},{3,1},{4,6},{6,4},{5,7},{7,5},{8,10},{10,8},{9,1... | collective-permute-start | bytes 2359304 | tf_op jit(solution)/shard_map/ppermute | solution.py:31
  7.4 19.2 %collective-permute-start = (bf16[6,32,512]{2,1,0:T(8,128)(2,1)}, bf16[6,32,512]{2,1,0:T(8,128)(2,1)}, u32[]{:S(2)}, u32[]{:S(2)}) collective-permute-start(bf16[6,32,512]{2,1,0:T(8,128)(2,1)} %get-tuple-element.39), channel_id=1, source_target_pairs={{0,12},{4,0},{8,4},{12,8},{1,13},{5,1},{9,5},{13,9},{2,14},{6,2},{... | collective-permute-start | bytes 589832 | tf_op jit(solution)/shard_map/ppermute | solution.py:31
  11.0 15.6 %collective-permute-start.1 = (bf16[6,32,512]{2,1,0:T(8,128)(2,1)}, bf16[6,32,512]{2,1,0:T(8,128)(2,1)}, u32[]{:S(2)}, u32[]{:S(2)}) collective-permute-start(bf16[6,32,512]{2,1,0:T(8,128)(2,1)} %get-tuple-element.40), channel_id=1, source_target_pairs={{0,4},{4,8},{8,12},{12,0},{1,5},{5,9},{9,13},{13,1},{2,6},{6,10},{... | collective-permute-start | bytes 589832 | tf_op jit(solution)/shard_map/ppermute | solution.py:31
  14.4 16.4 %collective-permute-start.3 = (bf16[6,32,512]{2,1,0:T(8,128)(2,1)}, bf16[6,32,512]{2,1,0:T(8,128)(2,1)S(1)}, u32[]{:S(2)}, u32[]{:S(2)}) collective-permute-start(bf16[6,32,512]{2,1,0:T(8,128)(2,1)} %get-tuple-element.43), channel_id=1, source_target_pairs={{0,12},{4,0},{8,4},{12,8},{1,13},{5,1},{9,5},{13,9},{2,14},{6,2},{... | collective-permute-start | bytes 589832 | tf_op jit(solution)/shard_map/ppermute | solution.py:31
  18.2 12.6 %collective-permute-start.4 = (bf16[6,32,512]{2,1,0:T(8,128)(2,1)}, bf16[6,32,512]{2,1,0:T(8,128)(2,1)S(1)}, u32[]{:S(2)}, u32[]{:S(2)}) collective-permute-start(bf16[6,32,512]{2,1,0:T(8,128)(2,1)} %get-tuple-element.44), channel_id=1, source_target_pairs={{0,4},{4,8},{8,12},{12,0},{1,5},{5,9},{9,13},{13,1},{2,6},{6,10},{... | collective-permute-start | bytes 589832 | tf_op jit(solution)/shard_map/ppermute | solution.py:31
  26.5 4.3 %copy-start.2 = (f32[2,27,2048]{2,1,0:T(8,128)}, f32[2,27,2048]{2,1,0:T(8,128)S(1)}, u32[]{:S(2)}) copy-start(f32[2,27,2048]{2,1,0:T(8,128)S(1)} %get-tuple-element.50.table_ref) | copy-start | bytes 1327108
  30.7 2.7 %collective-permute-start.5 = (bf16[6,32,2048]{2,1,0:T(8,128)(2,1)}, bf16[6,32,2048]{2,1,0:T(8,128)(2,1)}, u32[]{:S(2)}, u32[]{:S(2)}) collective-permute-start(bf16[6,32,2048]{2,1,0:T(8,128)(2,1)} %get-tuple-element.52.refs_0_), channel_id=1, source_target_pairs={{0,1},{1,0},{2,3},{3,2},{4,5},{5,4},{6,7},{7,6},{8,9},{9,8},{10,11... | collective-permute-start | bytes 2359304 | tf_op jit(solution)/shard_map/ppermute | solution.py:31
  30.8 3.7 %collective-permute-start.6 = (bf16[6,32,2048]{2,1,0:T(8,128)(2,1)}, bf16[6,32,2048]{2,1,0:T(8,128)(2,1)}, u32[]{:S(2)}, u32[]{:S(2)}) collective-permute-start(bf16[6,32,2048]{2,1,0:T(8,128)(2,1)} %collective-permute-done.2.refs_1_), channel_id=1, source_target_pairs={{0,1},{1,0},{2,3},{3,2},{4,5},{5,4},{6,7},{7,6},{8,9},{9,8},{10,11... | collective-permute-start | bytes 2359304 | tf_op jit(solution)/shard_map/ppermute | solution.py:31
  31.4 3.1 %copy-start.3 = (f32[2,27,2048]{2,1,0:T(8,128)S(1)}, f32[2,27,2048]{2,1,0:T(8,128)}, u32[]{:S(2)}) copy-start(f32[2,27,2048]{2,1,0:T(8,128)} %copy-done.2) | copy-start | bytes 1327108
  43.6 9.7 %collective-permute-start.7 = (bf16[2,64,512]{2,1,0:T(8,128)(2,1)S(1)}, bf16[2,64,512]{2,1,0:T(8,128)(2,1)S(1)}, u32[]{:S(2)}, u32[]{:S(2)}) collective-permute-start(bf16[2,64,512]{2,1,0:T(8,128)(2,1)S(1)} %get-tuple-element.54), channel_id=1, source_target_pairs={{0,2},{2,0},{1,3},{3,1},{4,6},{6,4},{5,7},{7,5},{8,10},{10,8},{9,1... | collective-permute-start | bytes 393224 | tf_op jit(solution)/shard_map/ppermute | solution.py:31
  51.8 12.2 %collective-permute-start.12 = (bf16[2,64,352]{2,1,0:T(8,128)(2,1)S(1)}, bf16[2,64,352]{2,1,0:T(8,128)(2,1)S(1)}, u32[]{:S(2)}, u32[]{:S(2)}) collective-permute-start(bf16[2,64,352]{2,1,0:T(8,128)(2,1)S(1)} %get-tuple-element.63), channel_id=1, source_target_pairs={{0,2},{2,0},{1,3},{3,1},{4,6},{6,4},{5,7},{7,5},{8,10},{10,8},{9,1... | collective-permute-start | bytes 270344 | tf_op jit(solution)/shard_map/ppermute | solution.py:31
  53.4 8.4 %collective-permute-start.10 = (bf16[64,512]{1,0:T(8,128)(2,1)S(1)}, bf16[64,512]{1,0:T(8,128)(2,1)S(1)}, u32[]{:S(2)}, u32[]{:S(2)}) collective-permute-start(bf16[64,512]{1,0:T(8,128)(2,1)S(1)} %get-tuple-element.70), channel_id=1, source_target_pairs={{0,8},{1,12},{4,9},{5,13},{8,0},{9,4},{12,1},{13,5},{2,10},{3,14},... | collective-permute-start | bytes 196616 | tf_op jit(solution)/shard_map/ppermute | solution.py:469
  54.0 7.8 %collective-permute-start.11 = (bf16[64,512]{1,0:T(8,128)(2,1)S(1)}, bf16[64,512]{1,0:T(8,128)(2,1)S(1)}, u32[]{:S(2)}, u32[]{:S(2)}) collective-permute-start(bf16[64,512]{1,0:T(8,128)(2,1)S(1)} %get-tuple-element.69), channel_id=1, source_target_pairs={{0,9},{1,13},{4,8},{5,12},{8,1},{9,5},{12,0},{13,4},{2,11},{3,15},... | collective-permute-start | bytes 196616 | tf_op jit(solution)/shard_map/ppermute | solution.py:469
  54.0 7.8 %collective-permute-start.8 = (bf16[64,512]{1,0:T(8,128)(2,1)S(1)}, bf16[64,512]{1,0:T(8,128)(2,1)S(1)}, u32[]{:S(2)}, u32[]{:S(2)}) collective-permute-start(bf16[64,512]{1,0:T(8,128)(2,1)S(1)} %get-tuple-element.72), channel_id=1, source_target_pairs={{0,0},{1,4},{4,1},{5,5},{8,8},{9,12},{12,9},{13,13},{2,2},{3,6},{6... | collective-permute-start | bytes 196616 | tf_op jit(solution)/shard_map/ppermute | solution.py:469
  54.7 9.3 %collective-permute-start.9 = (bf16[64,512]{1,0:T(8,128)(2,1)S(1)}, bf16[64,512]{1,0:T(8,128)(2,1)S(1)}, u32[]{:S(2)}, u32[]{:S(2)}) collective-permute-start(bf16[64,512]{1,0:T(8,128)(2,1)S(1)} %get-tuple-element.71), channel_id=1, source_target_pairs={{0,1},{1,5},{4,0},{5,4},{8,9},{9,13},{12,8},{13,12},{2,3},{3,7},{6... | collective-permute-start | bytes 196616 | tf_op jit(solution)/shard_map/ppermute | solution.py:469
  64.1 4.6 %collective-permute-start.13 = (bf16[64,352]{1,0:T(8,128)(2,1)S(1)}, bf16[64,352]{1,0:T(8,128)(2,1)S(1)}, u32[]{:S(2)}, u32[]{:S(2)}) collective-permute-start(bf16[64,352]{1,0:T(8,128)(2,1)S(1)} %get-tuple-element.73), channel_id=1, source_target_pairs={{0,0},{1,4},{4,1},{5,5},{8,8},{9,12},{12,9},{13,13},{2,2},{3,6},{6... | collective-permute-start | bytes 135176 | tf_op jit(solution)/shard_map/ppermute | solution.py:469
  64.7 4.6 %collective-permute-start.14 = (bf16[64,352]{1,0:T(8,128)(2,1)S(1)}, bf16[64,352]{1,0:T(8,128)(2,1)S(1)}, u32[]{:S(2)}, u32[]{:S(2)}) collective-permute-start(bf16[64,352]{1,0:T(8,128)(2,1)S(1)} %get-tuple-element.74), channel_id=1, source_target_pairs={{0,1},{1,5},{4,0},{5,4},{8,9},{9,13},{12,8},{13,12},{2,3},{3,7},{6... | collective-permute-start | bytes 135176 | tf_op jit(solution)/shard_map/ppermute | solution.py:469
  65.7 6.8 %collective-permute-start.15 = (bf16[64,352]{1,0:T(8,128)(2,1)S(1)}, bf16[64,352]{1,0:T(8,128)(2,1)S(1)}, u32[]{:S(2)}, u32[]{:S(2)}) collective-permute-start(bf16[64,352]{1,0:T(8,128)(2,1)S(1)} %get-tuple-element.75), channel_id=1, source_target_pairs={{0,8},{1,12},{4,9},{5,13},{8,0},{9,4},{12,1},{13,5},{2,10},{3,14},... | collective-permute-start | bytes 135176 | tf_op jit(solution)/shard_map/ppermute | solution.py:469
  67.7 5.9 %collective-permute-start.16 = (bf16[64,352]{1,0:T(8,128)(2,1)S(1)}, bf16[64,352]{1,0:T(8,128)(2,1)S(1)}, u32[]{:S(2)}, u32[]{:S(2)}) collective-permute-start(bf16[64,352]{1,0:T(8,128)(2,1)S(1)} %get-tuple-element.76), channel_id=1, source_target_pairs={{0,9},{1,13},{4,8},{5,12},{8,1},{9,5},{12,0},{13,4},{2,11},{3,15},... | collective-permute-start | bytes 135176 | tf_op jit(solution)/shard_map/ppermute | solution.py:469

commit v9 on v6

--- a/solution.py
+++ b/solution.py
@@ -20,7 +20,7 @@
 LOW = jnp.bfloat16
 WIDE = jnp.float32
 STEP = 2
-VMEM_LIMIT = 40 * 1024 * 1024
+VMEM_LIMIT = 56 * 1024 * 1024
 VMEM = pl.BlockSpec(memory_space=pltpu.VMEM)
 SMEM = pl.BlockSpec(memory_space=pltpu.SMEM)
 
@@ -104,17 +104,16 @@
     return [(1.0 - 6.0 * KAPPA) * a + KAPPA * b for a, b in zip(here, total)]
 
 
-def first_step(layer, tile, rows, field_ref, link_ref, back_ref):
-    layers = field_ref.shape[2] // PLANE
+def one_step(layer, layers, tile, rows, fetch, link_ref, back_ref, extra=None):
     total = [None] * 6
     if layer < layers - 1:
-        source = load(field_ref, rows, lanes_at(layer + 1, tile))
-        add_hop(total, link_at(link_ref, 0, layer, tile), source, False)
+        add_hop(total, link_at(link_ref, 0, layer, tile), fetch(layer + 1, tile), False)
     if layer > 0:
-        source = load(field_ref, rows, lanes_at(layer - 1, tile))
-        add_hop(total, link_at(link_ref, 0, layer - 1, tile), source, True)
-    fetch = lambda t: load(field_ref, rows, lanes_at(layer, t))
-    return combined(plane_hops(total, link_ref, back_ref, layer, tile, rows, fetch), total)
+        add_hop(total, link_at(link_ref, 0, layer - 1, tile), fetch(layer - 1, tile), True)
+    here = plane_hops(total, link_ref, back_ref, layer, tile, rows, lambda t: fetch(layer, t))
+    if extra is not None:
+        total = [a + b for a, b in zip(total, extra)]
+    return combined(here, total)
 
 
 def open_kernel(vector_ref, link_ref, field_ref, raw_ref, down_ref, up_ref):
@@ -158,7 +157,8 @@
         def _(tile):
             lanes = lanes_at(0, tile)
             for rows in row_groups(field_ref):
-                new = first_step(layer, tile, rows, field_ref, link_ref, back_ref)
+                fetch = lambda at, t: load(field_ref, rows, lanes_at(at, t))
+                new = one_step(layer, layers, tile, rows, fetch, link_ref, back_ref)
                 store(rim_ref, rows, lanes_at(place, tile), new)
                 if place == 0:
                     store(down_ref, rows, lanes, new)
@@ -179,9 +179,7 @@
     return 1.0 - 2.0 * sine * sine, 2.0 * sine * cosine
 
 
-def local_kernel(
-    total_x, place_ref, field_ref, link_ref, back_ref, rim_ref, momenta_ref, out_ref, table_ref, one_ref
-):
+def inner_kernel(total_x, place_ref, field_ref, link_ref, back_ref, momenta_ref, out_ref, table_ref):
     layers = field_ref.shape[2] // PLANE
     count = momenta_ref.shape[0]
     momenta = momenta_ref[...].astype(WIDE)
@@ -200,66 +198,55 @@
             table_ref[1, :, lanes_at(layer, tile)] = sine
 
 
-    one_ref[:, :, pl.ds(0, PLANE)] = rim_ref[:, :, pl.ds(0, PLANE)]
-    one_ref[:, :, pl.ds((layers - 1) * PLANE, PLANE)] = rim_ref[:, :, pl.ds(PLANE, PLANE)]
     for layer in range(1, layers - 1):
 
         @pl.loop(0, TILES)
         def _(tile):
             for rows in row_groups(field_ref):
-                new = first_step(layer, tile, rows, field_ref, link_ref, back_ref)
-                store(one_ref, rows, lanes_at(layer, tile), new)
+                fetch = lambda at, t: load(field_ref, rows, lanes_at(at, t))
+                new = one_step(layer, layers, tile, rows, fetch, link_ref, back_ref)
+                store(out_ref, rows, lanes_at(layer - 1, tile), new)
+
+
+def second_kernel(
+    field_ref, inner_ref, rim_ref, ahead_ref, behind_ref, link_ref, back_ref, out_ref, most_ref, token_ref, edge_ref
+):
+    layers = field_ref.shape[2] // PLANE
+    token_ref[...] = jnp.zeros_like(token_ref)
+
+    @pl.loop(0, TILES)
+    def _(tile):
+        lanes, high = lanes_at(0, tile), lanes_at(1, tile)
+        for rows in row_groups(field_ref):
+            new = zip(load(rim_ref, rows, lanes), load(behind_ref, rows, lanes))
+            store(edge_ref, rows, lanes, [a + KAPPA * b for a, b in new])
+            hop = [None] * 6
+            add_hop(hop, link_at(link_ref, 0, layers - 1, tile), load(ahead_ref, rows, lanes), False)
+            store(edge_ref, rows, high, [a + KAPPA * b for a, b in zip(load(rim_ref, rows, high), hop)])
 
     for layer in range(layers):
 
         @pl.loop(0, TILES)
         def _(tile):
             for rows in row_groups(field_ref):
-                new = first_step(layer, tile, rows, one_ref, link_ref, back_ref)
+
+                def fetch(at, t):
+                    if at in (0, layers - 1):
+                        return load(edge_ref, rows, lanes_at(min(at, 1), t))
+                    return load(inner_ref, rows, lanes_at(at - 1, t))
+
+                extra = None
                 if layer in (0, layers - 1):
-                    own = load(field_ref, rows, lanes_at(layer, tile))
-                    new = [a + KAPPA * KAPPA * b for a, b in zip(new, own)]
-                store(out_ref, rows, lanes_at(layer, tile), new)
-
-
-def close_kernel(part_ref, ahead_ref, behind_ref, link_ref, back_ref, out_ref, token_ref, change_ref):
-    layers = part_ref.shape[2] // PLANE
-    token_ref[...] = jnp.zeros_like(token_ref)
-
-    @pl.loop(0, TILES)
-    def _(tile):
-        lanes = lanes_at(0, tile)
-        for rows in row_groups(part_ref):
-            store(change_ref, rows, lanes, [KAPPA * a for a in load(behind_ref, rows, lanes)])
-            high = [None] * 6
-            add_hop(high, link_at(link_ref, 0, layers - 1, tile), load(ahead_ref, rows, lanes), False)
-            store(change_ref, rows, lanes_at(1, tile), [KAPPA * a for a in high])
-
-    for layer in range(layers):
-
-        @pl.loop(0, TILES)
-        def _(tile):
-            for rows in row_groups(part_ref):
-                new = load(part_ref, rows, lanes_at(layer, tile))
-                change = lambda place, t: load(change_ref, rows, lanes_at(place, t))
-                hops = [None] * 6
-                if layer == 1:
-                    add_hop(hops, link_at(link_ref, 0, 0, tile), change(0, tile), True)
-                if layer == layers - 2:
-                    add_hop(hops, link_at(link_ref, 0, layer, tile), change(1, tile), False)
-                for place, edge in ((0, 0), (1, layers - 1)):
-                    if layer == edge:
-                        if hops[0] is None:
-                            hops = [jnp.zeros_like(a) for a in new]
-                        here = plane_hops(hops, link_ref, back_ref, layer, tile, rows, lambda t: change(place, t))
-                        new = [a + (1.0 - 6.0 * KAPPA) * b for a, b in zip(new, here)]
-                if hops[0] is not None:
-                    new = [a + KAPPA * b for a, b in zip(new, hops)]
-                store(out_ref, rows, lanes_at(layer, tile), new)
+                    extra = [KAPPA * a for a in load(field_ref, rows, lanes_at(layer, tile))]
+                new = one_step(layer, layers, tile, rows, fetch, link_ref, back_ref, extra)
+                if layer in (0, layers - 1):
+                    store(most_ref, rows, lanes_at(min(layer, 1), tile), new)
+                else:
+                    store(out_ref, rows, lanes_at(layer - 1, tile), new)
 
 
 def face_kernel(most_ref, ahead_ref, behind_ref, link_ref, token_ref, out_ref):
-    layers = most_ref.shape[2] // PLANE
+    layers = link_ref.shape[0] // 54 // TILES
 
     @pl.loop(0, TILES)
     def _(tile):
@@ -269,15 +256,15 @@
             store(out_ref, rows, lanes, [a + KAPPA * b for a, b in new])
             hop = [None] * 6
             add_hop(hop, link_at(link_ref, 0, layers - 1, tile), load(ahead_ref, rows, lanes), False)
-            new = zip(load(most_ref, rows, lanes_at(layers - 1, tile)), hop)
+            new = zip(load(most_ref, rows, high), hop)
             store(out_ref, rows, high, [a + KAPPA * b for a, b in new])
 
 
-def product_kernel(columns, count, scale, slot_ref, most_ref, face_ref, table_ref, *refs):
+def product_kernel(columns, count, scale, slot_ref, inner_ref, face_ref, table_ref, *refs):
     groups = len(columns)
     raw_refs, out_refs, (total_ref, left_ref, right_ref) = refs[:groups], refs[groups:-3], refs[-3:]
-    vectors = most_ref.shape[1]
-    layers = most_ref.shape[2] // PLANE
+    vectors = inner_ref.shape[1]
+    layers = table_ref.shape[2] // PLANE
     depth = 6 * LANES
     step = left_ref.shape[1] // depth
     total_ref[...] = jnp.zeros_like(total_ref)
@@ -314,7 +301,7 @@
 
     @pl.loop(0, (layers - 2) * blocks)
     def _(block):
-        add(most_ref, lambda part: (lanes_at(1, block * step + part),) * 2)
+        add(inner_ref, lambda part: (lanes_at(0, block * step + part), lanes_at(1, block * step + part)))
 
     @pl.loop(0, 2 * blocks)
     def _(block):
@@ -326,6 +313,18 @@
     for g in range(groups):
         block = total_ref[pl.ds(g * width, width), :] * scale
         out_refs[columns[g]][slot_ref[g]] = block.astype(LOW)
+
+
+def sum_kernel(*refs):
+    *share_refs, out_ref = refs
+    width = out_ref.shape[1]
+    count = out_ref.shape[0] // (2 * width)
+    total = sum(ref[...].astype(WIDE) for ref in share_refs)
+    for p in range(count):
+        block = total[:, p * width : (p + 1) * width]
+        for part in range(2):
+            rows = pl.ds(2 * p + part, width, stride=2 * count)
+            out_ref[rows, :] = block[part * width : (part + 1) * width]
 
 
 def call(kernel, name, shapes, operands, flops=0, scratch=(), smem=False):
@@ -346,7 +345,7 @@
     groups = vecs * subs
     width, sites = vectors.shape[0], vectors.shape[3]
     layers, tiles = sites // PLANE, sites // LANES
-    assert groups == bricks and layers > 1 and ITERS == 2
+    assert groups == bricks and layers > 2 and ITERS == 2
     total_x = bricks * layers
     count = momenta.shape[0]
     brick, vec, sub = (lax.axis_index(axis) for axis in ("brick", "vec", "sub"))
@@ -371,21 +370,20 @@
     )
     ahead_two, behind_two = shifted(down_two, "brick", -1), shifted(up_two, "brick", 1)
     place = (brick * layers).astype(jnp.int32).reshape((1,))
-    part, table = call(
-        functools.partial(local_kernel, total_x),
-        "local",
-        ((full, WIDE), ((2, count, sites), WIDE)),
-        (place, field, links, back, rim, momenta),
+    inner, table = call(
+        functools.partial(inner_kernel, total_x),
+        "inner",
+        (((6, width, sites - 2 * PLANE), WIDE), ((2, count, sites), WIDE)),
+        (place, field, links, back, momenta),
+        flops=1 << 24,
+        smem=True,
+    )
+    smeared, most, token = call(
+        second_kernel,
+        "second",
+        (((6, width, sites - 2 * PLANE), WIDE), ((6, width, 2 * PLANE), WIDE), ((8, LANES), WIDE)),
+        (field, inner, rim, ahead, behind, links, back),
         flops=1 << 25,
-        scratch=(pltpu.VMEM(full, WIDE),),
-        smem=True,
-    )
-    most, token = call(
-        close_kernel,
-        "close",
-        ((full, WIDE), ((8, LANES), WIDE)),
-        (part, ahead, behind, links, back),
-        flops=1 << 24,
         scratch=(pltpu.VMEM((6, width, 2 * PLANE), WIDE),),
     )
     late, token = lax.optimization_barrier((raw, token))
@@ -408,7 +406,7 @@
         functools.partial(product_kernel, [-a % vecs for a, b in offsets], count, scale),
         "product",
         (((subs, 2 * width, columns), LOW),) * vecs,
-        (slots, most, faces, table, *raws),
+        (slots, smeared, faces, table, *raws),
         flops=1 << 32,
         scratch=(
             pltpu.VMEM((groups * 2 * width, columns), WIDE),
@@ -431,8 +429,8 @@
                 for s in range(subs)
             ]
             shares.append(lax.ppermute(block[r], ("brick", "sub"), pairs))
-    total = functools.reduce(jnp.add, [share.astype(WIDE) for share in shares])
-    return jnp.transpose(total.reshape((2, width, count, width)), (1, 2, 0, 3))
+    (total,) = call(sum_kernel, "sum", (((width * count * 2, width), WIDE),), shares, flops=1 << 20)
+    return total.reshape((width, count, 2, width))
 
 
 def solution(mesh):

time: 71.5 us -> 80.3 us (1.12)
  Pallas kernels: 31 us -> 42.6 us
  waiting for transfers between devices: 17.8 us -> 15.3 us
  local copies, waits for them, and re-layouts: 4.57 us -> 2.98 us
  other arithmetic: 0.18 us -> 1.54 us
    pallas_call x6 -> x7, Pallas kernels: 31 us -> 42.6 us  [call(): pl.pallas_call(kernel, out_shape=tuple((jax.ShapeDtypeStruct(shape, dtype...]
    ppermute x8, waiting for transfers between devices: 9.92 us -> 7.38 us  [shifted(): lax.ppermute(array, axis, [(i, (i + by) % peers) for i in range(peers)])]
    transpose x1 -> x0, local copies, waits for them, and re-layouts: 1.61 us -> none  [shards(): return jnp.transpose(total.reshape((2, width, count, width)), (1, 2, 0, 3))]
    select_n x1, other arithmetic: 0.05 us -> 0.99 us  [shards(): block = jnp.where(place == a, held[a], block)]
    unnamed x13 -> x25, local copies, waits for them, and re-layouts: 2.53 us -> 2.94 us
  transfers between devices with their start and end apart: 12 -> 12, of which waited for: 5 -> 3; matrix products, arithmetic and copies ran while one was open for 0% -> 2% of each run, Pallas kernels for 23% -> 28%
where the time goes in v9:
time: 80.3 us; the launch traced here: 80 us
  Pallas kernels  42.6 us (53%)
  starting transfers between devices  17.4 us (22%)
  waiting for transfers between devices  15.3 us (19%)
  local copies, waits for them, and re-layouts  2.98 us (4%)
  other arithmetic  1.54 us (2%)
    pallas_call x7, Pallas kernels, call(): pl.pallas_call(kernel, out_shape=tuple((jax.ShapeDtypeStruct(shape, dtype...  42.6 us
    ppermute x8, starting transfers between devices, shifted(): lax.ppermute(array, axis, [(i, (i + by) % peers) for i in range(peers)])  11.5 us
    ppermute x4, waiting for transfers between devices, shards(): shares.append(lax.ppermute(block[r], ('brick', 'sub'), pairs))  7.89 us
    ppermute x8, waiting for transfers between devices, shifted(): lax.ppermute(array, axis, [(i, (i + by) % peers) for i in range(peers)])  7.38 us
    ppermute x4, starting transfers between devices, shards(): shares.append(lax.ppermute(block[r], ('brick', 'sub'), pairs))  5.98 us
    unnamed x25, local copies, waits for them, and re-layouts  2.94 us
  transfers between devices with their start and end apart: 12, of which 3 were waited for; matrix products, arithmetic and copies ran while one was open for 2% of the time, Pallas kernels for 28%

profile of v9, /device:TPU:0, one launch (start us, length us, event | category | flops | bytes accessed | tf_op | source)
XLA Modules:
  0.0 80.0 jit_solution(11517120724007536588)
XLA Ops:
  0.0 4.2 %open.1 = (f32[6,32,2048]{2,1,0:T(8,128)}, bf16[6,32,2048]{2,1,0:T(8,128)(2,1)}, bf16[6,32,512]{2,1,0:T(8,128)(2,1)}, bf16[6,32,512]{2,1,0:T(8,128)(2,1)}) custom-call(f32[3072,128]{1,0:T(8,128)} %bitcast.27, f32[864,128]{1,0:T(8,128)} %bitcast.22), custom_call_target="tpu_custom_call" | custom-call | flops 4194304 | bytes 1048576 | tf_op jit(solution)/shard_map/open/pallas_call | solution.py:331
  4.2 2.9 %collective-permute-start.2 = (bf16[6,32,2048]{2,1,0:T(8,128)(2,1)}, bf16[6,32,2048]{2,1,0:T(8,128)(2,1)S(1)}, u32[]{:S(2)}, u32[]{:S(2)}) collective-permute-start(bf16[6,32,2048]{2,1,0:T(8,128)(2,1)} %get-tuple-element.44.refs_0_), channel_id=1, source_target_pairs={{0,2},{2,0},{1,3},{3,1},{4,6},{6,4},{5,7},{7,5},{8,10},{10,8},{9,1... | collective-permute-start | bytes 2359304 | tf_op jit(solution)/shard_map/ppermute | solution.py:30
  7.1 3.6 %collective-permute-start = (bf16[6,32,512]{2,1,0:T(8,128)(2,1)}, bf16[6,32,512]{2,1,0:T(8,128)(2,1)S(1)}, u32[]{:S(2)}, u32[]{:S(2)}) collective-permute-start(bf16[6,32,512]{2,1,0:T(8,128)(2,1)} %get-tuple-element.30), channel_id=1, source_target_pairs={{0,12},{4,0},{8,4},{12,8},{1,13},{5,1},{9,5},{13,9},{2,14},{6,2},{... | collective-permute-start | bytes 589832 | tf_op jit(solution)/shard_map/ppermute | solution.py:30
  10.8 5.1 %rim.1 = (bf16[6,32,512]{2,1,0:T(8,128)(2,1)}, bf16[6,32,512]{2,1,0:T(8,128)(2,1)}, f32[6,32,1024]{2,1,0:T(8,128)}, f32[2,16,2048]{2,1,0:T(8,128)}) custom-call(f32[6,32,2048]{2,1,0:T(8,128)} %get-tuple-element.26.field_ref, f32[864,128]{1,0:T(8,128)} %bitcast.23), custom_call_target="tpu_custom_call" | custom-call | flops 16777216 | bytes 1048576 | tf_op jit(solution)/shard_map/rim/pallas_call | solution.py:331
  15.9 3.8 %collective-permute-start.3 = (bf16[6,32,512]{2,1,0:T(8,128)(2,1)}, bf16[6,32,512]{2,1,0:T(8,128)(2,1)S(1)}, u32[]{:S(2)}, u32[]{:S(2)}) collective-permute-start(bf16[6,32,512]{2,1,0:T(8,128)(2,1)} %get-tuple-element.35), channel_id=1, source_target_pairs={{0,12},{4,0},{8,4},{12,8},{1,13},{5,1},{9,5},{13,9},{2,14},{6,2},{... | collective-permute-start | bytes 589832 | tf_op jit(solution)/shard_map/ppermute | solution.py:30
  19.7 0.7 copy.6.momenta_ref
  20.4 5.9 %inner.1 = (f32[6,32,1024]{2,1,0:T(8,128)}, f32[2,27,2048]{2,1,0:T(8,128)}) custom-call(s32[1]{0:T(128)} %bitcast.8.place_ref, f32[6,32,2048]{2,1,0:T(8,128)} %get-tuple-element.26.field_ref, f32[864,128]{1,0:T(8,128)} %bitcast.24, f32[2,16,2048]{2,1,0:T(8,128)} %get-tuple-element.27.back_ref, s32[27,3]{1,0:T(8,128)} %copy.6.momenta_ref), custom_call_target="tpu_custom_call" | custom-call | flops 16777216 | bytes 1048576 | tf_op jit(solution)/shard_map/inner/pallas_call | solution.py:331
  26.3 0.6 copy-done
  27.1 8.4 %second.1 = (f32[6,32,1024]{2,1,0:T(8,128)}, f32[6,32,1024]{2,1,0:T(8,128)}, f32[8,128]{1,0:T(8,128)}) custom-call(f32[6,32,2048]{2,1,0:T(8,128)} %get-tuple-element.26.field_ref, f32[6,32,1024]{2,1,0:T(8,128)} %get-tuple-element.28.inner_ref, f32[6,32,1024]{2,1,0:T(8,128)} %get-tuple-element.29.rim_ref, bf16[6,32,512]{2,1,0:T(8,128)(2,1)} %copy-done, ...), custom_call_target="tpu_custom_call" | custom-call | flops 33554432 | bytes 1048576 | tf_op jit(solution)/shard_map/second/pallas_call | solution.py:331
  35.6 0.6 collective-permute-start.6
  36.1 0.6 pad_add_fusion.slot_ref
  36.7 2.6 %face.1.face_ref = f32[6,32,1024]{2,1,0:T(8,128)} custom-call(f32[6,32,1024]{2,1,0:T(8,128)} %get-tuple-element.33.most_ref, bf16[6,32,512]{2,1,0:T(8,128)(2,1)} %copy-done.2, bf16[6,32,512]{2,1,0:T(8,128)(2,1)} %copy-done.3, f32[864,128]{1,0:T(8,128)} %bitcast.26, f32[8,128]{1,0:T(8,128)} %get-tuple-element.41.token_ref), custom_call_target="tpu_custom_call" | custom-call | flops 4194304 | bytes 1048576 | tf_op jit(solution)/shard_map/face/pallas_call | solution.py:331
  39.3 0.9 %copy-done.11 = bf16[6,32,2048]{2,1,0:T(8,128)(2,1)} copy-done((bf16[6,32,2048]{2,1,0:T(8,128)(2,1)}, bf16[6,32,2048]{2,1,0:T(8,128)(2,1)S(1)}, u32[]{:S(2)}) %copy-start.11) | copy-done | bytes 786456
  40.1 14.2 %product.1 = (bf16[2,64,864]{2,1,0:T(8,128)(2,1)}, bf16[2,64,864]{2,1,0:T(8,128)(2,1)}) custom-call(s32[4]{0:T(128)} %pad_add_fusion.slot_ref, f32[6,32,1024]{2,1,0:T(8,128)} %get-tuple-element.32.inner_ref, f32[6,32,1024]{2,1,0:T(8,128)} %face.1.face_ref, f32[2,27,2048]{2,1,0:T(8,128)} %get-tuple-element.42.table_ref, ...), custom_call_target="tpu_custom_call" | custom-call | flops 4294967296 | bytes 1048576 | tf_op jit(solution)/shard_map/product/pallas_call | solution.py:331
  54.3 0.5 collective-permute-start.7
  54.8 7.4 %collective-permute-done.7 = bf16[2,64,864]{2,1,0:T(8,128)(2,1)S(1)} collective-permute-done((bf16[2,64,864]{2,1,0:T(8,128)(2,1)}, bf16[2,64,864]{2,1,0:T(8,128)(2,1)S(1)}, u32[]{:S(2)}, u32[]{:S(2)}) %collective-permute-start.7) | collective-permute-done | bytes 221216 | tf_op jit(solution)/shard_map/ppermute | solution.py:30
  62.2 1.0 %broadcast_select_fusion = (bf16[2,64,864]{2,1,0:T(8,128)(2,1)S(1)}, bf16[2,64,864]{2,1,0:T(8,128)(2,1)S(1)}) fusion(bf16[2,64,864]{2,1,0:T(8,128)(2,1)S(1)} %collective-permute-done.7, bf16[2,64,864]{2,1,0:T(8,128)(2,1)} %get-tuple-element.46, pred[]{:T(512)S(6)} %eq.15, pred[]{:T(512)S(6)} %eq.14), kind=kLoop, calls=%fused_computation | loop fusion | flops 221184 | bytes 884738 | tf_op jit(solution)/shard_map/jit(_where)/select_n | solution.py:424
  63.2 0.6 collective-permute-start.10
  63.9 0.7 collective-permute-start.8
  64.6 4.7 %collective-permute-start.9 = (bf16[64,864]{1,0:T(8,128)(2,1)S(1)}, bf16[64,864]{1,0:T(8,128)(2,1)S(1)}, u32[]{:S(2)}, u32[]{:S(2)}) collective-permute-start(bf16[64,864]{1,0:T(8,128)(2,1)S(1)} %get-tuple-element.51), channel_id=1, source_target_pairs={{0,1},{1,5},{4,0},{5,4},{8,9},{9,13},{12,8},{13,12},{2,3},{3,7},{6... | collective-permute-start | bytes 331784 | tf_op jit(solution)/shard_map/ppermute | solution.py:431
  69.2 5.3 %collective-permute-done.10.refs_2_ = bf16[64,864]{1,0:T(8,128)(2,1)S(1)} collective-permute-done((bf16[64,864]{1,0:T(8,128)(2,1)S(1)}, bf16[64,864]{1,0:T(8,128)(2,1)S(1)}, u32[]{:S(2)}, u32[]{:S(2)}) %collective-permute-start.10) | collective-permute-done | bytes 110624 | tf_op jit(solution)/shard_map/ppermute | solution.py:431
  74.6 2.5 %collective-permute-done.9.refs_1_ = bf16[64,864]{1,0:T(8,128)(2,1)S(1)} collective-permute-done((bf16[64,864]{1,0:T(8,128)(2,1)S(1)}, bf16[64,864]{1,0:T(8,128)(2,1)S(1)}, u32[]{:S(2)}, u32[]{:S(2)}) %collective-permute-start.9) | collective-permute-done | bytes 110624 | tf_op jit(solution)/shard_map/ppermute | solution.py:431
  77.2 0.6 copy-done.7
  77.8 2.2 %sum.1 = f32[1728,32]{1,0:T(8,128)} custom-call(bf16[64,864]{1,0:T(8,128)(2,1)} %copy-done.6, bf16[64,864]{1,0:T(8,128)(2,1)} %copy-done.7, bf16[64,864]{1,0:T(8,128)(2,1)} %copy-done.4, bf16[64,864]{1,0:T(8,128)(2,1)} %copy-done.5), custom_call_target="tpu_custom_call" | custom-call | flops 1048576 | bytes 1048576 | tf_op jit(solution)/shard_map/sum/pallas_call | solution.py:331
  (36 shorter events, 0.2 us)
Async XLA Ops:
  0.0 19.7 %copy-start.8 = (s32[27,3]{0,1:T(4,128)S(1)}, s32[27,3]{0,1:T(4,128)}, u32[]{:S(2)}) copy-start(s32[27,3]{0,1:T(4,128)} %param.5) | copy-start | bytes 976
  4.2 31.3 %collective-permute-start.2 = (bf16[6,32,2048]{2,1,0:T(8,128)(2,1)}, bf16[6,32,2048]{2,1,0:T(8,128)(2,1)S(1)}, u32[]{:S(2)}, u32[]{:S(2)}) collective-permute-start(bf16[6,32,2048]{2,1,0:T(8,128)(2,1)} %get-tuple-element.44.refs_0_), channel_id=1, source_target_pairs={{0,2},{2,0},{1,3},{3,1},{4,6},{6,4},{5,7},{7,5},{8,10},{10,8},{9,1... | collective-permute-start | bytes 2359304 | tf_op jit(solution)/shard_map/ppermute | solution.py:30
  7.1 19.2 %collective-permute-start = (bf16[6,32,512]{2,1,0:T(8,128)(2,1)}, bf16[6,32,512]{2,1,0:T(8,128)(2,1)S(1)}, u32[]{:S(2)}, u32[]{:S(2)}) collective-permute-start(bf16[6,32,512]{2,1,0:T(8,128)(2,1)} %get-tuple-element.30), channel_id=1, source_target_pairs={{0,12},{4,0},{8,4},{12,8},{1,13},{5,1},{9,5},{13,9},{2,14},{6,2},{... | collective-permute-start | bytes 589832 | tf_op jit(solution)/shard_map/ppermute | solution.py:30
  10.8 15.6 %collective-permute-start.1 = (bf16[6,32,512]{2,1,0:T(8,128)(2,1)}, bf16[6,32,512]{2,1,0:T(8,128)(2,1)S(1)}, u32[]{:S(2)}, u32[]{:S(2)}) collective-permute-start(bf16[6,32,512]{2,1,0:T(8,128)(2,1)} %get-tuple-element.31), channel_id=1, source_target_pairs={{0,4},{4,8},{8,12},{12,0},{1,5},{5,9},{9,13},{13,1},{2,6},{6,10},{... | collective-permute-start | bytes 589832 | tf_op jit(solution)/shard_map/ppermute | solution.py:30
  15.9 19.6 %collective-permute-start.3 = (bf16[6,32,512]{2,1,0:T(8,128)(2,1)}, bf16[6,32,512]{2,1,0:T(8,128)(2,1)S(1)}, u32[]{:S(2)}, u32[]{:S(2)}) collective-permute-start(bf16[6,32,512]{2,1,0:T(8,128)(2,1)} %get-tuple-element.35), channel_id=1, source_target_pairs={{0,12},{4,0},{8,4},{12,8},{1,13},{5,1},{9,5},{13,9},{2,14},{6,2},{... | collective-permute-start | bytes 589832 | tf_op jit(solution)/shard_map/ppermute | solution.py:30
  19.7 15.8 %collective-permute-start.4 = (bf16[6,32,512]{2,1,0:T(8,128)(2,1)}, bf16[6,32,512]{2,1,0:T(8,128)(2,1)S(1)}, u32[]{:S(2)}, u32[]{:S(2)}) collective-permute-start(bf16[6,32,512]{2,1,0:T(8,128)(2,1)} %get-tuple-element.36), channel_id=1, source_target_pairs={{0,4},{4,8},{8,12},{12,0},{1,5},{5,9},{9,13},{13,1},{2,6},{6,10},{... | collective-permute-start | bytes 589832 | tf_op jit(solution)/shard_map/ppermute | solution.py:30
  26.3 0.7 copy-start
  26.3 0.7 copy-start.1
  27.0 8.4 %copy-start.9 = (bf16[6,32,2048]{2,1,0:T(8,128)(2,1)S(1)}, bf16[6,32,2048]{2,1,0:T(8,128)(2,1)}, u32[]{:S(2)}) copy-start(bf16[6,32,2048]{2,1,0:T(8,128)(2,1)} %get-tuple-element.44.refs_0_) | copy-start | bytes 2359300
  35.5 3.8 %collective-permute-start.5 = (bf16[6,32,2048]{2,1,0:T(8,128)(2,1)S(1)}, bf16[6,32,2048]{2,1,0:T(8,128)(2,1)S(1)}, u32[]{:S(2)}, u32[]{:S(2)}) collective-permute-start(bf16[6,32,2048]{2,1,0:T(8,128)(2,1)S(1)} %copy-done.9), channel_id=1, source_target_pairs={{0,1},{1,0},{2,3},{3,2},{4,5},{5,4},{6,7},{7,6},{8,9},{9,8},{10,11... | collective-permute-start | bytes 2359304 | tf_op jit(solution)/shard_map/ppermute | solution.py:30
  35.5 1.2 %copy-start.2 = (bf16[6,32,512]{2,1,0:T(8,128)(2,1)}, bf16[6,32,512]{2,1,0:T(8,128)(2,1)S(1)}, u32[]{:S(2)}) copy-start(bf16[6,32,512]{2,1,0:T(8,128)(2,1)S(1)} %collective-permute-done.3.ahead_ref) | copy-start | bytes 589828
  35.5 1.1 %copy-start.3 = (bf16[6,32,512]{2,1,0:T(8,128)(2,1)}, bf16[6,32,512]{2,1,0:T(8,128)(2,1)S(1)}, u32[]{:S(2)}) copy-start(bf16[6,32,512]{2,1,0:T(8,128)(2,1)S(1)} %collective-permute-done.4.behind_ref) | copy-start | bytes 589828
  35.5 3.7 %copy-start.10 = (bf16[6,32,2048]{2,1,0:T(8,128)(2,1)}, bf16[6,32,2048]{2,1,0:T(8,128)(2,1)S(1)}, u32[]{:S(2)}) copy-start(bf16[6,32,2048]{2,1,0:T(8,128)(2,1)S(1)} %collective-permute-done.2.refs_1_) | copy-start | bytes 2359300
  35.6 3.7 %collective-permute-start.6 = (bf16[6,32,2048]{2,1,0:T(8,128)(2,1)S(1)}, bf16[6,32,2048]{2,1,0:T(8,128)(2,1)}, u32[]{:S(2)}, u32[]{:S(2)}) collective-permute-start(bf16[6,32,2048]{2,1,0:T(8,128)(2,1)S(1)} %collective-permute-done.2.refs_1_), channel_id=1, source_target_pairs={{0,1},{1,0},{2,3},{3,2},{4,5},{5,4},{6,7},{7,6},{8,9},{9,8},{10,11... | collective-permute-start | bytes 2359304 | tf_op jit(solution)/shard_map/ppermute | solution.py:30
  39.2 0.9 %copy-start.11 = (bf16[6,32,2048]{2,1,0:T(8,128)(2,1)}, bf16[6,32,2048]{2,1,0:T(8,128)(2,1)S(1)}, u32[]{:S(2)}) copy-start(bf16[6,32,2048]{2,1,0:T(8,128)(2,1)S(1)} %collective-permute-done.5.refs_2_) | copy-start | bytes 2359300
  54.3 7.9 %collective-permute-start.7 = (bf16[2,64,864]{2,1,0:T(8,128)(2,1)}, bf16[2,64,864]{2,1,0:T(8,128)(2,1)S(1)}, u32[]{:S(2)}, u32[]{:S(2)}) collective-permute-start(bf16[2,64,864]{2,1,0:T(8,128)(2,1)} %get-tuple-element.45), channel_id=1, source_target_pairs={{0,2},{2,0},{1,3},{3,1},{4,6},{6,4},{5,7},{7,5},{8,10},{10,8},{9,1... | collective-permute-start | bytes 663560 | tf_op jit(solution)/shard_map/ppermute | solution.py:30
  63.2 11.4 %collective-permute-start.10 = (bf16[64,864]{1,0:T(8,128)(2,1)S(1)}, bf16[64,864]{1,0:T(8,128)(2,1)S(1)}, u32[]{:S(2)}, u32[]{:S(2)}) collective-permute-start(bf16[64,864]{1,0:T(8,128)(2,1)S(1)} %get-tuple-element.50), channel_id=1, source_target_pairs={{0,8},{1,12},{4,9},{5,13},{8,0},{9,4},{12,1},{13,5},{2,10},{3,14},... | collective-permute-start | bytes 331784 | tf_op jit(solution)/shard_map/ppermute | solution.py:431
  63.8 10.7 %collective-permute-start.11 = (bf16[64,864]{1,0:T(8,128)(2,1)S(1)}, bf16[64,864]{1,0:T(8,128)(2,1)S(1)}, u32[]{:S(2)}, u32[]{:S(2)}) collective-permute-start(bf16[64,864]{1,0:T(8,128)(2,1)S(1)} %get-tuple-element.49), channel_id=1, source_target_pairs={{0,9},{1,13},{4,8},{5,12},{8,1},{9,5},{12,0},{13,4},{2,11},{3,15},... | collective-permute-start | bytes 331784 | tf_op jit(solution)/shard_map/ppermute | solution.py:431
  63.9 10.7 %collective-permute-start.8 = (bf16[64,864]{1,0:T(8,128)(2,1)S(1)}, bf16[64,864]{1,0:T(8,128)(2,1)S(1)}, u32[]{:S(2)}, u32[]{:S(2)}) collective-permute-start(bf16[64,864]{1,0:T(8,128)(2,1)S(1)} %get-tuple-element.52), channel_id=1, source_target_pairs={{0,0},{1,4},{4,1},{5,5},{8,8},{9,12},{12,9},{13,13},{2,2},{3,6},{6... | collective-permute-start | bytes 331784 | tf_op jit(solution)/shard_map/ppermute | solution.py:431
  64.6 12.6 %collective-permute-start.9 = (bf16[64,864]{1,0:T(8,128)(2,1)S(1)}, bf16[64,864]{1,0:T(8,128)(2,1)S(1)}, u32[]{:S(2)}, u32[]{:S(2)}) collective-permute-start(bf16[64,864]{1,0:T(8,128)(2,1)S(1)} %get-tuple-element.51), channel_id=1, source_target_pairs={{0,1},{1,5},{4,0},{5,4},{8,9},{9,13},{12,8},{13,12},{2,3},{3,7},{6... | collective-permute-start | bytes 331784 | tf_op jit(solution)/shard_map/ppermute | solution.py:431
  74.6 2.6 %copy-start.4 = (bf16[64,864]{1,0:T(8,128)(2,1)}, bf16[64,864]{1,0:T(8,128)(2,1)S(1)}, u32[]{:S(2)}) copy-start(bf16[64,864]{1,0:T(8,128)(2,1)S(1)} %collective-permute-done.10.refs_2_) | copy-start | bytes 331780
  74.6 2.6 %copy-start.5 = (bf16[64,864]{1,0:T(8,128)(2,1)}, bf16[64,864]{1,0:T(8,128)(2,1)S(1)}, u32[]{:S(2)}) copy-start(bf16[64,864]{1,0:T(8,128)(2,1)S(1)} %collective-permute-done.11.refs_3_) | copy-start | bytes 331780
  74.6 2.5 %copy-start.6 = (bf16[64,864]{1,0:T(8,128)(2,1)}, bf16[64,864]{1,0:T(8,128)(2,1)S(1)}, u32[]{:S(2)}) copy-start(bf16[64,864]{1,0:T(8,128)(2,1)S(1)} %collective-permute-done.8.refs_0_) | copy-start | bytes 331780
  77.2 0.6 copy-start.7

commit v10 on v9

--- a/solution.py
+++ b/solution.py
@@ -20,7 +20,7 @@
 LOW = jnp.bfloat16
 WIDE = jnp.float32
 STEP = 2
-VMEM_LIMIT = 56 * 1024 * 1024
+VMEM_LIMIT = 40 * 1024 * 1024
 VMEM = pl.BlockSpec(memory_space=pltpu.VMEM)
 SMEM = pl.BlockSpec(memory_space=pltpu.SMEM)
 
@@ -209,7 +209,7 @@
 
 
 def second_kernel(
-    field_ref, inner_ref, rim_ref, ahead_ref, behind_ref, link_ref, back_ref, out_ref, most_ref, token_ref, edge_ref
+    field_ref, inner_ref, rim_ref, ahead_ref, behind_ref, link_ref, back_ref, out_ref, token_ref, edge_ref
 ):
     layers = field_ref.shape[2] // PLANE
     token_ref[...] = jnp.zeros_like(token_ref)
@@ -239,10 +239,7 @@
                 if layer in (0, layers - 1):
                     extra = [KAPPA * a for a in load(field_ref, rows, lanes_at(layer, tile))]
                 new = one_step(layer, layers, tile, rows, fetch, link_ref, back_ref, extra)
-                if layer in (0, layers - 1):
-                    store(most_ref, rows, lanes_at(min(layer, 1), tile), new)
-                else:
-                    store(out_ref, rows, lanes_at(layer - 1, tile), new)
+                store(out_ref, rows, lanes_at(layer, tile), new)
 
 
 def face_kernel(most_ref, ahead_ref, behind_ref, link_ref, token_ref, out_ref):
@@ -256,14 +253,14 @@
             store(out_ref, rows, lanes, [a + KAPPA * b for a, b in new])
             hop = [None] * 6
             add_hop(hop, link_at(link_ref, 0, layers - 1, tile), load(ahead_ref, rows, lanes), False)
-            new = zip(load(most_ref, rows, high), hop)
+            new = zip(load(most_ref, rows, lanes_at(layers - 1, tile)), hop)
             store(out_ref, rows, high, [a + KAPPA * b for a, b in new])
 
 
-def product_kernel(columns, count, scale, slot_ref, inner_ref, face_ref, table_ref, *refs):
+def product_kernel(columns, count, scale, slot_ref, most_ref, face_ref, table_ref, *refs):
     groups = len(columns)
     raw_refs, out_refs, (total_ref, left_ref, right_ref) = refs[:groups], refs[groups:-3], refs[-3:]
-    vectors = inner_ref.shape[1]
+    vectors = most_ref.shape[1]
     layers = table_ref.shape[2] // PLANE
     depth = 6 * LANES
     step = left_ref.shape[1] // depth
@@ -301,7 +298,7 @@
 
     @pl.loop(0, (layers - 2) * blocks)
     def _(block):
-        add(inner_ref, lambda part: (lanes_at(0, block * step + part), lanes_at(1, block * step + part)))
+        add(most_ref, lambda part: (lanes_at(1, block * step + part),) * 2)
 
     @pl.loop(0, 2 * blocks)
     def _(block):
@@ -327,13 +324,14 @@
             out_ref[rows, :] = block[part * width : (part + 1) * width]
 
 
-def call(kernel, name, shapes, operands, flops=0, scratch=(), smem=False):
+def call(kernel, name, shapes, operands, flops=0, scratch=(), smem=False, alias=None):
     return pl.pallas_call(
         kernel,
         out_shape=tuple(jax.ShapeDtypeStruct(shape, dtype) for shape, dtype in shapes),
         in_specs=[SMEM if smem and i == 0 else VMEM for i in range(len(operands))],
         out_specs=(VMEM,) * len(shapes),
         scratch_shapes=list(scratch),
+        input_output_aliases=alias or {},
         compiler_params=pltpu.CompilerParams(vmem_limit_bytes=VMEM_LIMIT),
         cost_estimate=pl.CostEstimate(flops=flops, bytes_accessed=BYTES, transcendentals=0),
         name=name,
@@ -378,11 +376,12 @@
         flops=1 << 24,
         smem=True,
     )
-    smeared, most, token = call(
+    most, token = call(
         second_kernel,
         "second",
-        (((6, width, sites - 2 * PLANE), WIDE), ((6, width, 2 * PLANE), WIDE), ((8, LANES), WIDE)),
+        ((full, WIDE), ((8, LANES), WIDE)),
         (field, inner, rim, ahead, behind, links, back),
+        alias={0: 0},
         flops=1 << 25,
         scratch=(pltpu.VMEM((6, width, 2 * PLANE), WIDE),),
     )
@@ -406,7 +405,7 @@
         functools.partial(product_kernel, [-a % vecs for a, b in offsets], count, scale),
         "product",
         (((subs, 2 * width, columns), LOW),) * vecs,
-        (slots, smeared, faces, table, *raws),
+        (slots, most, faces, table, *raws),
         flops=1 << 32,
         scratch=(
             pltpu.VMEM((groups * 2 * width, columns), WIDE),

time: 80.3 us -> 67.2 us (0.84)
  Pallas kernels: 42.6 us -> 29.1 us
  waiting for transfers between devices: 15.3 us -> 18.3 us
  other arithmetic: 1.54 us -> 0.13 us
    pallas_call x7, Pallas kernels: 42.6 us -> 29.1 us  [call(): pl.pallas_call(kernel, out_shape=tuple((jax.ShapeDtypeStruct(shape, dtype...]
    ppermute x8, waiting for transfers between devices: 7.38 us -> 10.1 us  [shifted(): lax.ppermute(array, axis, [(i, (i + by) % peers) for i in range(peers)])]
    select_n x1, other arithmetic: 0.99 us -> 0.05 us  [shards(): block = jnp.where(place == a, held[a], block)]
    unnamed x25 -> x13, local copies, waits for them, and re-layouts: 2.94 us -> 2.53 us
  transfers between devices with their start and end apart: 12 -> 12, of which waited for: 3 -> 5; matrix products, arithmetic and copies ran while one was open for 2% -> 0% of each run, Pallas kernels for 28% -> 20%
where the time goes in v10:
time: 67.2 us; the launch traced here: 66.9 us
  Pallas kernels  29.1 us (43%)
  waiting for transfers between devices  18.3 us (27%)
  starting transfers between devices  16.7 us (25%)
  local copies, waits for them, and re-layouts  2.57 us (4%)
    pallas_call x7, Pallas kernels, call(): pl.pallas_call(kernel, out_shape=tuple((jax.ShapeDtypeStruct(shape, dtype...  29.1 us
    ppermute x8, starting transfers between devices, shifted(): lax.ppermute(array, axis, [(i, (i + by) % peers) for i in range(peers)])  11 us
    ppermute x8, waiting for transfers between devices, shifted(): lax.ppermute(array, axis, [(i, (i + by) % peers) for i in range(peers)])  10.1 us
    ppermute x4, waiting for transfers between devices, shards(): shares.append(lax.ppermute(block[r], ('brick', 'sub'), pairs))  8.15 us
    ppermute x4, starting transfers between devices, shards(): shares.append(lax.ppermute(block[r], ('brick', 'sub'), pairs))  5.64 us
    unnamed x13, local copies, waits for them, and re-layouts  2.53 us
  transfers between devices with their start and end apart: 12, of which 5 were waited for; matrix products, arithmetic and copies ran while one was open for 0% of the time, Pallas kernels for 20%

profile of v10, /device:TPU:0, one launch (start us, length us, event | category | flops | bytes accessed | tf_op | source)
XLA Modules:
  0.0 66.9 jit_solution(10283763281662182531)
XLA Ops:
  0.0 1.0 %copy-done = f32[3,3,3,2,2048]{4,3,2,1,0:T(2,128)S(1)} copy-done((f32[3,3,3,2,2048]{4,3,2,1,0:T(2,128)S(1)}, f32[3,3,3,2,2048]{4,3,2,1,0:T(2,128)}, u32[]{:S(2)}) %copy-start) | copy-done | bytes 442392
  1.0 1.4 %copy-done.2 = f32[32,3,2,2048]{3,2,1,0:T(2,128)S(1)} copy-done((f32[32,3,2,2048]{3,2,1,0:T(2,128)S(1)}, f32[32,3,2,2048]{3,2,1,0:T(2,128)}, u32[]{:S(2)}) %copy-start.2) | copy-done | bytes 1572888
  2.4 2.2 %open.1 = (f32[6,32,2048]{2,1,0:T(8,128)S(1)}, bf16[6,32,2048]{2,1,0:T(8,128)(2,1)}, bf16[6,32,512]{2,1,0:T(8,128)(2,1)}, bf16[6,32,512]{2,1,0:T(8,128)(2,1)}) custom-call(f32[3072,128]{1,0:T(8,128)S(1)} %bitcast.27, f32[864,128]{1,0:T(8,128)S(1)} %bitcast.22), custom_call_target="tpu_custom_call" | custom-call | flops 4194304 | bytes 1048576 | tf_op jit(solution)/shard_map/open/pallas_call | solution.py:328
  4.6 2.9 %collective-permute-start.2 = (bf16[6,32,2048]{2,1,0:T(8,128)(2,1)}, bf16[6,32,2048]{2,1,0:T(8,128)(2,1)}, u32[]{:S(2)}, u32[]{:S(2)}) collective-permute-start(bf16[6,32,2048]{2,1,0:T(8,128)(2,1)} %get-tuple-element.42.refs_0_), channel_id=1, source_target_pairs={{0,2},{2,0},{1,3},{3,1},{4,6},{6,4},{5,7},{7,5},{8,10},{10,8},{9,1... | collective-permute-start | bytes 2359304 | tf_op jit(solution)/shard_map/ppermute | solution.py:30
  7.5 3.6 %collective-permute-start = (bf16[6,32,512]{2,1,0:T(8,128)(2,1)}, bf16[6,32,512]{2,1,0:T(8,128)(2,1)S(1)}, u32[]{:S(2)}, u32[]{:S(2)}) collective-permute-start(bf16[6,32,512]{2,1,0:T(8,128)(2,1)} %get-tuple-element.29), channel_id=1, source_target_pairs={{0,12},{4,0},{8,4},{12,8},{1,13},{5,1},{9,5},{13,9},{2,14},{6,2},{... | collective-permute-start | bytes 589832 | tf_op jit(solution)/shard_map/ppermute | solution.py:30
  11.2 3.4 %rim.1 = (bf16[6,32,512]{2,1,0:T(8,128)(2,1)}, bf16[6,32,512]{2,1,0:T(8,128)(2,1)}, f32[6,32,1024]{2,1,0:T(8,128)S(1)}, f32[2,16,2048]{2,1,0:T(8,128)S(1)}) custom-call(f32[6,32,2048]{2,1,0:T(8,128)S(1)} %get-tuple-element.25.field_ref, f32[864,128]{1,0:T(8,128)S(1)} %bitcast.23), custom_call_target="tpu_custom_call" | custom-call | flops 16777216 | bytes 1048576 | tf_op jit(solution)/shard_map/rim/pallas_call | solution.py:328
  14.5 3.8 %collective-permute-start.3 = (bf16[6,32,512]{2,1,0:T(8,128)(2,1)}, bf16[6,32,512]{2,1,0:T(8,128)(2,1)}, u32[]{:S(2)}, u32[]{:S(2)}) collective-permute-start(bf16[6,32,512]{2,1,0:T(8,128)(2,1)} %get-tuple-element.33), channel_id=1, source_target_pairs={{0,12},{4,0},{8,4},{12,8},{1,13},{5,1},{9,5},{13,9},{2,14},{6,2},{... | collective-permute-start | bytes 589832 | tf_op jit(solution)/shard_map/ppermute | solution.py:30
  18.4 0.1 copy.7.momenta_ref
  18.5 3.3 %inner.1 = (f32[6,32,1024]{2,1,0:T(8,128)S(1)}, f32[2,27,2048]{2,1,0:T(8,128)S(1)}) custom-call(s32[1]{0:T(128)} %bitcast.8.place_ref, f32[6,32,2048]{2,1,0:T(8,128)S(1)} %get-tuple-element.25.field_ref, f32[864,128]{1,0:T(8,128)S(1)} %bitcast.24, f32[2,16,2048]{2,1,0:T(8,128)S(1)} %get-tuple-element.26.back_ref, s32[27,3]{1,0:T(8,128)S(1)} %copy.7.momenta_ref), custom_call_target="tpu_custom_call" | custom-call | flops 16777216 | bytes 1048576 | tf_op jit(solution)/shard_map/inner/pallas_call | solution.py:328
  21.8 5.2 %second.1 = (f32[6,32,2048]{2,1,0:T(8,128)S(1)}, f32[8,128]{1,0:T(8,128)S(1)}) custom-call(f32[6,32,2048]{2,1,0:T(8,128)S(1)} %get-tuple-element.25.field_ref, f32[6,32,1024]{2,1,0:T(8,128)S(1)} %get-tuple-element.27.inner_ref, f32[6,32,1024]{2,1,0:T(8,128)S(1)} %get-tuple-element.28.rim_ref, ...), custom_call_target="tpu_custom_call", output_to_operand_aliasing={{0}: (0, {})} | custom-call | flops 33554432 | bytes 1048576 | tf_op jit(solution)/shard_map/second/pallas_call | solution.py:328
  27.1 1.8 %collective-permute-done.4.behind_ref = bf16[6,32,512]{2,1,0:T(8,128)(2,1)} collective-permute-done((bf16[6,32,512]{2,1,0:T(8,128)(2,1)}, bf16[6,32,512]{2,1,0:T(8,128)(2,1)}, u32[]{:S(2)}, u32[]{:S(2)}) %collective-permute-start.4) | collective-permute-done | bytes 196640 | tf_op jit(solution)/shard_map/ppermute | solution.py:30
  28.9 0.1 pad_add_fusion.slot_ref
  29.0 1.4 %face.1.face_ref = f32[6,32,1024]{2,1,0:T(8,128)S(1)} custom-call(f32[6,32,2048]{2,1,0:T(8,128)S(1)} %get-tuple-element.31.most_ref, bf16[6,32,512]{2,1,0:T(8,128)(2,1)} %collective-permute-done.3.ahead_ref, bf16[6,32,512]{2,1,0:T(8,128)(2,1)} %collective-permute-done.4.behind_ref, f32[864,128]{1,0:T(8,128)S(1)} %bitcast.26, ...), custom_call_target="tpu_custom_call" | custom-call | flops 4194304 | bytes 1048576 | tf_op jit(solution)/shard_map/face/pallas_call | solution.py:328
  30.4 1.2 %collective-permute-done.6.refs_3_ = bf16[6,32,2048]{2,1,0:T(8,128)(2,1)} collective-permute-done((bf16[6,32,2048]{2,1,0:T(8,128)(2,1)}, bf16[6,32,2048]{2,1,0:T(8,128)(2,1)}, u32[]{:S(2)}, u32[]{:S(2)}) %collective-permute-start.6) | collective-permute-done | bytes 786464 | tf_op jit(solution)/shard_map/ppermute | solution.py:30
  31.6 12.6 %product.1 = (bf16[2,64,864]{2,1,0:T(8,128)(2,1)S(1)}, bf16[2,64,864]{2,1,0:T(8,128)(2,1)S(1)}) custom-call(s32[4]{0:T(128)S(1)} %pad_add_fusion.slot_ref, f32[6,32,2048]{2,1,0:T(8,128)S(1)} %get-tuple-element.31.most_ref, f32[6,32,1024]{2,1,0:T(8,128)S(1)} %face.1.face_ref, f32[2,27,2048]{2,1,0:T(8,128)S(1)} %copy-done.4, ...), custom_call_target="tpu_custom_call" | custom-call | flops 4294967296 | bytes 1048576 | tf_op jit(solution)/shard_map/product/pallas_call | solution.py:328
  44.2 0.6 collective-permute-start.7
  44.8 7.1 %collective-permute-done.7 = bf16[2,64,864]{2,1,0:T(8,128)(2,1)S(1)} collective-permute-done((bf16[2,64,864]{2,1,0:T(8,128)(2,1)S(1)}, bf16[2,64,864]{2,1,0:T(8,128)(2,1)S(1)}, u32[]{:S(2)}, u32[]{:S(2)}) %collective-permute-start.7) | collective-permute-done | bytes 221216 | tf_op jit(solution)/shard_map/ppermute | solution.py:30
  51.9 1.8 %collective-permute-start.10 = (bf16[64,864]{1,0:T(8,128)(2,1)S(1)}, bf16[64,864]{1,0:T(8,128)(2,1)S(1)}, u32[]{:S(2)}, u32[]{:S(2)}) collective-permute-start(bf16[64,864]{1,0:T(8,128)(2,1)S(1)} %get-tuple-element.48), channel_id=1, source_target_pairs={{0,8},{1,12},{4,9},{5,13},{8,0},{9,4},{12,1},{13,5},{2,10},{3,14},... | collective-permute-start | bytes 331784 | tf_op jit(solution)/shard_map/ppermute | solution.py:430
  53.7 1.1 %collective-permute-start.11 = (bf16[64,864]{1,0:T(8,128)(2,1)S(1)}, bf16[64,864]{1,0:T(8,128)(2,1)S(1)}, u32[]{:S(2)}, u32[]{:S(2)}) collective-permute-start(bf16[64,864]{1,0:T(8,128)(2,1)S(1)} %get-tuple-element.47), channel_id=1, source_target_pairs={{0,9},{1,13},{4,8},{5,12},{8,1},{9,5},{12,0},{13,4},{2,11},{3,15},... | collective-permute-start | bytes 331784 | tf_op jit(solution)/shard_map/ppermute | solution.py:430
  54.8 0.7 collective-permute-start.8
  55.5 2.1 %collective-permute-start.9 = (bf16[64,864]{1,0:T(8,128)(2,1)S(1)}, bf16[64,864]{1,0:T(8,128)(2,1)S(1)}, u32[]{:S(2)}, u32[]{:S(2)}) collective-permute-start(bf16[64,864]{1,0:T(8,128)(2,1)S(1)} %get-tuple-element.49), channel_id=1, source_target_pairs={{0,1},{1,5},{4,0},{5,4},{8,9},{9,13},{12,8},{13,12},{2,3},{3,7},{6... | collective-permute-start | bytes 331784 | tf_op jit(solution)/shard_map/ppermute | solution.py:430
  57.6 5.7 %collective-permute-done.10.refs_2_ = bf16[64,864]{1,0:T(8,128)(2,1)S(1)} collective-permute-done((bf16[64,864]{1,0:T(8,128)(2,1)S(1)}, bf16[64,864]{1,0:T(8,128)(2,1)S(1)}, u32[]{:S(2)}, u32[]{:S(2)}) %collective-permute-start.10) | collective-permute-done | bytes 110624 | tf_op jit(solution)/shard_map/ppermute | solution.py:430
  63.3 2.5 %collective-permute-done.9.refs_1_ = bf16[64,864]{1,0:T(8,128)(2,1)S(1)} collective-permute-done((bf16[64,864]{1,0:T(8,128)(2,1)S(1)}, bf16[64,864]{1,0:T(8,128)(2,1)S(1)}, u32[]{:S(2)}, u32[]{:S(2)}) %collective-permute-start.9) | collective-permute-done | bytes 110624 | tf_op jit(solution)/shard_map/ppermute | solution.py:430
  65.8 1.2 %sum.1 = f32[1728,32]{1,0:T(8,128)} custom-call(bf16[64,864]{1,0:T(8,128)(2,1)S(1)} %collective-permute-done.8.refs_0_, bf16[64,864]{1,0:T(8,128)(2,1)S(1)} %collective-permute-done.9.refs_1_, bf16[64,864]{1,0:T(8,128)(2,1)S(1)} %collective-permute-done.10.refs_2_, bf16[64,864]{1,0:T(8,128)(2,1)S(1)} %collective-permute-done.11.refs_3_), custom_call_target="tpu_custom_call" | custom-call | flops 1048576 | bytes 1048576 | tf_op jit(solution)/shard_map/sum/pallas_call | solution.py:328
  (24 shorter events, 0.2 us)
Async XLA Ops:
  0.0 1.0 %copy-start = (f32[3,3,3,2,2048]{4,3,2,1,0:T(2,128)S(1)}, f32[3,3,3,2,2048]{4,3,2,1,0:T(2,128)}, u32[]{:S(2)}) copy-start(f32[3,3,3,2,2048]{4,3,2,1,0:T(2,128)} %param.4) | copy-start | bytes 1327108
  1.0 1.4 %copy-start.2 = (f32[32,3,2,2048]{3,2,1,0:T(2,128)S(1)}, f32[32,3,2,2048]{3,2,1,0:T(2,128)}, u32[]{:S(2)}) copy-start(f32[32,3,2,2048]{3,2,1,0:T(2,128)} %param.3) | copy-start | bytes 4718596
  2.4 15.9 %copy-start.5 = (s32[27,3]{0,1:T(4,128)S(1)}, s32[27,3]{0,1:T(4,128)}, u32[]{:S(2)}) copy-start(s32[27,3]{0,1:T(4,128)} %param.5) | copy-start | bytes 976
  2.4 16.0 %copy-start.1 = (f32[3,3,3,2,2048]{4,3,2,1,0:T(2,128)S(1)}, f32[3,3,3,2,2048]{4,3,2,1,0:T(2,128)}, u32[]{:S(2)}) copy-start(f32[3,3,3,2,2048]{4,3,2,1,0:T(2,128)} %param.4) | copy-start | bytes 1327108
  4.6 24.3 %collective-permute-start.2 = (bf16[6,32,2048]{2,1,0:T(8,128)(2,1)}, bf16[6,32,2048]{2,1,0:T(8,128)(2,1)}, u32[]{:S(2)}, u32[]{:S(2)}) collective-permute-start(bf16[6,32,2048]{2,1,0:T(8,128)(2,1)} %get-tuple-element.42.refs_0_), channel_id=1, source_target_pairs={{0,2},{2,0},{1,3},{3,1},{4,6},{6,4},{5,7},{7,5},{8,10},{10,8},{9,1... | collective-permute-start | bytes 2359304 | tf_op jit(solution)/shard_map/ppermute | solution.py:30
  7.5 14.2 %collective-permute-start = (bf16[6,32,512]{2,1,0:T(8,128)(2,1)}, bf16[6,32,512]{2,1,0:T(8,128)(2,1)S(1)}, u32[]{:S(2)}, u32[]{:S(2)}) collective-permute-start(bf16[6,32,512]{2,1,0:T(8,128)(2,1)} %get-tuple-element.29), channel_id=1, source_target_pairs={{0,12},{4,0},{8,4},{12,8},{1,13},{5,1},{9,5},{13,9},{2,14},{6,2},{... | collective-permute-start | bytes 589832 | tf_op jit(solution)/shard_map/ppermute | solution.py:30
  11.2 10.6 %collective-permute-start.1 = (bf16[6,32,512]{2,1,0:T(8,128)(2,1)}, bf16[6,32,512]{2,1,0:T(8,128)(2,1)S(1)}, u32[]{:S(2)}, u32[]{:S(2)}) collective-permute-start(bf16[6,32,512]{2,1,0:T(8,128)(2,1)} %get-tuple-element.30), channel_id=1, source_target_pairs={{0,4},{4,8},{8,12},{12,0},{1,5},{5,9},{9,13},{13,1},{2,6},{6,10},{... | collective-permute-start | bytes 589832 | tf_op jit(solution)/shard_map/ppermute | solution.py:30
  14.5 12.6 %collective-permute-start.3 = (bf16[6,32,512]{2,1,0:T(8,128)(2,1)}, bf16[6,32,512]{2,1,0:T(8,128)(2,1)}, u32[]{:S(2)}, u32[]{:S(2)}) collective-permute-start(bf16[6,32,512]{2,1,0:T(8,128)(2,1)} %get-tuple-element.33), channel_id=1, source_target_pairs={{0,12},{4,0},{8,4},{12,8},{1,13},{5,1},{9,5},{13,9},{2,14},{6,2},{... | collective-permute-start | bytes 589832 | tf_op jit(solution)/shard_map/ppermute | solution.py:30
  18.3 10.6 %collective-permute-start.4 = (bf16[6,32,512]{2,1,0:T(8,128)(2,1)}, bf16[6,32,512]{2,1,0:T(8,128)(2,1)}, u32[]{:S(2)}, u32[]{:S(2)}) collective-permute-start(bf16[6,32,512]{2,1,0:T(8,128)(2,1)} %get-tuple-element.34), channel_id=1, source_target_pairs={{0,4},{4,8},{8,12},{12,0},{1,5},{5,9},{9,13},{13,1},{2,6},{6,10},{... | collective-permute-start | bytes 589832 | tf_op jit(solution)/shard_map/ppermute | solution.py:30
  21.8 5.3 %copy-start.3 = (f32[2,27,2048]{2,1,0:T(8,128)}, f32[2,27,2048]{2,1,0:T(8,128)S(1)}, u32[]{:S(2)}) copy-start(f32[2,27,2048]{2,1,0:T(8,128)S(1)} %get-tuple-element.40.table_ref) | copy-start | bytes 1327108
  27.0 3.4 %collective-permute-start.5 = (bf16[6,32,2048]{2,1,0:T(8,128)(2,1)}, bf16[6,32,2048]{2,1,0:T(8,128)(2,1)S(1)}, u32[]{:S(2)}, u32[]{:S(2)}) collective-permute-start(bf16[6,32,2048]{2,1,0:T(8,128)(2,1)} %get-tuple-element.42.refs_0_), channel_id=1, source_target_pairs={{0,1},{1,0},{2,3},{3,2},{4,5},{5,4},{6,7},{7,6},{8,9},{9,8},{10,11... | collective-permute-start | bytes 2359304 | tf_op jit(solution)/shard_map/ppermute | solution.py:30
  28.9 2.6 %collective-permute-start.6 = (bf16[6,32,2048]{2,1,0:T(8,128)(2,1)}, bf16[6,32,2048]{2,1,0:T(8,128)(2,1)}, u32[]{:S(2)}, u32[]{:S(2)}) collective-permute-start(bf16[6,32,2048]{2,1,0:T(8,128)(2,1)} %collective-permute-done.2.refs_1_), channel_id=1, source_target_pairs={{0,1},{1,0},{2,3},{3,2},{4,5},{5,4},{6,7},{7,6},{8,9},{9,8},{10,11... | collective-permute-start | bytes 2359304 | tf_op jit(solution)/shard_map/ppermute | solution.py:30
  29.0 2.6 %copy-start.4 = (f32[2,27,2048]{2,1,0:T(8,128)S(1)}, f32[2,27,2048]{2,1,0:T(8,128)}, u32[]{:S(2)}) copy-start(f32[2,27,2048]{2,1,0:T(8,128)} %copy-done.3) | copy-start | bytes 1327108
  44.2 7.7 %collective-permute-start.7 = (bf16[2,64,864]{2,1,0:T(8,128)(2,1)S(1)}, bf16[2,64,864]{2,1,0:T(8,128)(2,1)S(1)}, u32[]{:S(2)}, u32[]{:S(2)}) collective-permute-start(bf16[2,64,864]{2,1,0:T(8,128)(2,1)S(1)} %get-tuple-element.43), channel_id=1, source_target_pairs={{0,2},{2,0},{1,3},{3,1},{4,6},{6,4},{5,7},{7,5},{8,10},{10,8},{9,1... | collective-permute-start | bytes 663560 | tf_op jit(solution)/shard_map/ppermute | solution.py:30
  51.9 11.3 %collective-permute-start.10 = (bf16[64,864]{1,0:T(8,128)(2,1)S(1)}, bf16[64,864]{1,0:T(8,128)(2,1)S(1)}, u32[]{:S(2)}, u32[]{:S(2)}) collective-permute-start(bf16[64,864]{1,0:T(8,128)(2,1)S(1)} %get-tuple-element.48), channel_id=1, source_target_pairs={{0,8},{1,12},{4,9},{5,13},{8,0},{9,4},{12,1},{13,5},{2,10},{3,14},... | collective-permute-start | bytes 331784 | tf_op jit(solution)/shard_map/ppermute | solution.py:430
  53.7 9.5 %collective-permute-start.11 = (bf16[64,864]{1,0:T(8,128)(2,1)S(1)}, bf16[64,864]{1,0:T(8,128)(2,1)S(1)}, u32[]{:S(2)}, u32[]{:S(2)}) collective-permute-start(bf16[64,864]{1,0:T(8,128)(2,1)S(1)} %get-tuple-element.47), channel_id=1, source_target_pairs={{0,9},{1,13},{4,8},{5,12},{8,1},{9,5},{12,0},{13,4},{2,11},{3,15},... | collective-permute-start | bytes 331784 | tf_op jit(solution)/shard_map/ppermute | solution.py:430
  54.8 8.4 %collective-permute-start.8 = (bf16[64,864]{1,0:T(8,128)(2,1)S(1)}, bf16[64,864]{1,0:T(8,128)(2,1)S(1)}, u32[]{:S(2)}, u32[]{:S(2)}) collective-permute-start(bf16[64,864]{1,0:T(8,128)(2,1)S(1)} %get-tuple-element.50), channel_id=1, source_target_pairs={{0,0},{1,4},{4,1},{5,5},{8,8},{9,12},{12,9},{13,13},{2,2},{3,6},{6... | collective-permute-start | bytes 331784 | tf_op jit(solution)/shard_map/ppermute | solution.py:430
  55.5 10.3 %collective-permute-start.9 = (bf16[64,864]{1,0:T(8,128)(2,1)S(1)}, bf16[64,864]{1,0:T(8,128)(2,1)S(1)}, u32[]{:S(2)}, u32[]{:S(2)}) collective-permute-start(bf16[64,864]{1,0:T(8,128)(2,1)S(1)} %get-tuple-element.49), channel_id=1, source_target_pairs={{0,1},{1,5},{4,0},{5,4},{8,9},{9,13},{12,8},{13,12},{2,3},{3,7},{6... | collective-permute-start | bytes 331784 | tf_op jit(solution)/shard_map/ppermute | solution.py:430

commit v11 on v10

--- a/solution.py
+++ b/solution.py
@@ -22,6 +22,7 @@
 STEP = 2
 VMEM_LIMIT = 40 * 1024 * 1024
 VMEM = pl.BlockSpec(memory_space=pltpu.VMEM)
+AWAY = pl.BlockSpec(memory_space=pltpu.HBM)
 SMEM = pl.BlockSpec(memory_space=pltpu.SMEM)
 
 
@@ -179,7 +180,8 @@
     return 1.0 - 2.0 * sine * sine, 2.0 * sine * cosine
 
 
-def inner_kernel(total_x, place_ref, field_ref, link_ref, back_ref, momenta_ref, out_ref, table_ref):
+def inner_kernel(total_x, place_ref, field_ref, link_ref, back_ref, momenta_ref, *refs):
+    out_ref, table_ref = refs[-2:]
     layers = field_ref.shape[2] // PLANE
     count = momenta_ref.shape[0]
     momenta = momenta_ref[...].astype(WIDE)
@@ -324,11 +326,11 @@
             out_ref[rows, :] = block[part * width : (part + 1) * width]
 
 
-def call(kernel, name, shapes, operands, flops=0, scratch=(), smem=False, alias=None):
+def call(kernel, name, shapes, operands, flops=0, scratch=(), smem=False, alias=None, away=0):
     return pl.pallas_call(
         kernel,
         out_shape=tuple(jax.ShapeDtypeStruct(shape, dtype) for shape, dtype in shapes),
-        in_specs=[SMEM if smem and i == 0 else VMEM for i in range(len(operands))],
+        in_specs=([SMEM] if smem else []) + [VMEM] * (len(operands) - smem - away) + [AWAY] * away,
         out_specs=(VMEM,) * len(shapes),
         scratch_shapes=list(scratch),
         input_output_aliases=alias or {},
@@ -359,6 +361,7 @@
     )
     ahead, behind = shifted(down, "brick", -1), shifted(up, "brick", 1)
     across = [shifted(raw, "vec", a) for a in range(1, vecs)]
+    beside = [shifted(raw, "sub", b) for b in range(1, subs)]
     down_two, up_two, rim, back = call(
         rim_kernel,
         "rim",
@@ -372,7 +375,8 @@
         functools.partial(inner_kernel, total_x),
         "inner",
         (((6, width, sites - 2 * PLANE), WIDE), ((2, count, sites), WIDE)),
-        (place, field, links, back, momenta),
+        (place, field, links, back, momenta, *beside),
+        away=subs - 1,
         flops=1 << 24,
         smem=True,
     )
@@ -385,10 +389,10 @@
         flops=1 << 25,
         scratch=(pltpu.VMEM((6, width, 2 * PLANE), WIDE),),
     )
-    late, token = lax.optimization_barrier((raw, token))
     *across, ahead_two, behind_two, token = lax.optimization_barrier((*across, ahead_two, behind_two, token))
-    raws = [raw, *across] + [shifted(array, "sub", b) for b in range(1, subs) for array in (late, *across)]
-    offsets = [(a, b) for b in range(subs) for a in range(vecs)]
+    raws = [raw, *across, *beside] + [shifted(array, "sub", b) for b in range(1, subs) for array in across]
+    offsets = [(a, 0) for a in range(vecs)] + [(0, b) for b in range(1, subs)]
+    offsets += [(a, b) for b in range(1, subs) for a in range(1, vecs)]
     (faces,) = call(
         face_kernel,
         "face",

time: 67.2 us -> 67.5 us (level)
  local copies, waits for them, and re-layouts: 2.57 us -> 4.63 us
  waiting for transfers between devices: 18.3 us -> 16.8 us
    unnamed x13 -> x19, local copies, waits for them, and re-layouts: 2.53 us -> 4.59 us
    ppermute x8, waiting for transfers between devices: 10.1 us -> 8.64 us  [shifted(): lax.ppermute(array, axis, [(i, (i + by) % peers) for i in range(peers)])]
where the time goes in v11:
time: 67.5 us; the launch traced here: 67.2 us
  Pallas kernels  29 us (43%)
  waiting for transfers between devices  16.8 us (25%)
  starting transfers between devices  16.6 us (25%)
  local copies, waits for them, and re-layouts  4.63 us (7%)
    pallas_call x7, Pallas kernels, call(): pl.pallas_call(kernel, out_shape=tuple((jax.ShapeDtypeStruct(shape, dtype...  29 us
    ppermute x8, starting transfers between devices, shifted(): lax.ppermute(array, axis, [(i, (i + by) % peers) for i in range(peers)])  11 us
    ppermute x8, waiting for transfers between devices, shifted(): lax.ppermute(array, axis, [(i, (i + by) % peers) for i in range(peers)])  8.64 us
    ppermute x4, waiting for transfers between devices, shards(): shares.append(lax.ppermute(block[r], ('brick', 'sub'), pairs))  8.15 us
    ppermute x4, starting transfers between devices, shards(): shares.append(lax.ppermute(block[r], ('brick', 'sub'), pairs))  5.64 us
    unnamed x19, local copies, waits for them, and re-layouts  4.59 us
  transfers between devices with their start and end apart: 12, of which 5 were waited for; matrix products, arithmetic and copies ran while one was open for 0% of the time, Pallas kernels for 20%

profile of v11, /device:TPU:0, one launch (start us, length us, event | category | flops | bytes accessed | tf_op | source)
XLA Modules:
  0.0 67.2 jit_solution(7956544844972742835)
XLA Ops:
  0.0 1.0 %copy-done = f32[3,3,3,2,2048]{4,3,2,1,0:T(2,128)S(1)} copy-done((f32[3,3,3,2,2048]{4,3,2,1,0:T(2,128)S(1)}, f32[3,3,3,2,2048]{4,3,2,1,0:T(2,128)}, u32[]{:S(2)}) %copy-start) | copy-done | bytes 442392
  1.0 1.4 %copy-done.2 = f32[32,3,2,2048]{3,2,1,0:T(2,128)S(1)} copy-done((f32[32,3,2,2048]{3,2,1,0:T(2,128)S(1)}, f32[32,3,2,2048]{3,2,1,0:T(2,128)}, u32[]{:S(2)}) %copy-start.2) | copy-done | bytes 1572888
  2.4 2.2 %open.1 = (f32[6,32,2048]{2,1,0:T(8,128)S(1)}, bf16[6,32,2048]{2,1,0:T(8,128)(2,1)}, bf16[6,32,512]{2,1,0:T(8,128)(2,1)}, bf16[6,32,512]{2,1,0:T(8,128)(2,1)}) custom-call(f32[3072,128]{1,0:T(8,128)S(1)} %bitcast.27, f32[864,128]{1,0:T(8,128)S(1)} %bitcast.22), custom_call_target="tpu_custom_call" | custom-call | flops 4194304 | bytes 1048576 | tf_op jit(solution)/shard_map/open/pallas_call | solution.py:330
  5.1 2.5 %collective-permute-start.3 = (bf16[6,32,2048]{2,1,0:T(8,128)(2,1)}, bf16[6,32,2048]{2,1,0:T(8,128)(2,1)}, u32[]{:S(2)}, u32[]{:S(2)}) collective-permute-start(bf16[6,32,2048]{2,1,0:T(8,128)(2,1)} %get-tuple-element.25.refs_0_), channel_id=1, source_target_pairs={{0,2},{2,0},{1,3},{3,1},{4,6},{6,4},{5,7},{7,5},{8,10},{10,8},{9,1... | collective-permute-start | bytes 2359304 | tf_op jit(solution)/shard_map/ppermute | solution.py:31
  7.6 3.6 %collective-permute-start.1 = (bf16[6,32,512]{2,1,0:T(8,128)(2,1)}, bf16[6,32,512]{2,1,0:T(8,128)(2,1)S(1)}, u32[]{:S(2)}, u32[]{:S(2)}) collective-permute-start(bf16[6,32,512]{2,1,0:T(8,128)(2,1)} %get-tuple-element.28), channel_id=1, source_target_pairs={{0,12},{4,0},{8,4},{12,8},{1,13},{5,1},{9,5},{13,9},{2,14},{6,2},{... | collective-permute-start | bytes 589832 | tf_op jit(solution)/shard_map/ppermute | solution.py:31
  11.2 3.4 %rim.1 = (bf16[6,32,512]{2,1,0:T(8,128)(2,1)}, bf16[6,32,512]{2,1,0:T(8,128)(2,1)}, f32[6,32,1024]{2,1,0:T(8,128)S(1)}, f32[2,16,2048]{2,1,0:T(8,128)S(1)}) custom-call(f32[6,32,2048]{2,1,0:T(8,128)S(1)} %get-tuple-element.23.field_ref, f32[864,128]{1,0:T(8,128)S(1)} %bitcast.23), custom_call_target="tpu_custom_call" | custom-call | flops 16777216 | bytes 1048576 | tf_op jit(solution)/shard_map/rim/pallas_call | solution.py:330
  14.5 3.8 %collective-permute-start.4 = (bf16[6,32,512]{2,1,0:T(8,128)(2,1)}, bf16[6,32,512]{2,1,0:T(8,128)(2,1)}, u32[]{:S(2)}, u32[]{:S(2)}) collective-permute-start(bf16[6,32,512]{2,1,0:T(8,128)(2,1)} %get-tuple-element.31), channel_id=1, source_target_pairs={{0,12},{4,0},{8,4},{12,8},{1,13},{5,1},{9,5},{13,9},{2,14},{6,2},{... | collective-permute-start | bytes 589832 | tf_op jit(solution)/shard_map/ppermute | solution.py:31
  18.4 0.9 %copy-done.3 = bf16[6,32,2048]{2,1,0:T(8,128)(2,1)} copy-done((bf16[6,32,2048]{2,1,0:T(8,128)(2,1)}, bf16[6,32,2048]{2,1,0:T(8,128)(2,1)S(1)}, u32[]{:S(2)}) %copy-start.3) | copy-done | bytes 786456
  19.4 1.1 %copy-done.4 = bf16[6,32,2048]{2,1,0:T(8,128)(2,1)S(1)} copy-done((bf16[6,32,2048]{2,1,0:T(8,128)(2,1)S(1)}, bf16[6,32,2048]{2,1,0:T(8,128)(2,1)}, u32[]{:S(2)}) %copy-start.4) | copy-done | bytes 786456
  20.5 3.3 %inner.1 = (f32[6,32,1024]{2,1,0:T(8,128)S(1)}, f32[2,27,2048]{2,1,0:T(8,128)S(1)}) custom-call(s32[1]{0:T(128)} %bitcast.8.place_ref, f32[6,32,2048]{2,1,0:T(8,128)S(1)} %get-tuple-element.23.field_ref, f32[864,128]{1,0:T(8,128)S(1)} %bitcast.24, f32[2,16,2048]{2,1,0:T(8,128)S(1)} %get-tuple-element.24.back_ref, s32[27,3]{1,0:T(8,128)S(1)} %copy.7.momenta_ref, ...), custom_call_target="tpu_custom_call" | custom-call | flops 16777216 | bytes 1048576 | tf_op jit(solution)/shard_map/inner/pallas_call | solution.py:330
  23.9 5.2 %second.1 = (f32[6,32,2048]{2,1,0:T(8,128)S(1)}, f32[8,128]{1,0:T(8,128)S(1)}) custom-call(f32[6,32,2048]{2,1,0:T(8,128)S(1)} %get-tuple-element.23.field_ref, f32[6,32,1024]{2,1,0:T(8,128)S(1)} %get-tuple-element.26.inner_ref, f32[6,32,1024]{2,1,0:T(8,128)S(1)} %get-tuple-element.27.rim_ref, ...), custom_call_target="tpu_custom_call", output_to_operand_aliasing={{0}: (0, {})} | custom-call | flops 33554432 | bytes 1048576 | tf_op jit(solution)/shard_map/second/pallas_call | solution.py:330
  29.1 0.5 collective-permute-done.5.behind_ref
  29.7 1.4 %face.1.face_ref = f32[6,32,1024]{2,1,0:T(8,128)S(1)} custom-call(f32[6,32,2048]{2,1,0:T(8,128)S(1)} %get-tuple-element.30.most_ref, bf16[6,32,512]{2,1,0:T(8,128)(2,1)} %collective-permute-done.4.ahead_ref, bf16[6,32,512]{2,1,0:T(8,128)(2,1)} %collective-permute-done.5.behind_ref, f32[864,128]{1,0:T(8,128)S(1)} %bitcast.26, ...), custom_call_target="tpu_custom_call" | custom-call | flops 4194304 | bytes 1048576 | tf_op jit(solution)/shard_map/face/pallas_call | solution.py:330
  31.1 1.0 %collective-permute-done.6.refs_3_ = bf16[6,32,2048]{2,1,0:T(8,128)(2,1)S(1)} collective-permute-done((bf16[6,32,2048]{2,1,0:T(8,128)(2,1)}, bf16[6,32,2048]{2,1,0:T(8,128)(2,1)S(1)}, u32[]{:S(2)}, u32[]{:S(2)}) %collective-permute-start.6) | collective-permute-done | bytes 786464 | tf_op jit(solution)/shard_map/ppermute | solution.py:31
  32.1 12.3 %product.1 = (bf16[2,64,864]{2,1,0:T(8,128)(2,1)S(1)}, bf16[2,64,864]{2,1,0:T(8,128)(2,1)S(1)}) custom-call(s32[4]{0:T(128)S(1)} %pad_add_fusion.slot_ref, f32[6,32,2048]{2,1,0:T(8,128)S(1)} %get-tuple-element.30.most_ref, f32[6,32,1024]{2,1,0:T(8,128)S(1)} %face.1.face_ref, f32[2,27,2048]{2,1,0:T(8,128)S(1)} %copy-done.7, ...), custom_call_target="tpu_custom_call" | custom-call | flops 4294967296 | bytes 1048576 | tf_op jit(solution)/shard_map/product/pallas_call | solution.py:330
  44.5 0.6 collective-permute-start.7
  45.1 7.1 %collective-permute-done.7 = bf16[2,64,864]{2,1,0:T(8,128)(2,1)S(1)} collective-permute-done((bf16[2,64,864]{2,1,0:T(8,128)(2,1)S(1)}, bf16[2,64,864]{2,1,0:T(8,128)(2,1)S(1)}, u32[]{:S(2)}, u32[]{:S(2)}) %collective-permute-start.7) | collective-permute-done | bytes 221216 | tf_op jit(solution)/shard_map/ppermute | solution.py:31
  52.3 0.8 %collective-permute-start.10 = (bf16[64,864]{1,0:T(8,128)(2,1)S(1)}, bf16[64,864]{1,0:T(8,128)(2,1)S(1)}, u32[]{:S(2)}, u32[]{:S(2)}) collective-permute-start(bf16[64,864]{1,0:T(8,128)(2,1)S(1)} %get-tuple-element.44), channel_id=1, source_target_pairs={{0,8},{1,12},{4,9},{5,13},{8,0},{9,4},{12,1},{13,5},{2,10},{3,14},... | collective-permute-start | bytes 331784 | tf_op jit(solution)/shard_map/ppermute | solution.py:434
  53.0 2.1 %collective-permute-start.11 = (bf16[64,864]{1,0:T(8,128)(2,1)S(1)}, bf16[64,864]{1,0:T(8,128)(2,1)S(1)}, u32[]{:S(2)}, u32[]{:S(2)}) collective-permute-start(bf16[64,864]{1,0:T(8,128)(2,1)S(1)} %get-tuple-element.43), channel_id=1, source_target_pairs={{0,9},{1,13},{4,8},{5,12},{8,1},{9,5},{12,0},{13,4},{2,11},{3,15},... | collective-permute-start | bytes 331784 | tf_op jit(solution)/shard_map/ppermute | solution.py:434
  55.2 0.7 collective-permute-start.8
  55.8 2.1 %collective-permute-start.9 = (bf16[64,864]{1,0:T(8,128)(2,1)S(1)}, bf16[64,864]{1,0:T(8,128)(2,1)S(1)}, u32[]{:S(2)}, u32[]{:S(2)}) collective-permute-start(bf16[64,864]{1,0:T(8,128)(2,1)S(1)} %get-tuple-element.45), channel_id=1, source_target_pairs={{0,1},{1,5},{4,0},{5,4},{8,9},{9,13},{12,8},{13,12},{2,3},{3,7},{6... | collective-permute-start | bytes 331784 | tf_op jit(solution)/shard_map/ppermute | solution.py:434
  57.9 5.7 %collective-permute-done.10.refs_2_ = bf16[64,864]{1,0:T(8,128)(2,1)S(1)} collective-permute-done((bf16[64,864]{1,0:T(8,128)(2,1)S(1)}, bf16[64,864]{1,0:T(8,128)(2,1)S(1)}, u32[]{:S(2)}, u32[]{:S(2)}) %collective-permute-start.10) | collective-permute-done | bytes 110624 | tf_op jit(solution)/shard_map/ppermute | solution.py:434
  63.6 2.5 %collective-permute-done.9.refs_1_ = bf16[64,864]{1,0:T(8,128)(2,1)S(1)} collective-permute-done((bf16[64,864]{1,0:T(8,128)(2,1)S(1)}, bf16[64,864]{1,0:T(8,128)(2,1)S(1)}, u32[]{:S(2)}, u32[]{:S(2)}) %collective-permute-start.9) | collective-permute-done | bytes 110624 | tf_op jit(solution)/shard_map/ppermute | solution.py:434
  66.1 1.2 %sum.1 = f32[1728,32]{1,0:T(8,128)} custom-call(bf16[64,864]{1,0:T(8,128)(2,1)S(1)} %collective-permute-done.8.refs_0_, bf16[64,864]{1,0:T(8,128)(2,1)S(1)} %collective-permute-done.9.refs_1_, bf16[64,864]{1,0:T(8,128)(2,1)S(1)} %collective-permute-done.10.refs_2_, bf16[64,864]{1,0:T(8,128)(2,1)S(1)} %collective-permute-done.11.refs_3_), custom_call_target="tpu_custom_call" | custom-call | flops 1048576 | bytes 1048576 | tf_op jit(solution)/shard_map/sum/pallas_call | solution.py:330
  (30 shorter events, 0.8 us)
Async XLA Ops:
  0.0 1.0 %copy-start = (f32[3,3,3,2,2048]{4,3,2,1,0:T(2,128)S(1)}, f32[3,3,3,2,2048]{4,3,2,1,0:T(2,128)}, u32[]{:S(2)}) copy-start(f32[3,3,3,2,2048]{4,3,2,1,0:T(2,128)} %param.4) | copy-start | bytes 1327108
  1.0 1.4 %copy-start.2 = (f32[32,3,2,2048]{3,2,1,0:T(2,128)S(1)}, f32[32,3,2,2048]{3,2,1,0:T(2,128)}, u32[]{:S(2)}) copy-start(f32[32,3,2,2048]{3,2,1,0:T(2,128)} %param.3) | copy-start | bytes 4718596
  2.4 16.9 %copy-start.8 = (s32[27,3]{0,1:T(4,128)S(1)}, s32[27,3]{0,1:T(4,128)}, u32[]{:S(2)}) copy-start(s32[27,3]{0,1:T(4,128)} %param.5) | copy-start | bytes 976
  2.4 17.0 %copy-start.1 = (f32[3,3,3,2,2048]{4,3,2,1,0:T(2,128)S(1)}, f32[3,3,3,2,2048]{4,3,2,1,0:T(2,128)}, u32[]{:S(2)}) copy-start(f32[3,3,3,2,2048]{4,3,2,1,0:T(2,128)} %param.4) | copy-start | bytes 1327108
  4.6 13.7 %collective-permute-start = (bf16[6,32,2048]{2,1,0:T(8,128)(2,1)}, bf16[6,32,2048]{2,1,0:T(8,128)(2,1)S(1)}, u32[]{:S(2)}, u32[]{:S(2)}) collective-permute-start(bf16[6,32,2048]{2,1,0:T(8,128)(2,1)} %get-tuple-element.25.refs_0_), channel_id=1, source_target_pairs={{0,1},{1,0},{2,3},{3,2},{4,5},{5,4},{6,7},{7,6},{8,9},{9,8},{10,11... | collective-permute-start | bytes 2359304 | tf_op jit(solution)/shard_map/ppermute | solution.py:31
  5.1 24.6 %collective-permute-start.3 = (bf16[6,32,2048]{2,1,0:T(8,128)(2,1)}, bf16[6,32,2048]{2,1,0:T(8,128)(2,1)}, u32[]{:S(2)}, u32[]{:S(2)}) collective-permute-start(bf16[6,32,2048]{2,1,0:T(8,128)(2,1)} %get-tuple-element.25.refs_0_), channel_id=1, source_target_pairs={{0,2},{2,0},{1,3},{3,1},{4,6},{6,4},{5,7},{7,5},{8,10},{10,8},{9,1... | collective-permute-start | bytes 2359304 | tf_op jit(solution)/shard_map/ppermute | solution.py:31
  7.6 16.3 %collective-permute-start.1 = (bf16[6,32,512]{2,1,0:T(8,128)(2,1)}, bf16[6,32,512]{2,1,0:T(8,128)(2,1)S(1)}, u32[]{:S(2)}, u32[]{:S(2)}) collective-permute-start(bf16[6,32,512]{2,1,0:T(8,128)(2,1)} %get-tuple-element.28), channel_id=1, source_target_pairs={{0,12},{4,0},{8,4},{12,8},{1,13},{5,1},{9,5},{13,9},{2,14},{6,2},{... | collective-permute-start | bytes 589832 | tf_op jit(solution)/shard_map/ppermute | solution.py:31
  11.2 12.7 %collective-permute-start.2 = (bf16[6,32,512]{2,1,0:T(8,128)(2,1)}, bf16[6,32,512]{2,1,0:T(8,128)(2,1)S(1)}, u32[]{:S(2)}, u32[]{:S(2)}) collective-permute-start(bf16[6,32,512]{2,1,0:T(8,128)(2,1)} %get-tuple-element.29), channel_id=1, source_target_pairs={{0,4},{4,8},{8,12},{12,0},{1,5},{5,9},{9,13},{13,1},{2,6},{6,10},{... | collective-permute-start | bytes 589832 | tf_op jit(solution)/shard_map/ppermute | solution.py:31
  14.5 14.6 %collective-permute-start.4 = (bf16[6,32,512]{2,1,0:T(8,128)(2,1)}, bf16[6,32,512]{2,1,0:T(8,128)(2,1)}, u32[]{:S(2)}, u32[]{:S(2)}) collective-permute-start(bf16[6,32,512]{2,1,0:T(8,128)(2,1)} %get-tuple-element.31), channel_id=1, source_target_pairs={{0,12},{4,0},{8,4},{12,8},{1,13},{5,1},{9,5},{13,9},{2,14},{6,2},{... | collective-permute-start | bytes 589832 | tf_op jit(solution)/shard_map/ppermute | solution.py:31
  18.4 0.9 %copy-start.3 = (bf16[6,32,2048]{2,1,0:T(8,128)(2,1)}, bf16[6,32,2048]{2,1,0:T(8,128)(2,1)S(1)}, u32[]{:S(2)}) copy-start(bf16[6,32,2048]{2,1,0:T(8,128)(2,1)S(1)} %collective-permute-done.refs_0_.refs_2_) | copy-start | bytes 2359300
  19.3 10.3 %collective-permute-start.5 = (bf16[6,32,512]{2,1,0:T(8,128)(2,1)}, bf16[6,32,512]{2,1,0:T(8,128)(2,1)}, u32[]{:S(2)}, u32[]{:S(2)}) collective-permute-start(bf16[6,32,512]{2,1,0:T(8,128)(2,1)} %get-tuple-element.32), channel_id=1, source_target_pairs={{0,4},{4,8},{8,12},{12,0},{1,5},{5,9},{9,13},{13,1},{2,6},{6,10},{... | collective-permute-start | bytes 589832 | tf_op jit(solution)/shard_map/ppermute | solution.py:31
  19.4 1.1 %copy-start.4 = (bf16[6,32,2048]{2,1,0:T(8,128)(2,1)S(1)}, bf16[6,32,2048]{2,1,0:T(8,128)(2,1)}, u32[]{:S(2)}) copy-start(bf16[6,32,2048]{2,1,0:T(8,128)(2,1)} %copy-done.3) | copy-start | bytes 2359300
  23.8 5.3 %copy-start.6 = (f32[2,27,2048]{2,1,0:T(8,128)}, f32[2,27,2048]{2,1,0:T(8,128)S(1)}, u32[]{:S(2)}) copy-start(f32[2,27,2048]{2,1,0:T(8,128)S(1)} %get-tuple-element.37.table_ref) | copy-start | bytes 1327108
  29.6 2.5 %collective-permute-start.6 = (bf16[6,32,2048]{2,1,0:T(8,128)(2,1)}, bf16[6,32,2048]{2,1,0:T(8,128)(2,1)S(1)}, u32[]{:S(2)}, u32[]{:S(2)}) collective-permute-start(bf16[6,32,2048]{2,1,0:T(8,128)(2,1)} %collective-permute-done.3.refs_1_), channel_id=1, source_target_pairs={{0,1},{1,0},{2,3},{3,2},{4,5},{5,4},{6,7},{7,6},{8,9},{9,8},{10,11... | collective-permute-start | bytes 2359304 | tf_op jit(solution)/shard_map/ppermute | solution.py:31
  29.7 2.4 %copy-start.5 = (bf16[6,32,2048]{2,1,0:T(8,128)(2,1)S(1)}, bf16[6,32,2048]{2,1,0:T(8,128)(2,1)}, u32[]{:S(2)}) copy-start(bf16[6,32,2048]{2,1,0:T(8,128)(2,1)} %copy-done.3) | copy-start | bytes 2359300
  29.7 2.4 %copy-start.7 = (f32[2,27,2048]{2,1,0:T(8,128)S(1)}, f32[2,27,2048]{2,1,0:T(8,128)}, u32[]{:S(2)}) copy-start(f32[2,27,2048]{2,1,0:T(8,128)} %copy-done.6) | copy-start | bytes 1327108
  44.5 7.7 %collective-permute-start.7 = (bf16[2,64,864]{2,1,0:T(8,128)(2,1)S(1)}, bf16[2,64,864]{2,1,0:T(8,128)(2,1)S(1)}, u32[]{:S(2)}, u32[]{:S(2)}) collective-permute-start(bf16[2,64,864]{2,1,0:T(8,128)(2,1)S(1)} %get-tuple-element.39), channel_id=1, source_target_pairs={{0,2},{2,0},{1,3},{3,1},{4,6},{6,4},{5,7},{7,5},{8,10},{10,8},{9,1... | collective-permute-start | bytes 663560 | tf_op jit(solution)/shard_map/ppermute | solution.py:31
  52.3 11.3 %collective-permute-start.10 = (bf16[64,864]{1,0:T(8,128)(2,1)S(1)}, bf16[64,864]{1,0:T(8,128)(2,1)S(1)}, u32[]{:S(2)}, u32[]{:S(2)}) collective-permute-start(bf16[64,864]{1,0:T(8,128)(2,1)S(1)} %get-tuple-element.44), channel_id=1, source_target_pairs={{0,8},{1,12},{4,9},{5,13},{8,0},{9,4},{12,1},{13,5},{2,10},{3,14},... | collective-permute-start | bytes 331784 | tf_op jit(solution)/shard_map/ppermute | solution.py:434
  53.0 10.6 %collective-permute-start.11 = (bf16[64,864]{1,0:T(8,128)(2,1)S(1)}, bf16[64,864]{1,0:T(8,128)(2,1)S(1)}, u32[]{:S(2)}, u32[]{:S(2)}) collective-permute-start(bf16[64,864]{1,0:T(8,128)(2,1)S(1)} %get-tuple-element.43), channel_id=1, source_target_pairs={{0,9},{1,13},{4,8},{5,12},{8,1},{9,5},{12,0},{13,4},{2,11},{3,15},... | collective-permute-start | bytes 331784 | tf_op jit(solution)/shard_map/ppermute | solution.py:434
  55.2 8.4 %collective-permute-start.8 = (bf16[64,864]{1,0:T(8,128)(2,1)S(1)}, bf16[64,864]{1,0:T(8,128)(2,1)S(1)}, u32[]{:S(2)}, u32[]{:S(2)}) collective-permute-start(bf16[64,864]{1,0:T(8,128)(2,1)S(1)} %get-tuple-element.46), channel_id=1, source_target_pairs={{0,0},{1,4},{4,1},{5,5},{8,8},{9,12},{12,9},{13,13},{2,2},{3,6},{6... | collective-permute-start | bytes 331784 | tf_op jit(solution)/shard_map/ppermute | solution.py:434
  55.8 10.2 %collective-permute-start.9 = (bf16[64,864]{1,0:T(8,128)(2,1)S(1)}, bf16[64,864]{1,0:T(8,128)(2,1)S(1)}, u32[]{:S(2)}, u32[]{:S(2)}) collective-permute-start(bf16[64,864]{1,0:T(8,128)(2,1)S(1)} %get-tuple-element.45), channel_id=1, source_target_pairs={{0,1},{1,5},{4,0},{5,4},{8,9},{9,13},{12,8},{13,12},{2,3},{3,7},{6... | collective-permute-start | bytes 331784 | tf_op jit(solution)/shard_map/ppermute | solution.py:434

commit v12 on v11

--- a/solution.py
+++ b/solution.py
@@ -22,7 +22,6 @@
 STEP = 2
 VMEM_LIMIT = 40 * 1024 * 1024
 VMEM = pl.BlockSpec(memory_space=pltpu.VMEM)
-AWAY = pl.BlockSpec(memory_space=pltpu.HBM)
 SMEM = pl.BlockSpec(memory_space=pltpu.SMEM)
 
 
@@ -326,11 +325,11 @@
             out_ref[rows, :] = block[part * width : (part + 1) * width]
 
 
-def call(kernel, name, shapes, operands, flops=0, scratch=(), smem=False, alias=None, away=0):
+def call(kernel, name, shapes, operands, flops=0, scratch=(), smem=False, alias=None):
     return pl.pallas_call(
         kernel,
         out_shape=tuple(jax.ShapeDtypeStruct(shape, dtype) for shape, dtype in shapes),
-        in_specs=([SMEM] if smem else []) + [VMEM] * (len(operands) - smem - away) + [AWAY] * away,
+        in_specs=([SMEM] if smem else []) + [VMEM] * (len(operands) - smem),
         out_specs=(VMEM,) * len(shapes),
         scratch_shapes=list(scratch),
         input_output_aliases=alias or {},
@@ -375,8 +374,7 @@
         functools.partial(inner_kernel, total_x),
         "inner",
         (((6, width, sites - 2 * PLANE), WIDE), ((2, count, sites), WIDE)),
-        (place, field, links, back, momenta, *beside),
-        away=subs - 1,
+        (place, field, links, back, momenta, *(array[0, :ROWS, :LANES] for array in beside)),
         flops=1 << 24,
         smem=True,
     )

time: 67.5 us -> 68.1 us (level)
  local copies, waits for them, and re-layouts: 4.63 us -> 5.54 us
    squeeze x0 -> x1, local copies, waits for them, and re-layouts: none -> 0.68 us  [shards(): array[0, :ROWS, :LANES]]
  transfers between devices with their start and end apart: 12 -> 12, of which waited for: 5 -> 5; matrix products, arithmetic and copies ran while one was open for 0% -> 1% of each run, Pallas kernels for 20% -> 19%
where the time goes in v12:
time: 68.1 us; the launch traced here: 67.8 us
  Pallas kernels  29 us (43%)
  starting transfers between devices  16.6 us (24%)
  waiting for transfers between devices  16.3 us (24%)
  local copies, waits for them, and re-layouts  5.54 us (8%)
    pallas_call x7, Pallas kernels, call(): pl.pallas_call(kernel, out_shape=tuple((jax.ShapeDtypeStruct(shape, dtype...  29 us
    ppermute x8, starting transfers between devices, shifted(): lax.ppermute(array, axis, [(i, (i + by) % peers) for i in range(peers)])  11 us
    ppermute x8, waiting for transfers between devices, shifted(): lax.ppermute(array, axis, [(i, (i + by) % peers) for i in range(peers)])  8.67 us
    ppermute x4, waiting for transfers between devices, shards(): shares.append(lax.ppermute(block[r], ('brick', 'sub'), pairs))  7.66 us
    ppermute x4, starting transfers between devices, shards(): shares.append(lax.ppermute(block[r], ('brick', 'sub'), pairs))  5.64 us
    unnamed x19, local copies, waits for them, and re-layouts  4.82 us
  transfers between devices with their start and end apart: 12, of which 5 were waited for; matrix products, arithmetic and copies ran while one was open for 1% of the time, Pallas kernels for 19%

profile of v12, /device:TPU:0, one launch (start us, length us, event | category | flops | bytes accessed | tf_op | source)
XLA Modules:
  0.0 67.8 jit_solution(10696994230341826300)
XLA Ops:
  0.0 1.0 %copy-done = f32[3,3,3,2,2048]{4,3,2,1,0:T(2,128)S(1)} copy-done((f32[3,3,3,2,2048]{4,3,2,1,0:T(2,128)S(1)}, f32[3,3,3,2,2048]{4,3,2,1,0:T(2,128)}, u32[]{:S(2)}) %copy-start) | copy-done | bytes 442392
  1.0 1.4 %copy-done.2 = f32[32,3,2,2048]{3,2,1,0:T(2,128)S(1)} copy-done((f32[32,3,2,2048]{3,2,1,0:T(2,128)S(1)}, f32[32,3,2,2048]{3,2,1,0:T(2,128)}, u32[]{:S(2)}) %copy-start.2) | copy-done | bytes 1572888
  2.4 2.2 %open.1 = (f32[6,32,2048]{2,1,0:T(8,128)S(1)}, bf16[6,32,2048]{2,1,0:T(8,128)(2,1)}, bf16[6,32,512]{2,1,0:T(8,128)(2,1)}, bf16[6,32,512]{2,1,0:T(8,128)(2,1)}) custom-call(f32[3072,128]{1,0:T(8,128)S(1)} %bitcast.29, f32[864,128]{1,0:T(8,128)S(1)} %bitcast.24), custom_call_target="tpu_custom_call" | custom-call | flops 4194304 | bytes 1048576 | tf_op jit(solution)/shard_map/open/pallas_call | solution.py:329
  5.1 2.5 %collective-permute-start.3 = (bf16[6,32,2048]{2,1,0:T(8,128)(2,1)}, bf16[6,32,2048]{2,1,0:T(8,128)(2,1)}, u32[]{:S(2)}, u32[]{:S(2)}) collective-permute-start(bf16[6,32,2048]{2,1,0:T(8,128)(2,1)} %get-tuple-element.25.refs_0_), channel_id=1, source_target_pairs={{0,2},{2,0},{1,3},{3,1},{4,6},{6,4},{5,7},{7,5},{8,10},{10,8},{9,1... | collective-permute-start | bytes 2359304 | tf_op jit(solution)/shard_map/ppermute | solution.py:30
  7.6 3.6 %collective-permute-start.1 = (bf16[6,32,512]{2,1,0:T(8,128)(2,1)}, bf16[6,32,512]{2,1,0:T(8,128)(2,1)S(1)}, u32[]{:S(2)}, u32[]{:S(2)}) collective-permute-start(bf16[6,32,512]{2,1,0:T(8,128)(2,1)} %get-tuple-element.28), channel_id=1, source_target_pairs={{0,12},{4,0},{8,4},{12,8},{1,13},{5,1},{9,5},{13,9},{2,14},{6,2},{... | collective-permute-start | bytes 589832 | tf_op jit(solution)/shard_map/ppermute | solution.py:30
  11.2 3.3 %rim.1 = (bf16[6,32,512]{2,1,0:T(8,128)(2,1)}, bf16[6,32,512]{2,1,0:T(8,128)(2,1)S(1)}, f32[6,32,1024]{2,1,0:T(8,128)S(1)}, f32[2,16,2048]{2,1,0:T(8,128)S(1)}) custom-call(f32[6,32,2048]{2,1,0:T(8,128)S(1)} %get-tuple-element.23.field_ref, f32[864,128]{1,0:T(8,128)S(1)} %bitcast.25), custom_call_target="tpu_custom_call" | custom-call | flops 16777216 | bytes 1048576 | tf_op jit(solution)/shard_map/rim/pallas_call | solution.py:329
  14.5 0.7 %copy-done.7 = bf16[6,32,512]{2,1,0:T(8,128)(2,1)} copy-done((bf16[6,32,512]{2,1,0:T(8,128)(2,1)}, bf16[6,32,512]{2,1,0:T(8,128)(2,1)S(1)}, u32[]{:S(2)}) %copy-start.7) | copy-done | bytes 196632
  15.2 3.8 %collective-permute-start.4 = (bf16[6,32,512]{2,1,0:T(8,128)(2,1)}, bf16[6,32,512]{2,1,0:T(8,128)(2,1)}, u32[]{:S(2)}, u32[]{:S(2)}) collective-permute-start(bf16[6,32,512]{2,1,0:T(8,128)(2,1)} %get-tuple-element.31), channel_id=1, source_target_pairs={{0,12},{4,0},{8,4},{12,8},{1,13},{5,1},{9,5},{13,9},{2,14},{6,2},{... | collective-permute-start | bytes 589832 | tf_op jit(solution)/shard_map/ppermute | solution.py:30
  19.2 0.7 %slice_bitcast_fusion.4.refs_0_ = bf16[16,128]{1,0:T(8,128)(2,1)S(1)} fusion(bf16[6,32,2048]{2,1,0:T(8,128)(2,1)} %collective-permute-done.refs_2_), kind=kLoop, calls=%fused_computation.6 | loop fusion | bytes 8192 | tf_op jit(solution)/shard_map/squeeze | solution.py:377
  19.9 3.3 %inner.1 = (f32[6,32,1024]{2,1,0:T(8,128)S(1)}, f32[2,27,2048]{2,1,0:T(8,128)S(1)}) custom-call(s32[1]{0:T(128)} %bitcast.8.place_ref, f32[6,32,2048]{2,1,0:T(8,128)S(1)} %get-tuple-element.23.field_ref, f32[864,128]{1,0:T(8,128)S(1)} %bitcast.26, f32[2,16,2048]{2,1,0:T(8,128)S(1)} %get-tuple-element.24.back_ref, s32[27,3]{1,0:T(8,128)S(1)} %copy.7.momenta_ref, ...), custom_call_target="tpu_custom_call" | custom-call | flops 16777216 | bytes 1048576 | tf_op jit(solution)/shard_map/inner/pallas_call | solution.py:329
  23.2 5.2 %second.1 = (f32[6,32,2048]{2,1,0:T(8,128)S(1)}, f32[8,128]{1,0:T(8,128)S(1)}) custom-call(f32[6,32,2048]{2,1,0:T(8,128)S(1)} %get-tuple-element.23.field_ref, f32[6,32,1024]{2,1,0:T(8,128)S(1)} %get-tuple-element.26.inner_ref, f32[6,32,1024]{2,1,0:T(8,128)S(1)} %get-tuple-element.27.rim_ref, ...), custom_call_target="tpu_custom_call", output_to_operand_aliasing={{0}: (0, {})} | custom-call | flops 33554432 | bytes 1048576 | tf_op jit(solution)/shard_map/second/pallas_call | solution.py:329
  28.4 1.2 %collective-permute-done.5.behind_ref = bf16[6,32,512]{2,1,0:T(8,128)(2,1)S(1)} collective-permute-done((bf16[6,32,512]{2,1,0:T(8,128)(2,1)}, bf16[6,32,512]{2,1,0:T(8,128)(2,1)S(1)}, u32[]{:S(2)}, u32[]{:S(2)}) %collective-permute-start.5) | collective-permute-done | bytes 196640 | tf_op jit(solution)/shard_map/ppermute | solution.py:30
  29.6 0.7 copy-done.3
  30.3 0.9 %copy-done.4 = bf16[6,32,512]{2,1,0:T(8,128)(2,1)S(1)} copy-done((bf16[6,32,512]{2,1,0:T(8,128)(2,1)S(1)}, bf16[6,32,512]{2,1,0:T(8,128)(2,1)}, u32[]{:S(2)}) %copy-start.4) | copy-done | bytes 196632
  31.3 1.3 %face.1.face_ref = f32[6,32,1024]{2,1,0:T(8,128)S(1)} custom-call(f32[6,32,2048]{2,1,0:T(8,128)S(1)} %get-tuple-element.30.most_ref, bf16[6,32,512]{2,1,0:T(8,128)(2,1)} %collective-permute-done.4.ahead_ref, bf16[6,32,512]{2,1,0:T(8,128)(2,1)S(1)} %copy-done.4, f32[864,128]{1,0:T(8,128)S(1)} %bitcast.28, f32[8,128]{1,0:T(8,128)S(1)} %get-tuple-element.36.token_ref), custom_call_target="tpu_custom_call" | custom-call | flops 4194304 | bytes 1048576 | tf_op jit(solution)/shard_map/face/pallas_call | solution.py:329
  32.8 12.6 %product.1 = (bf16[2,64,864]{2,1,0:T(8,128)(2,1)S(1)}, bf16[2,64,864]{2,1,0:T(8,128)(2,1)S(1)}) custom-call(s32[4]{0:T(128)S(1)} %pad_add_fusion.slot_ref, f32[6,32,2048]{2,1,0:T(8,128)S(1)} %get-tuple-element.30.most_ref, f32[6,32,1024]{2,1,0:T(8,128)S(1)} %face.1.face_ref, f32[2,27,2048]{2,1,0:T(8,128)S(1)} %copy-done.6, ...), custom_call_target="tpu_custom_call" | custom-call | flops 4294967296 | bytes 1048576 | tf_op jit(solution)/shard_map/product/pallas_call | solution.py:329
  45.9 7.3 %collective-permute-done.7 = bf16[2,64,864]{2,1,0:T(8,128)(2,1)S(1)} collective-permute-done((bf16[2,64,864]{2,1,0:T(8,128)(2,1)S(1)}, bf16[2,64,864]{2,1,0:T(8,128)(2,1)S(1)}, u32[]{:S(2)}, u32[]{:S(2)}) %collective-permute-start.7) | collective-permute-done | bytes 221216 | tf_op jit(solution)/shard_map/ppermute | solution.py:30
  53.3 0.7 %collective-permute-start.10 = (bf16[64,864]{1,0:T(8,128)(2,1)S(1)}, bf16[64,864]{1,0:T(8,128)(2,1)S(1)}, u32[]{:S(2)}, u32[]{:S(2)}) collective-permute-start(bf16[64,864]{1,0:T(8,128)(2,1)S(1)} %get-tuple-element.44), channel_id=1, source_target_pairs={{0,8},{1,12},{4,9},{5,13},{8,0},{9,4},{12,1},{13,5},{2,10},{3,14},... | collective-permute-start | bytes 331784 | tf_op jit(solution)/shard_map/ppermute | solution.py:432
  54.0 2.1 %collective-permute-start.11 = (bf16[64,864]{1,0:T(8,128)(2,1)S(1)}, bf16[64,864]{1,0:T(8,128)(2,1)S(1)}, u32[]{:S(2)}, u32[]{:S(2)}) collective-permute-start(bf16[64,864]{1,0:T(8,128)(2,1)S(1)} %get-tuple-element.43), channel_id=1, source_target_pairs={{0,9},{1,13},{4,8},{5,12},{8,1},{9,5},{12,0},{13,4},{2,11},{3,15},... | collective-permute-start | bytes 331784 | tf_op jit(solution)/shard_map/ppermute | solution.py:432
  56.1 0.7 collective-permute-start.8
  56.8 2.2 %collective-permute-start.9 = (bf16[64,864]{1,0:T(8,128)(2,1)S(1)}, bf16[64,864]{1,0:T(8,128)(2,1)S(1)}, u32[]{:S(2)}, u32[]{:S(2)}) collective-permute-start(bf16[64,864]{1,0:T(8,128)(2,1)S(1)} %get-tuple-element.45), channel_id=1, source_target_pairs={{0,1},{1,5},{4,0},{5,4},{8,9},{9,13},{12,8},{13,12},{2,3},{3,7},{6... | collective-permute-start | bytes 331784 | tf_op jit(solution)/shard_map/ppermute | solution.py:432
  59.0 5.9 %collective-permute-done.10.refs_2_ = bf16[64,864]{1,0:T(8,128)(2,1)S(1)} collective-permute-done((bf16[64,864]{1,0:T(8,128)(2,1)S(1)}, bf16[64,864]{1,0:T(8,128)(2,1)S(1)}, u32[]{:S(2)}, u32[]{:S(2)}) %collective-permute-start.10) | collective-permute-done | bytes 110624 | tf_op jit(solution)/shard_map/ppermute | solution.py:432
  64.8 1.8 %collective-permute-done.9.refs_1_ = bf16[64,864]{1,0:T(8,128)(2,1)S(1)} collective-permute-done((bf16[64,864]{1,0:T(8,128)(2,1)S(1)}, bf16[64,864]{1,0:T(8,128)(2,1)S(1)}, u32[]{:S(2)}, u32[]{:S(2)}) %collective-permute-start.9) | collective-permute-done | bytes 110624 | tf_op jit(solution)/shard_map/ppermute | solution.py:432
  66.6 1.2 %sum.1 = f32[1728,32]{1,0:T(8,128)} custom-call(bf16[64,864]{1,0:T(8,128)(2,1)S(1)} %collective-permute-done.8.refs_0_, bf16[64,864]{1,0:T(8,128)(2,1)S(1)} %collective-permute-done.9.refs_1_, bf16[64,864]{1,0:T(8,128)(2,1)S(1)} %collective-permute-done.10.refs_2_, bf16[64,864]{1,0:T(8,128)(2,1)S(1)} %collective-permute-done.11.refs_3_), custom_call_target="tpu_custom_call" | custom-call | flops 1048576 | bytes 1048576 | tf_op jit(solution)/shard_map/sum/pallas_call | solution.py:329
  (31 shorter events, 1.6 us)
Async XLA Ops:
  0.0 1.0 %copy-start = (f32[3,3,3,2,2048]{4,3,2,1,0:T(2,128)S(1)}, f32[3,3,3,2,2048]{4,3,2,1,0:T(2,128)}, u32[]{:S(2)}) copy-start(f32[3,3,3,2,2048]{4,3,2,1,0:T(2,128)} %param.4) | copy-start | bytes 1327108
  1.0 1.4 %copy-start.2 = (f32[32,3,2,2048]{3,2,1,0:T(2,128)S(1)}, f32[32,3,2,2048]{3,2,1,0:T(2,128)}, u32[]{:S(2)}) copy-start(f32[32,3,2,2048]{3,2,1,0:T(2,128)} %param.3) | copy-start | bytes 4718596
  2.4 16.6 %copy-start.8 = (s32[27,3]{0,1:T(4,128)S(1)}, s32[27,3]{0,1:T(4,128)}, u32[]{:S(2)}) copy-start(s32[27,3]{0,1:T(4,128)} %param.5) | copy-start | bytes 976
  2.4 17.4 %copy-start.1 = (f32[3,3,3,2,2048]{4,3,2,1,0:T(2,128)S(1)}, f32[3,3,3,2,2048]{4,3,2,1,0:T(2,128)}, u32[]{:S(2)}) copy-start(f32[3,3,3,2,2048]{4,3,2,1,0:T(2,128)} %param.4) | copy-start | bytes 1327108
  4.6 14.5 %collective-permute-start = (bf16[6,32,2048]{2,1,0:T(8,128)(2,1)}, bf16[6,32,2048]{2,1,0:T(8,128)(2,1)}, u32[]{:S(2)}, u32[]{:S(2)}) collective-permute-start(bf16[6,32,2048]{2,1,0:T(8,128)(2,1)} %get-tuple-element.25.refs_0_), channel_id=1, source_target_pairs={{0,1},{1,0},{2,3},{3,2},{4,5},{5,4},{6,7},{7,6},{8,9},{9,8},{10,11... | collective-permute-start | bytes 2359304 | tf_op jit(solution)/shard_map/ppermute | solution.py:30
  5.1 25.2 %collective-permute-start.3 = (bf16[6,32,2048]{2,1,0:T(8,128)(2,1)}, bf16[6,32,2048]{2,1,0:T(8,128)(2,1)}, u32[]{:S(2)}, u32[]{:S(2)}) collective-permute-start(bf16[6,32,2048]{2,1,0:T(8,128)(2,1)} %get-tuple-element.25.refs_0_), channel_id=1, source_target_pairs={{0,2},{2,0},{1,3},{3,1},{4,6},{6,4},{5,7},{7,5},{8,10},{10,8},{9,1... | collective-permute-start | bytes 2359304 | tf_op jit(solution)/shard_map/ppermute | solution.py:30
  7.6 15.6 %collective-permute-start.1 = (bf16[6,32,512]{2,1,0:T(8,128)(2,1)}, bf16[6,32,512]{2,1,0:T(8,128)(2,1)S(1)}, u32[]{:S(2)}, u32[]{:S(2)}) collective-permute-start(bf16[6,32,512]{2,1,0:T(8,128)(2,1)} %get-tuple-element.28), channel_id=1, source_target_pairs={{0,12},{4,0},{8,4},{12,8},{1,13},{5,1},{9,5},{13,9},{2,14},{6,2},{... | collective-permute-start | bytes 589832 | tf_op jit(solution)/shard_map/ppermute | solution.py:30
  11.2 12.0 %collective-permute-start.2 = (bf16[6,32,512]{2,1,0:T(8,128)(2,1)}, bf16[6,32,512]{2,1,0:T(8,128)(2,1)S(1)}, u32[]{:S(2)}, u32[]{:S(2)}) collective-permute-start(bf16[6,32,512]{2,1,0:T(8,128)(2,1)} %get-tuple-element.29), channel_id=1, source_target_pairs={{0,4},{4,8},{8,12},{12,0},{1,5},{5,9},{9,13},{13,1},{2,6},{6,10},{... | collective-permute-start | bytes 589832 | tf_op jit(solution)/shard_map/ppermute | solution.py:30
  14.5 0.7 %copy-start.7 = (bf16[6,32,512]{2,1,0:T(8,128)(2,1)}, bf16[6,32,512]{2,1,0:T(8,128)(2,1)S(1)}, u32[]{:S(2)}) copy-start(bf16[6,32,512]{2,1,0:T(8,128)(2,1)S(1)} %get-tuple-element.32) | copy-start | bytes 589828
  15.2 13.2 %collective-permute-start.4 = (bf16[6,32,512]{2,1,0:T(8,128)(2,1)}, bf16[6,32,512]{2,1,0:T(8,128)(2,1)}, u32[]{:S(2)}, u32[]{:S(2)}) collective-permute-start(bf16[6,32,512]{2,1,0:T(8,128)(2,1)} %get-tuple-element.31), channel_id=1, source_target_pairs={{0,12},{4,0},{8,4},{12,8},{1,13},{5,1},{9,5},{13,9},{2,14},{6,2},{... | collective-permute-start | bytes 589832 | tf_op jit(solution)/shard_map/ppermute | solution.py:30
  19.1 10.5 %collective-permute-start.5 = (bf16[6,32,512]{2,1,0:T(8,128)(2,1)}, bf16[6,32,512]{2,1,0:T(8,128)(2,1)S(1)}, u32[]{:S(2)}, u32[]{:S(2)}) collective-permute-start(bf16[6,32,512]{2,1,0:T(8,128)(2,1)} %copy-done.7), channel_id=1, source_target_pairs={{0,4},{4,8},{8,12},{12,0},{1,5},{5,9},{9,13},{13,1},{2,6},{6,10},{... | collective-permute-start | bytes 589832 | tf_op jit(solution)/shard_map/ppermute | solution.py:30
  23.1 5.3 %copy-start.5 = (f32[2,27,2048]{2,1,0:T(8,128)}, f32[2,27,2048]{2,1,0:T(8,128)S(1)}, u32[]{:S(2)}) copy-start(f32[2,27,2048]{2,1,0:T(8,128)S(1)} %get-tuple-element.37.table_ref) | copy-start | bytes 1327108
  29.6 0.7 copy-start.3
  30.3 2.5 %collective-permute-start.6 = (bf16[6,32,2048]{2,1,0:T(8,128)(2,1)}, bf16[6,32,2048]{2,1,0:T(8,128)(2,1)S(1)}, u32[]{:S(2)}, u32[]{:S(2)}) collective-permute-start(bf16[6,32,2048]{2,1,0:T(8,128)(2,1)} %collective-permute-done.3.refs_1_), channel_id=1, source_target_pairs={{0,1},{1,0},{2,3},{3,2},{4,5},{5,4},{6,7},{7,6},{8,9},{9,8},{10,11... | collective-permute-start | bytes 2359304 | tf_op jit(solution)/shard_map/ppermute | solution.py:30
  30.3 0.9 %copy-start.4 = (bf16[6,32,512]{2,1,0:T(8,128)(2,1)S(1)}, bf16[6,32,512]{2,1,0:T(8,128)(2,1)}, u32[]{:S(2)}) copy-start(bf16[6,32,512]{2,1,0:T(8,128)(2,1)} %copy-done.3) | copy-start | bytes 589828
  31.3 1.5 %copy-start.6 = (f32[2,27,2048]{2,1,0:T(8,128)S(1)}, f32[2,27,2048]{2,1,0:T(8,128)}, u32[]{:S(2)}) copy-start(f32[2,27,2048]{2,1,0:T(8,128)} %copy-done.5) | copy-start | bytes 1327108
  45.3 7.9 %collective-permute-start.7 = (bf16[2,64,864]{2,1,0:T(8,128)(2,1)S(1)}, bf16[2,64,864]{2,1,0:T(8,128)(2,1)S(1)}, u32[]{:S(2)}, u32[]{:S(2)}) collective-permute-start(bf16[2,64,864]{2,1,0:T(8,128)(2,1)S(1)} %get-tuple-element.39), channel_id=1, source_target_pairs={{0,2},{2,0},{1,3},{3,1},{4,6},{6,4},{5,7},{7,5},{8,10},{10,8},{9,1... | collective-permute-start | bytes 663560 | tf_op jit(solution)/shard_map/ppermute | solution.py:30
  53.3 11.5 %collective-permute-start.10 = (bf16[64,864]{1,0:T(8,128)(2,1)S(1)}, bf16[64,864]{1,0:T(8,128)(2,1)S(1)}, u32[]{:S(2)}, u32[]{:S(2)}) collective-permute-start(bf16[64,864]{1,0:T(8,128)(2,1)S(1)} %get-tuple-element.44), channel_id=1, source_target_pairs={{0,8},{1,12},{4,9},{5,13},{8,0},{9,4},{12,1},{13,5},{2,10},{3,14},... | collective-permute-start | bytes 331784 | tf_op jit(solution)/shard_map/ppermute | solution.py:432
  54.0 10.8 %collective-permute-start.11 = (bf16[64,864]{1,0:T(8,128)(2,1)S(1)}, bf16[64,864]{1,0:T(8,128)(2,1)S(1)}, u32[]{:S(2)}, u32[]{:S(2)}) collective-permute-start(bf16[64,864]{1,0:T(8,128)(2,1)S(1)} %get-tuple-element.43), channel_id=1, source_target_pairs={{0,9},{1,13},{4,8},{5,12},{8,1},{9,5},{12,0},{13,4},{2,11},{3,15},... | collective-permute-start | bytes 331784 | tf_op jit(solution)/shard_map/ppermute | solution.py:432
  56.1 8.7 %collective-permute-start.8 = (bf16[64,864]{1,0:T(8,128)(2,1)S(1)}, bf16[64,864]{1,0:T(8,128)(2,1)S(1)}, u32[]{:S(2)}, u32[]{:S(2)}) collective-permute-start(bf16[64,864]{1,0:T(8,128)(2,1)S(1)} %get-tuple-element.46), channel_id=1, source_target_pairs={{0,0},{1,4},{4,1},{5,5},{8,8},{9,12},{12,9},{13,13},{2,2},{3,6},{6... | collective-permute-start | bytes 331784 | tf_op jit(solution)/shard_map/ppermute | solution.py:432
  56.8 9.8 %collective-permute-start.9 = (bf16[64,864]{1,0:T(8,128)(2,1)S(1)}, bf16[64,864]{1,0:T(8,128)(2,1)S(1)}, u32[]{:S(2)}, u32[]{:S(2)}) collective-permute-start(bf16[64,864]{1,0:T(8,128)(2,1)S(1)} %get-tuple-element.45), channel_id=1, source_target_pairs={{0,1},{1,5},{4,0},{5,4},{8,9},{9,13},{12,8},{13,12},{2,3},{3,7},{6... | collective-permute-start | bytes 331784 | tf_op jit(solution)/shard_map/ppermute | solution.py:432

commit v13 on v10

--- a/solution.py
+++ b/solution.py
@@ -130,7 +130,7 @@
             if tile < TILES:
                 down_ref[k, :, pl.ds(tile * LANES, LANES)] = low
 
-    @pl.loop(0, TILES)
+    @pl.loop(0, TILES, unroll=True)
     def _(tile):
         for rows in row_groups(field_ref):
             turned = [None] * 6
@@ -153,7 +153,7 @@
 
     for place, layer in enumerate((0, layers - 1)):
 
-        @pl.loop(0, TILES)
+        @pl.loop(0, TILES, unroll=True)
         def _(tile):
             lanes = lanes_at(0, tile)
             for rows in row_groups(field_ref):
@@ -185,7 +185,7 @@
     momenta = momenta_ref[...].astype(WIDE)
     lane = lax.broadcasted_iota(jnp.int32, (count, LANES), 1)
 
-    @pl.loop(0, TILES)
+    @pl.loop(0, TILES, unroll=True)
     def _(tile):
         column = (tile * (LANES // LZ) + lane // LZ).astype(WIDE)
         depth = (lane % LZ).astype(WIDE)
@@ -200,7 +200,7 @@
 
     for layer in range(1, layers - 1):
 
-        @pl.loop(0, TILES)
+        @pl.loop(0, TILES, unroll=True)
         def _(tile):
             for rows in row_groups(field_ref):
                 fetch = lambda at, t: load(field_ref, rows, lanes_at(at, t))
@@ -214,7 +214,7 @@
     layers = field_ref.shape[2] // PLANE
     token_ref[...] = jnp.zeros_like(token_ref)
 
-    @pl.loop(0, TILES)
+    @pl.loop(0, TILES, unroll=True)
     def _(tile):
         lanes, high = lanes_at(0, tile), lanes_at(1, tile)
         for rows in row_groups(field_ref):
@@ -226,7 +226,7 @@
 
     for layer in range(layers):
 
-        @pl.loop(0, TILES)
+        @pl.loop(0, TILES, unroll=True)
         def _(tile):
             for rows in row_groups(field_ref):
 
@@ -245,7 +245,7 @@
 def face_kernel(most_ref, ahead_ref, behind_ref, link_ref, token_ref, out_ref):
     layers = link_ref.shape[0] // 54 // TILES
 
-    @pl.loop(0, TILES)
+    @pl.loop(0, TILES, unroll=True)
     def _(tile):
         lanes, high = lanes_at(0, tile), lanes_at(1, tile)
         for rows in row_groups(most_ref):

time: 67.2 us -> 66.3 us (0.987)
  Pallas kernels: 29.1 us -> 26.8 us
  waiting for transfers between devices: 18.3 us -> 19.7 us
    pallas_call x7, Pallas kernels: 29.1 us -> 26.8 us  [call(): pl.pallas_call(kernel, out_shape=tuple((jax.ShapeDtypeStruct(shape, dtype...]
    ppermute x8, waiting for transfers between devices: 10.1 us -> 12.3 us  [shifted(): lax.ppermute(array, axis, [(i, (i + by) % peers) for i in range(peers)])]
    ppermute x4, waiting for transfers between devices: 8.15 us -> 7.45 us  [shards(): shares.append(lax.ppermute(block[r], ('brick', 'sub'), pairs))]
  transfers between devices with their start and end apart: 12 -> 12, of which waited for: 5 -> 6; matrix products, arithmetic and copies ran while one was open for 0% -> 0% of each run, Pallas kernels for 20% -> 17%
where the time goes in v13:
time: 66.3 us; the launch traced here: 66 us
  Pallas kernels  26.8 us (40%)
  waiting for transfers between devices  19.7 us (30%)
  starting transfers between devices  16.7 us (25%)
  local copies, waits for them, and re-layouts  2.57 us (4%)
    pallas_call x7, Pallas kernels, call(): pl.pallas_call(kernel, out_shape=tuple((jax.ShapeDtypeStruct(shape, dtype...  26.8 us
    ppermute x8, waiting for transfers between devices, shifted(): lax.ppermute(array, axis, [(i, (i + by) % peers) for i in range(peers)])  12.3 us
    ppermute x8, starting transfers between devices, shifted(): lax.ppermute(array, axis, [(i, (i + by) % peers) for i in range(peers)])  11 us
    ppermute x4, waiting for transfers between devices, shards(): shares.append(lax.ppermute(block[r], ('brick', 'sub'), pairs))  7.45 us
    ppermute x4, starting transfers between devices, shards(): shares.append(lax.ppermute(block[r], ('brick', 'sub'), pairs))  5.64 us
    unnamed x13, local copies, waits for them, and re-layouts  2.53 us
  transfers between devices with their start and end apart: 12, of which 6 were waited for; matrix products, arithmetic and copies ran while one was open for 0% of the time, Pallas kernels for 17%

profile of v13, /device:TPU:0, one launch (start us, length us, event | category | flops | bytes accessed | tf_op | source)
XLA Modules:
  0.0 66.0 jit_solution(17648010830314917922)
XLA Ops:
  0.0 1.0 %copy-done = f32[3,3,3,2,2048]{4,3,2,1,0:T(2,128)S(1)} copy-done((f32[3,3,3,2,2048]{4,3,2,1,0:T(2,128)S(1)}, f32[3,3,3,2,2048]{4,3,2,1,0:T(2,128)}, u32[]{:S(2)}) %copy-start) | copy-done | bytes 442392
  1.0 1.4 %copy-done.2 = f32[32,3,2,2048]{3,2,1,0:T(2,128)S(1)} copy-done((f32[32,3,2,2048]{3,2,1,0:T(2,128)S(1)}, f32[32,3,2,2048]{3,2,1,0:T(2,128)}, u32[]{:S(2)}) %copy-start.2) | copy-done | bytes 1572888
  2.4 2.0 %open.1 = (f32[6,32,2048]{2,1,0:T(8,128)S(1)}, bf16[6,32,2048]{2,1,0:T(8,128)(2,1)}, bf16[6,32,512]{2,1,0:T(8,128)(2,1)}, bf16[6,32,512]{2,1,0:T(8,128)(2,1)}) custom-call(f32[3072,128]{1,0:T(8,128)S(1)} %bitcast.27, f32[864,128]{1,0:T(8,128)S(1)} %bitcast.22), custom_call_target="tpu_custom_call" | custom-call | flops 4194304 | bytes 1048576 | tf_op jit(solution)/shard_map/open/pallas_call | solution.py:328
  4.4 2.9 %collective-permute-start.2 = (bf16[6,32,2048]{2,1,0:T(8,128)(2,1)}, bf16[6,32,2048]{2,1,0:T(8,128)(2,1)}, u32[]{:S(2)}, u32[]{:S(2)}) collective-permute-start(bf16[6,32,2048]{2,1,0:T(8,128)(2,1)} %get-tuple-element.42.refs_0_), channel_id=1, source_target_pairs={{0,2},{2,0},{1,3},{3,1},{4,6},{6,4},{5,7},{7,5},{8,10},{10,8},{9,1... | collective-permute-start | bytes 2359304 | tf_op jit(solution)/shard_map/ppermute | solution.py:30
  7.3 3.6 %collective-permute-start = (bf16[6,32,512]{2,1,0:T(8,128)(2,1)}, bf16[6,32,512]{2,1,0:T(8,128)(2,1)S(1)}, u32[]{:S(2)}, u32[]{:S(2)}) collective-permute-start(bf16[6,32,512]{2,1,0:T(8,128)(2,1)} %get-tuple-element.29), channel_id=1, source_target_pairs={{0,12},{4,0},{8,4},{12,8},{1,13},{5,1},{9,5},{13,9},{2,14},{6,2},{... | collective-permute-start | bytes 589832 | tf_op jit(solution)/shard_map/ppermute | solution.py:30
  10.9 2.8 %rim.1 = (bf16[6,32,512]{2,1,0:T(8,128)(2,1)}, bf16[6,32,512]{2,1,0:T(8,128)(2,1)}, f32[6,32,1024]{2,1,0:T(8,128)S(1)}, f32[2,16,2048]{2,1,0:T(8,128)S(1)}) custom-call(f32[6,32,2048]{2,1,0:T(8,128)S(1)} %get-tuple-element.25.field_ref, f32[864,128]{1,0:T(8,128)S(1)} %bitcast.23), custom_call_target="tpu_custom_call" | custom-call | flops 16777216 | bytes 1048576 | tf_op jit(solution)/shard_map/rim/pallas_call | solution.py:328
  13.7 3.8 %collective-permute-start.3 = (bf16[6,32,512]{2,1,0:T(8,128)(2,1)}, bf16[6,32,512]{2,1,0:T(8,128)(2,1)}, u32[]{:S(2)}, u32[]{:S(2)}) collective-permute-start(bf16[6,32,512]{2,1,0:T(8,128)(2,1)} %get-tuple-element.33), channel_id=1, source_target_pairs={{0,12},{4,0},{8,4},{12,8},{1,13},{5,1},{9,5},{13,9},{2,14},{6,2},{... | collective-permute-start | bytes 589832 | tf_op jit(solution)/shard_map/ppermute | solution.py:30
  17.6 0.1 copy.7.momenta_ref
  17.7 2.6 %inner.1 = (f32[6,32,1024]{2,1,0:T(8,128)S(1)}, f32[2,27,2048]{2,1,0:T(8,128)S(1)}) custom-call(s32[1]{0:T(128)} %bitcast.8.place_ref, f32[6,32,2048]{2,1,0:T(8,128)S(1)} %get-tuple-element.25.field_ref, f32[864,128]{1,0:T(8,128)S(1)} %bitcast.24, f32[2,16,2048]{2,1,0:T(8,128)S(1)} %get-tuple-element.26.back_ref, s32[27,3]{1,0:T(8,128)S(1)} %copy.7.momenta_ref), custom_call_target="tpu_custom_call" | custom-call | flops 16777216 | bytes 1048576 | tf_op jit(solution)/shard_map/inner/pallas_call | solution.py:328
  20.3 0.9 %collective-permute-done.1.behind_ref = bf16[6,32,512]{2,1,0:T(8,128)(2,1)S(1)} collective-permute-done((bf16[6,32,512]{2,1,0:T(8,128)(2,1)}, bf16[6,32,512]{2,1,0:T(8,128)(2,1)S(1)}, u32[]{:S(2)}, u32[]{:S(2)}) %collective-permute-start.1) | collective-permute-done | bytes 196640 | tf_op jit(solution)/shard_map/ppermute | solution.py:30
  21.2 4.4 %second.1 = (f32[6,32,2048]{2,1,0:T(8,128)S(1)}, f32[8,128]{1,0:T(8,128)S(1)}) custom-call(f32[6,32,2048]{2,1,0:T(8,128)S(1)} %get-tuple-element.25.field_ref, f32[6,32,1024]{2,1,0:T(8,128)S(1)} %get-tuple-element.27.inner_ref, f32[6,32,1024]{2,1,0:T(8,128)S(1)} %get-tuple-element.28.rim_ref, ...), custom_call_target="tpu_custom_call", output_to_operand_aliasing={{0}: (0, {})} | custom-call | flops 33554432 | bytes 1048576 | tf_op jit(solution)/shard_map/second/pallas_call | solution.py:328
  25.7 3.0 %collective-permute-done.4.behind_ref = bf16[6,32,512]{2,1,0:T(8,128)(2,1)} collective-permute-done((bf16[6,32,512]{2,1,0:T(8,128)(2,1)}, bf16[6,32,512]{2,1,0:T(8,128)(2,1)}, u32[]{:S(2)}, u32[]{:S(2)}) %collective-permute-start.4) | collective-permute-done | bytes 196640 | tf_op jit(solution)/shard_map/ppermute | solution.py:30
  28.8 1.3 %face.1.face_ref = f32[6,32,1024]{2,1,0:T(8,128)S(1)} custom-call(f32[6,32,2048]{2,1,0:T(8,128)S(1)} %get-tuple-element.31.most_ref, bf16[6,32,512]{2,1,0:T(8,128)(2,1)} %collective-permute-done.3.ahead_ref, bf16[6,32,512]{2,1,0:T(8,128)(2,1)} %collective-permute-done.4.behind_ref, f32[864,128]{1,0:T(8,128)S(1)} %bitcast.26, ...), custom_call_target="tpu_custom_call" | custom-call | flops 4194304 | bytes 1048576 | tf_op jit(solution)/shard_map/face/pallas_call | solution.py:328
  30.1 1.2 %collective-permute-done.6.refs_3_ = bf16[6,32,2048]{2,1,0:T(8,128)(2,1)} collective-permute-done((bf16[6,32,2048]{2,1,0:T(8,128)(2,1)}, bf16[6,32,2048]{2,1,0:T(8,128)(2,1)}, u32[]{:S(2)}, u32[]{:S(2)}) %collective-permute-start.6) | collective-permute-done | bytes 786464 | tf_op jit(solution)/shard_map/ppermute | solution.py:30
  31.4 12.6 %product.1 = (bf16[2,64,864]{2,1,0:T(8,128)(2,1)S(1)}, bf16[2,64,864]{2,1,0:T(8,128)(2,1)S(1)}) custom-call(s32[4]{0:T(128)S(1)} %pad_add_fusion.slot_ref, f32[6,32,2048]{2,1,0:T(8,128)S(1)} %get-tuple-element.31.most_ref, f32[6,32,1024]{2,1,0:T(8,128)S(1)} %face.1.face_ref, f32[2,27,2048]{2,1,0:T(8,128)S(1)} %copy-done.4, ...), custom_call_target="tpu_custom_call" | custom-call | flops 4294967296 | bytes 1048576 | tf_op jit(solution)/shard_map/product/pallas_call | solution.py:328
  43.9 0.6 collective-permute-start.7
  44.5 7.1 %collective-permute-done.7 = bf16[2,64,864]{2,1,0:T(8,128)(2,1)S(1)} collective-permute-done((bf16[2,64,864]{2,1,0:T(8,128)(2,1)S(1)}, bf16[2,64,864]{2,1,0:T(8,128)(2,1)S(1)}, u32[]{:S(2)}, u32[]{:S(2)}) %collective-permute-start.7) | collective-permute-done | bytes 221216 | tf_op jit(solution)/shard_map/ppermute | solution.py:30
  51.7 1.0 %collective-permute-start.10 = (bf16[64,864]{1,0:T(8,128)(2,1)S(1)}, bf16[64,864]{1,0:T(8,128)(2,1)S(1)}, u32[]{:S(2)}, u32[]{:S(2)}) collective-permute-start(bf16[64,864]{1,0:T(8,128)(2,1)S(1)} %get-tuple-element.48), channel_id=1, source_target_pairs={{0,8},{1,12},{4,9},{5,13},{8,0},{9,4},{12,1},{13,5},{2,10},{3,14},... | collective-permute-start | bytes 331784 | tf_op jit(solution)/shard_map/ppermute | solution.py:430
  52.7 1.9 %collective-permute-start.11 = (bf16[64,864]{1,0:T(8,128)(2,1)S(1)}, bf16[64,864]{1,0:T(8,128)(2,1)S(1)}, u32[]{:S(2)}, u32[]{:S(2)}) collective-permute-start(bf16[64,864]{1,0:T(8,128)(2,1)S(1)} %get-tuple-element.47), channel_id=1, source_target_pairs={{0,9},{1,13},{4,8},{5,12},{8,1},{9,5},{12,0},{13,4},{2,11},{3,15},... | collective-permute-start | bytes 331784 | tf_op jit(solution)/shard_map/ppermute | solution.py:430
  54.6 0.7 %collective-permute-start.8 = (bf16[64,864]{1,0:T(8,128)(2,1)S(1)}, bf16[64,864]{1,0:T(8,128)(2,1)S(1)}, u32[]{:S(2)}, u32[]{:S(2)}) collective-permute-start(bf16[64,864]{1,0:T(8,128)(2,1)S(1)} %get-tuple-element.50), channel_id=1, source_target_pairs={{0,0},{1,4},{4,1},{5,5},{8,8},{9,12},{12,9},{13,13},{2,2},{3,6},{6... | collective-permute-start | bytes 331784 | tf_op jit(solution)/shard_map/ppermute | solution.py:430
  55.3 2.1 %collective-permute-start.9 = (bf16[64,864]{1,0:T(8,128)(2,1)S(1)}, bf16[64,864]{1,0:T(8,128)(2,1)S(1)}, u32[]{:S(2)}, u32[]{:S(2)}) collective-permute-start(bf16[64,864]{1,0:T(8,128)(2,1)S(1)} %get-tuple-element.49), channel_id=1, source_target_pairs={{0,1},{1,5},{4,0},{5,4},{8,9},{9,13},{12,8},{13,12},{2,3},{3,7},{6... | collective-permute-start | bytes 331784 | tf_op jit(solution)/shard_map/ppermute | solution.py:430
  57.4 5.7 %collective-permute-done.10.refs_2_ = bf16[64,864]{1,0:T(8,128)(2,1)S(1)} collective-permute-done((bf16[64,864]{1,0:T(8,128)(2,1)S(1)}, bf16[64,864]{1,0:T(8,128)(2,1)S(1)}, u32[]{:S(2)}, u32[]{:S(2)}) %collective-permute-start.10) | collective-permute-done | bytes 110624 | tf_op jit(solution)/shard_map/ppermute | solution.py:430
  63.1 1.8 %collective-permute-done.9.refs_1_ = bf16[64,864]{1,0:T(8,128)(2,1)S(1)} collective-permute-done((bf16[64,864]{1,0:T(8,128)(2,1)S(1)}, bf16[64,864]{1,0:T(8,128)(2,1)S(1)}, u32[]{:S(2)}, u32[]{:S(2)}) %collective-permute-start.9) | collective-permute-done | bytes 110624 | tf_op jit(solution)/shard_map/ppermute | solution.py:430
  64.9 1.2 %sum.1 = f32[1728,32]{1,0:T(8,128)} custom-call(bf16[64,864]{1,0:T(8,128)(2,1)S(1)} %collective-permute-done.8.refs_0_, bf16[64,864]{1,0:T(8,128)(2,1)S(1)} %collective-permute-done.9.refs_1_, bf16[64,864]{1,0:T(8,128)(2,1)S(1)} %collective-permute-done.10.refs_2_, bf16[64,864]{1,0:T(8,128)(2,1)S(1)} %collective-permute-done.11.refs_3_), custom_call_target="tpu_custom_call" | custom-call | flops 1048576 | bytes 1048576 | tf_op jit(solution)/shard_map/sum/pallas_call | solution.py:328
  (24 shorter events, 0.3 us)
Async XLA Ops:
  0.0 1.0 %copy-start = (f32[3,3,3,2,2048]{4,3,2,1,0:T(2,128)S(1)}, f32[3,3,3,2,2048]{4,3,2,1,0:T(2,128)}, u32[]{:S(2)}) copy-start(f32[3,3,3,2,2048]{4,3,2,1,0:T(2,128)} %param.4) | copy-start | bytes 1327108
  1.0 1.4 %copy-start.2 = (f32[32,3,2,2048]{3,2,1,0:T(2,128)S(1)}, f32[32,3,2,2048]{3,2,1,0:T(2,128)}, u32[]{:S(2)}) copy-start(f32[32,3,2,2048]{3,2,1,0:T(2,128)} %param.3) | copy-start | bytes 4718596
  2.4 15.2 %copy-start.5 = (s32[27,3]{0,1:T(4,128)S(1)}, s32[27,3]{0,1:T(4,128)}, u32[]{:S(2)}) copy-start(s32[27,3]{0,1:T(4,128)} %param.5) | copy-start | bytes 976
  2.4 15.3 %copy-start.1 = (f32[3,3,3,2,2048]{4,3,2,1,0:T(2,128)S(1)}, f32[3,3,3,2,2048]{4,3,2,1,0:T(2,128)}, u32[]{:S(2)}) copy-start(f32[3,3,3,2,2048]{4,3,2,1,0:T(2,128)} %param.4) | copy-start | bytes 1327108
  4.4 24.3 %collective-permute-start.2 = (bf16[6,32,2048]{2,1,0:T(8,128)(2,1)}, bf16[6,32,2048]{2,1,0:T(8,128)(2,1)}, u32[]{:S(2)}, u32[]{:S(2)}) collective-permute-start(bf16[6,32,2048]{2,1,0:T(8,128)(2,1)} %get-tuple-element.42.refs_0_), channel_id=1, source_target_pairs={{0,2},{2,0},{1,3},{3,1},{4,6},{6,4},{5,7},{7,5},{8,10},{10,8},{9,1... | collective-permute-start | bytes 2359304 | tf_op jit(solution)/shard_map/ppermute | solution.py:30
  7.3 13.0 %collective-permute-start = (bf16[6,32,512]{2,1,0:T(8,128)(2,1)}, bf16[6,32,512]{2,1,0:T(8,128)(2,1)S(1)}, u32[]{:S(2)}, u32[]{:S(2)}) collective-permute-start(bf16[6,32,512]{2,1,0:T(8,128)(2,1)} %get-tuple-element.29), channel_id=1, source_target_pairs={{0,12},{4,0},{8,4},{12,8},{1,13},{5,1},{9,5},{13,9},{2,14},{6,2},{... | collective-permute-start | bytes 589832 | tf_op jit(solution)/shard_map/ppermute | solution.py:30
  10.9 10.3 %collective-permute-start.1 = (bf16[6,32,512]{2,1,0:T(8,128)(2,1)}, bf16[6,32,512]{2,1,0:T(8,128)(2,1)S(1)}, u32[]{:S(2)}, u32[]{:S(2)}) collective-permute-start(bf16[6,32,512]{2,1,0:T(8,128)(2,1)} %get-tuple-element.30), channel_id=1, source_target_pairs={{0,4},{4,8},{8,12},{12,0},{1,5},{5,9},{9,13},{13,1},{2,6},{6,10},{... | collective-permute-start | bytes 589832 | tf_op jit(solution)/shard_map/ppermute | solution.py:30
  13.7 12.0 %collective-permute-start.3 = (bf16[6,32,512]{2,1,0:T(8,128)(2,1)}, bf16[6,32,512]{2,1,0:T(8,128)(2,1)}, u32[]{:S(2)}, u32[]{:S(2)}) collective-permute-start(bf16[6,32,512]{2,1,0:T(8,128)(2,1)} %get-tuple-element.33), channel_id=1, source_target_pairs={{0,12},{4,0},{8,4},{12,8},{1,13},{5,1},{9,5},{13,9},{2,14},{6,2},{... | collective-permute-start | bytes 589832 | tf_op jit(solution)/shard_map/ppermute | solution.py:30
  17.6 11.2 %collective-permute-start.4 = (bf16[6,32,512]{2,1,0:T(8,128)(2,1)}, bf16[6,32,512]{2,1,0:T(8,128)(2,1)}, u32[]{:S(2)}, u32[]{:S(2)}) collective-permute-start(bf16[6,32,512]{2,1,0:T(8,128)(2,1)} %get-tuple-element.34), channel_id=1, source_target_pairs={{0,4},{4,8},{8,12},{12,0},{1,5},{5,9},{9,13},{13,1},{2,6},{6,10},{... | collective-permute-start | bytes 589832 | tf_op jit(solution)/shard_map/ppermute | solution.py:30
  20.3 5.3 %copy-start.3 = (f32[2,27,2048]{2,1,0:T(8,128)}, f32[2,27,2048]{2,1,0:T(8,128)S(1)}, u32[]{:S(2)}) copy-start(f32[2,27,2048]{2,1,0:T(8,128)S(1)} %get-tuple-element.40.table_ref) | copy-start | bytes 1327108
  25.6 4.5 %collective-permute-start.5 = (bf16[6,32,2048]{2,1,0:T(8,128)(2,1)}, bf16[6,32,2048]{2,1,0:T(8,128)(2,1)S(1)}, u32[]{:S(2)}, u32[]{:S(2)}) collective-permute-start(bf16[6,32,2048]{2,1,0:T(8,128)(2,1)} %get-tuple-element.42.refs_0_), channel_id=1, source_target_pairs={{0,1},{1,0},{2,3},{3,2},{4,5},{5,4},{6,7},{7,6},{8,9},{9,8},{10,11... | collective-permute-start | bytes 2359304 | tf_op jit(solution)/shard_map/ppermute | solution.py:30
  28.7 2.6 %collective-permute-start.6 = (bf16[6,32,2048]{2,1,0:T(8,128)(2,1)}, bf16[6,32,2048]{2,1,0:T(8,128)(2,1)}, u32[]{:S(2)}, u32[]{:S(2)}) collective-permute-start(bf16[6,32,2048]{2,1,0:T(8,128)(2,1)} %collective-permute-done.2.refs_1_), channel_id=1, source_target_pairs={{0,1},{1,0},{2,3},{3,2},{4,5},{5,4},{6,7},{7,6},{8,9},{9,8},{10,11... | collective-permute-start | bytes 2359304 | tf_op jit(solution)/shard_map/ppermute | solution.py:30
  28.8 2.6 %copy-start.4 = (f32[2,27,2048]{2,1,0:T(8,128)S(1)}, f32[2,27,2048]{2,1,0:T(8,128)}, u32[]{:S(2)}) copy-start(f32[2,27,2048]{2,1,0:T(8,128)} %copy-done.3) | copy-start | bytes 1327108
  43.9 7.7 %collective-permute-start.7 = (bf16[2,64,864]{2,1,0:T(8,128)(2,1)S(1)}, bf16[2,64,864]{2,1,0:T(8,128)(2,1)S(1)}, u32[]{:S(2)}, u32[]{:S(2)}) collective-permute-start(bf16[2,64,864]{2,1,0:T(8,128)(2,1)S(1)} %get-tuple-element.43), channel_id=1, source_target_pairs={{0,2},{2,0},{1,3},{3,1},{4,6},{6,4},{5,7},{7,5},{8,10},{10,8},{9,1... | collective-permute-start | bytes 663560 | tf_op jit(solution)/shard_map/ppermute | solution.py:30
  51.7 11.3 %collective-permute-start.10 = (bf16[64,864]{1,0:T(8,128)(2,1)S(1)}, bf16[64,864]{1,0:T(8,128)(2,1)S(1)}, u32[]{:S(2)}, u32[]{:S(2)}) collective-permute-start(bf16[64,864]{1,0:T(8,128)(2,1)S(1)} %get-tuple-element.48), channel_id=1, source_target_pairs={{0,8},{1,12},{4,9},{5,13},{8,0},{9,4},{12,1},{13,5},{2,10},{3,14},... | collective-permute-start | bytes 331784 | tf_op jit(solution)/shard_map/ppermute | solution.py:430
  52.7 10.4 %collective-permute-start.11 = (bf16[64,864]{1,0:T(8,128)(2,1)S(1)}, bf16[64,864]{1,0:T(8,128)(2,1)S(1)}, u32[]{:S(2)}, u32[]{:S(2)}) collective-permute-start(bf16[64,864]{1,0:T(8,128)(2,1)S(1)} %get-tuple-element.47), channel_id=1, source_target_pairs={{0,9},{1,13},{4,8},{5,12},{8,1},{9,5},{12,0},{13,4},{2,11},{3,15},... | collective-permute-start | bytes 331784 | tf_op jit(solution)/shard_map/ppermute | solution.py:430
  54.6 8.4 %collective-permute-start.8 = (bf16[64,864]{1,0:T(8,128)(2,1)S(1)}, bf16[64,864]{1,0:T(8,128)(2,1)S(1)}, u32[]{:S(2)}, u32[]{:S(2)}) collective-permute-start(bf16[64,864]{1,0:T(8,128)(2,1)S(1)} %get-tuple-element.50), channel_id=1, source_target_pairs={{0,0},{1,4},{4,1},{5,5},{8,8},{9,12},{12,9},{13,13},{2,2},{3,6},{6... | collective-permute-start | bytes 331784 | tf_op jit(solution)/shard_map/ppermute | solution.py:430
  55.3 9.6 %collective-permute-start.9 = (bf16[64,864]{1,0:T(8,128)(2,1)S(1)}, bf16[64,864]{1,0:T(8,128)(2,1)S(1)}, u32[]{:S(2)}, u32[]{:S(2)}) collective-permute-start(bf16[64,864]{1,0:T(8,128)(2,1)S(1)} %get-tuple-element.49), channel_id=1, source_target_pairs={{0,1},{1,5},{4,0},{5,4},{8,9},{9,13},{12,8},{13,12},{2,3},{3,7},{6... | collective-permute-start | bytes 331784 | tf_op jit(solution)/shard_map/ppermute | solution.py:430
